TPU v7x, 32 devices: a whole 2x2x4 slice. The times are simulated.
32 devices in a mesh: gene: 4 (over y, x), bin: 8 (over z, core).
Axes of the slice: x: 2, y: 2, z: 4, core: 2. Of those that a mesh axis runs over, the one named last changes fastest.
Arguments:
- counts: bfloat16 [24576, 18432], P('bin', 'gene'), may hold values from 2 to 80
- factors: float32 [24576, 256], P('bin'), may hold values from 0.01 to 1
- loadings: float32 [256, 18432], P(None, 'gene'), may hold values from 0.01 to 1
- position: int32 [24576], P('bin'), may hold values from 0 to 24575, as said below
- edge_codes: int32 [96, 256], P('bin'), may hold values from 1 to 15
Outputs:
- factors_new: float32 [24576, 256], P('bin')
- loadings_new: float32 [256, 18432], P(None, 'gene')
Inputs may be any that keep to these rules, and one draw needn't show every extreme that they name: Each grid position is named by exactly one barcode. The barcodes of one index s of bin (rows s * 3072 on) fall in 8 aligned groups of 384; group t holds positions in grid rows t * 12 to (t + 1) * 12 - 1, 384 from every such index.
All inputs are finite; a program needn't handle non-finite values.
Results may differ from a plain program's by a relative error of at most 0.0003.
Values sent between devices are 32-bit elements; how exact they have to be, the bound alone decides.
No kernel may reach another device: no remote copies, remote signals or barrier semaphores. Data moves between devices by JAX's collectives and lax.ppermute only.
A program may use at most 128 MiB of HBM per device.

v0:
```python
import jax
import jax.numpy as jnp
from jax import lax
from jax.experimental import pallas as pl
from jax.experimental.pallas import tpu as pltpu
from jax.sharding import PartitionSpec as P

K = 256
G = 18432
PENALTY = float(G * K) / 64.0
EXTRA = 8
HALVES = 2
STEP = 512
READS = 4
MIB = 1024 * 1024
MINOR = (((1,), (1,)), ((), ()))
PLAIN = (((1,), (0,)), ((), ()))
F32 = jnp.float32
BF16 = jnp.bfloat16
ANY_SPEC = pl.BlockSpec(memory_space=pl.ANY)
VMEM_SPEC = pl.BlockSpec(memory_space=pltpu.VMEM)
SMEM_SPEC = pl.BlockSpec(memory_space=pltpu.SMEM)


def dot(a, b, dims, precision=None):
    return lax.dot_general(a, b, dims, precision=precision, preferred_element_type=F32)


def kernel_call(body, out_shape, us, limit=10, **kw):
    return pl.pallas_call(
        body,
        out_shape=out_shape,
        compiler_params=pltpu.CompilerParams(vmem_limit_bytes=limit * MIB),
        cost_estimate=pl.CostEstimate(flops=0, bytes_accessed=int(us * 3.69e6), transcendentals=0),
        **kw,
    )


def shape(*dims, dtype=F32):
    return jax.ShapeDtypeStruct(dims, dtype)


def pack(factors, position, me, width, bins):
    rows, width_all = factors.shape
    group = rows // bins
    lanes = 128 if width_all % 128 == 0 and 128 % width == 0 else width_all

    def body(me_ref, fac_ref, pos_ref, out_ref, turned):
        turned[...] = fac_ref[...].T
        first = pl.multiple_of(lax.rem(me_ref[0] * width, lanes), width)
        out_ref[0, :width, :] = turned[pl.ds(first, width), :]
        out_ref[0, width:, :] = jnp.broadcast_to(pos_ref[0], (EXTRA, group))

    grid_spec = pltpu.PrefetchScalarGridSpec(
        num_scalar_prefetch=1,
        grid=(bins,),
        in_specs=[
            pl.BlockSpec((group, lanes), lambda t, m: (t, m[0] * width // lanes)),
            pl.BlockSpec((1, 1, group), lambda t, m: (t, 0, 0)),
        ],
        out_specs=pl.BlockSpec((1, width + EXTRA, group), lambda t, m: (t, 0, 0)),
        scratch_shapes=[pltpu.VMEM((lanes, group), F32)],
    )
    return kernel_call(
        body, shape(bins, width + EXTRA, group), 3, grid_spec=grid_spec
    )(me, factors, position.astype(F32).reshape(bins, 1, group))


def to_grid(got, edge_codes, bin_me, token):
    bins, wide, group = got.shape
    width = wide - EXTRA
    grid_rows, grid_cols = edge_codes.shape
    rows = bins * group
    per = 4

    def body(me_ref, got_ref, code_ref, _, grid_ref, first_ref, last_ref, cell_ref, masked):
        block = jnp.concatenate([got_ref[s] for s in range(bins)], axis=1)
        cell = block[width : width + 1].astype(jnp.int32) - me_ref[0] * rows
        cell_ref[...] = cell
        at_row, at_col = cell // grid_cols, cell % grid_cols
        col_hot = jnp.where(
            lax.broadcasted_iota(jnp.int32, (grid_cols, rows), 0) == at_col, 1.0, 0.0
        ).astype(BF16)
        values = block[:width]
        high = values.astype(BF16)
        both = jnp.concatenate([high, (values - high.astype(F32)).astype(BF16)], axis=0)
        scale = code_ref[...].astype(F32) / 8.0
        for r in range(grid_rows):
            at = r % per * 2 * width
            if at == 0:
                for i in range(per):
                    mask = jnp.where(at_row == r + i, 1.0, 0.0).astype(BF16)
                    masked[i * 2 * width : (i + 1) * 2 * width, :] = both * mask
                placed = dot(masked[...], col_hot, MINOR)
            line = placed[at : at + width] + placed[at + width : at + 2 * width]
            row_scale = scale[r : r + 1]
            weighted = jnp.concatenate(
                [line * row_scale, jnp.broadcast_to(row_scale, (EXTRA, grid_cols))], axis=0
            )
            grid_ref[r] = weighted
            if r == 0:
                first_ref[...] = weighted
            if r == grid_rows - 1:
                last_ref[...] = weighted

    return kernel_call(
        body,
        (
            shape(grid_rows, wide, grid_cols),
            shape(wide, grid_cols),
            shape(wide, grid_cols),
            shape(1, rows, dtype=jnp.int32),
        ),
        3,
        limit=12,
        in_specs=[SMEM_SPEC, VMEM_SPEC, VMEM_SPEC, ANY_SPEC],
        out_specs=(VMEM_SPEC,) * 4,
        scratch_shapes=[pltpu.VMEM((per * 2 * width, rows), BF16)],
    )(bin_me, got, edge_codes, token)


def from_grid(grid, above, below, cell, edge_codes, bins, token):
    grid_rows, wide, grid_cols = grid.shape
    rows = cell.shape[1]
    group = rows // bins

    def body(grid_ref, above_ref, below_ref, cell_ref, code_ref, _, out_ref, halves):
        scale = code_ref[...].astype(F32) / 8.0
        lane = lax.broadcasted_iota(jnp.int32, (wide, grid_cols), 1)
        for r in range(grid_rows):
            here = grid_ref[r]
            upper = above_ref[...] if r == 0 else grid_ref[r - 1]
            lower = below_ref[...] if r == grid_rows - 1 else grid_ref[r + 1]
            left = jnp.where(lane == 0, 0.0, pltpu.roll(here, 1, 1))
            right = jnp.where(lane == grid_cols - 1, 0.0, pltpu.roll(here, grid_cols - 1, 1))
            value = scale[r : r + 1] * (left + right + 0.5 * (upper + lower))
            high = value.astype(BF16)
            halves[r * wide : (r + 1) * wide, :grid_cols] = high
            halves[r * wide : (r + 1) * wide, grid_cols:] = (value - high.astype(F32)).astype(BF16)
        cell = cell_ref[...]
        at_row, at_col = cell // grid_cols, cell % grid_cols
        for s in range(bins // 2):
            lo, hi = 2 * s * group, (2 * s + 2) * group
            hot = jnp.where(
                lax.broadcasted_iota(jnp.int32, (grid_cols, hi - lo), 0) == at_col[:, lo:hi], 1.0, 0.0
            ).astype(BF16)
            lines = dot(halves[...], jnp.concatenate([hot, hot], axis=0), PLAIN)
            row_here = at_row[:, lo:hi]
            total = jnp.zeros((wide, hi - lo), F32)
            for r in range(grid_rows):
                total = total + jnp.where(row_here == r, lines[r * wide : (r + 1) * wide], 0.0)
            out_ref[2 * s] = total[:, :group]
            out_ref[2 * s + 1] = total[:, group:]

    return kernel_call(
        body,
        shape(bins, wide, group),
        4,
        in_specs=[VMEM_SPEC] * 5 + [ANY_SPEC],
        out_specs=VMEM_SPEC,
        scratch_shapes=[pltpu.VMEM((grid_rows * wide, 2 * grid_cols), BF16)],
    )(grid, above, below, cell, edge_codes, token)


def numer_part(counts, loadings, me, genes_n, token):
    rows, genes = counts.shape
    width_all = loadings.shape[0]
    width = width_all // genes_n
    steps = rows // STEP
    side = genes // 2

    def body(me_ref, left_ref, right_ref, load_ref, _, *rest):
        outs, (load_f, load_bf, load_t, turned, sems) = rest[:genes_n], rest[genes_n:]
        at = pl.program_id(0)
        firsts = [pl.multiple_of((k ^ me_ref[0]) * width, width) for k in range(genes_n)]

        @pl.when(at == 0)
        def _():
            reads = [
                pltpu.make_async_copy(
                    load_ref.at[pl.ds(first, width), :], load_f.at[pl.ds(k * width, width), :], sems.at[k]
                )
                for k, first in enumerate(firsts)
            ]
            for copy in reads:
                copy.start()
            for copy in reads:
                copy.wait()
            load_bf[...] = load_f[...].astype(BF16)
            load_t[...] = load_bf[...].T

        def put(part):
            for k, out in enumerate(outs):
                out[...] = part[k * width : (k + 1) * width]

        @pl.when(at < steps)
        def _():
            part = dot(left_ref[...], load_t[:side, :], PLAIN)
            put((part + dot(right_ref[...], load_t[side:, :], PLAIN)).T)

        @pl.when(at == steps)
        def _():
            local = dot(load_bf[...], load_t[...], PLAIN)
            for k, first in enumerate(firsts):
                turned[pl.ds(first, width), :] = local[k * width : (k + 1) * width]
            put(jnp.concatenate([turned[...].T, jnp.zeros((width_all, STEP - width_all), F32)], axis=1))

    row_at = lambda i: jnp.minimum(i, steps - 1)
    grid_spec = pltpu.PrefetchScalarGridSpec(
        num_scalar_prefetch=1,
        grid=(steps + 1,),
        in_specs=[
            pl.BlockSpec((STEP, side), lambda i, m: (row_at(i), 0)),
            pl.BlockSpec((STEP, side), lambda i, m: (row_at(i), 1)),
            ANY_SPEC,
            ANY_SPEC,
        ],
        out_specs=(pl.BlockSpec((width, STEP), lambda i, m: (0, i)),) * genes_n,
        scratch_shapes=[
            pltpu.VMEM((width_all, genes), F32),
            pltpu.VMEM((width_all, genes), BF16),
            pltpu.VMEM((genes, width_all), BF16),
            pltpu.VMEM((width_all, width_all), F32),
            pltpu.SemaphoreType.DMA((genes_n,)),
        ],
    )
    return kernel_call(
        body, (shape(width, rows + STEP),) * genes_n, 14, limit=30, grid_spec=grid_spec
    )(me, counts, counts, loadings, token)


def swap(block, axis, bit):
    return lax.ppermute(block, axis, [(i, i ^ bit) for i in range(lax.axis_size(axis))])


def plain_terms(parts, factors, token):
    rows, width_all = factors.shape
    width = parts[0].shape[0]
    half_rows = rows // 2

    def body(*refs):
        n = len(parts)
        fac_ref, _, numer_ref, plain_ref, gram = refs[n:]

        def total(cols):
            out = refs[0][:, cols]
            for ref in refs[1:n]:
                out = out + ref[:, cols]
            return out

        @pl.when(pl.program_id(0) == 0)
        def _():
            gram[...] = total(slice(rows, rows + width_all))
            numer_ref[...] = total(slice(0, rows))

        plain_ref[...] = dot(fac_ref[...], gram[...], MINOR, lax.Precision.HIGHEST).T

    return kernel_call(
        body,
        (shape(width, rows),) * 2,
        60,
        limit=16,
        grid=(2,),
        in_specs=[VMEM_SPEC] * len(parts)
        + [pl.BlockSpec((half_rows, width_all), lambda i: (i, 0)), ANY_SPEC],
        out_specs=(VMEM_SPEC, pl.BlockSpec((width, half_rows), lambda i: (0, i))),
        scratch_shapes=[pltpu.VMEM((width, width_all), F32)],
    )(*parts, factors, token)


def new_factors(payload, back, numer, plain):
    bins, wide, group = payload.shape
    width = wide - EXTRA

    def body(pay_ref, back_ref, numer_ref, plain_ref, out_ref):
        pay = jnp.concatenate([pay_ref[s] for s in range(bins)], axis=1)
        got = jnp.concatenate([back_ref[s] for s in range(bins)], axis=1)
        fac, smooth, degree = pay[:width], got[:width], got[width : width + 1]
        out_ref[...] = (
            fac * (numer_ref[...] + PENALTY * smooth) / (plain_ref[...] + PENALTY * degree * fac)
        )

    return kernel_call(
        body,
        shape(width, bins * group),
        0.02,
        in_specs=[VMEM_SPEC] * 4,
        out_specs=VMEM_SPEC,
    )(payload, back, numer, plain)


def sent_on(blocks, token):
    n = len(blocks)

    def body(*refs):
        for src, dst in zip(refs[:n], refs[n + 1 :]):
            dst[...] = src[...]

    return kernel_call(
        body,
        tuple(shape(*b.shape) for b in blocks),
        0.02,
        in_specs=[VMEM_SPEC] * n + [ANY_SPEC],
        out_specs=(VMEM_SPEC,) * n,
    )(*blocks, token)


def turned_back(blocks, ids, width, me, token):
    rows = blocks[0].shape[1]
    width_all = len(ids) * width
    step = 384
    steps = rows // step

    def body(me_ref, *refs):
        out_ref, _, block = refs[-3:]
        for ref, k in zip(refs, ids):
            block[pl.ds(pl.multiple_of((k ^ me_ref[0]) * width, width), width), :] = ref[...]
        out_ref[...] = block[...].T

    grid_spec = pltpu.PrefetchScalarGridSpec(
        num_scalar_prefetch=1,
        grid=(steps,),
        in_specs=[pl.BlockSpec((width, step), lambda i, m: (0, i))] * len(ids) + [ANY_SPEC],
        out_specs=(pl.BlockSpec((step, width_all), lambda i, m: (i, 0)), VMEM_SPEC),
        scratch_shapes=[pltpu.VMEM((width_all, step), F32)],
    )
    outs = (pltpu.HBM((rows, width_all), F32), shape(8, 128))
    return kernel_call(body, outs, 0.02, limit=8, grid_spec=grid_spec)(me, *blocks, token)


def cross_part(blocks, n_old, counts, half, with_gram, width_all, tokens):
    width, rows = blocks[0].shape
    genes = counts.shape[1]
    cols = genes // HALVES
    step = 384
    steps = cols // step
    n = len(blocks) - n_old
    deep = rows // READS
    use = blocks if with_gram else blocks[n_old:]
    skip = len(use) - n

    def body(*refs):
        outs, fac = refs[-1 - n : -1], refs[-1]
        at = pl.program_id(0)

        @pl.when(at == 0)
        def _():
            for j, ref in enumerate(refs[READS : READS + len(use)]):
                fac[j * width : (j + 1) * width, :] = ref[...].astype(BF16)

        def put(part, where):
            for j, out in enumerate(outs):
                out[:, where] = part[j * width : (j + 1) * width]

        new = lambda i: fac[skip * width :, i * deep : (i + 1) * deep]
        part = dot(new(0), refs[0][...], PLAIN)
        for i in range(1, READS):
            part = part + dot(new(i), refs[i][...], PLAIN)
        put(part, pl.ds(pl.multiple_of(at * step, step), step))

        if with_gram:

            @pl.when(at == steps - 1)
            def _():
                near = dot(fac[skip * width :, :], fac[...], MINOR)
                if near.shape[1] < width_all:
                    gap = jnp.zeros((near.shape[0], width_all - near.shape[1]), F32)
                    near = jnp.concatenate([near, gap], axis=1)
                put(near, slice(cols, cols + width_all))

    read = lambda i: pl.BlockSpec((deep, step), lambda g: (i, half * steps + g))
    return kernel_call(
        body,
        (shape(width, cols + with_gram * width_all),) * n,
        0.02,
        limit=24,
        grid=(steps,),
        in_specs=[read(i) for i in range(READS)] + [VMEM_SPEC] * len(use) + [ANY_SPEC] * len(tokens),
        out_specs=(VMEM_SPEC,) * n,
        scratch_shapes=[pltpu.VMEM((len(use) * width, rows), BF16)],
    )(*[counts] * READS, *use, *tokens)


def tiny_token(arrays):
    def body(*refs):
        refs[-1][...] = jnp.zeros(refs[-1].shape, F32)

    return kernel_call(
        body, shape(8, 128), 0.02, in_specs=[ANY_SPEC] * len(arrays), out_specs=VMEM_SPEC
    )(*arrays)


def both_cores(parts, came, token):
    n = len(parts)

    def body(*refs):
        for a, b, out in zip(refs[:n], refs[n : 2 * n], refs[2 * n + 1 :]):
            out[...] = a[...] + b[...]

    return kernel_call(
        body,
        tuple(shape(*part.shape) for part in parts),
        0.02,
        in_specs=[VMEM_SPEC] * (2 * n) + [ANY_SPEC],
        out_specs=(VMEM_SPEC,) * n,
    )(*parts, *came, token)


def line_slot(flags, t, chunks, own, come, token):
    line = lax.axis_size("bin") // 2
    places = [q for q in range(line - 1) if 0 <= t - q < chunks]
    hops = [(2 * q, 2 * q + 2) for q in places]
    hops += [(2 * (line - 1 - q) + 1, 2 * (line - 2 - q) + 1) for q in places]
    if t == 0:
        return lax.ppermute(own[0], "bin", hops), token
    arrays = [own[t - q] for q in places]

    def body(flag_ref, come_ref, _, *refs):
        for i, q in enumerate(places):

            @pl.when(flag_ref[2] == q)
            def _():
                value = refs[i][...]
                refs[-1][...] = value if q == 0 else value + come_ref[...]

    send = kernel_call(
        body,
        shape(*come.shape),
        0.02,
        in_specs=[SMEM_SPEC, VMEM_SPEC, ANY_SPEC] + [VMEM_SPEC] * len(arrays),
        out_specs=VMEM_SPEC,
    )(flags, come, token, *arrays)
    return lax.ppermute(send, "bin", hops), send


def line_end(flags, come, token):
    def body(flag_ref, _, *refs):
        out = refs[-1]

        @pl.when(flag_ref[2] == 0)
        def _():
            out[...] = jnp.zeros(out.shape, F32)

        for d in range(len(come)):

            @pl.when(flag_ref[2] == d + 1)
            def _():
                out[...] = refs[d][...]

    end = kernel_call(
        body,
        shape(*come[0].shape),
        0.02,
        in_specs=[SMEM_SPEC, ANY_SPEC] + [VMEM_SPEC] * len(come),
        out_specs=VMEM_SPEC,
    )(flags, token, *come)
    return end, swap(end, "bin", 1)


def shares(loadings, sums, ids, cols, me, token):
    width_all, genes = loadings.shape
    width = width_all // len(ids)
    steps = 6
    step = genes // steps
    arrays = [x for terms in sums for x in terms]

    def body(me_ref, load_ref, *refs):
        out_ref, tiny, load, gram = refs[-4:]
        firsts = [pl.multiple_of((k ^ me_ref[0]) * width, width) for k in ids]

        @pl.when(pl.program_id(0) == 0)
        def _():
            behind = slice(cols, cols + width_all)
            for j in range(len(sums)):
                own, end, other = refs[3 * j : 3 * j + 3]
                gram[j * width : (j + 1) * width, :] = own[:, behind] + (end[:, behind] + other[:, behind])
            low = gram[...]
            row = lax.broadcasted_iota(jnp.int32, low.shape, 0) // width
            col = lax.broadcasted_iota(jnp.int32, low.shape, 1) // width
            gram[...] = jnp.where(col <= row, low, low.T)

        for j, first in enumerate(firsts):
            load[j * width : (j + 1) * width, :] = load_ref[pl.ds(first, width), :]
        value = load[...]
        value = value / dot(gram[...], value, PLAIN, lax.Precision.HIGHEST)
        for j, first in enumerate(firsts):
            out_ref[pl.ds(first, width), :] = value[j * width : (j + 1) * width]

    block = pl.BlockSpec((width_all, step), lambda i, f: (0, i))
    return kernel_call(
        body,
        (shape(width_all, genes), shape(8, 128)),
        0.02,
        limit=12,
        grid_spec=pltpu.PrefetchScalarGridSpec(
            num_scalar_prefetch=1,
            grid=(steps,),
            in_specs=[block] + [VMEM_SPEC] * len(arrays) + [ANY_SPEC],
            out_specs=(block, VMEM_SPEC),
            scratch_shapes=[
                pltpu.VMEM((width_all, step), F32),
                pltpu.VMEM((width_all, width_all), F32),
            ],
        ),
    )(me, loadings, *arrays, token)


def new_loadings(share, parts, k, width, me, before, token):
    width_all, genes = share.shape
    halves = sorted(parts)
    cols = genes // HALVES
    arrays = [x for h in halves for x in parts[h]]

    def body(me_ref, share_ref, _, *refs):
        out_ref = refs[-2]
        at = pl.ds(pl.multiple_of((k ^ me_ref[0]) * width, width), width)
        for i, h in enumerate(halves):
            own, end, other = refs[3 * i : 3 * i + 3]
            here = slice(h * cols, (h + 1) * cols)
            total = own[:, :cols] + (end[:, :cols] + other[:, :cols])
            out_ref[:, i * cols : (i + 1) * cols] = share_ref[at, here] * total

    operands = [me, share, token] + arrays
    specs = [VMEM_SPEC, ANY_SPEC] + [VMEM_SPEC] * len(arrays)
    aliases = {}
    if before is not None:
        operands.append(before)
        specs.append(ANY_SPEC)
        aliases = {len(operands) - 1: 0}
    column = 0 if len(halves) == HALVES else halves[0]
    return kernel_call(
        body,
        (pltpu.HBM((width_all, genes), F32), shape(8, 128)),
        0.02,
        limit=6,
        grid_spec=pltpu.PrefetchScalarGridSpec(
            num_scalar_prefetch=1,
            grid=(1,),
            in_specs=specs,
            out_specs=(
                pl.BlockSpec((width, len(halves) * cols), lambda i, m: (k ^ m[0], column)),
                VMEM_SPEC,
            ),
        ),
        input_output_aliases=aliases,
    )(*operands)


def on_device(counts, factors, loadings, position, edge_codes):
    bins, genes_n = lax.axis_size("bin"), lax.axis_size("gene")
    line = bins // 2
    me, bin_me = lax.axis_index("gene"), lax.axis_index("bin")
    rows, width_all = factors.shape
    width = width_all // genes_n
    scalar = lambda x: jnp.asarray(x, jnp.int32).reshape(1)
    me1, bin1 = scalar(me), scalar(bin_me)
    core, chip = bin1 & 1, bin1 >> 1
    flags = jnp.concatenate([me1, core, jnp.where(core == 0, chip, line - 1 - chip)])
    bits = [1 << b for b in range(genes_n.bit_length() - 1)]

    counts = pltpu.with_memory_space_constraint(counts, pltpu.HBM)
    payload = pack(factors, position, me1, width, bins)
    got = lax.all_to_all(payload, "bin", split_axis=0, concat_axis=0, tiled=True)
    parts = numer_part(
        counts, pltpu.with_memory_space_constraint(loadings, pltpu.HBM), me1, genes_n, payload
    )
    parts = [parts[0]] + [swap(parts[k], "gene", k) for k in range(1, genes_n)]
    grid, first, last, cell = to_grid(got, edge_codes, bin1, parts[0])
    above = lax.ppermute(last, "bin", [(i, i + 1) for i in range(bins - 1)])
    below = lax.ppermute(first, "bin", [(i + 1, i) for i in range(bins - 1)])
    smooth = from_grid(grid, above, below, cell, edge_codes, bins, grid)
    back = lax.all_to_all(smooth, "bin", split_axis=0, concat_axis=0, tiled=True)
    numer, plain = plain_terms(parts, factors, smooth)
    own_block = new_factors(payload, back, numer, plain)

    ids = sorted(range(genes_n), key=lambda k: (bin(k).count("1"), k))
    groups = [[k for k in ids if bin(k).count("1") == n] for n in range(len(bits) + 1)]
    chunks = len(ids)
    blocks = {0: own_block}
    for k in bits:
        blocks[k] = swap(own_block, "gene", k)

    def come_on(group, token):
        outs = sent_on([blocks[k & (k - 1)] for k in group], token)
        for k, out in zip(group, outs):
            blocks[k] = swap(out, "gene", k & -k)
        return outs[-1]

    pending = [[None] * len(groups) for _ in range(HALVES)]
    own = [{} for _ in range(HALVES)]
    come = [[] for _ in range(HALVES)]
    ends = [{} for _ in range(HALVES)]

    def product(g, half, *tokens):
        upto = ids.index(groups[g][-1]) + 1
        n_old = upto - len(groups[g])
        parts = cross_part(
            [blocks[k] for k in ids[:upto]], n_old, counts, half, half == 0, width_all, tokens
        )
        pending[half][g] = (parts, [swap(part, "bin", 1) for part in parts])
        return parts[-1]

    def own_chunks(g, half, token):
        arrays = both_cores(*pending[half][g], token)
        for k, array in zip(groups[g], arrays):
            own[half][ids.index(k)] = array
        return arrays[-1]

    def slot(half, t, token):
        before = come[half][-1] if come[half] else None
        got, token = line_slot(flags, t, chunks, own[half], before, token)
        come[half].append(got)
        return token

    def end(c, half, token):
        ends[half][c] = line_end(flags, come[half][c : c + line - 1], token)
        return ends[half][c][0]

    def final(c, before, token, halves=range(HALVES)):
        sums = {h: (own[h][c],) + ends[h][c] for h in halves}
        return new_loadings(share, sums, ids[c], width, me1, before, token)

    def both(step, *args):
        nonlocal token
        for half in range(HALVES):
            token = step(*args, half, token)

    def awaited(arrays, token):
        return tiny_token(list(arrays) + [token])

    token = own_block
    both(product, 0)
    token = awaited([blocks[k] for k in bits], token)
    if len(groups) > 2:
        token = come_on(groups[2], token)
    for half in range(HALVES):
        token = own_chunks(0, half, token)
        token = slot(half, 0, token)
    both(product, 1)
    firsts = {ids.index(group[0]): g for g, group in enumerate(groups)}
    last_slot = chunks + line - 3
    for t in range(1, last_slot + 1):
        if t in firsts:
            arrived = [come[half][-1] for half in range(HALVES)]
            if firsts[t] + 1 < len(groups):
                arrived += [blocks[k] for k in groups[firsts[t] + 1]]
            token = awaited(arrived, token)
        for half in range(HALVES):
            if t in firsts:
                token = own_chunks(firsts[t], half, token)
            token = slot(half, t, token)
        g = firsts.get(t, len(groups)) + 1
        if g < len(groups):
            both(product, g)
            if g + 1 < len(groups):
                token = come_on(groups[g + 1], token)
        if t == chunks - 1:
            factors_new, token = turned_back([blocks[k] for k in ids], ids, width, me1, token)
        c = t - (line - 1)
        if c - 1 in ends[0]:
            token = awaited([ends[half][c - 1][1] for half in range(HALVES)], token)
        if 0 <= c < chunks:
            both(end, c)
    share = loadings_new = None
    for c in range(chunks):
        if c not in ends[0]:
            both(end, c)
    sums = [(own[0][c],) + ends[0][c] for c in range(chunks)]
    share, token = shares(loadings, sums, ids, counts.shape[1] // HALVES, me1, token)
    for c in range(chunks - 1):
        loadings_new, token = final(c, loadings_new, token)
    for half in range(HALVES):
        loadings_new, token = final(chunks - 1, loadings_new, token, [half])
    return factors_new, loadings_new


def solution(mesh):
    placed = (P("bin", "gene"), P("bin", None), P(None, "gene"), P("bin"), P("bin", None))
    return jax.shard_map(
        on_device,
        mesh=mesh,
        in_specs=placed,
        out_specs=(P("bin", None), P(None, "gene")),
        check_vma=False,
    )
```

profile of v0, /device:TPU:0, one launch (start us, length us, event | category | flops | bytes accessed | tf_op | source)
XLA Modules:
  0.0 252.5 jit_solution(16014094806784079250)
XLA Ops:
  1.3 1.9 copy-done
  3.2 3.4 %shard_map.68._.pay_ref = f32[8,72,384]{2,1,0:T(8,128)} custom-call(s32[1]{0:T(128)} %bitcast.me_ref, f32[3072,256]{1,0:T(8,128)S(1)} %copy-done, f32[8,1,384]{2,1,0:T(1,128)S(1)} %bitcast.5), custom_call_target="tpu_custom_call" | custom-call | bytes 11070000 | tf_op jit(solution)/shard_map/pallas_call | solution.py:64
  6.6 6.3 %all-to-all-start = ((f32[8,72,384]{2,1,0:T(8,128)}), f32[8,72,384]{2,1,0:T(8,128)}, u32[]{:S(2)}, u32[]{:S(2)}) async-start(f32[8,72,384]{2,1,0:T(8,128)} %shard_map.68._.pay_ref), calls=%async_computation | async-start | bytes 1769472 | tf_op jit(solution)/shard_map/all_to_all | solution.py:563
  13.0 18.2 %shard_map.69 = (f32[64,3584]{1,0:T(8,128)S(1)}, f32[64,3584]{1,0:T(8,128)S(1)}, f32[64,3584]{1,0:T(8,128)S(1)}, f32[64,3584]{1,0:T(8,128)S(1)}) custom-call(s32[1]{0:T(128)} %bitcast.me_ref, bf16[3072,4608]{1,0:T(8,128)(2,1)} %refs_3_.11, bf16[3072,4608]{1,0:T(8,128)(2,1)} %refs_3_.11, f32[256,4608]{1,0:T(8,128)} %load_ref.3, f32[8,72,384]{2,1,0:T(8,128)} %shard_map.68._.pay_ref), custom_call_target="tpu_custom_call" | custom-call | bytes 51660000 | tf_op jit(solution)/shard_map/pallas_call | solution.py:227
  34.9 1.2 all-to-all-done.got_ref
  36.1 1.2 copy-done.5
  37.3 3.8 %shard_map.70 = (f32[12,72,256]{2,1,0:T(8,128)S(1)}, f32[72,256]{1,0:T(8,128)S(1)}, f32[72,256]{1,0:T(8,128)S(1)}, s32[1,3072]{1,0:T(1,128)S(1)}) custom-call(s32[1]{0:T(128)} %bitcast.2.me_ref, f32[8,72,384]{2,1,0:T(8,128)} %all-to-all-done.got_ref, s32[12,256]{1,0:T(8,128)S(1)} %copy-done.11, f32[64,3584]{1,0:T(8,128)S(1)} %copy-done.5), custom_call_target="tpu_custom_call" | custom-call | bytes 11070000 | tf_op jit(solution)/shard_map/pallas_call | solution.py:106
  41.2 1.7 collective-permute-start
  42.9 1.3 collective-permute-start.1
  44.2 2.6 %collective-permute-done.1.below_ref = f32[72,256]{1,0:T(8,128)S(1)} collective-permute-done((f32[72,256]{1,0:T(8,128)S(1)}, f32[72,256]{1,0:T(8,128)S(1)}, u32[]{:S(2)}, u32[]{:S(2)}) %collective-permute-start.1) | collective-permute-done | bytes 73760 | tf_op jit(solution)/shard_map/ppermute | solution.py:570
  46.8 3.2 %shard_map.71.refs_5_ = f32[8,72,384]{2,1,0:T(8,128)S(1)} custom-call(f32[12,72,256]{2,1,0:T(8,128)S(1)} %get-tuple-element.34.grid_ref._, f32[72,256]{1,0:T(8,128)S(1)} %collective-permute-done.above_ref, f32[72,256]{1,0:T(8,128)S(1)} %collective-permute-done.1.below_ref, s32[1,3072]{1,0:T(1,128)S(1)} %get-tuple-element.37.cell_ref, ...), custom_call_target="tpu_custom_call" | custom-call | bytes 14760000 | tf_op jit(solution)/shard_map/pallas_call | solution.py:155
  51.0 6.3 %all-to-all-start.1 = ((f32[8,72,384]{2,1,0:T(8,128)}), f32[8,72,384]{2,1,0:T(8,128)}, u32[]{:S(2)}, u32[]{:S(2)}) async-start(f32[8,72,384]{2,1,0:T(8,128)} %copy-done.2), calls=%async_computation.1 | async-start | bytes 1769472 | tf_op jit(solution)/shard_map/all_to_all | solution.py:572
  57.2 1.5 collective-permute-start.2
  58.7 1.5 collective-permute-start.3
  60.7 19.9 %collective-permute-done.2.refs_1_ = f32[64,3584]{1,0:T(8,128)S(1)} collective-permute-done((f32[64,3584]{1,0:T(8,128)}, f32[64,3584]{1,0:T(8,128)S(1)}, u32[]{:S(2)}, u32[]{:S(2)}) %collective-permute-start.2) | collective-permute-done | bytes 917536 | tf_op jit(solution)/shard_map/ppermute | solution.py:233
  80.6 21.0 %collective-permute-done.3.refs_2_ = f32[64,3584]{1,0:T(8,128)S(1)} collective-permute-done((f32[64,3584]{1,0:T(8,128)}, f32[64,3584]{1,0:T(8,128)S(1)}, u32[]{:S(2)}, u32[]{:S(2)}) %collective-permute-start.3) | collective-permute-done | bytes 917536 | tf_op jit(solution)/shard_map/ppermute | solution.py:233
  101.6 1.2 copy-done.3
  102.8 1.2 copy-done.6
  104.0 3.1 %shard_map.72 = (f32[64,3072]{1,0:T(8,128)S(1)}, f32[64,3072]{1,0:T(8,128)S(1)}) custom-call(f32[64,3584]{1,0:T(8,128)S(1)} %copy-done.6, f32[64,3584]{1,0:T(8,128)S(1)} %collective-permute-done.2.refs_1_, f32[64,3584]{1,0:T(8,128)S(1)} %collective-permute-done.3.refs_2_, f32[64,3584]{1,0:T(8,128)S(1)} %collective-permute-done.4.refs_3_, ...), custom_call_target="tpu_custom_call" | custom-call | bytes 221400000 | tf_op jit(solution)/shard_map/pallas_call | solution.py:258
  111.1 1.6 shard_map.73.refs_4_.refs_5_.refs_0_
  112.7 1.2 collective-permute-start.5
  114.8 7.8 %shard_map.74.refs_5_.refs_0_ = f32[64,2560]{1,0:T(8,128)S(1)} custom-call(bf16[3072,4608]{1,0:T(8,128)(2,1)} %refs_3_.11, bf16[3072,4608]{1,0:T(8,128)(2,1)} %refs_3_.11, bf16[3072,4608]{1,0:T(8,128)(2,1)} %refs_3_.11, bf16[3072,4608]{1,0:T(8,128)(2,1)} %refs_3_.11, f32[64,3072]{1,0:T(8,128)S(1)} %shard_map.73.refs_4_.refs_5_.refs_0_, ...), custom_call_target="tpu_custom_call" | custom-call | bytes 73800 | tf_op jit(solution)/shard_map/pallas_call | solution.py:372
  122.7 7.5 %shard_map.75.refs_2_.refs_0_ = f32[64,2304]{1,0:T(8,128)S(1)} custom-call(bf16[3072,4608]{1,0:T(8,128)(2,1)} %refs_3_.11, bf16[3072,4608]{1,0:T(8,128)(2,1)} %refs_3_.11, bf16[3072,4608]{1,0:T(8,128)(2,1)} %refs_3_.11, bf16[3072,4608]{1,0:T(8,128)(2,1)} %refs_3_.11, f32[64,3072]{1,0:T(8,128)S(1)} %shard_map.73.refs_4_.refs_5_.refs_0_, ...), custom_call_target="tpu_custom_call" | custom-call | bytes 73800 | tf_op jit(solution)/shard_map/pallas_call | solution.py:372
  130.7 1.3 collective-permute-done.5.refs_0_.refs_5_.refs_4_.refs_1_
  132.0 1.2 collective-permute-done.6.refs_1_.refs_0_.refs_6_.refs_5_.refs_2_
  133.3 3.0 %collective-permute-start.13 = (f32[64,2560]{1,0:T(8,128)S(1)}, f32[64,2560]{1,0:T(8,128)S(1)}, u32[]{:S(2)}, u32[]{:S(2)}) collective-permute-start(f32[64,2560]{1,0:T(8,128)S(1)} %shard_map.78.refs_2_.refs_1_.refs_0_), channel_id=1, source_target_pairs={{0,2},{7,5},{8,10},{15,13},{16,18},{23,21},{24,26},{31,29}} | collective-permute-start | bytes 1966088 | tf_op jit(solution)/shard_map/ppermute | solution.py:415
  136.4 1.5 collective-permute-start.10
  138.6 8.3 %shard_map.80 = (f32[64,2560]{1,0:T(8,128)S(1)}, f32[64,2560]{1,0:T(8,128)S(1)}) custom-call(bf16[3072,4608]{1,0:T(8,128)(2,1)} %refs_3_.11, bf16[3072,4608]{1,0:T(8,128)(2,1)} %refs_3_.11, bf16[3072,4608]{1,0:T(8,128)(2,1)} %refs_3_.11, bf16[3072,4608]{1,0:T(8,128)(2,1)} %refs_3_.11, f32[64,3072]{1,0:T(8,128)S(1)} %shard_map.73.refs_4_.refs_5_.refs_0_, ...), custom_call_target="tpu_custom_call" | custom-call | bytes 73800 | tf_op jit(solution)/shard_map/pallas_call | solution.py:372
  147.5 7.8 %shard_map.81 = (f32[64,2304]{1,0:T(8,128)S(1)}, f32[64,2304]{1,0:T(8,128)S(1)}) custom-call(bf16[3072,4608]{1,0:T(8,128)(2,1)} %refs_3_.11, bf16[3072,4608]{1,0:T(8,128)(2,1)} %refs_3_.11, bf16[3072,4608]{1,0:T(8,128)(2,1)} %refs_3_.11, bf16[3072,4608]{1,0:T(8,128)(2,1)} %refs_3_.11, f32[64,3072]{1,0:T(8,128)S(1)} %collective-permute-done.5.refs_0_.refs_5_.refs_4_.refs_1_, ...), custom_call_target="tpu_custom_call" | custom-call | bytes 73800 | tf_op jit(solution)/shard_map/pallas_call | solution.py:372
  156.7 1.3 collective-permute-start.17
  158.9 3.2 %collective-permute-start.16 = (f32[64,2304]{1,0:T(8,128)S(1)}, f32[64,2304]{1,0:T(8,128)S(1)}, u32[]{:S(2)}, u32[]{:S(2)}) collective-permute-start(f32[64,2304]{1,0:T(8,128)S(1)} %shard_map.86.refs_8_), channel_id=1, source_target_pairs={{0,2},{2,4},{7,5},{5,3},{8,10},{10,12},{15,13},{13,11},{16,18},{18... | collective-permute-start | bytes 1769480 | tf_op jit(solution)/shard_map/ppermute | solution.py:433
  162.1 8.2 %shard_map.87.refs_5_.refs_0_ = f32[64,2560]{1,0:T(8,128)S(1)} custom-call(bf16[3072,4608]{1,0:T(8,128)(2,1)} %refs_3_.11, bf16[3072,4608]{1,0:T(8,128)(2,1)} %refs_3_.11, bf16[3072,4608]{1,0:T(8,128)(2,1)} %refs_3_.11, bf16[3072,4608]{1,0:T(8,128)(2,1)} %refs_3_.11, f32[64,3072]{1,0:T(8,128)S(1)} %shard_map.73.refs_4_.refs_5_.refs_0_, ...), custom_call_target="tpu_custom_call" | custom-call | bytes 73800 | tf_op jit(solution)/shard_map/pallas_call | solution.py:372
  170.3 7.5 %shard_map.88._.refs_0_ = f32[64,2304]{1,0:T(8,128)S(1)} custom-call(bf16[3072,4608]{1,0:T(8,128)(2,1)} %refs_3_.11, bf16[3072,4608]{1,0:T(8,128)(2,1)} %refs_3_.11, bf16[3072,4608]{1,0:T(8,128)(2,1)} %refs_3_.11, bf16[3072,4608]{1,0:T(8,128)(2,1)} %refs_3_.11, f32[64,3072]{1,0:T(8,128)S(1)} %collective-permute-done.7.refs_2_.refs_7_.refs_4_.refs_3_, ...), custom_call_target="tpu_custom_call" | custom-call | bytes 73800 | tf_op jit(solution)/shard_map/pallas_call | solution.py:372
  178.5 2.0 collective-permute-start.20
  181.2 1.9 collective-permute-start.18
  183.2 11.6 %collective-permute-done.18.refs_1_.come_ref.refs_2_.refs_0_ = f32[64,2304]{1,0:T(8,128)S(1)} collective-permute-done((f32[64,2304]{1,0:T(8,128)S(1)}, f32[64,2304]{1,0:T(8,128)S(1)}, u32[]{:S(2)}, u32[]{:S(2)}) %collective-permute-start.18) | collective-permute-done | bytes 589856 | tf_op jit(solution)/shard_map/ppermute | solution.py:433
  195.5 4.5 %collective-permute-start.25 = (f32[64,2560]{1,0:T(8,128)S(1)}, f32[64,2560]{1,0:T(8,128)S(1)}, u32[]{:S(2)}, u32[]{:S(2)}) collective-permute-start(f32[64,2560]{1,0:T(8,128)S(1)} %shard_map.93.refs_2_), channel_id=1, source_target_pairs={{0,2},{2,4},{4,6},{7,5},{5,3},{3,1},{8,10},{10,12},{12,14},{15,13}... | collective-permute-start | bytes 1966088 | tf_op jit(solution)/shard_map/ppermute | solution.py:433
  200.7 1.9 collective-permute-start.24
  202.6 4.2 %shard_map.96 = (f32[3072,256]{1,0:T(8,128)}, f32[8,128]{1,0:T(8,128)S(1)}) custom-call(s32[1]{0:T(128)} %bitcast.me_ref, f32[64,3072]{1,0:T(8,128)S(1)} %shard_map.73.refs_4_.refs_5_.refs_0_, f32[64,3072]{1,0:T(8,128)S(1)} %collective-permute-done.5.refs_0_.refs_5_.refs_4_.refs_1_, ...), custom_call_target="tpu_custom_call" | custom-call | bytes 73800 | tf_op jit(solution)/shard_map/pallas_call | solution.py:328
  210.6 3.8 %collective-permute-done.24.come_ref.refs_2_.refs_1_.refs_0_ = f32[64,2304]{1,0:T(8,128)S(1)} collective-permute-done((f32[64,2304]{1,0:T(8,128)S(1)}, f32[64,2304]{1,0:T(8,128)S(1)}, u32[]{:S(2)}, u32[]{:S(2)}) %collective-permute-start.24) | collective-permute-done | bytes 589856 | tf_op jit(solution)/shard_map/ppermute | solution.py:433
  218.3 4.2 %collective-permute-start.27 = (f32[64,2304]{1,0:T(8,128)S(1)}, f32[64,2304]{1,0:T(8,128)S(1)}, u32[]{:S(2)}, u32[]{:S(2)}) collective-permute-start(f32[64,2304]{1,0:T(8,128)S(1)} %shard_map.103._.refs_4_), channel_id=1, source_target_pairs={{0,1},{1,0},{2,3},{3,2},{4,5},{5,4},{6,7},{7,6},{8,9},{9,8},{10,11... | collective-permute-start | bytes 1769480 | tf_op jit(solution)/shard_map/ppermute | solution.py:233
  224.7 4.7 %collective-permute-start.30 = (f32[64,2560]{1,0:T(8,128)S(1)}, f32[64,2560]{1,0:T(8,128)S(1)}, u32[]{:S(2)}, u32[]{:S(2)}) collective-permute-start(f32[64,2560]{1,0:T(8,128)S(1)} %shard_map.107._.refs_7_.refs_1_), channel_id=1, source_target_pairs={{0,1},{1,0},{2,3},{3,2},{4,5},{5,4},{6,7},{7,6},{8,9},{9,8},{10,11... | collective-permute-start | bytes 1966088 | tf_op jit(solution)/shard_map/ppermute | solution.py:233
  230.7 3.9 %collective-permute-start.32 = (f32[64,2560]{1,0:T(8,128)S(1)}, f32[64,2560]{1,0:T(8,128)S(1)}, u32[]{:S(2)}, u32[]{:S(2)}) collective-permute-start(f32[64,2560]{1,0:T(8,128)S(1)} %shard_map.109._.refs_10_.refs_1_), channel_id=1, source_target_pairs={{0,1},{1,0},{2,3},{3,2},{4,5},{5,4},{6,7},{7,6},{8,9},{9,8},{10,11... | collective-permute-start | bytes 1966088 | tf_op jit(solution)/shard_map/ppermute | solution.py:233
  235.2 5.6 %collective-permute-start.35 = (f32[64,2304]{1,0:T(8,128)S(1)}, f32[64,2304]{1,0:T(8,128)S(1)}, u32[]{:S(2)}, u32[]{:S(2)}) collective-permute-start(f32[64,2304]{1,0:T(8,128)S(1)} %shard_map.110.refs_12_.refs_1_), channel_id=1, source_target_pairs={{0,1},{1,0},{2,3},{3,2},{4,5},{5,4},{6,7},{7,6},{8,9},{9,8},{10,11... | collective-permute-start | bytes 1769480 | tf_op jit(solution)/shard_map/ppermute | solution.py:233
  240.9 5.8 %shard_map.111 = (f32[256,4608]{1,0:T(8,128)S(1)}, f32[8,128]{1,0:T(8,128)S(1)}) custom-call(s32[1]{0:T(128)} %bitcast.me_ref, f32[256,4608]{1,0:T(8,128)S(1)} %bitcast.4, f32[64,2560]{1,0:T(8,128)S(1)} %shard_map.78.refs_2_.refs_1_.refs_0_, f32[64,2560]{1,0:T(8,128)S(1)} %shard_map.97._.refs_1_, f32[64,2560]{1,0:T(8,128)S(1)} %collective-permute-done.22.refs_0_.refs_2_, ...), custom_call_target="tpu_custom_call" | custom-call | bytes 73800 | tf_op jit(solution)/shard_map/pallas_call | solution.py:490
  246.7 1.3 shard_map.112
  248.0 1.3 shard_map.113
  249.3 1.3 shard_map.114
  (114 shorter events, 31.5 us)
Async XLA Ops:
  1.3 1.9 copy-start
  6.6 29.5 %all-to-all-start = ((f32[8,72,384]{2,1,0:T(8,128)}), f32[8,72,384]{2,1,0:T(8,128)}, u32[]{:S(2)}, u32[]{:S(2)}) async-start(f32[8,72,384]{2,1,0:T(8,128)} %shard_map.68._.pay_ref), calls=%async_computation | async-start | bytes 1769472 | tf_op jit(solution)/shard_map/all_to_all | solution.py:563
  12.9 23.2 %copy-start.11 = (s32[12,256]{1,0:T(8,128)S(1)}, s32[12,256]{1,0:T(8,128)}, u32[]{:S(2)}) copy-start(s32[12,256]{1,0:T(8,128)} %code_ref.3) | copy-start | bytes 36868
  34.9 66.7 %copy-start.1 = (f32[3072,256]{1,0:T(8,128)S(1)}, f32[3072,256]{1,0:T(8,128)}, u32[]{:S(2)}) copy-start(f32[3072,256]{1,0:T(8,128)} %refs_4_.1) | copy-start | bytes 9437188
  36.1 1.2 copy-start.5
  41.2 3.1 %collective-permute-start = (f32[72,256]{1,0:T(8,128)S(1)}, f32[72,256]{1,0:T(8,128)S(1)}, u32[]{:S(2)}, u32[]{:S(2)}) collective-permute-start(f32[72,256]{1,0:T(8,128)S(1)} %get-tuple-element.35), channel_id=1, source_target_pairs={{0,1},{1,2},{2,3},{3,4},{4,5},{5,6},{6,7},{8,9},{9,10},{10,11},{11... | collective-permute-start | bytes 221192 | tf_op jit(solution)/shard_map/ppermute | solution.py:569
  42.9 3.9 %collective-permute-start.1 = (f32[72,256]{1,0:T(8,128)S(1)}, f32[72,256]{1,0:T(8,128)S(1)}, u32[]{:S(2)}, u32[]{:S(2)}) collective-permute-start(f32[72,256]{1,0:T(8,128)S(1)} %get-tuple-element.36), channel_id=1, source_target_pairs={{1,0},{2,1},{3,2},{4,3},{5,4},{6,5},{7,6},{9,8},{10,9},{11,10},{12... | collective-permute-start | bytes 221192 | tf_op jit(solution)/shard_map/ppermute | solution.py:570
  51.0 57.8 %all-to-all-start.1 = ((f32[8,72,384]{2,1,0:T(8,128)}), f32[8,72,384]{2,1,0:T(8,128)}, u32[]{:S(2)}, u32[]{:S(2)}) async-start(f32[8,72,384]{2,1,0:T(8,128)} %copy-done.2), calls=%async_computation.1 | async-start | bytes 1769472 | tf_op jit(solution)/shard_map/all_to_all | solution.py:572
  57.2 23.4 %collective-permute-start.2 = (f32[64,3584]{1,0:T(8,128)}, f32[64,3584]{1,0:T(8,128)S(1)}, u32[]{:S(2)}, u32[]{:S(2)}) collective-permute-start(f32[64,3584]{1,0:T(8,128)} %copy-done.14), channel_id=1, source_target_pairs={{0,8},{8,0},{16,24},{24,16},{1,9},{9,1},{17,25},{25,17},{2,10},{10... | collective-permute-start | bytes 2752520 | tf_op jit(solution)/shard_map/ppermute | solution.py:233
  58.7 42.9 %collective-permute-start.3 = (f32[64,3584]{1,0:T(8,128)}, f32[64,3584]{1,0:T(8,128)S(1)}, u32[]{:S(2)}, u32[]{:S(2)}) collective-permute-start(f32[64,3584]{1,0:T(8,128)} %copy-done.13), channel_id=1, source_target_pairs={{0,16},{8,24},{16,0},{24,8},{1,17},{9,25},{17,1},{25,9},{2,18},{10... | collective-permute-start | bytes 2752520 | tf_op jit(solution)/shard_map/ppermute | solution.py:233
  60.2 41.4 %collective-permute-start.4 = (f32[64,3584]{1,0:T(8,128)}, f32[64,3584]{1,0:T(8,128)S(1)}, u32[]{:S(2)}, u32[]{:S(2)}) collective-permute-start(f32[64,3584]{1,0:T(8,128)} %copy-done.12), channel_id=1, source_target_pairs={{0,24},{8,16},{16,8},{24,0},{1,25},{9,17},{17,9},{25,1},{2,26},{10... | collective-permute-start | bytes 2752520 | tf_op jit(solution)/shard_map/ppermute | solution.py:233
  101.6 1.2 copy-start.3
  102.8 1.2 copy-start.6
  108.8 1.1 copy-start.8
  109.9 1.1 copy-start.10
  112.7 19.3 %collective-permute-start.5 = (f32[64,3072]{1,0:T(8,128)S(1)}, f32[64,3072]{1,0:T(8,128)S(1)}, u32[]{:S(2)}, u32[]{:S(2)}) collective-permute-start(f32[64,3072]{1,0:T(8,128)S(1)} %shard_map.73.refs_4_.refs_5_.refs_0_), channel_id=1, source_target_pairs={{0,8},{8,0},{16,24},{24,16},{1,9},{9,1},{17,25},{25,17},{2,10},{10... | collective-permute-start | bytes 2359304 | tf_op jit(solution)/shard_map/ppermute | solution.py:233
  113.9 19.3 %collective-permute-start.6 = (f32[64,3072]{1,0:T(8,128)S(1)}, f32[64,3072]{1,0:T(8,128)S(1)}, u32[]{:S(2)}, u32[]{:S(2)}) collective-permute-start(f32[64,3072]{1,0:T(8,128)S(1)} %shard_map.73.refs_4_.refs_5_.refs_0_), channel_id=1, source_target_pairs={{0,16},{8,24},{16,0},{24,8},{1,17},{9,25},{17,1},{25,9},{2,18},{10... | collective-permute-start | bytes 2359304 | tf_op jit(solution)/shard_map/ppermute | solution.py:233
  122.6 10.6 %collective-permute-start.9 = (f32[64,2560]{1,0:T(8,128)S(1)}, f32[64,2560]{1,0:T(8,128)S(1)}, u32[]{:S(2)}, u32[]{:S(2)}) collective-permute-start(f32[64,2560]{1,0:T(8,128)S(1)} %shard_map.74.refs_5_.refs_0_), channel_id=1, source_target_pairs={{0,1},{1,0},{2,3},{3,2},{4,5},{5,4},{6,7},{7,6},{8,9},{9,8},{10,11... | collective-permute-start | bytes 1966088 | tf_op jit(solution)/shard_map/ppermute | solution.py:233
  130.2 6.1 %collective-permute-start.8 = (f32[64,2304]{1,0:T(8,128)S(1)}, f32[64,2304]{1,0:T(8,128)S(1)}, u32[]{:S(2)}, u32[]{:S(2)}) collective-permute-start(f32[64,2304]{1,0:T(8,128)S(1)} %shard_map.75.refs_2_.refs_0_), channel_id=1, source_target_pairs={{0,1},{1,0},{2,3},{3,2},{4,5},{5,4},{6,7},{7,6},{8,9},{9,8},{10,11... | collective-permute-start | bytes 1769480 | tf_op jit(solution)/shard_map/ppermute | solution.py:233
  133.3 22.1 %collective-permute-start.13 = (f32[64,2560]{1,0:T(8,128)S(1)}, f32[64,2560]{1,0:T(8,128)S(1)}, u32[]{:S(2)}, u32[]{:S(2)}) collective-permute-start(f32[64,2560]{1,0:T(8,128)S(1)} %shard_map.78.refs_2_.refs_1_.refs_0_), channel_id=1, source_target_pairs={{0,2},{7,5},{8,10},{15,13},{16,18},{23,21},{24,26},{31,29}} | collective-permute-start | bytes 1966088 | tf_op jit(solution)/shard_map/ppermute | solution.py:415
  136.4 18.8 %collective-permute-start.10 = (f32[64,2304]{1,0:T(8,128)S(1)}, f32[64,2304]{1,0:T(8,128)S(1)}, u32[]{:S(2)}, u32[]{:S(2)}) collective-permute-start(f32[64,2304]{1,0:T(8,128)S(1)} %shard_map.79.refs_7_.refs_1_.refs_2_.refs_3_), channel_id=1, source_target_pairs={{0,2},{7,5},{8,10},{15,13},{16,18},{23,21},{24,26},{31,29}} | collective-permute-start | bytes 1769480 | tf_op jit(solution)/shard_map/ppermute | solution.py:415
  137.9 18.0 %collective-permute-start.7 = (f32[64,3072]{1,0:T(8,128)S(1)}, f32[64,3072]{1,0:T(8,128)S(1)}, u32[]{:S(2)}, u32[]{:S(2)}) collective-permute-start(f32[64,3072]{1,0:T(8,128)S(1)} %shard_map.77.refs_2_), channel_id=1, source_target_pairs={{0,8},{8,0},{16,24},{24,16},{1,9},{9,1},{17,25},{25,17},{2,10},{10... | collective-permute-start | bytes 2359304 | tf_op jit(solution)/shard_map/ppermute | solution.py:233
  146.9 9.0 %collective-permute-start.14 = (f32[64,2560]{1,0:T(8,128)S(1)}, f32[64,2560]{1,0:T(8,128)S(1)}, u32[]{:S(2)}, u32[]{:S(2)}) collective-permute-start(f32[64,2560]{1,0:T(8,128)S(1)} %get-tuple-element.46.refs_0_), channel_id=1, source_target_pairs={{0,1},{1,0},{2,3},{3,2},{4,5},{5,4},{6,7},{7,6},{8,9},{9,8},{10,11... | collective-permute-start | bytes 1966088 | tf_op jit(solution)/shard_map/ppermute | solution.py:233
  147.0 8.9 %collective-permute-start.15 = (f32[64,2560]{1,0:T(8,128)S(1)}, f32[64,2560]{1,0:T(8,128)S(1)}, u32[]{:S(2)}, u32[]{:S(2)}) collective-permute-start(f32[64,2560]{1,0:T(8,128)S(1)} %get-tuple-element.43.refs_6_.refs_1_), channel_id=1, source_target_pairs={{0,1},{1,0},{2,3},{3,2},{4,5},{5,4},{6,7},{7,6},{8,9},{9,8},{10,11... | collective-permute-start | bytes 1966088 | tf_op jit(solution)/shard_map/ppermute | solution.py:233
  155.2 2.8 %collective-permute-start.11 = (f32[64,2304]{1,0:T(8,128)S(1)}, f32[64,2304]{1,0:T(8,128)S(1)}, u32[]{:S(2)}, u32[]{:S(2)}) collective-permute-start(f32[64,2304]{1,0:T(8,128)S(1)} %get-tuple-element.44.refs_0_), channel_id=1, source_target_pairs={{0,1},{1,0},{2,3},{3,2},{4,5},{5,4},{6,7},{7,6},{8,9},{9,8},{10,11... | collective-permute-start | bytes 1769480 | tf_op jit(solution)/shard_map/ppermute | solution.py:233
  155.4 2.8 %collective-permute-start.12 = (f32[64,2304]{1,0:T(8,128)S(1)}, f32[64,2304]{1,0:T(8,128)S(1)}, u32[]{:S(2)}, u32[]{:S(2)}) collective-permute-start(f32[64,2304]{1,0:T(8,128)S(1)} %get-tuple-element.45.refs_3_.refs_1_), channel_id=1, source_target_pairs={{0,1},{1,0},{2,3},{3,2},{4,5},{5,4},{6,7},{7,6},{8,9},{9,8},{10,11... | collective-permute-start | bytes 1769480 | tf_op jit(solution)/shard_map/ppermute | solution.py:233
  156.7 21.2 %collective-permute-start.17 = (f32[64,2560]{1,0:T(8,128)S(1)}, f32[64,2560]{1,0:T(8,128)S(1)}, u32[]{:S(2)}, u32[]{:S(2)}) collective-permute-start(f32[64,2560]{1,0:T(8,128)S(1)} %shard_map.84.refs_4_), channel_id=1, source_target_pairs={{0,2},{2,4},{7,5},{5,3},{8,10},{10,12},{15,13},{13,11},{16,18},{18... | collective-permute-start | bytes 1966088 | tf_op jit(solution)/shard_map/ppermute | solution.py:433
  158.9 21.6 %collective-permute-start.16 = (f32[64,2304]{1,0:T(8,128)S(1)}, f32[64,2304]{1,0:T(8,128)S(1)}, u32[]{:S(2)}, u32[]{:S(2)}) collective-permute-start(f32[64,2304]{1,0:T(8,128)S(1)} %shard_map.86.refs_8_), channel_id=1, source_target_pairs={{0,2},{2,4},{7,5},{5,3},{8,10},{10,12},{15,13},{13,11},{16,18},{18... | collective-permute-start | bytes 1769480 | tf_op jit(solution)/shard_map/ppermute | solution.py:433
  178.5 16.3 %collective-permute-start.20 = (f32[64,2560]{1,0:T(8,128)S(1)}, f32[64,2560]{1,0:T(8,128)S(1)}, u32[]{:S(2)}, u32[]{:S(2)}) collective-permute-start(f32[64,2560]{1,0:T(8,128)S(1)} %shard_map.89._), channel_id=1, source_target_pairs={{0,2},{2,4},{4,6},{7,5},{5,3},{3,1},{8,10},{10,12},{12,14},{15,13}... | collective-permute-start | bytes 1966088 | tf_op jit(solution)/shard_map/ppermute | solution.py:433
  180.5 14.4 %collective-permute-start.21 = (f32[64,2560]{1,0:T(8,128)S(1)}, f32[64,2560]{1,0:T(8,128)S(1)}, u32[]{:S(2)}, u32[]{:S(2)}) collective-permute-start(f32[64,2560]{1,0:T(8,128)S(1)} %shard_map.87.refs_5_.refs_0_), channel_id=1, source_target_pairs={{0,1},{1,0},{2,3},{3,2},{4,5},{5,4},{6,7},{7,6},{8,9},{9,8},{10,11... | collective-permute-start | bytes 1966088 | tf_op jit(solution)/shard_map/ppermute | solution.py:233
  181.2 13.7 %collective-permute-start.18 = (f32[64,2304]{1,0:T(8,128)S(1)}, f32[64,2304]{1,0:T(8,128)S(1)}, u32[]{:S(2)}, u32[]{:S(2)}) collective-permute-start(f32[64,2304]{1,0:T(8,128)S(1)} %shard_map.90.refs_2_), channel_id=1, source_target_pairs={{0,2},{2,4},{4,6},{7,5},{5,3},{3,1},{8,10},{10,12},{12,14},{15,13}... | collective-permute-start | bytes 1769480 | tf_op jit(solution)/shard_map/ppermute | solution.py:433
  183.1 16.9 %collective-permute-start.19 = (f32[64,2304]{1,0:T(8,128)S(1)}, f32[64,2304]{1,0:T(8,128)S(1)}, u32[]{:S(2)}, u32[]{:S(2)}) collective-permute-start(f32[64,2304]{1,0:T(8,128)S(1)} %shard_map.88._.refs_0_), channel_id=1, source_target_pairs={{0,1},{1,0},{2,3},{3,2},{4,5},{5,4},{6,7},{7,6},{8,9},{9,8},{10,11... | collective-permute-start | bytes 1769480 | tf_op jit(solution)/shard_map/ppermute | solution.py:233
  195.5 12.6 %collective-permute-start.25 = (f32[64,2560]{1,0:T(8,128)S(1)}, f32[64,2560]{1,0:T(8,128)S(1)}, u32[]{:S(2)}, u32[]{:S(2)}) collective-permute-start(f32[64,2560]{1,0:T(8,128)S(1)} %shard_map.93.refs_2_), channel_id=1, source_target_pairs={{0,2},{2,4},{4,6},{7,5},{5,3},{3,1},{8,10},{10,12},{12,14},{15,13}... | collective-permute-start | bytes 1966088 | tf_op jit(solution)/shard_map/ppermute | solution.py:433
  200.7 13.7 %collective-permute-start.24 = (f32[64,2304]{1,0:T(8,128)S(1)}, f32[64,2304]{1,0:T(8,128)S(1)}, u32[]{:S(2)}, u32[]{:S(2)}) collective-permute-start(f32[64,2304]{1,0:T(8,128)S(1)} %shard_map.95.refs_4_), channel_id=1, source_target_pairs={{0,2},{2,4},{4,6},{7,5},{5,3},{3,1},{8,10},{10,12},{12,14},{15,13}... | collective-permute-start | bytes 1769480 | tf_op jit(solution)/shard_map/ppermute | solution.py:433
  207.4 8.2 %collective-permute-start.22 = (f32[64,2560]{1,0:T(8,128)S(1)}, f32[64,2560]{1,0:T(8,128)S(1)}, u32[]{:S(2)}, u32[]{:S(2)}) collective-permute-start(f32[64,2560]{1,0:T(8,128)S(1)} %shard_map.97._.refs_1_), channel_id=1, source_target_pairs={{0,1},{1,0},{2,3},{3,2},{4,5},{5,4},{6,7},{7,6},{8,9},{9,8},{10,11... | collective-permute-start | bytes 1966088 | tf_op jit(solution)/shard_map/ppermute | solution.py:233
  208.7 8.3 %collective-permute-start.29 = (f32[64,2560]{1,0:T(8,128)S(1)}, f32[64,2560]{1,0:T(8,128)S(1)}, u32[]{:S(2)}, u32[]{:S(2)}) collective-permute-start(f32[64,2560]{1,0:T(8,128)S(1)} %shard_map.99._), channel_id=1, source_target_pairs={{2,4},{4,6},{5,3},{3,1},{10,12},{12,14},{13,11},{11,9},{18,20},{20... | collective-permute-start | bytes 1966088 | tf_op jit(solution)/shard_map/ppermute | solution.py:433
  209.4 6.2 %collective-permute-start.23 = (f32[64,2304]{1,0:T(8,128)S(1)}, f32[64,2304]{1,0:T(8,128)S(1)}, u32[]{:S(2)}, u32[]{:S(2)}) collective-permute-start(f32[64,2304]{1,0:T(8,128)S(1)} %shard_map.98._.refs_4_), channel_id=1, source_target_pairs={{0,1},{1,0},{2,3},{3,2},{4,5},{5,4},{6,7},{7,6},{8,9},{9,8},{10,11... | collective-permute-start | bytes 1769480 | tf_op jit(solution)/shard_map/ppermute | solution.py:233
  214.9 7.5 %collective-permute-start.28 = (f32[64,2304]{1,0:T(8,128)S(1)}, f32[64,2304]{1,0:T(8,128)S(1)}, u32[]{:S(2)}, u32[]{:S(2)}) collective-permute-start(f32[64,2304]{1,0:T(8,128)S(1)} %shard_map.100.refs_2_), channel_id=1, source_target_pairs={{2,4},{4,6},{5,3},{3,1},{10,12},{12,14},{13,11},{11,9},{18,20},{20... | collective-permute-start | bytes 1769480 | tf_op jit(solution)/shard_map/ppermute | solution.py:433
  216.3 7.8 %collective-permute-start.26 = (f32[64,2560]{1,0:T(8,128)S(1)}, f32[64,2560]{1,0:T(8,128)S(1)}, u32[]{:S(2)}, u32[]{:S(2)}) collective-permute-start(f32[64,2560]{1,0:T(8,128)S(1)} %shard_map.102._.refs_4_.refs_1_), channel_id=1, source_target_pairs={{0,1},{1,0},{2,3},{3,2},{4,5},{5,4},{6,7},{7,6},{8,9},{9,8},{10,11... | collective-permute-start | bytes 1966088 | tf_op jit(solution)/shard_map/ppermute | solution.py:233
  217.6 12.5 %collective-permute-start.31 = (f32[64,2560]{1,0:T(8,128)S(1)}, f32[64,2560]{1,0:T(8,128)S(1)}, u32[]{:S(2)}, u32[]{:S(2)}) collective-permute-start(f32[64,2560]{1,0:T(8,128)S(1)} %shard_map.104._), channel_id=1, source_target_pairs={{4,6},{3,1},{12,14},{11,9},{20,22},{19,17},{28,30},{27,25}} | collective-permute-start | bytes 1966088 | tf_op jit(solution)/shard_map/ppermute | solution.py:433
  218.3 5.8 %collective-permute-start.27 = (f32[64,2304]{1,0:T(8,128)S(1)}, f32[64,2304]{1,0:T(8,128)S(1)}, u32[]{:S(2)}, u32[]{:S(2)}) collective-permute-start(f32[64,2304]{1,0:T(8,128)S(1)} %shard_map.103._.refs_4_), channel_id=1, source_target_pairs={{0,1},{1,0},{2,3},{3,2},{4,5},{5,4},{6,7},{7,6},{8,9},{9,8},{10,11... | collective-permute-start | bytes 1769480 | tf_op jit(solution)/shard_map/ppermute | solution.py:233
  223.0 11.6 %collective-permute-start.33 = (f32[64,2304]{1,0:T(8,128)S(1)}, f32[64,2304]{1,0:T(8,128)S(1)}, u32[]{:S(2)}, u32[]{:S(2)}) collective-permute-start(f32[64,2304]{1,0:T(8,128)S(1)} %shard_map.105.refs_2_), channel_id=1, source_target_pairs={{4,6},{3,1},{12,14},{11,9},{20,22},{19,17},{28,30},{27,25}} | collective-permute-start | bytes 1769480 | tf_op jit(solution)/shard_map/ppermute | solution.py:433
  224.1 16.8 %slice-start = ((s8[4718592]{0:T(1024)(128)(4,1)}), s8[4194304]{0:T(1024)(128)(4,1)S(1)}, s32[]{:S(2)}) async-start(s8[4718592]{0:T(1024)(128)(4,1)} %bitcast.3), calls=%async_computation.2 | async-start | bytes 8388608
  224.7 16.2 %slice-start.1 = ((s8[4718592]{0:T(1024)(128)(4,1)}), s8[524288]{0:T(1024)(128)(4,1)S(1)}, s32[]{:S(2)}) async-start(s8[4718592]{0:T(1024)(128)(4,1)} %bitcast.3), calls=%async_computation.3 | async-start | bytes 1048576
  224.7 16.2 %collective-permute-start.30 = (f32[64,2560]{1,0:T(8,128)S(1)}, f32[64,2560]{1,0:T(8,128)S(1)}, u32[]{:S(2)}, u32[]{:S(2)}) collective-permute-start(f32[64,2560]{1,0:T(8,128)S(1)} %shard_map.107._.refs_7_.refs_1_), channel_id=1, source_target_pairs={{0,1},{1,0},{2,3},{3,2},{4,5},{5,4},{6,7},{7,6},{8,9},{9,8},{10,11... | collective-permute-start | bytes 1966088 | tf_op jit(solution)/shard_map/ppermute | solution.py:233
  230.7 10.2 %collective-permute-start.32 = (f32[64,2560]{1,0:T(8,128)S(1)}, f32[64,2560]{1,0:T(8,128)S(1)}, u32[]{:S(2)}, u32[]{:S(2)}) collective-permute-start(f32[64,2560]{1,0:T(8,128)S(1)} %shard_map.109._.refs_10_.refs_1_), channel_id=1, source_target_pairs={{0,1},{1,0},{2,3},{3,2},{4,5},{5,4},{6,7},{7,6},{8,9},{9,8},{10,11... | collective-permute-start | bytes 1966088 | tf_op jit(solution)/shard_map/ppermute | solution.py:233
  234.6 14.8 %collective-permute-start.34 = (f32[64,2304]{1,0:T(8,128)S(1)}, f32[64,2304]{1,0:T(8,128)S(1)}, u32[]{:S(2)}, u32[]{:S(2)}) collective-permute-start(f32[64,2304]{1,0:T(8,128)S(1)} %shard_map.108._.refs_4_), channel_id=1, source_target_pairs={{0,1},{1,0},{2,3},{3,2},{4,5},{5,4},{6,7},{7,6},{8,9},{9,8},{10,11... | collective-permute-start | bytes 1769480 | tf_op jit(solution)/shard_map/ppermute | solution.py:233
  235.2 16.3 %collective-permute-start.35 = (f32[64,2304]{1,0:T(8,128)S(1)}, f32[64,2304]{1,0:T(8,128)S(1)}, u32[]{:S(2)}, u32[]{:S(2)}) collective-permute-start(f32[64,2304]{1,0:T(8,128)S(1)} %shard_map.110.refs_12_.refs_1_), channel_id=1, source_target_pairs={{0,1},{1,0},{2,3},{3,2},{4,5},{5,4},{6,7},{7,6},{8,9},{9,8},{10,11... | collective-permute-start | bytes 1769480 | tf_op jit(solution)/shard_map/ppermute | solution.py:233
  (7 other events, 6.5 us)
where the time goes:
time: 254 us; the launch traced here: 252 us
  Pallas kernels  107 us (42%)
  starting transfers between devices  65.7 us (26%)
  waiting for transfers between devices  63.1 us (25%)
  local copies, waits for them, and re-layouts  14.2 us (6%)
    pallas_call x6, Pallas kernels, cross_part(): kernel_call(body, (shape(width, cols + with_gram * width_all),) * n, 0.02...  47.1 us
    ppermute x22, waiting for transfers between devices, swap(): lax.ppermute(block, axis, [(i, i ^ bit) for i in range(lax.axis_size(axis...  43.8 us
    ppermute x22, starting transfers between devices, swap(): lax.ppermute(block, axis, [(i, i ^ bit) for i in range(lax.axis_size(axis...  27.9 us
    pallas_call x1, Pallas kernels, numer_part(): kernel_call(body, (shape(width, rows + STEP),) * genes_n, 14, limit=30, g...  18.2 us
    ppermute x10, starting transfers between devices, line_slot(): return (lax.ppermute(send, 'bin', hops), send)  17.6 us
    ppermute x10, waiting for transfers between devices, line_slot(): return (lax.ppermute(send, 'bin', hops), send)  15.5 us
    unnamed x34, local copies, waits for them, and re-layouts  14.2 us
    all_to_all x1, starting transfers between devices, on_device(): lax.all_to_all(payload, 'bin', split_axis=0, concat_axis=0, tiled=True)  6.33 us
  transfers between devices with their start and end apart: 38, of which 10 were waited for; matrix products, arithmetic and copies ran while one was open for 0% of the time, Pallas kernels for 37%

commit v1 on v0

--- a/solution.py
+++ b/solution.py
@@ -11,7 +11,7 @@
 EXTRA = 8
 HALVES = 2
 STEP = 512
-READS = 4
+READS = 2
 MIB = 1024 * 1024
 MINOR = (((1,), (1,)), ((), ()))
 PLAIN = (((1,), (0,)), ((), ()))
@@ -162,110 +162,157 @@
     )(grid, above, below, cell, edge_codes, token)
 
 
-def numer_part(counts, loadings, me, genes_n, token):
+def numer_part(counts, loadings, me, genes_n, half, send_ids, token):
     rows, genes = counts.shape
-    width_all = loadings.shape[0]
+    first_call = loadings.dtype == F32
+    width_all = loadings.shape[0] if first_call else loadings.shape[1]
     width = width_all // genes_n
-    steps = rows // STEP
+    half_rows = rows // 2
+    steps = half_rows // STEP
     side = genes // 2
-
-    def body(me_ref, left_ref, right_ref, load_ref, _, *rest):
-        outs, (load_f, load_bf, load_t, turned, sems) = rest[:genes_n], rest[genes_n:]
+    keep_ids = [k for k in range(genes_n) if k not in send_ids]
+    total_cols = half_rows + first_call * width_all
+
+    def body(me_ref, left_ref, right_ref, *refs):
         at = pl.program_id(0)
         firsts = [pl.multiple_of((k ^ me_ref[0]) * width, width) for k in range(genes_n)]
-
-        @pl.when(at == 0)
-        def _():
-            reads = [
-                pltpu.make_async_copy(
-                    load_ref.at[pl.ds(first, width), :], load_f.at[pl.ds(k * width, width), :], sems.at[k]
-                )
-                for k, first in enumerate(firsts)
-            ]
-            for copy in reads:
-                copy.start()
-            for copy in reads:
-                copy.wait()
-            load_bf[...] = load_f[...].astype(BF16)
-            load_t[...] = load_bf[...].T
-
-        def put(part):
-            for k, out in enumerate(outs):
-                out[...] = part[k * width : (k + 1) * width]
-
-        @pl.when(at < steps)
-        def _():
-            part = dot(left_ref[...], load_t[:side, :], PLAIN)
-            put((part + dot(right_ref[...], load_t[side:, :], PLAIN)).T)
-
-        @pl.when(at == steps)
-        def _():
-            local = dot(load_bf[...], load_t[...], PLAIN)
-            for k, first in enumerate(firsts):
-                turned[pl.ds(first, width), :] = local[k * width : (k + 1) * width]
-            put(jnp.concatenate([turned[...].T, jnp.zeros((width_all, STEP - width_all), F32)], axis=1))
-
-    row_at = lambda i: jnp.minimum(i, steps - 1)
+        if first_call:
+            load_ref, _, send_ref, keep_ref, load_t, load_bf, load_f, turned, sems = refs
+
+            @pl.when(at == 0)
+            def _():
+                reads = [
+                    pltpu.make_async_copy(
+                        load_ref.at[pl.ds(first, width), :],
+                        load_f.at[pl.ds(k * width, width), :],
+                        sems.at[k],
+                    )
+                    for k, first in enumerate(firsts)
+                ]
+                for copy in reads:
+                    copy.start()
+                for k, copy in enumerate(reads):
+                    copy.wait()
+                    here = slice(k * width, (k + 1) * width)
+                    load_bf[here, :] = load_f[here, :].astype(BF16)
+                load_t[...] = load_bf[...].T
+
+        else:
+            load_t, _, send_ref, keep_ref = refs
+
+        def put(part, cols):
+            for i, k in enumerate(send_ids):
+                send_ref[i, :, cols] = part[k * width : (k + 1) * width]
+            for i, k in enumerate(keep_ids):
+                keep_ref[i, :, cols] = part[k * width : (k + 1) * width]
+
+        part = dot(left_ref[...], load_t[:side, :], PLAIN)
+        part = part + dot(right_ref[...], load_t[side:, :], PLAIN)
+        put(part.T, pl.ds(pl.multiple_of(at * STEP, STEP), STEP))
+
+        if first_call:
+
+            @pl.when(at == 0)
+            def _():
+                local = dot(load_bf[...], load_t[...], PLAIN)
+                for k, first in enumerate(firsts):
+                    turned[pl.ds(first, width), :] = local[k * width : (k + 1) * width]
+                put(turned[...].T, slice(half_rows, total_cols))
+
+    out = shape(genes_n // 2, width, total_cols)
+    out_spec = pl.BlockSpec(out.shape, lambda i, m: (0, 0, 0))
+    outs, out_specs, scratch = (out, out), (out_spec, out_spec), []
+    if first_call:
+        outs += (shape(genes, width_all, dtype=BF16),)
+        out_specs += (pl.BlockSpec((genes, width_all), lambda i, m: (0, 0)),)
+        scratch = [
+            pltpu.VMEM((width_all, genes), BF16),
+            pltpu.VMEM((width_all, genes), F32),
+            pltpu.VMEM((width_all, width_all), F32),
+            pltpu.SemaphoreType.DMA((genes_n,)),
+        ]
+        load_spec = ANY_SPEC
+    else:
+        load_spec = pl.BlockSpec((genes, width_all), lambda i, m: (0, 0))
     grid_spec = pltpu.PrefetchScalarGridSpec(
         num_scalar_prefetch=1,
-        grid=(steps + 1,),
+        grid=(steps,),
         in_specs=[
-            pl.BlockSpec((STEP, side), lambda i, m: (row_at(i), 0)),
-            pl.BlockSpec((STEP, side), lambda i, m: (row_at(i), 1)),
-            ANY_SPEC,
+            pl.BlockSpec((STEP, side), lambda i, m: (i + half * steps, 0)),
+            pl.BlockSpec((STEP, side), lambda i, m: (i + half * steps, 1)),
+            load_spec,
             ANY_SPEC,
         ],
-        out_specs=(pl.BlockSpec((width, STEP), lambda i, m: (0, i)),) * genes_n,
-        scratch_shapes=[
-            pltpu.VMEM((width_all, genes), F32),
-            pltpu.VMEM((width_all, genes), BF16),
-            pltpu.VMEM((genes, width_all), BF16),
-            pltpu.VMEM((width_all, width_all), F32),
-            pltpu.SemaphoreType.DMA((genes_n,)),
-        ],
+        out_specs=out_specs,
+        scratch_shapes=scratch,
     )
-    return kernel_call(
-        body, (shape(width, rows + STEP),) * genes_n, 14, limit=30, grid_spec=grid_spec
-    )(me, counts, counts, loadings, token)
+    return kernel_call(body, outs, 7, limit=36, grid_spec=grid_spec)(me, counts, counts, loadings, token)
 
 
 def swap(block, axis, bit):
     return lax.ppermute(block, axis, [(i, i ^ bit) for i in range(lax.axis_size(axis))])
 
 
-def plain_terms(parts, factors, token):
+def picked_sum(arrays, ids, token):
+    _, width, cols = arrays[0].shape
+    first, step = ids[0], (ids[1] - ids[0] if len(ids) > 1 else 1)
+
+    def body(*refs):
+        total = refs[0][...]
+        for ref in refs[1:-2]:
+            total = total + ref[...]
+        refs[-1][...] = total
+
+    return kernel_call(
+        body,
+        shape(len(ids), width, cols),
+        0.02,
+        grid=(len(ids),),
+        in_specs=[pl.BlockSpec((1, width, cols), lambda i: (first + step * i, 0, 0))] * len(arrays)
+        + [ANY_SPEC],
+        out_specs=pl.BlockSpec((1, width, cols), lambda i: (i, 0, 0)),
+    )(*arrays, token)
+
+
+def plain_terms(first, second, factors, token):
     rows, width_all = factors.shape
-    width = parts[0].shape[0]
+    width = first[0].shape[1]
     half_rows = rows // 2
+    n = len(first)
 
     def body(*refs):
-        n = len(parts)
-        fac_ref, _, numer_ref, plain_ref, gram = refs[n:]
-
-        def total(cols):
-            out = refs[0][:, cols]
-            for ref in refs[1:n]:
-                out = out + ref[:, cols]
+        fac_ref, _, numer_ref, plain_ref, gram = refs[2 * n :]
+
+        def total(part, cols):
+            out = part[0][0, :, cols]
+            for ref in part[1:]:
+                out = out + ref[0, :, cols]
             return out
 
         @pl.when(pl.program_id(0) == 0)
         def _():
-            gram[...] = total(slice(rows, rows + width_all))
-            numer_ref[...] = total(slice(0, rows))
+            gram[...] = total(refs[n : 2 * n], slice(half_rows, half_rows + width_all))
+            numer_ref[...] = total(refs[:n], slice(0, half_rows))
+
+        @pl.when(pl.program_id(0) == 1)
+        def _():
+            numer_ref[...] = total(refs[n : 2 * n], slice(0, half_rows))
 
         plain_ref[...] = dot(fac_ref[...], gram[...], MINOR, lax.Precision.HIGHEST).T
 
+    out_spec = pl.BlockSpec((width, half_rows), lambda i: (0, i))
+    arrays = list(first) + list(second)
     return kernel_call(
         body,
         (shape(width, rows),) * 2,
-        60,
-        limit=16,
+        4,
+        limit=24,
         grid=(2,),
-        in_specs=[VMEM_SPEC] * len(parts)
+        in_specs=[pl.BlockSpec((1,) + x.shape[1:], lambda i: (0, 0, 0)) for x in arrays]
         + [pl.BlockSpec((half_rows, width_all), lambda i: (i, 0)), ANY_SPEC],
-        out_specs=(VMEM_SPEC, pl.BlockSpec((width, half_rows), lambda i: (0, i))),
+        out_specs=(out_spec, out_spec),
         scratch_shapes=[pltpu.VMEM((width, width_all), F32)],
-    )(*parts, factors, token)
+    )(*arrays, factors, token)
 
 
 def new_factors(payload, back, numer, plain):
@@ -273,19 +320,22 @@
     width = wide - EXTRA
 
     def body(pay_ref, back_ref, numer_ref, plain_ref, out_ref):
-        pay = jnp.concatenate([pay_ref[s] for s in range(bins)], axis=1)
-        got = jnp.concatenate([back_ref[s] for s in range(bins)], axis=1)
+        pay = jnp.concatenate([pay_ref[0], pay_ref[1]], axis=1)
+        got = jnp.concatenate([back_ref[0], back_ref[1]], axis=1)
         fac, smooth, degree = pay[:width], got[:width], got[width : width + 1]
         out_ref[...] = (
             fac * (numer_ref[...] + PENALTY * smooth) / (plain_ref[...] + PENALTY * degree * fac)
         )
 
+    pair = pl.BlockSpec((2, wide, group), lambda i: (i, 0, 0))
+    cols = pl.BlockSpec((width, 2 * group), lambda i: (0, i))
     return kernel_call(
         body,
         shape(width, bins * group),
         0.02,
-        in_specs=[VMEM_SPEC] * 4,
-        out_specs=VMEM_SPEC,
+        grid=(bins // 2,),
+        in_specs=[pair, pair, cols, cols],
+        out_specs=cols,
     )(payload, back, numer, plain)
 
 
@@ -330,12 +380,9 @@
 
 def cross_part(blocks, n_old, counts, half, with_gram, width_all, tokens):
     width, rows = blocks[0].shape
-    genes = counts.shape[1]
-    cols = genes // HALVES
-    step = 384
-    steps = cols // step
+    cols = counts.shape[1] // HALVES
     n = len(blocks) - n_old
-    deep = rows // READS
+    deep = STEP // READS
     use = blocks if with_gram else blocks[n_old:]
     skip = len(use) - n
 
@@ -348,33 +395,36 @@
             for j, ref in enumerate(refs[READS : READS + len(use)]):
                 fac[j * width : (j + 1) * width, :] = ref[...].astype(BF16)
 
-        def put(part, where):
+        def put(part, where, add):
             for j, out in enumerate(outs):
-                out[:, where] = part[j * width : (j + 1) * width]
-
-        new = lambda i: fac[skip * width :, i * deep : (i + 1) * deep]
-        part = dot(new(0), refs[0][...], PLAIN)
-        for i in range(1, READS):
-            part = part + dot(new(i), refs[i][...], PLAIN)
-        put(part, pl.ds(pl.multiple_of(at * step, step), step))
+                value = part[j * width : (j + 1) * width]
+                out[:, where] = out[:, where] + value if add else value
+
+        part = None
+        for i in range(READS):
+            new = fac[skip * width :, pl.ds(pl.multiple_of(at * STEP + i * deep, deep), deep)]
+            more = dot(new, refs[i][...], PLAIN)
+            part = more if part is None else part + more
+        pl.when(at == 0)(lambda: put(part, slice(0, cols), False))
+        pl.when(at > 0)(lambda: put(part, slice(0, cols), True))
 
         if with_gram:
 
-            @pl.when(at == steps - 1)
+            @pl.when(at == 0)
             def _():
                 near = dot(fac[skip * width :, :], fac[...], MINOR)
                 if near.shape[1] < width_all:
                     gap = jnp.zeros((near.shape[0], width_all - near.shape[1]), F32)
                     near = jnp.concatenate([near, gap], axis=1)
-                put(near, slice(cols, cols + width_all))
-
-    read = lambda i: pl.BlockSpec((deep, step), lambda g: (i, half * steps + g))
+                put(near, slice(cols, cols + width_all), False)
+
+    read = lambda i: pl.BlockSpec((deep, cols), lambda g: (g * READS + i, half))
     return kernel_call(
         body,
         (shape(width, cols + with_gram * width_all),) * n,
         0.02,
         limit=24,
-        grid=(steps,),
+        grid=(rows // STEP,),
         in_specs=[read(i) for i in range(READS)] + [VMEM_SPEC] * len(use) + [ANY_SPEC] * len(tokens),
         out_specs=(VMEM_SPEC,) * n,
         scratch_shapes=[pltpu.VMEM((len(use) * width, rows), BF16)],
@@ -561,16 +611,38 @@
     counts = pltpu.with_memory_space_constraint(counts, pltpu.HBM)
     payload = pack(factors, position, me1, width, bins)
     got = lax.all_to_all(payload, "bin", split_axis=0, concat_axis=0, tiled=True)
-    parts = numer_part(
-        counts, pltpu.with_memory_space_constraint(loadings, pltpu.HBM), me1, genes_n, payload
-    )
-    parts = [parts[0]] + [swap(parts[k], "gene", k) for k in range(1, genes_n)]
-    grid, first, last, cell = to_grid(got, edge_codes, bin1, parts[0])
+    orders = (bits, bits[::-1])
+    token, load = payload, pltpu.with_memory_space_constraint(loadings, pltpu.HBM)
+    parts, keeps = [None, None], [None, None]
+    for half in (1, 0):
+        bit = orders[half][0]
+        send_ids = [k for k in range(genes_n) if k & bit]
+        keeps[half] = [k for k in range(genes_n) if not k & bit]
+        send, keep, *made = numer_part(counts, load, me1, genes_n, half, send_ids, token)
+        load = made[0] if made else load
+        token = keep
+        parts[half] = [keep, swap(send, "gene", bit)]
+
+    def scatter_more(half, bit, token):
+        out_ids = [i for i, k in enumerate(keeps[half]) if k & bit]
+        in_ids = [i for i, k in enumerate(keeps[half]) if not k & bit]
+        keeps[half] = [keeps[half][i] for i in in_ids]
+        send = picked_sum(parts[half], out_ids, token)
+        if len(in_ids) > 1:
+            parts[half] = [picked_sum(parts[half], in_ids, send)]
+        parts[half] = parts[half] + [swap(send, "gene", bit)]
+        return send
+
+    grid, first, last, cell = to_grid(got, edge_codes, bin1, token)
     above = lax.ppermute(last, "bin", [(i, i + 1) for i in range(bins - 1)])
     below = lax.ppermute(first, "bin", [(i + 1, i) for i in range(bins - 1)])
-    smooth = from_grid(grid, above, below, cell, edge_codes, bins, grid)
+    token = grid
+    for i in range(1, len(bits)):
+        for half in (1, 0):
+            token = scatter_more(half, orders[half][i], token)
+    smooth = from_grid(grid, above, below, cell, edge_codes, bins, token)
     back = lax.all_to_all(smooth, "bin", split_axis=0, concat_axis=0, tiled=True)
-    numer, plain = plain_terms(parts, factors, smooth)
+    numer, plain = plain_terms(*parts, factors, smooth)
     own_block = new_factors(payload, back, numer, plain)
 
     ids = sorted(range(genes_n), key=lambda k: (bin(k).count("1"), k))
@@ -661,12 +733,14 @@
             token = awaited([ends[half][c - 1][1] for half in range(HALVES)], token)
         if 0 <= c < chunks:
             both(end, c)
-    share = loadings_new = None
-    for c in range(chunks):
-        if c not in ends[0]:
-            both(end, c)
+    rest = [c for c in range(chunks) if c not in ends[0]]
+    for c in rest:
+        token = end(c, 0, token)
     sums = [(own[0][c],) + ends[0][c] for c in range(chunks)]
+    loadings_new = None
     share, token = shares(loadings, sums, ids, counts.shape[1] // HALVES, me1, token)
+    for c in rest:
+        token = end(c, 1, token)
     for c in range(chunks - 1):
         loadings_new, token = final(c, loadings_new, token)
     for half in range(HALVES):

time: 254 us -> 252 us (level)
  waiting for transfers between devices: 63.1 us -> 44.9 us
  starting transfers between devices: 65.7 us -> 74.5 us
  Pallas kernels: 107 us -> 113 us
    ppermute x22 -> x23, waiting for transfers between devices: 43.8 us -> 25.9 us  [swap(): lax.ppermute(block, axis, [(i, i ^ bit) for i in range(lax.axis_size(axis...]
    ppermute x22 -> x23, starting transfers between devices: 27.9 us -> 34.3 us  [swap(): lax.ppermute(block, axis, [(i, i ^ bit) for i in range(lax.axis_size(axis...]
    pallas_call x3 -> x6, Pallas kernels: 22.8 us -> 28.4 us  [the longest x2 20.8 us: numer_part(): kernel_call(body, outs, 7, limit=36, grid_spec=grid_spec)]
    ppermute x10, starting transfers between devices: 17.6 us -> 21.5 us  [line_slot(): return (lax.ppermute(send, 'bin', hops), send)]
    ppermute x10, waiting for transfers between devices: 15.5 us -> 19 us  [line_slot(): return (lax.ppermute(send, 'bin', hops), send)]
    ppermute x1, waiting for transfers between devices: 2.55 us -> 0.01 us  [on_device(): below = lax.ppermute(first, 'bin', [(i + 1, i) for i in range(bins - 1)])]
    unnamed x34 -> x42, local copies, waits for them, and re-layouts: 14.2 us -> 15.9 us
  transfers between devices with their start and end apart: 38 -> 39, of which waited for: 10 -> 12; matrix products, arithmetic and copies ran while one was open for 0% -> 0% of each run, Pallas kernels for 37% -> 41%
where the time goes in v1:
time: 252 us; the launch traced here: 251 us
  Pallas kernels  113 us (45%)
  starting transfers between devices  74.5 us (30%)
  waiting for transfers between devices  44.9 us (18%)
  local copies, waits for them, and re-layouts  15.9 us (6%)
    pallas_call x6, Pallas kernels, cross_part(): kernel_call(body, (shape(width, cols + with_gram * width_all),) * n, 0.02...  48.2 us
    ppermute x23, starting transfers between devices, swap(): lax.ppermute(block, axis, [(i, i ^ bit) for i in range(lax.axis_size(axis...  34.3 us
    ppermute x23, waiting for transfers between devices, swap(): lax.ppermute(block, axis, [(i, i ^ bit) for i in range(lax.axis_size(axis...  25.9 us
    ppermute x10, starting transfers between devices, line_slot(): return (lax.ppermute(send, 'bin', hops), send)  21.5 us
    pallas_call x2, Pallas kernels, numer_part(): kernel_call(body, outs, 7, limit=36, grid_spec=grid_spec)  20.8 us
    ppermute x10, waiting for transfers between devices, line_slot(): return (lax.ppermute(send, 'bin', hops), send)  19 us
    unnamed x42, local copies, waits for them, and re-layouts  15.9 us
    all_to_all x1, starting transfers between devices, on_device(): lax.all_to_all(payload, 'bin', split_axis=0, concat_axis=0, tiled=True)  6.33 us
  transfers between devices with their start and end apart: 39, of which 12 were waited for; matrix products, arithmetic and copies ran while one was open for 0% of the time, Pallas kernels for 41%

profile of v1, /device:TPU:0, one launch (start us, length us, event | category | flops | bytes accessed | tf_op | source)
XLA Modules:
  0.0 250.8 jit_solution(2044615440324519399)
XLA Ops:
  1.3 1.9 copy-done
  3.2 3.4 %shard_map.68.refs_1_.pay_ref = f32[8,72,384]{2,1,0:T(8,128)} custom-call(s32[1]{0:T(128)} %bitcast.me_ref, f32[3072,256]{1,0:T(8,128)S(1)} %copy-done, f32[8,1,384]{2,1,0:T(1,128)S(1)} %bitcast.5), custom_call_target="tpu_custom_call" | custom-call | bytes 11070000 | tf_op jit(solution)/shard_map/pallas_call | solution.py:64
  6.6 6.3 %all-to-all-start = ((f32[8,72,384]{2,1,0:T(8,128)}), f32[8,72,384]{2,1,0:T(8,128)S(1)}, u32[]{:S(2)}, u32[]{:S(2)}) async-start(f32[8,72,384]{2,1,0:T(8,128)} %shard_map.68.refs_1_.pay_ref), calls=%async_computation | async-start | bytes 1769472 | tf_op jit(solution)/shard_map/all_to_all | solution.py:613
  13.0 12.2 %shard_map.69 = (f32[2,64,1792]{2,1,0:T(8,128)S(1)}, f32[2,64,1792]{2,1,0:T(8,128)S(1)}, bf16[4608,256]{1,0:T(8,128)(2,1)S(1)}) custom-call(s32[1]{0:T(128)} %bitcast.me_ref, bf16[3072,4608]{1,0:T(8,128)(2,1)} %refs_1_.11, bf16[3072,4608]{1,0:T(8,128)(2,1)} %refs_1_.11, f32[256,4608]{1,0:T(8,128)} %load_ref.1, f32[8,72,384]{2,1,0:T(8,128)} %shard_map.68.refs_1_.pay_ref), custom_call_target="tpu_custom_call" | custom-call | bytes 25830000 | tf_op jit(solution)/shard_map/pallas_call | solution.py:249
  25.1 1.6 collective-permute-start.3
  26.7 8.6 %shard_map.70 = (f32[2,64,1536]{2,1,0:T(8,128)}, f32[2,64,1536]{2,1,0:T(8,128)S(1)}) custom-call(s32[1]{0:T(128)} %bitcast.me_ref, bf16[3072,4608]{1,0:T(8,128)(2,1)} %refs_1_.11, bf16[3072,4608]{1,0:T(8,128)(2,1)} %refs_1_.11, bf16[4608,256]{1,0:T(8,128)(2,1)S(1)} %get-tuple-element.34.refs_0_, f32[2,64,1792]{2,1,0:T(8,128)S(1)} %get-tuple-element.35.refs_1_.refs_0_.refs_3_), custom_call_target="tpu_custom_call" | custom-call | bytes 25830000 | tf_op jit(solution)/shard_map/pallas_call | solution.py:249
  35.3 1.5 collective-permute-start.2
  36.8 2.7 %shard_map.71 = (f32[12,72,256]{2,1,0:T(8,128)S(1)}, f32[72,256]{1,0:T(8,128)S(1)}, f32[72,256]{1,0:T(8,128)S(1)}, s32[1,3072]{1,0:T(1,128)S(1)}) custom-call(s32[1]{0:T(128)} %bitcast.2.me_ref, f32[8,72,384]{2,1,0:T(8,128)S(1)} %all-to-all-done.got_ref, s32[12,256]{1,0:T(8,128)S(1)} %copy-done.18, f32[2,64,1536]{2,1,0:T(8,128)S(1)} %get-tuple-element.36._.refs_0_), custom_call_target="tpu_custom_call" | custom-call | bytes 11070000 | tf_op jit(solution)/shard_map/pallas_call | solution.py:106
  39.5 1.9 collective-permute-start
  41.4 1.3 collective-permute-start.1
  42.7 5.3 %collective-permute-done.3.refs_1_.refs_4_ = f32[2,64,1792]{2,1,0:T(8,128)S(1)} collective-permute-done((f32[2,64,1792]{2,1,0:T(8,128)S(1)}, f32[2,64,1792]{2,1,0:T(8,128)S(1)}, u32[]{:S(2)}, u32[]{:S(2)}) %collective-permute-start.3) | collective-permute-done | bytes 917536 | tf_op jit(solution)/shard_map/ppermute | solution.py:253
  48.9 1.2 copy-done.3
  51.3 4.0 %collective-permute-done.2.refs_1_ = f32[2,64,1536]{2,1,0:T(8,128)} collective-permute-done((f32[2,64,1536]{2,1,0:T(8,128)}, f32[2,64,1536]{2,1,0:T(8,128)}, u32[]{:S(2)}, u32[]{:S(2)}) %collective-permute-start.2) | collective-permute-done | bytes 786464 | tf_op jit(solution)/shard_map/ppermute | solution.py:253
  57.5 3.2 %shard_map.74.refs_7_ = f32[8,72,384]{2,1,0:T(8,128)S(1)} custom-call(f32[12,72,256]{2,1,0:T(8,128)S(1)} %get-tuple-element.37.refs_2_.grid_ref, f32[72,256]{1,0:T(8,128)S(1)} %collective-permute-done.above_ref, f32[72,256]{1,0:T(8,128)S(1)} %collective-permute-done.1.below_ref, s32[1,3072]{1,0:T(1,128)S(1)} %get-tuple-element.40.cell_ref, ...), custom_call_target="tpu_custom_call" | custom-call | bytes 14760000 | tf_op jit(solution)/shard_map/pallas_call | solution.py:155
  61.7 4.7 %all-to-all-start.1 = ((f32[8,72,384]{2,1,0:T(8,128)}), f32[8,72,384]{2,1,0:T(8,128)}, u32[]{:S(2)}, u32[]{:S(2)}) async-start(f32[8,72,384]{2,1,0:T(8,128)} %copy-done.5), calls=%async_computation.1 | async-start | bytes 1769472 | tf_op jit(solution)/shard_map/all_to_all | solution.py:644
  66.4 1.5 collective-permute-start.5
  68.5 10.7 %collective-permute-done.4.refs_2_ = f32[1,64,1536]{2,1,0:T(8,128)S(1)} collective-permute-done((f32[1,64,1536]{2,1,0:T(8,128)S(1)}, f32[1,64,1536]{2,1,0:T(8,128)S(1)}, u32[]{:S(2)}, u32[]{:S(2)}) %collective-permute-start.4) | collective-permute-done | bytes 393248 | tf_op jit(solution)/shard_map/ppermute | solution.py:253
  79.6 1.2 copy-done.4
  84.2 4.1 %shard_map.75 = (f32[64,3072]{1,0:T(8,128)S(1)}, f32[64,3072]{1,0:T(8,128)S(1)}) custom-call(f32[2,64,1536]{2,1,0:T(8,128)S(1)} %copy-done.9, f32[2,64,1536]{2,1,0:T(8,128)} %collective-permute-done.2.refs_1_, f32[1,64,1536]{2,1,0:T(8,128)S(1)} %collective-permute-done.4.refs_2_, f32[2,64,1792]{2,1,0:T(8,128)S(1)} %copy-done.4, ...), custom_call_target="tpu_custom_call" | custom-call | bytes 14760000 | tf_op jit(solution)/shard_map/pallas_call | solution.py:305
  92.4 2.5 shard_map.76.refs_2_.refs_3_.refs_0_
  94.9 1.6 collective-permute-start.6
  97.0 8.0 %shard_map.77.refs_3_.refs_0_ = f32[64,2560]{1,0:T(8,128)S(1)} custom-call(bf16[3072,4608]{1,0:T(8,128)(2,1)} %refs_1_.11, bf16[3072,4608]{1,0:T(8,128)(2,1)} %refs_1_.11, f32[64,3072]{1,0:T(8,128)S(1)} %shard_map.76.refs_2_.refs_3_.refs_0_, f32[64,3072]{1,0:T(8,128)S(1)} %shard_map.76.refs_2_.refs_3_.refs_0_), custom_call_target="tpu_custom_call" | custom-call | bytes 73800 | tf_op jit(solution)/shard_map/pallas_call | solution.py:422
  105.0 7.8 %shard_map.78.refs_2_.refs_0_ = f32[64,2304]{1,0:T(8,128)S(1)} custom-call(bf16[3072,4608]{1,0:T(8,128)(2,1)} %refs_1_.11, bf16[3072,4608]{1,0:T(8,128)(2,1)} %refs_1_.11, f32[64,3072]{1,0:T(8,128)S(1)} %shard_map.76.refs_2_.refs_3_.refs_0_, f32[64,2560]{1,0:T(8,128)S(1)} %shard_map.77.refs_3_.refs_0_), custom_call_target="tpu_custom_call" | custom-call | bytes 73800 | tf_op jit(solution)/shard_map/pallas_call | solution.py:422
  114.2 1.2 collective-permute-done.7.refs_1_.refs_0_.refs_4_.refs_3_.refs_2_
  115.6 3.2 %collective-permute-start.14 = (f32[64,2560]{1,0:T(8,128)S(1)}, f32[64,2560]{1,0:T(8,128)S(1)}, u32[]{:S(2)}, u32[]{:S(2)}) collective-permute-start(f32[64,2560]{1,0:T(8,128)S(1)} %shard_map.81.refs_2_.refs_1_.refs_0_), channel_id=1, source_target_pairs={{0,2},{7,5},{8,10},{15,13},{16,18},{23,21},{24,26},{31,29}} | collective-permute-start | bytes 1966088 | tf_op jit(solution)/shard_map/ppermute | solution.py:465
  118.9 1.3 collective-permute-start.11
  120.8 8.4 %shard_map.83 = (f32[64,2560]{1,0:T(8,128)S(1)}, f32[64,2560]{1,0:T(8,128)S(1)}) custom-call(bf16[3072,4608]{1,0:T(8,128)(2,1)} %refs_1_.11, bf16[3072,4608]{1,0:T(8,128)(2,1)} %refs_1_.11, f32[64,3072]{1,0:T(8,128)S(1)} %shard_map.76.refs_2_.refs_3_.refs_0_, f32[64,3072]{1,0:T(8,128)S(1)} %collective-permute-done.6.refs_0_.refs_3_.refs_2_.refs_1_, ...), custom_call_target="tpu_custom_call" | custom-call | bytes 73800 | tf_op jit(solution)/shard_map/pallas_call | solution.py:422
  129.7 7.8 %shard_map.84 = (f32[64,2304]{1,0:T(8,128)S(1)}, f32[64,2304]{1,0:T(8,128)S(1)}) custom-call(bf16[3072,4608]{1,0:T(8,128)(2,1)} %refs_1_.11, bf16[3072,4608]{1,0:T(8,128)(2,1)} %refs_1_.11, f32[64,3072]{1,0:T(8,128)S(1)} %collective-permute-done.6.refs_0_.refs_3_.refs_2_.refs_1_, ...), custom_call_target="tpu_custom_call" | custom-call | bytes 73800 | tf_op jit(solution)/shard_map/pallas_call | solution.py:422
  139.0 1.3 collective-permute-start.18
  141.2 3.5 %collective-permute-start.17 = (f32[64,2304]{1,0:T(8,128)S(1)}, f32[64,2304]{1,0:T(8,128)S(1)}, u32[]{:S(2)}, u32[]{:S(2)}) collective-permute-start(f32[64,2304]{1,0:T(8,128)S(1)} %shard_map.89.refs_6_), channel_id=1, source_target_pairs={{0,2},{2,4},{7,5},{5,3},{8,10},{10,12},{15,13},{13,11},{16,18},{18... | collective-permute-start | bytes 1769480 | tf_op jit(solution)/shard_map/ppermute | solution.py:483
  144.8 8.5 %shard_map.90.refs_3_.refs_0_ = f32[64,2560]{1,0:T(8,128)S(1)} custom-call(bf16[3072,4608]{1,0:T(8,128)(2,1)} %refs_1_.11, bf16[3072,4608]{1,0:T(8,128)(2,1)} %refs_1_.11, f32[64,3072]{1,0:T(8,128)S(1)} %shard_map.76.refs_2_.refs_3_.refs_0_, f32[64,3072]{1,0:T(8,128)S(1)} %collective-permute-done.6.refs_0_.refs_3_.refs_2_.refs_1_, ...), custom_call_target="tpu_custom_call" | custom-call | bytes 73800 | tf_op jit(solution)/shard_map/pallas_call | solution.py:422
  153.3 7.8 %shard_map.91._.refs_0_ = f32[64,2304]{1,0:T(8,128)S(1)} custom-call(bf16[3072,4608]{1,0:T(8,128)(2,1)} %refs_1_.11, bf16[3072,4608]{1,0:T(8,128)(2,1)} %refs_1_.11, f32[64,3072]{1,0:T(8,128)S(1)} %collective-permute-done.8.refs_2_.refs_5_.refs_3_, f32[64,2560]{1,0:T(8,128)S(1)} %shard_map.90.refs_3_.refs_0_), custom_call_target="tpu_custom_call" | custom-call | bytes 73800 | tf_op jit(solution)/shard_map/pallas_call | solution.py:422
  161.7 1.9 collective-permute-start.21
  164.3 1.9 collective-permute-start.19
  166.3 11.7 %collective-permute-done.19.refs_1_.come_ref.refs_2_.refs_0_ = f32[64,2304]{1,0:T(8,128)S(1)} collective-permute-done((f32[64,2304]{1,0:T(8,128)S(1)}, f32[64,2304]{1,0:T(8,128)S(1)}, u32[]{:S(2)}, u32[]{:S(2)}) %collective-permute-start.19) | collective-permute-done | bytes 589856 | tf_op jit(solution)/shard_map/ppermute | solution.py:483
  178.7 4.5 %collective-permute-start.26 = (f32[64,2560]{1,0:T(8,128)S(1)}, f32[64,2560]{1,0:T(8,128)S(1)}, u32[]{:S(2)}, u32[]{:S(2)}) collective-permute-start(f32[64,2560]{1,0:T(8,128)S(1)} %shard_map.96.refs_2_), channel_id=1, source_target_pairs={{0,2},{2,4},{4,6},{7,5},{5,3},{3,1},{8,10},{10,12},{12,14},{15,13}... | collective-permute-start | bytes 1966088 | tf_op jit(solution)/shard_map/ppermute | solution.py:483
  183.3 2.0 collective-permute-done.20.refs_1_
  185.9 4.2 %shard_map.99 = (f32[3072,256]{1,0:T(8,128)}, f32[8,128]{1,0:T(8,128)S(1)}) custom-call(s32[1]{0:T(128)} %bitcast.me_ref, f32[64,3072]{1,0:T(8,128)S(1)} %shard_map.76.refs_2_.refs_3_.refs_0_, f32[64,3072]{1,0:T(8,128)S(1)} %collective-permute-done.6.refs_0_.refs_3_.refs_2_.refs_1_, ...), custom_call_target="tpu_custom_call" | custom-call | bytes 73800 | tf_op jit(solution)/shard_map/pallas_call | solution.py:378
  192.8 5.5 %collective-permute-start.25 = (f32[64,2304]{1,0:T(8,128)S(1)}, f32[64,2304]{1,0:T(8,128)S(1)}, u32[]{:S(2)}, u32[]{:S(2)}) collective-permute-start(f32[64,2304]{1,0:T(8,128)S(1)} %shard_map.98.refs_4_), channel_id=1, source_target_pairs={{0,2},{2,4},{4,6},{7,5},{5,3},{3,1},{8,10},{10,12},{12,14},{15,13}... | collective-permute-start | bytes 1769480 | tf_op jit(solution)/shard_map/ppermute | solution.py:483
  198.4 7.3 %collective-permute-done.25.come_ref.refs_2_.refs_1_.refs_0_ = f32[64,2304]{1,0:T(8,128)S(1)} collective-permute-done((f32[64,2304]{1,0:T(8,128)S(1)}, f32[64,2304]{1,0:T(8,128)S(1)}, u32[]{:S(2)}, u32[]{:S(2)}) %collective-permute-start.25) | collective-permute-done | bytes 589856 | tf_op jit(solution)/shard_map/ppermute | solution.py:483
  206.8 4.6 %collective-permute-start.27 = (f32[64,2560]{1,0:T(8,128)S(1)}, f32[64,2560]{1,0:T(8,128)S(1)}, u32[]{:S(2)}, u32[]{:S(2)}) collective-permute-start(f32[64,2560]{1,0:T(8,128)S(1)} %shard_map.105._.refs_4_.refs_1_), channel_id=1, source_target_pairs={{0,1},{1,0},{2,3},{3,2},{4,5},{5,4},{6,7},{7,6},{8,9},{9,8},{10,11... | collective-permute-start | bytes 1966088 | tf_op jit(solution)/shard_map/ppermute | solution.py:253
  214.0 1.3 collective-permute-start.28
  217.5 14.0 %collective-permute-start.31 = (f32[64,2560]{1,0:T(8,128)S(1)}, f32[64,2560]{1,0:T(8,128)S(1)}, u32[]{:S(2)}, u32[]{:S(2)}) collective-permute-start(f32[64,2560]{1,0:T(8,128)S(1)} %shard_map.110._.refs_7_.refs_1_), channel_id=1, source_target_pairs={{0,1},{1,0},{2,3},{3,2},{4,5},{5,4},{6,7},{7,6},{8,9},{9,8},{10,11... | collective-permute-start | bytes 1966088 | tf_op jit(solution)/shard_map/ppermute | solution.py:253
  235.2 5.8 %shard_map.113 = (f32[256,4608]{1,0:T(8,128)S(1)}, f32[8,128]{1,0:T(8,128)S(1)}) custom-call(s32[1]{0:T(128)} %bitcast.me_ref, f32[256,4608]{1,0:T(8,128)S(1)} %bitcast.4, f32[64,2560]{1,0:T(8,128)S(1)} %shard_map.81.refs_2_.refs_1_.refs_0_, f32[64,2560]{1,0:T(8,128)S(1)} %shard_map.100._.refs_1_, f32[64,2560]{1,0:T(8,128)S(1)} %collective-permute-done.23.refs_0_.refs_2_, ...), custom_call_target="tpu_custom_call" | custom-call | bytes 73800 | tf_op jit(solution)/shard_map/pallas_call | solution.py:540
  241.6 3.3 %collective-permute-start.36 = (f32[64,2304]{1,0:T(8,128)S(1)}, f32[64,2304]{1,0:T(8,128)S(1)}, u32[]{:S(2)}, u32[]{:S(2)}) collective-permute-start(f32[64,2304]{1,0:T(8,128)S(1)} %shard_map.114._.refs_1_), channel_id=1, source_target_pairs={{0,1},{1,0},{2,3},{3,2},{4,5},{5,4},{6,7},{7,6},{8,9},{9,8},{10,11... | collective-permute-start | bytes 1769480 | tf_op jit(solution)/shard_map/ppermute | solution.py:253
  244.9 1.3 shard_map.115
  246.2 1.3 shard_map.116
  247.5 1.3 shard_map.117
  (127 shorter events, 37.6 us)
Async XLA Ops:
  1.3 1.9 copy-start
  6.6 30.2 %all-to-all-start = ((f32[8,72,384]{2,1,0:T(8,128)}), f32[8,72,384]{2,1,0:T(8,128)S(1)}, u32[]{:S(2)}, u32[]{:S(2)}) async-start(f32[8,72,384]{2,1,0:T(8,128)} %shard_map.68.refs_1_.pay_ref), calls=%async_computation | async-start | bytes 1769472 | tf_op jit(solution)/shard_map/all_to_all | solution.py:613
  25.1 10.2 %copy-start.2 = (f32[2,64,1792]{2,1,0:T(8,128)}, f32[2,64,1792]{2,1,0:T(8,128)S(1)}, u32[]{:S(2)}) copy-start(f32[2,64,1792]{2,1,0:T(8,128)S(1)} %get-tuple-element.35.refs_1_.refs_0_.refs_3_) | copy-start | bytes 2752516
  25.1 22.8 %collective-permute-start.3 = (f32[2,64,1792]{2,1,0:T(8,128)S(1)}, f32[2,64,1792]{2,1,0:T(8,128)S(1)}, u32[]{:S(2)}, u32[]{:S(2)}) collective-permute-start(f32[2,64,1792]{2,1,0:T(8,128)S(1)} %get-tuple-element.42), channel_id=1, source_target_pairs={{0,16},{8,24},{16,0},{24,8},{1,17},{9,25},{17,1},{25,9},{2,18},{10... | collective-permute-start | bytes 2752520 | tf_op jit(solution)/shard_map/ppermute | solution.py:253
  26.7 10.1 %copy-start.18 = (s32[12,256]{1,0:T(8,128)S(1)}, s32[12,256]{1,0:T(8,128)}, u32[]{:S(2)}) copy-start(s32[12,256]{1,0:T(8,128)} %code_ref.3) | copy-start | bytes 36868
  35.3 12.6 %copy-start.7 = (f32[2,64,1536]{2,1,0:T(8,128)}, f32[2,64,1536]{2,1,0:T(8,128)S(1)}, u32[]{:S(2)}) copy-start(f32[2,64,1536]{2,1,0:T(8,128)S(1)} %get-tuple-element.36._.refs_0_) | copy-start | bytes 2359300
  35.3 20.0 %collective-permute-start.2 = (f32[2,64,1536]{2,1,0:T(8,128)}, f32[2,64,1536]{2,1,0:T(8,128)}, u32[]{:S(2)}, u32[]{:S(2)}) collective-permute-start(f32[2,64,1536]{2,1,0:T(8,128)} %get-tuple-element.41), channel_id=1, source_target_pairs={{0,8},{8,0},{16,24},{24,16},{1,9},{9,1},{17,25},{25,17},{2,10},{10... | collective-permute-start | bytes 2359304 | tf_op jit(solution)/shard_map/ppermute | solution.py:253
  39.5 18.0 %collective-permute-start = (f32[72,256]{1,0:T(8,128)S(1)}, f32[72,256]{1,0:T(8,128)S(1)}, u32[]{:S(2)}, u32[]{:S(2)}) collective-permute-start(f32[72,256]{1,0:T(8,128)S(1)} %get-tuple-element.38), channel_id=1, source_target_pairs={{0,1},{1,2},{2,3},{3,4},{4,5},{5,6},{6,7},{8,9},{9,10},{10,11},{11... | collective-permute-start | bytes 221192 | tf_op jit(solution)/shard_map/ppermute | solution.py:637
  41.4 16.1 %collective-permute-start.1 = (f32[72,256]{1,0:T(8,128)S(1)}, f32[72,256]{1,0:T(8,128)S(1)}, u32[]{:S(2)}, u32[]{:S(2)}) collective-permute-start(f32[72,256]{1,0:T(8,128)S(1)} %get-tuple-element.39), channel_id=1, source_target_pairs={{1,0},{2,1},{3,2},{4,3},{5,4},{6,5},{7,6},{9,8},{10,9},{11,10},{12... | collective-permute-start | bytes 221192 | tf_op jit(solution)/shard_map/ppermute | solution.py:638
  51.3 28.3 %copy-start.1 = (f32[3072,256]{1,0:T(8,128)S(1)}, f32[3072,256]{1,0:T(8,128)}, u32[]{:S(2)}) copy-start(f32[3072,256]{1,0:T(8,128)} %refs_6_.1) | copy-start | bytes 9437188
  51.3 6.2 %copy-start.13 = (f32[1,64,1792]{2,1,0:T(8,128)}, f32[1,64,1792]{2,1,0:T(8,128)S(1)}, u32[]{:S(2)}) copy-start(f32[1,64,1792]{2,1,0:T(8,128)S(1)} %shard_map.72.refs_2_) | copy-start | bytes 1376260
  61.7 28.4 %all-to-all-start.1 = ((f32[8,72,384]{2,1,0:T(8,128)}), f32[8,72,384]{2,1,0:T(8,128)}, u32[]{:S(2)}, u32[]{:S(2)}) async-start(f32[8,72,384]{2,1,0:T(8,128)} %copy-done.5), calls=%async_computation.1 | async-start | bytes 1769472 | tf_op jit(solution)/shard_map/all_to_all | solution.py:644
  66.4 13.1 %collective-permute-start.5 = (f32[1,64,1792]{2,1,0:T(8,128)}, f32[1,64,1792]{2,1,0:T(8,128)S(1)}, u32[]{:S(2)}, u32[]{:S(2)}) collective-permute-start(f32[1,64,1792]{2,1,0:T(8,128)} %copy-done.13), channel_id=1, source_target_pairs={{0,8},{8,0},{16,24},{24,16},{1,9},{9,1},{17,25},{25,17},{2,10},{10... | collective-permute-start | bytes 1376264 | tf_op jit(solution)/shard_map/ppermute | solution.py:253
  67.9 11.2 %collective-permute-start.4 = (f32[1,64,1536]{2,1,0:T(8,128)S(1)}, f32[1,64,1536]{2,1,0:T(8,128)S(1)}, u32[]{:S(2)}, u32[]{:S(2)}) collective-permute-start(f32[1,64,1536]{2,1,0:T(8,128)S(1)} %shard_map.73._), channel_id=1, source_target_pairs={{0,16},{8,24},{16,0},{24,8},{1,17},{9,25},{17,1},{25,9},{2,18},{10... | collective-permute-start | bytes 1179656 | tf_op jit(solution)/shard_map/ppermute | solution.py:253
  79.6 1.2 copy-start.4
  94.9 19.3 %collective-permute-start.6 = (f32[64,3072]{1,0:T(8,128)S(1)}, f32[64,3072]{1,0:T(8,128)S(1)}, u32[]{:S(2)}, u32[]{:S(2)}) collective-permute-start(f32[64,3072]{1,0:T(8,128)S(1)} %shard_map.76.refs_2_.refs_3_.refs_0_), channel_id=1, source_target_pairs={{0,8},{8,0},{16,24},{24,16},{1,9},{9,1},{17,25},{25,17},{2,10},{10... | collective-permute-start | bytes 2359304 | tf_op jit(solution)/shard_map/ppermute | solution.py:253
  96.4 19.0 %collective-permute-start.7 = (f32[64,3072]{1,0:T(8,128)S(1)}, f32[64,3072]{1,0:T(8,128)S(1)}, u32[]{:S(2)}, u32[]{:S(2)}) collective-permute-start(f32[64,3072]{1,0:T(8,128)S(1)} %shard_map.76.refs_2_.refs_3_.refs_0_), channel_id=1, source_target_pairs={{0,16},{8,24},{16,0},{24,8},{1,17},{9,25},{17,1},{25,9},{2,18},{10... | collective-permute-start | bytes 2359304 | tf_op jit(solution)/shard_map/ppermute | solution.py:253
  105.0 10.5 %collective-permute-start.10 = (f32[64,2560]{1,0:T(8,128)S(1)}, f32[64,2560]{1,0:T(8,128)S(1)}, u32[]{:S(2)}, u32[]{:S(2)}) collective-permute-start(f32[64,2560]{1,0:T(8,128)S(1)} %shard_map.77.refs_3_.refs_0_), channel_id=1, source_target_pairs={{0,1},{1,0},{2,3},{3,2},{4,5},{5,4},{6,7},{7,6},{8,9},{9,8},{10,11... | collective-permute-start | bytes 1966088 | tf_op jit(solution)/shard_map/ppermute | solution.py:253
  112.8 5.9 %collective-permute-start.9 = (f32[64,2304]{1,0:T(8,128)S(1)}, f32[64,2304]{1,0:T(8,128)S(1)}, u32[]{:S(2)}, u32[]{:S(2)}) collective-permute-start(f32[64,2304]{1,0:T(8,128)S(1)} %shard_map.78.refs_2_.refs_0_), channel_id=1, source_target_pairs={{0,1},{1,0},{2,3},{3,2},{4,5},{5,4},{6,7},{7,6},{8,9},{9,8},{10,11... | collective-permute-start | bytes 1769480 | tf_op jit(solution)/shard_map/ppermute | solution.py:253
  115.6 22.1 %collective-permute-start.14 = (f32[64,2560]{1,0:T(8,128)S(1)}, f32[64,2560]{1,0:T(8,128)S(1)}, u32[]{:S(2)}, u32[]{:S(2)}) collective-permute-start(f32[64,2560]{1,0:T(8,128)S(1)} %shard_map.81.refs_2_.refs_1_.refs_0_), channel_id=1, source_target_pairs={{0,2},{7,5},{8,10},{15,13},{16,18},{23,21},{24,26},{31,29}} | collective-permute-start | bytes 1966088 | tf_op jit(solution)/shard_map/ppermute | solution.py:465
  118.9 18.7 %collective-permute-start.11 = (f32[64,2304]{1,0:T(8,128)S(1)}, f32[64,2304]{1,0:T(8,128)S(1)}, u32[]{:S(2)}, u32[]{:S(2)}) collective-permute-start(f32[64,2304]{1,0:T(8,128)S(1)} %shard_map.82.refs_5_.refs_1_.refs_2_.refs_3_), channel_id=1, source_target_pairs={{0,2},{7,5},{8,10},{15,13},{16,18},{23,21},{24,26},{31,29}} | collective-permute-start | bytes 1769480 | tf_op jit(solution)/shard_map/ppermute | solution.py:465
  120.2 18.0 %collective-permute-start.8 = (f32[64,3072]{1,0:T(8,128)S(1)}, f32[64,3072]{1,0:T(8,128)S(1)}, u32[]{:S(2)}, u32[]{:S(2)}) collective-permute-start(f32[64,3072]{1,0:T(8,128)S(1)} %shard_map.80.refs_2_), channel_id=1, source_target_pairs={{0,8},{8,0},{16,24},{24,16},{1,9},{9,1},{17,25},{25,17},{2,10},{10... | collective-permute-start | bytes 2359304 | tf_op jit(solution)/shard_map/ppermute | solution.py:253
  129.2 9.1 %collective-permute-start.15 = (f32[64,2560]{1,0:T(8,128)S(1)}, f32[64,2560]{1,0:T(8,128)S(1)}, u32[]{:S(2)}, u32[]{:S(2)}) collective-permute-start(f32[64,2560]{1,0:T(8,128)S(1)} %get-tuple-element.48.refs_0_), channel_id=1, source_target_pairs={{0,1},{1,0},{2,3},{3,2},{4,5},{5,4},{6,7},{7,6},{8,9},{9,8},{10,11... | collective-permute-start | bytes 1966088 | tf_op jit(solution)/shard_map/ppermute | solution.py:253
  129.2 9.0 %collective-permute-start.16 = (f32[64,2560]{1,0:T(8,128)S(1)}, f32[64,2560]{1,0:T(8,128)S(1)}, u32[]{:S(2)}, u32[]{:S(2)}) collective-permute-start(f32[64,2560]{1,0:T(8,128)S(1)} %get-tuple-element.45.refs_4_.refs_1_), channel_id=1, source_target_pairs={{0,1},{1,0},{2,3},{3,2},{4,5},{5,4},{6,7},{7,6},{8,9},{9,8},{10,11... | collective-permute-start | bytes 1966088 | tf_op jit(solution)/shard_map/ppermute | solution.py:253
  137.5 2.8 %collective-permute-start.12 = (f32[64,2304]{1,0:T(8,128)S(1)}, f32[64,2304]{1,0:T(8,128)S(1)}, u32[]{:S(2)}, u32[]{:S(2)}) collective-permute-start(f32[64,2304]{1,0:T(8,128)S(1)} %get-tuple-element.46.refs_0_), channel_id=1, source_target_pairs={{0,1},{1,0},{2,3},{3,2},{4,5},{5,4},{6,7},{7,6},{8,9},{9,8},{10,11... | collective-permute-start | bytes 1769480 | tf_op jit(solution)/shard_map/ppermute | solution.py:253
  137.7 2.8 %collective-permute-start.13 = (f32[64,2304]{1,0:T(8,128)S(1)}, f32[64,2304]{1,0:T(8,128)S(1)}, u32[]{:S(2)}, u32[]{:S(2)}) collective-permute-start(f32[64,2304]{1,0:T(8,128)S(1)} %get-tuple-element.47.refs_3_.refs_1_), channel_id=1, source_target_pairs={{0,1},{1,0},{2,3},{3,2},{4,5},{5,4},{6,7},{7,6},{8,9},{9,8},{10,11... | collective-permute-start | bytes 1769480 | tf_op jit(solution)/shard_map/ppermute | solution.py:253
  139.0 22.1 %collective-permute-start.18 = (f32[64,2560]{1,0:T(8,128)S(1)}, f32[64,2560]{1,0:T(8,128)S(1)}, u32[]{:S(2)}, u32[]{:S(2)}) collective-permute-start(f32[64,2560]{1,0:T(8,128)S(1)} %shard_map.87.refs_4_), channel_id=1, source_target_pairs={{0,2},{2,4},{7,5},{5,3},{8,10},{10,12},{15,13},{13,11},{16,18},{18... | collective-permute-start | bytes 1966088 | tf_op jit(solution)/shard_map/ppermute | solution.py:483
  141.2 22.5 %collective-permute-start.17 = (f32[64,2304]{1,0:T(8,128)S(1)}, f32[64,2304]{1,0:T(8,128)S(1)}, u32[]{:S(2)}, u32[]{:S(2)}) collective-permute-start(f32[64,2304]{1,0:T(8,128)S(1)} %shard_map.89.refs_6_), channel_id=1, source_target_pairs={{0,2},{2,4},{7,5},{5,3},{8,10},{10,12},{15,13},{13,11},{16,18},{18... | collective-permute-start | bytes 1769480 | tf_op jit(solution)/shard_map/ppermute | solution.py:483
  161.7 16.3 %collective-permute-start.21 = (f32[64,2560]{1,0:T(8,128)S(1)}, f32[64,2560]{1,0:T(8,128)S(1)}, u32[]{:S(2)}, u32[]{:S(2)}) collective-permute-start(f32[64,2560]{1,0:T(8,128)S(1)} %shard_map.92._), channel_id=1, source_target_pairs={{0,2},{2,4},{4,6},{7,5},{5,3},{3,1},{8,10},{10,12},{12,14},{15,13}... | collective-permute-start | bytes 1966088 | tf_op jit(solution)/shard_map/ppermute | solution.py:483
  163.6 14.4 %collective-permute-start.22 = (f32[64,2560]{1,0:T(8,128)S(1)}, f32[64,2560]{1,0:T(8,128)S(1)}, u32[]{:S(2)}, u32[]{:S(2)}) collective-permute-start(f32[64,2560]{1,0:T(8,128)S(1)} %shard_map.90.refs_3_.refs_0_), channel_id=1, source_target_pairs={{0,1},{1,0},{2,3},{3,2},{4,5},{5,4},{6,7},{7,6},{8,9},{9,8},{10,11... | collective-permute-start | bytes 1966088 | tf_op jit(solution)/shard_map/ppermute | solution.py:253
  164.3 13.7 %collective-permute-start.19 = (f32[64,2304]{1,0:T(8,128)S(1)}, f32[64,2304]{1,0:T(8,128)S(1)}, u32[]{:S(2)}, u32[]{:S(2)}) collective-permute-start(f32[64,2304]{1,0:T(8,128)S(1)} %shard_map.93.refs_2_), channel_id=1, source_target_pairs={{0,2},{2,4},{4,6},{7,5},{5,3},{3,1},{8,10},{10,12},{12,14},{15,13}... | collective-permute-start | bytes 1769480 | tf_op jit(solution)/shard_map/ppermute | solution.py:483
  178.7 12.8 %collective-permute-start.26 = (f32[64,2560]{1,0:T(8,128)S(1)}, f32[64,2560]{1,0:T(8,128)S(1)}, u32[]{:S(2)}, u32[]{:S(2)}) collective-permute-start(f32[64,2560]{1,0:T(8,128)S(1)} %shard_map.96.refs_2_), channel_id=1, source_target_pairs={{0,2},{2,4},{4,6},{7,5},{5,3},{3,1},{8,10},{10,12},{12,14},{15,13}... | collective-permute-start | bytes 1966088 | tf_op jit(solution)/shard_map/ppermute | solution.py:483
  183.2 2.1 collective-permute-start.20
  190.7 15.5 %collective-permute-start.23 = (f32[64,2560]{1,0:T(8,128)S(1)}, f32[64,2560]{1,0:T(8,128)S(1)}, u32[]{:S(2)}, u32[]{:S(2)}) collective-permute-start(f32[64,2560]{1,0:T(8,128)S(1)} %shard_map.100._.refs_1_), channel_id=1, source_target_pairs={{0,1},{1,0},{2,3},{3,2},{4,5},{5,4},{6,7},{7,6},{8,9},{9,8},{10,11... | collective-permute-start | bytes 1966088 | tf_op jit(solution)/shard_map/ppermute | solution.py:253
  192.1 20.0 %collective-permute-start.30 = (f32[64,2560]{1,0:T(8,128)S(1)}, f32[64,2560]{1,0:T(8,128)S(1)}, u32[]{:S(2)}, u32[]{:S(2)}) collective-permute-start(f32[64,2560]{1,0:T(8,128)S(1)} %shard_map.102._), channel_id=1, source_target_pairs={{2,4},{4,6},{5,3},{3,1},{10,12},{12,14},{13,11},{11,9},{18,20},{20... | collective-permute-start | bytes 1966088 | tf_op jit(solution)/shard_map/ppermute | solution.py:483
  192.8 12.8 %collective-permute-start.25 = (f32[64,2304]{1,0:T(8,128)S(1)}, f32[64,2304]{1,0:T(8,128)S(1)}, u32[]{:S(2)}, u32[]{:S(2)}) collective-permute-start(f32[64,2304]{1,0:T(8,128)S(1)} %shard_map.98.refs_4_), channel_id=1, source_target_pairs={{0,2},{2,4},{4,6},{7,5},{5,3},{3,1},{8,10},{10,12},{12,14},{15,13}... | collective-permute-start | bytes 1769480 | tf_op jit(solution)/shard_map/ppermute | solution.py:483
  198.3 7.9 %collective-permute-start.24 = (f32[64,2304]{1,0:T(8,128)S(1)}, f32[64,2304]{1,0:T(8,128)S(1)}, u32[]{:S(2)}, u32[]{:S(2)}) collective-permute-start(f32[64,2304]{1,0:T(8,128)S(1)} %shard_map.101._.refs_4_), channel_id=1, source_target_pairs={{0,1},{1,0},{2,3},{3,2},{4,5},{5,4},{6,7},{7,6},{8,9},{9,8},{10,11... | collective-permute-start | bytes 1769480 | tf_op jit(solution)/shard_map/ppermute | solution.py:253
  206.8 10.1 %collective-permute-start.27 = (f32[64,2560]{1,0:T(8,128)S(1)}, f32[64,2560]{1,0:T(8,128)S(1)}, u32[]{:S(2)}, u32[]{:S(2)}) collective-permute-start(f32[64,2560]{1,0:T(8,128)S(1)} %shard_map.105._.refs_4_.refs_1_), channel_id=1, source_target_pairs={{0,1},{1,0},{2,3},{3,2},{4,5},{5,4},{6,7},{7,6},{8,9},{9,8},{10,11... | collective-permute-start | bytes 1966088 | tf_op jit(solution)/shard_map/ppermute | solution.py:253
  212.6 19.8 %collective-permute-start.32 = (f32[64,2560]{1,0:T(8,128)S(1)}, f32[64,2560]{1,0:T(8,128)S(1)}, u32[]{:S(2)}, u32[]{:S(2)}) collective-permute-start(f32[64,2560]{1,0:T(8,128)S(1)} %shard_map.107._), channel_id=1, source_target_pairs={{4,6},{3,1},{12,14},{11,9},{20,22},{19,17},{28,30},{27,25}} | collective-permute-start | bytes 1966088 | tf_op jit(solution)/shard_map/ppermute | solution.py:483
  213.3 2.0 collective-permute-start.29
  214.0 2.9 %collective-permute-start.28 = (f32[64,2304]{1,0:T(8,128)S(1)}, f32[64,2304]{1,0:T(8,128)S(1)}, u32[]{:S(2)}, u32[]{:S(2)}) collective-permute-start(f32[64,2304]{1,0:T(8,128)S(1)} %shard_map.106._.refs_4_), channel_id=1, source_target_pairs={{0,1},{1,0},{2,3},{3,2},{4,5},{5,4},{6,7},{7,6},{8,9},{9,8},{10,11... | collective-permute-start | bytes 1769480 | tf_op jit(solution)/shard_map/ppermute | solution.py:253
  215.3 19.9 %slice-start = ((s8[4718592]{0:T(1024)(128)(4,1)}), s8[4194304]{0:T(1024)(128)(4,1)S(1)}, s32[]{:S(2)}) async-start(s8[4718592]{0:T(1024)(128)(4,1)} %bitcast.3), calls=%async_computation.2 | async-start | bytes 8388608
  216.9 18.3 %slice-start.1 = ((s8[4718592]{0:T(1024)(128)(4,1)}), s8[524288]{0:T(1024)(128)(4,1)S(1)}, s32[]{:S(2)}) async-start(s8[4718592]{0:T(1024)(128)(4,1)} %bitcast.3), calls=%async_computation.3 | async-start | bytes 1048576
  217.5 17.4 %collective-permute-start.31 = (f32[64,2560]{1,0:T(8,128)S(1)}, f32[64,2560]{1,0:T(8,128)S(1)}, u32[]{:S(2)}, u32[]{:S(2)}) collective-permute-start(f32[64,2560]{1,0:T(8,128)S(1)} %shard_map.110._.refs_7_.refs_1_), channel_id=1, source_target_pairs={{0,1},{1,0},{2,3},{3,2},{4,5},{5,4},{6,7},{7,6},{8,9},{9,8},{10,11... | collective-permute-start | bytes 1966088 | tf_op jit(solution)/shard_map/ppermute | solution.py:253
  233.0 2.2 collective-permute-start.33
  233.1 7.9 %collective-permute-start.34 = (f32[64,2304]{1,0:T(8,128)S(1)}, f32[64,2304]{1,0:T(8,128)S(1)}, u32[]{:S(2)}, u32[]{:S(2)}) collective-permute-start(f32[64,2304]{1,0:T(8,128)S(1)} %shard_map.108.refs_2_), channel_id=1, source_target_pairs={{4,6},{3,1},{12,14},{11,9},{20,22},{19,17},{28,30},{27,25}} | collective-permute-start | bytes 1769480 | tf_op jit(solution)/shard_map/ppermute | solution.py:483
  233.8 13.7 %collective-permute-start.35 = (f32[64,2304]{1,0:T(8,128)S(1)}, f32[64,2304]{1,0:T(8,128)S(1)}, u32[]{:S(2)}, u32[]{:S(2)}) collective-permute-start(f32[64,2304]{1,0:T(8,128)S(1)} %shard_map.111._.refs_4_), channel_id=1, source_target_pairs={{0,1},{1,0},{2,3},{3,2},{4,5},{5,4},{6,7},{7,6},{8,9},{9,8},{10,11... | collective-permute-start | bytes 1769480 | tf_op jit(solution)/shard_map/ppermute | solution.py:253
  241.6 8.2 %collective-permute-start.36 = (f32[64,2304]{1,0:T(8,128)S(1)}, f32[64,2304]{1,0:T(8,128)S(1)}, u32[]{:S(2)}, u32[]{:S(2)}) collective-permute-start(f32[64,2304]{1,0:T(8,128)S(1)} %shard_map.114._.refs_1_), channel_id=1, source_target_pairs={{0,1},{1,0},{2,3},{3,2},{4,5},{5,4},{6,7},{7,6},{8,9},{9,8},{10,11... | collective-permute-start | bytes 1769480 | tf_op jit(solution)/shard_map/ppermute | solution.py:253
  (12 other events, 12.8 us)

commit v2 on v1

--- a/solution.py
+++ b/solution.py
@@ -220,7 +220,7 @@
                 put(turned[...].T, slice(half_rows, total_cols))
 
     out = shape(genes_n // 2, width, total_cols)
-    out_spec = pl.BlockSpec(out.shape, lambda i, m: (0, 0, 0))
+    out_spec = pl.BlockSpec((genes_n // 2, width, total_cols), lambda i, m: (0, 0, 0))
     outs, out_specs, scratch = (out, out), (out_spec, out_spec), []
     if first_call:
         outs += (shape(genes, width_all, dtype=BF16),)
@@ -304,7 +304,7 @@
     arrays = list(first) + list(second)
     return kernel_call(
         body,
-        (shape(width, rows),) * 2,
+        (pltpu.HBM((width, rows), F32),) * 2,
         4,
         limit=24,
         grid=(2,),
@@ -350,6 +350,7 @@
         body,
         tuple(shape(*b.shape) for b in blocks),
         0.02,
+        limit=1,
         in_specs=[VMEM_SPEC] * n + [ANY_SPEC],
         out_specs=(VMEM_SPEC,) * n,
     )(*blocks, token)
@@ -378,57 +379,93 @@
     return kernel_call(body, outs, 0.02, limit=8, grid_spec=grid_spec)(me, *blocks, token)
 
 
-def cross_part(blocks, n_old, counts, half, with_gram, width_all, tokens):
+def put_rounded(fac, refs, width):
+    for j, ref in enumerate(refs):
+        fac[j * width : (j + 1) * width, :] = ref[...].astype(BF16)
+
+
+def near_products(new, fac, width_all):
+    near = dot(new, fac, MINOR)
+    if near.shape[1] < width_all:
+        near = jnp.concatenate([near, jnp.zeros((near.shape[0], width_all - near.shape[1]), F32)], axis=1)
+    return near
+
+
+def first_cross(block, counts, width_all, token):
+    width, rows = block.shape
+    genes = counts.shape[1]
+    cols = genes // HALVES
+    step = STEP
+    steps = rows // step
+
+    def body(counts_ref, block_ref, _, *refs):
+        outs, held, (fac, sems) = refs[:HALVES], refs[HALVES : HALVES + steps], refs[HALVES + steps :]
+        copies = [
+            pltpu.make_async_copy(
+                counts_ref.at[pl.ds(i * step, step), :], held[i], sems.at[i]
+            )
+            for i in range(steps)
+        ]
+        for copy in copies:
+            copy.start()
+        put_rounded(fac, [block_ref], width)
+        near = near_products(fac[...], fac[...], width_all)
+        for out in outs:
+            out[:, cols:] = near
+        for i, copy in enumerate(copies):
+            copy.wait()
+            at = slice(i * step, (i + 1) * step)
+            for h, out in enumerate(outs):
+                part = dot(fac[:, at], held[i][:, h * cols : (h + 1) * cols], PLAIN)
+                out[:, :cols] = part if i == 0 else out[:, :cols] + part
+
+    return kernel_call(
+        body,
+        (shape(width, cols + width_all),) * HALVES + (pltpu.VMEM((step, genes), BF16),) * steps,
+        0.02,
+        limit=8,
+        in_specs=[ANY_SPEC, VMEM_SPEC, ANY_SPEC],
+        out_specs=(VMEM_SPEC,) * (HALVES + steps),
+        scratch_shapes=[pltpu.VMEM((width, rows), BF16), pltpu.SemaphoreType.DMA((steps,))],
+    )(counts, block, token)
+
+
+def cross_part(blocks, n_old, held, half, width_all, tokens):
     width, rows = blocks[0].shape
-    cols = counts.shape[1] // HALVES
+    cols = held[0].shape[1] // HALVES
+    steps = 3
+    step = cols // steps
     n = len(blocks) - n_old
-    deep = STEP // READS
-    use = blocks if with_gram else blocks[n_old:]
-    skip = len(use) - n
 
     def body(*refs):
+        pieces, refs = refs[: len(held)], refs[len(held) :]
         outs, fac = refs[-1 - n : -1], refs[-1]
-        at = pl.program_id(0)
-
-        @pl.when(at == 0)
-        def _():
-            for j, ref in enumerate(refs[READS : READS + len(use)]):
-                fac[j * width : (j + 1) * width, :] = ref[...].astype(BF16)
-
-        def put(part, where, add):
+        put_rounded(fac, refs[: len(blocks)], width)
+        new = fac[n_old * width :, :]
+
+        def put(part, where):
             for j, out in enumerate(outs):
-                value = part[j * width : (j + 1) * width]
-                out[:, where] = out[:, where] + value if add else value
-
-        part = None
-        for i in range(READS):
-            new = fac[skip * width :, pl.ds(pl.multiple_of(at * STEP + i * deep, deep), deep)]
-            more = dot(new, refs[i][...], PLAIN)
-            part = more if part is None else part + more
-        pl.when(at == 0)(lambda: put(part, slice(0, cols), False))
-        pl.when(at > 0)(lambda: put(part, slice(0, cols), True))
-
-        if with_gram:
-
-            @pl.when(at == 0)
-            def _():
-                near = dot(fac[skip * width :, :], fac[...], MINOR)
-                if near.shape[1] < width_all:
-                    gap = jnp.zeros((near.shape[0], width_all - near.shape[1]), F32)
-                    near = jnp.concatenate([near, gap], axis=1)
-                put(near, slice(cols, cols + width_all), False)
-
-    read = lambda i: pl.BlockSpec((deep, cols), lambda g: (g * READS + i, half))
-    return kernel_call(
-        body,
-        (shape(width, cols + with_gram * width_all),) * n,
-        0.02,
-        limit=24,
-        grid=(rows // STEP,),
-        in_specs=[read(i) for i in range(READS)] + [VMEM_SPEC] * len(use) + [ANY_SPEC] * len(tokens),
+                out[:, where] = part[j * width : (j + 1) * width]
+
+        for i in range(steps):
+            at = slice(half * cols + i * step, half * cols + (i + 1) * step)
+            part = None
+            for j, piece in enumerate(pieces):
+                here = slice(j * piece.shape[0], (j + 1) * piece.shape[0])
+                more = dot(new[:, here], piece[:, at], PLAIN)
+                part = more if part is None else part + more
+            put(part, slice(i * step, (i + 1) * step))
+        put(near_products(new, fac[...], width_all), slice(cols, cols + width_all))
+
+    return kernel_call(
+        body,
+        (shape(width, cols + width_all),) * n,
+        0.02,
+        limit=8,
+        in_specs=[VMEM_SPEC] * (len(held) + len(blocks)) + [ANY_SPEC] * len(tokens),
         out_specs=(VMEM_SPEC,) * n,
-        scratch_shapes=[pltpu.VMEM((len(use) * width, rows), BF16)],
-    )(*[counts] * READS, *use, *tokens)
+        scratch_shapes=[pltpu.VMEM((len(blocks) * width, rows), BF16)],
+    )(*held, *blocks, *tokens)
 
 
 def tiny_token(arrays):
@@ -436,7 +473,7 @@
         refs[-1][...] = jnp.zeros(refs[-1].shape, F32)
 
     return kernel_call(
-        body, shape(8, 128), 0.02, in_specs=[ANY_SPEC] * len(arrays), out_specs=VMEM_SPEC
+        body, shape(8, 128), 0.02, limit=1, in_specs=[ANY_SPEC] * len(arrays), out_specs=VMEM_SPEC
     )(*arrays)
 
 
@@ -451,6 +488,7 @@
         body,
         tuple(shape(*part.shape) for part in parts),
         0.02,
+        limit=1,
         in_specs=[VMEM_SPEC] * (2 * n) + [ANY_SPEC],
         out_specs=(VMEM_SPEC,) * n,
     )(*parts, *came, token)
@@ -477,6 +515,7 @@
         body,
         shape(*come.shape),
         0.02,
+        limit=1,
         in_specs=[SMEM_SPEC, VMEM_SPEC, ANY_SPEC] + [VMEM_SPEC] * len(arrays),
         out_specs=VMEM_SPEC,
     )(flags, come, token, *arrays)
@@ -501,6 +540,7 @@
         body,
         shape(*come[0].shape),
         0.02,
+        limit=1,
         in_specs=[SMEM_SPEC, ANY_SPEC] + [VMEM_SPEC] * len(come),
         out_specs=VMEM_SPEC,
     )(flags, token, *come)
@@ -611,6 +651,8 @@
     counts = pltpu.with_memory_space_constraint(counts, pltpu.HBM)
     payload = pack(factors, position, me1, width, bins)
     got = lax.all_to_all(payload, "bin", split_axis=0, concat_axis=0, tiled=True)
+    in_hbm = lambda x: pltpu.with_memory_space_constraint(x, pltpu.HBM)
+
     orders = (bits, bits[::-1])
     token, load = payload, pltpu.with_memory_space_constraint(loadings, pltpu.HBM)
     parts, keeps = [None, None], [None, None]
@@ -627,6 +669,7 @@
         out_ids = [i for i, k in enumerate(keeps[half]) if k & bit]
         in_ids = [i for i, k in enumerate(keeps[half]) if not k & bit]
         keeps[half] = [keeps[half][i] for i in in_ids]
+        parts[half] = [in_hbm(x) for x in parts[half]]
         send = picked_sum(parts[half], out_ids, token)
         if len(in_ids) > 1:
             parts[half] = [picked_sum(parts[half], in_ids, send)]
@@ -642,8 +685,8 @@
             token = scatter_more(half, orders[half][i], token)
     smooth = from_grid(grid, above, below, cell, edge_codes, bins, token)
     back = lax.all_to_all(smooth, "bin", split_axis=0, concat_axis=0, tiled=True)
-    numer, plain = plain_terms(*parts, factors, smooth)
-    own_block = new_factors(payload, back, numer, plain)
+    numer, plain = plain_terms(*[[in_hbm(x) for x in p] for p in parts], in_hbm(factors), smooth)
+    own_block = new_factors(*[in_hbm(x) for x in (payload, back, numer, plain)])
 
     ids = sorted(range(genes_n), key=lambda k: (bin(k).count("1"), k))
     groups = [[k for k in ids if bin(k).count("1") == n] for n in range(len(bits) + 1)]
@@ -666,9 +709,7 @@
     def product(g, half, *tokens):
         upto = ids.index(groups[g][-1]) + 1
         n_old = upto - len(groups[g])
-        parts = cross_part(
-            [blocks[k] for k in ids[:upto]], n_old, counts, half, half == 0, width_all, tokens
-        )
+        parts = cross_part([blocks[k] for k in ids[:upto]], n_old, held, half, width_all, tokens)
         pending[half][g] = (parts, [swap(part, "bin", 1) for part in parts])
         return parts[-1]
 
@@ -700,9 +741,11 @@
     def awaited(arrays, token):
         return tiny_token(list(arrays) + [token])
 
-    token = own_block
-    both(product, 0)
-    token = awaited([blocks[k] for k in bits], token)
+    made = first_cross(own_block, counts, width_all, own_block)
+    parts, held = made[:HALVES], made[HALVES:]
+    for half in range(HALVES):
+        pending[half][0] = ((parts[half],), [swap(parts[half], "bin", 1)])
+    token = awaited([blocks[k] for k in bits], parts[-1])
     if len(groups) > 2:
         token = come_on(groups[2], token)
     for half in range(HALVES):
@@ -712,11 +755,9 @@
     firsts = {ids.index(group[0]): g for g, group in enumerate(groups)}
     last_slot = chunks + line - 3
     for t in range(1, last_slot + 1):
-        if t in firsts:
-            arrived = [come[half][-1] for half in range(HALVES)]
-            if firsts[t] + 1 < len(groups):
-                arrived += [blocks[k] for k in groups[firsts[t] + 1]]
-            token = awaited(arrived, token)
+        if t in firsts and firsts[t] + 1 < len(groups):
+            token = awaited([blocks[k] for k in groups[firsts[t] + 1]], token)
+            token = awaited([come[half][-1] for half in range(HALVES)], token)
         for half in range(HALVES):
             if t in firsts:
                 token = own_chunks(firsts[t], half, token)

time: 252 us -> 220 us (0.87)
  Pallas kernels: 113 us -> 90.4 us
  local copies, waits for them, and re-layouts: 15.9 us -> 4.18 us
  waiting for transfers between devices: 44.9 us -> 49.9 us
    pallas_call x37 -> x36, Pallas kernels: 63.8 us -> 38.7 us  [the longest x4 11.2 us: cross_part(): kernel_call(body, (shape(width, cols + width_all),) * n, 0.02, limit=8, i...]
    ppermute x23, waiting for transfers between devices: 25.9 us -> 38.7 us  [swap(): lax.ppermute(block, axis, [(i, i ^ bit) for i in range(lax.axis_size(axis...]
    unnamed x42 -> x18, local copies, waits for them, and re-layouts: 15.9 us -> 4.18 us
    ppermute x10, waiting for transfers between devices: 19 us -> 7.31 us  [line_slot(): return (lax.ppermute(send, 'bin', hops), send)]
    ppermute x10, starting transfers between devices: 21.5 us -> 25.2 us  [line_slot(): return (lax.ppermute(send, 'bin', hops), send)]
    ppermute x23, starting transfers between devices: 34.3 us -> 31 us  [swap(): lax.ppermute(block, axis, [(i, i ^ bit) for i in range(lax.axis_size(axis...]
    all_to_all x1, waiting for transfers between devices: 0.01 us -> 2.89 us  [on_device(): lax.all_to_all(smooth, 'bin', split_axis=0, concat_axis=0, tiled=True)]
  transfers between devices with their start and end apart: 39 -> 39, of which waited for: 12 -> 15; matrix products, arithmetic and copies ran while one was open for 0% -> 0% of each run, Pallas kernels for 41% -> 36%
where the time goes in v2:
time: 220 us
  Pallas kernels  90.4 us (41%)
  starting transfers between devices  73.1 us (33%)
  waiting for transfers between devices  49.9 us (23%)
  local copies, waits for them, and re-layouts  4.18 us (2%)
    ppermute x23, waiting for transfers between devices, swap(): lax.ppermute(block, axis, [(i, i ^ bit) for i in range(lax.axis_size(axis...  38.7 us
    ppermute x23, starting transfers between devices, swap(): lax.ppermute(block, axis, [(i, i ^ bit) for i in range(lax.axis_size(axis...  31 us
    ppermute x10, starting transfers between devices, line_slot(): return (lax.ppermute(send, 'bin', hops), send)  25.2 us
    pallas_call x2, Pallas kernels, numer_part(): kernel_call(body, outs, 7, limit=36, grid_spec=grid_spec)  20.8 us
    pallas_call x4, Pallas kernels, cross_part(): kernel_call(body, (shape(width, cols + width_all),) * n, 0.02, limit=8, i...  11.2 us
    pallas_call x1, Pallas kernels, first_cross(): kernel_call(body, (shape(width, cols + width_all),) * HALVES + (pltpu.VME...  10.2 us
    ppermute x10, waiting for transfers between devices, line_slot(): return (lax.ppermute(send, 'bin', hops), send)  7.31 us
    all_to_all x1, starting transfers between devices, on_device(): lax.all_to_all(payload, 'bin', split_axis=0, concat_axis=0, tiled=True)  6.33 us
  transfers between devices with their start and end apart: 39, of which 15 were waited for; matrix products, arithmetic and copies ran while one was open for 0% of the time, Pallas kernels for 36%

profile of v2, /device:TPU:0, one launch (start us, length us, event | category | flops | bytes accessed | tf_op | source)
XLA Modules:
  0.0 219.6 jit_solution(13182954929737199725)
XLA Ops:
  1.3 1.9 copy-done
  3.2 3.4 %shard_map.68.refs_1_.pay_ref = f32[8,72,384]{2,1,0:T(8,128)} custom-call(s32[1]{0:T(128)} %bitcast.me_ref, f32[3072,256]{1,0:T(8,128)S(1)} %copy-done, f32[8,1,384]{2,1,0:T(1,128)S(1)} %bitcast.5), custom_call_target="tpu_custom_call" | custom-call | bytes 11070000 | tf_op jit(solution)/shard_map/pallas_call | solution.py:64
  6.6 6.3 %all-to-all-start = ((f32[8,72,384]{2,1,0:T(8,128)}), f32[8,72,384]{2,1,0:T(8,128)S(1)}, u32[]{:S(2)}, u32[]{:S(2)}) async-start(f32[8,72,384]{2,1,0:T(8,128)} %shard_map.68.refs_1_.pay_ref), calls=%async_computation | async-start | bytes 1769472 | tf_op jit(solution)/shard_map/all_to_all | solution.py:653
  13.0 12.2 %shard_map.69 = (f32[2,64,1792]{2,1,0:T(8,128)S(1)}, f32[2,64,1792]{2,1,0:T(8,128)S(1)}, bf16[4608,256]{1,0:T(8,128)(2,1)S(1)}) custom-call(s32[1]{0:T(128)} %bitcast.me_ref, bf16[3072,4608]{1,0:T(8,128)(2,1)} %counts_ref.1, bf16[3072,4608]{1,0:T(8,128)(2,1)} %counts_ref.1, f32[256,4608]{1,0:T(8,128)} %load_ref.1, f32[8,72,384]{2,1,0:T(8,128)} %shard_map.68.refs_1_.pay_ref), custom_call_target="tpu_custom_call" | custom-call | bytes 25830000 | tf_op jit(solution)/shard_map/pallas_call | solution.py:249
  25.2 1.6 collective-permute-start.3
  26.7 8.6 %shard_map.70 = (f32[2,64,1536]{2,1,0:T(8,128)}, f32[2,64,1536]{2,1,0:T(8,128)S(1)}) custom-call(s32[1]{0:T(128)} %bitcast.me_ref, bf16[3072,4608]{1,0:T(8,128)(2,1)} %counts_ref.1, bf16[3072,4608]{1,0:T(8,128)(2,1)} %counts_ref.1, bf16[4608,256]{1,0:T(8,128)(2,1)S(1)} %get-tuple-element.42.refs_0_, f32[2,64,1792]{2,1,0:T(8,128)S(1)} %get-tuple-element.43.refs_1_.refs_0_.refs_3_), custom_call_target="tpu_custom_call" | custom-call | bytes 25830000 | tf_op jit(solution)/shard_map/pallas_call | solution.py:249
  35.3 1.5 collective-permute-start.2
  36.8 2.7 %shard_map.71 = (f32[12,72,256]{2,1,0:T(8,128)S(1)}, f32[72,256]{1,0:T(8,128)S(1)}, f32[72,256]{1,0:T(8,128)S(1)}, s32[1,3072]{1,0:T(1,128)S(1)}) custom-call(s32[1]{0:T(128)} %bitcast.2.me_ref, f32[8,72,384]{2,1,0:T(8,128)S(1)} %all-to-all-done.got_ref, s32[12,256]{1,0:T(8,128)S(1)} %copy-done.3, f32[2,64,1536]{2,1,0:T(8,128)S(1)} %get-tuple-element.44._.refs_0_), custom_call_target="tpu_custom_call" | custom-call | bytes 11070000 | tf_op jit(solution)/shard_map/pallas_call | solution.py:106
  39.5 1.8 collective-permute-start
  41.4 1.3 collective-permute-start.1
  42.7 5.4 %collective-permute-done.3.refs_1_.refs_4_ = f32[2,64,1792]{2,1,0:T(8,128)} collective-permute-done((f32[2,64,1792]{2,1,0:T(8,128)S(1)}, f32[2,64,1792]{2,1,0:T(8,128)}, u32[]{:S(2)}, u32[]{:S(2)}) %collective-permute-start.3) | collective-permute-done | bytes 917536 | tf_op jit(solution)/shard_map/ppermute | solution.py:253
  49.3 6.0 %collective-permute-done.2.refs_1_ = f32[2,64,1536]{2,1,0:T(8,128)} collective-permute-done((f32[2,64,1536]{2,1,0:T(8,128)}, f32[2,64,1536]{2,1,0:T(8,128)}, u32[]{:S(2)}, u32[]{:S(2)}) %collective-permute-start.2) | collective-permute-done | bytes 786464 | tf_op jit(solution)/shard_map/ppermute | solution.py:253
  56.5 4.2 %shard_map.74.refs_7_ = f32[8,72,384]{2,1,0:T(8,128)} custom-call(f32[12,72,256]{2,1,0:T(8,128)S(1)} %get-tuple-element.45.refs_2_.grid_ref, f32[72,256]{1,0:T(8,128)S(1)} %collective-permute-done.above_ref, f32[72,256]{1,0:T(8,128)S(1)} %collective-permute-done.1.below_ref, s32[1,3072]{1,0:T(1,128)S(1)} %get-tuple-element.48.cell_ref, ...), custom_call_target="tpu_custom_call" | custom-call | bytes 14760000 | tf_op jit(solution)/shard_map/pallas_call | solution.py:155
  60.7 4.7 %all-to-all-start.1 = ((f32[8,72,384]{2,1,0:T(8,128)}), f32[8,72,384]{2,1,0:T(8,128)S(1)}, u32[]{:S(2)}, u32[]{:S(2)}) async-start(f32[8,72,384]{2,1,0:T(8,128)} %shard_map.74.refs_7_), calls=%async_computation.1 | async-start | bytes 1769472 | tf_op jit(solution)/shard_map/all_to_all | solution.py:687
  65.4 1.5 collective-permute-start.5
  67.5 10.7 %collective-permute-done.4.refs_2_ = f32[1,64,1536]{2,1,0:T(8,128)S(1)} collective-permute-done((f32[1,64,1536]{2,1,0:T(8,128)S(1)}, f32[1,64,1536]{2,1,0:T(8,128)S(1)}, u32[]{:S(2)}, u32[]{:S(2)}) %collective-permute-start.4) | collective-permute-done | bytes 393248 | tf_op jit(solution)/shard_map/ppermute | solution.py:253
  79.7 5.9 %shard_map.75 = (f32[64,3072]{1,0:T(8,128)}, f32[64,3072]{1,0:T(8,128)}) custom-call(f32[2,64,1536]{2,1,0:T(8,128)} %copy-done.2, f32[2,64,1536]{2,1,0:T(8,128)} %collective-permute-done.2.refs_1_, f32[1,64,1536]{2,1,0:T(8,128)} %copy-done.6, f32[2,64,1792]{2,1,0:T(8,128)} %copy-done.1, f32[2,64,1792]{2,1,0:T(8,128)} %collective-permute-done.3.refs_1_.refs_4_, ...), custom_call_target="tpu_custom_call" | custom-call | bytes 14760000 | tf_op jit(solution)/shard_map/pallas_call | solution.py:305
  85.6 2.9 %all-to-all-done.1.back_ref = f32[8,72,384]{2,1,0:T(8,128)S(1)} async-done(((f32[8,72,384]{2,1,0:T(8,128)}), f32[8,72,384]{2,1,0:T(8,128)S(1)}, u32[]{:S(2)}, u32[]{:S(2)}) %all-to-all-start.1) | async-done | bytes 884768 | tf_op jit(solution)/shard_map/all_to_all | solution.py:687
  89.4 2.8 %shard_map.76.block_ref._.refs_6_.refs_0_ = f32[64,3072]{1,0:T(8,128)S(1)} custom-call(f32[8,72,384]{2,1,0:T(8,128)} %shard_map.68.refs_1_.pay_ref, f32[8,72,384]{2,1,0:T(8,128)} %copy-done.4, f32[64,3072]{1,0:T(8,128)} %get-tuple-element.51.numer_ref, f32[64,3072]{1,0:T(8,128)} %get-tuple-element.52.plain_ref), custom_call_target="tpu_custom_call" | custom-call | bytes 73800 | tf_op jit(solution)/shard_map/pallas_call | solution.py:332
  92.3 1.6 collective-permute-start.6
  94.4 10.2 %shard_map.77 = (f32[64,2560]{1,0:T(8,128)S(1)}, f32[64,2560]{1,0:T(8,128)S(1)}, bf16[512,4608]{1,0:T(8,128)(2,1)S(1)}, bf16[512,4608]{1,0:T(8,128)(2,1)S(1)}, b...) custom-call(bf16[3072,4608]{1,0:T(8,128)(2,1)} %counts_ref.1, ...), custom_call_target="tpu_custom_call" | custom-call | bytes 73800 | tf_op jit(solution)/shard_map/pallas_call | solution.py:422
  105.1 6.3 %collective-permute-done.6.refs_0_.refs_7_.refs_1_ = f32[64,3072]{1,0:T(8,128)S(1)} collective-permute-done((f32[64,3072]{1,0:T(8,128)S(1)}, f32[64,3072]{1,0:T(8,128)S(1)}, u32[]{:S(2)}, u32[]{:S(2)}) %collective-permute-start.6) | collective-permute-done | bytes 786464 | tf_op jit(solution)/shard_map/ppermute | solution.py:253
  111.4 1.2 collective-permute-done.7.refs_1_.refs_0_.refs_8_.refs_2_
  113.4 1.3 collective-permute-start.11
  114.8 1.3 collective-permute-start.14
  116.1 2.6 %shard_map.82 = (f32[64,2560]{1,0:T(8,128)S(1)}, f32[64,2560]{1,0:T(8,128)S(1)}) custom-call(bf16[512,4608]{1,0:T(8,128)(2,1)S(1)} %get-tuple-element.55.refs_0_, bf16[512,4608]{1,0:T(8,128)(2,1)S(1)} %get-tuple-element.56.refs_1_, bf16[512,4608]{1,0:T(8,128)(2,1)S(1)} %get-tuple-element.57.refs_2_, bf16[512,4608]{1,0:T(8,128)(2,1)S(1)} %get-tuple-element.58.refs_3_, ...), custom_call_target="tpu_custom_call" | custom-call | bytes 73800 | tf_op jit(solution)/shard_map/pallas_call | solution.py:460
  119.3 2.5 %shard_map.83 = (f32[64,2560]{1,0:T(8,128)S(1)}, f32[64,2560]{1,0:T(8,128)S(1)}) custom-call(bf16[512,4608]{1,0:T(8,128)(2,1)S(1)} %get-tuple-element.55.refs_0_, bf16[512,4608]{1,0:T(8,128)(2,1)S(1)} %get-tuple-element.56.refs_1_, bf16[512,4608]{1,0:T(8,128)(2,1)S(1)} %get-tuple-element.57.refs_2_, bf16[512,4608]{1,0:T(8,128)(2,1)S(1)} %get-tuple-element.58.refs_3_, ...), custom_call_target="tpu_custom_call" | custom-call | bytes 73800 | tf_op jit(solution)/shard_map/pallas_call | solution.py:460
  122.8 7.8 %collective-permute-done.8.refs_0_.refs_9_.refs_3_ = f32[64,3072]{1,0:T(8,128)S(1)} collective-permute-done((f32[64,3072]{1,0:T(8,128)S(1)}, f32[64,3072]{1,0:T(8,128)S(1)}, u32[]{:S(2)}, u32[]{:S(2)}) %collective-permute-start.8) | collective-permute-done | bytes 786464 | tf_op jit(solution)/shard_map/ppermute | solution.py:253
  131.5 3.6 %collective-permute-start.18 = (f32[64,2560]{1,0:T(8,128)S(1)}, f32[64,2560]{1,0:T(8,128)S(1)}, u32[]{:S(2)}, u32[]{:S(2)}) collective-permute-start(f32[64,2560]{1,0:T(8,128)S(1)} %shard_map.87.refs_4_), channel_id=1, source_target_pairs={{0,2},{2,4},{7,5},{5,3},{8,10},{10,12},{15,13},{13,11},{16,18},{18... | collective-permute-start | bytes 1966088 | tf_op jit(solution)/shard_map/ppermute | solution.py:522
  135.8 2.2 collective-permute-start.17
  138.0 3.1 %shard_map.90.refs_10_.refs_0_ = f32[64,2560]{1,0:T(8,128)S(1)} custom-call(bf16[512,4608]{1,0:T(8,128)(2,1)S(1)} %get-tuple-element.55.refs_0_, bf16[512,4608]{1,0:T(8,128)(2,1)S(1)} %get-tuple-element.56.refs_1_, bf16[512,4608]{1,0:T(8,128)(2,1)S(1)} %get-tuple-element.57.refs_2_, bf16[512,4608]{1,0:T(8,128)(2,1)S(1)} %get-tuple-element.58.refs_3_, ...), custom_call_target="tpu_custom_call" | custom-call | bytes 73800 | tf_op jit(solution)/shard_map/pallas_call | solution.py:460
  141.2 3.1 %shard_map.91._.refs_0_ = f32[64,2560]{1,0:T(8,128)S(1)} custom-call(bf16[512,4608]{1,0:T(8,128)(2,1)S(1)} %get-tuple-element.55.refs_0_, bf16[512,4608]{1,0:T(8,128)(2,1)S(1)} %get-tuple-element.56.refs_1_, bf16[512,4608]{1,0:T(8,128)(2,1)S(1)} %get-tuple-element.57.refs_2_, bf16[512,4608]{1,0:T(8,128)(2,1)S(1)} %get-tuple-element.58.refs_3_, ...), custom_call_target="tpu_custom_call" | custom-call | bytes 73800 | tf_op jit(solution)/shard_map/pallas_call | solution.py:460
  144.9 3.3 %collective-permute-start.21 = (f32[64,2560]{1,0:T(8,128)S(1)}, f32[64,2560]{1,0:T(8,128)S(1)}, u32[]{:S(2)}, u32[]{:S(2)}) collective-permute-start(f32[64,2560]{1,0:T(8,128)S(1)} %shard_map.92._), channel_id=1, source_target_pairs={{0,2},{2,4},{4,6},{7,5},{5,3},{3,1},{8,10},{10,12},{12,14},{15,13}... | collective-permute-start | bytes 1966088 | tf_op jit(solution)/shard_map/ppermute | solution.py:522
  148.3 1.9 collective-permute-done.17.come_ref.refs_1_.refs_0_
  150.7 4.5 %collective-permute-start.19 = (f32[64,2560]{1,0:T(8,128)S(1)}, f32[64,2560]{1,0:T(8,128)S(1)}, u32[]{:S(2)}, u32[]{:S(2)}) collective-permute-start(f32[64,2560]{1,0:T(8,128)S(1)} %shard_map.93.refs_2_), channel_id=1, source_target_pairs={{0,2},{2,4},{4,6},{7,5},{5,3},{3,1},{8,10},{10,12},{12,14},{15,13}... | collective-permute-start | bytes 1966088 | tf_op jit(solution)/shard_map/ppermute | solution.py:522
  155.3 1.8 collective-permute-done.21.come_ref.refs_2_.refs_1_.refs_0_
  157.8 4.5 %collective-permute-start.26 = (f32[64,2560]{1,0:T(8,128)S(1)}, f32[64,2560]{1,0:T(8,128)S(1)}, u32[]{:S(2)}, u32[]{:S(2)}) collective-permute-start(f32[64,2560]{1,0:T(8,128)S(1)} %shard_map.95.refs_2_), channel_id=1, source_target_pairs={{0,2},{2,4},{4,6},{7,5},{5,3},{3,1},{8,10},{10,12},{12,14},{15,13}... | collective-permute-start | bytes 1966088 | tf_op jit(solution)/shard_map/ppermute | solution.py:522
  162.3 1.9 collective-permute-done.19.come_ref.refs_2_.refs_1_.refs_0_
  164.8 4.5 %collective-permute-start.25 = (f32[64,2560]{1,0:T(8,128)S(1)}, f32[64,2560]{1,0:T(8,128)S(1)}, u32[]{:S(2)}, u32[]{:S(2)}) collective-permute-start(f32[64,2560]{1,0:T(8,128)S(1)} %shard_map.97.refs_4_), channel_id=1, source_target_pairs={{0,2},{2,4},{4,6},{7,5},{5,3},{3,1},{8,10},{10,12},{12,14},{15,13}... | collective-permute-start | bytes 1966088 | tf_op jit(solution)/shard_map/ppermute | solution.py:522
  169.3 4.2 %shard_map.98 = (f32[3072,256]{1,0:T(8,128)}, f32[8,128]{1,0:T(8,128)S(1)}) custom-call(s32[1]{0:T(128)} %bitcast.me_ref, f32[64,3072]{1,0:T(8,128)S(1)} %shard_map.76.block_ref._.refs_6_.refs_0_, f32[64,3072]{1,0:T(8,128)S(1)} %collective-permute-done.6.refs_0_.refs_7_.refs_1_, f32[64,3072]{1,0:T(8,128)S(1)} %collective-permute-done.7.refs_1_.refs_0_.refs_8_.refs_2_, ...), custom_call_target="tpu_custom_call" | custom-call | bytes 73800 | tf_op jit(solution)/shard_map/pallas_call | solution.py:379
  176.5 1.7 collective-permute-done.25.come_ref.refs_2_.refs_1_.refs_0_
  184.5 11.0 %collective-permute-start.31 = (f32[64,2560]{1,0:T(8,128)S(1)}, f32[64,2560]{1,0:T(8,128)S(1)}, u32[]{:S(2)}, u32[]{:S(2)}) collective-permute-start(f32[64,2560]{1,0:T(8,128)S(1)} %shard_map.109._.refs_7_.refs_1_), channel_id=1, source_target_pairs={{0,1},{1,0},{2,3},{3,2},{4,5},{5,4},{6,7},{7,6},{8,9},{9,8},{10,11... | collective-permute-start | bytes 1966088 | tf_op jit(solution)/shard_map/ppermute | solution.py:253
  196.8 5.2 %collective-permute-start.33 = (f32[64,2560]{1,0:T(8,128)S(1)}, f32[64,2560]{1,0:T(8,128)S(1)}, u32[]{:S(2)}, u32[]{:S(2)}) collective-permute-start(f32[64,2560]{1,0:T(8,128)S(1)} %shard_map.111.refs_10_.refs_12_.refs_1_), channel_id=1, source_target_pairs={{0,1},{1,0},{2,3},{3,2},{4,5},{5,4},{6,7},{7,6},{8,9},{9,8},{10,11... | collective-permute-start | bytes 1966088 | tf_op jit(solution)/shard_map/ppermute | solution.py:253
  203.7 5.8 %shard_map.112 = (f32[256,4608]{1,0:T(8,128)S(1)}, f32[8,128]{1,0:T(8,128)S(1)}) custom-call(s32[1]{0:T(128)} %bitcast.me_ref, f32[256,4608]{1,0:T(8,128)S(1)} %bitcast.4, f32[64,2560]{1,0:T(8,128)S(1)} %shard_map.80.refs_2_.refs_1_.refs_0_, f32[64,2560]{1,0:T(8,128)S(1)} %shard_map.99._.refs_1_, f32[64,2560]{1,0:T(8,128)S(1)} %collective-permute-done.23.refs_0_.refs_2_, ...), custom_call_target="tpu_custom_call" | custom-call | bytes 73800 | tf_op jit(solution)/shard_map/pallas_call | solution.py:580
  210.1 3.9 %collective-permute-start.36 = (f32[64,2560]{1,0:T(8,128)S(1)}, f32[64,2560]{1,0:T(8,128)S(1)}, u32[]{:S(2)}, u32[]{:S(2)}) collective-permute-start(f32[64,2560]{1,0:T(8,128)S(1)} %shard_map.113._.refs_1_), channel_id=1, source_target_pairs={{0,1},{1,0},{2,3},{3,2},{4,5},{5,4},{6,7},{7,6},{8,9},{9,8},{10,11... | collective-permute-start | bytes 1966088 | tf_op jit(solution)/shard_map/ppermute | solution.py:253
  214.0 1.3 shard_map.114
  215.2 1.3 shard_map.115
  216.5 1.2 shard_map.116
  (102 shorter events, 28.4 us)
Async XLA Ops:
  1.3 1.9 copy-start
  6.6 30.2 %all-to-all-start = ((f32[8,72,384]{2,1,0:T(8,128)}), f32[8,72,384]{2,1,0:T(8,128)S(1)}, u32[]{:S(2)}, u32[]{:S(2)}) async-start(f32[8,72,384]{2,1,0:T(8,128)} %shard_map.68.refs_1_.pay_ref), calls=%async_computation | async-start | bytes 1769472 | tf_op jit(solution)/shard_map/all_to_all | solution.py:653
  25.1 10.2 %copy-start.1 = (f32[2,64,1792]{2,1,0:T(8,128)}, f32[2,64,1792]{2,1,0:T(8,128)S(1)}, u32[]{:S(2)}) copy-start(f32[2,64,1792]{2,1,0:T(8,128)S(1)} %get-tuple-element.43.refs_1_.refs_0_.refs_3_) | copy-start | bytes 2752516
  25.2 22.9 %collective-permute-start.3 = (f32[2,64,1792]{2,1,0:T(8,128)S(1)}, f32[2,64,1792]{2,1,0:T(8,128)}, u32[]{:S(2)}, u32[]{:S(2)}) collective-permute-start(f32[2,64,1792]{2,1,0:T(8,128)S(1)} %get-tuple-element.50), channel_id=1, source_target_pairs={{0,16},{8,24},{16,0},{24,8},{1,17},{9,25},{17,1},{25,9},{2,18},{10... | collective-permute-start | bytes 2752520 | tf_op jit(solution)/shard_map/ppermute | solution.py:253
  26.7 10.1 %copy-start.3 = (s32[12,256]{1,0:T(8,128)S(1)}, s32[12,256]{1,0:T(8,128)}, u32[]{:S(2)}) copy-start(s32[12,256]{1,0:T(8,128)} %code_ref.3) | copy-start | bytes 36868
  35.3 20.0 %copy-start.2 = (f32[2,64,1536]{2,1,0:T(8,128)}, f32[2,64,1536]{2,1,0:T(8,128)S(1)}, u32[]{:S(2)}) copy-start(f32[2,64,1536]{2,1,0:T(8,128)S(1)} %get-tuple-element.44._.refs_0_) | copy-start | bytes 2359300
  35.3 20.0 %collective-permute-start.2 = (f32[2,64,1536]{2,1,0:T(8,128)}, f32[2,64,1536]{2,1,0:T(8,128)}, u32[]{:S(2)}, u32[]{:S(2)}) collective-permute-start(f32[2,64,1536]{2,1,0:T(8,128)} %get-tuple-element.49), channel_id=1, source_target_pairs={{0,8},{8,0},{16,24},{24,16},{1,9},{9,1},{17,25},{25,17},{2,10},{10... | collective-permute-start | bytes 2359304 | tf_op jit(solution)/shard_map/ppermute | solution.py:253
  39.5 17.0 %collective-permute-start = (f32[72,256]{1,0:T(8,128)S(1)}, f32[72,256]{1,0:T(8,128)S(1)}, u32[]{:S(2)}, u32[]{:S(2)}) collective-permute-start(f32[72,256]{1,0:T(8,128)S(1)} %get-tuple-element.46), channel_id=1, source_target_pairs={{0,1},{1,2},{2,3},{3,4},{4,5},{5,6},{6,7},{8,9},{9,10},{10,11},{11... | collective-permute-start | bytes 221192 | tf_op jit(solution)/shard_map/ppermute | solution.py:680
  41.4 15.1 %collective-permute-start.1 = (f32[72,256]{1,0:T(8,128)S(1)}, f32[72,256]{1,0:T(8,128)S(1)}, u32[]{:S(2)}, u32[]{:S(2)}) collective-permute-start(f32[72,256]{1,0:T(8,128)S(1)} %get-tuple-element.47), channel_id=1, source_target_pairs={{1,0},{2,1},{3,2},{4,3},{5,4},{6,5},{7,6},{9,8},{10,9},{11,10},{12... | collective-permute-start | bytes 221192 | tf_op jit(solution)/shard_map/ppermute | solution.py:681
  60.7 27.8 %all-to-all-start.1 = ((f32[8,72,384]{2,1,0:T(8,128)}), f32[8,72,384]{2,1,0:T(8,128)S(1)}, u32[]{:S(2)}, u32[]{:S(2)}) async-start(f32[8,72,384]{2,1,0:T(8,128)} %shard_map.74.refs_7_), calls=%async_computation.1 | async-start | bytes 1769472 | tf_op jit(solution)/shard_map/all_to_all | solution.py:687
  65.4 12.9 %collective-permute-start.5 = (f32[1,64,1792]{2,1,0:T(8,128)S(1)}, f32[1,64,1792]{2,1,0:T(8,128)S(1)}, u32[]{:S(2)}, u32[]{:S(2)}) collective-permute-start(f32[1,64,1792]{2,1,0:T(8,128)S(1)} %shard_map.72.refs_2_), channel_id=1, source_target_pairs={{0,8},{8,0},{16,24},{24,16},{1,9},{9,1},{17,25},{25,17},{2,10},{10... | collective-permute-start | bytes 1376264 | tf_op jit(solution)/shard_map/ppermute | solution.py:253
  66.9 11.2 %collective-permute-start.4 = (f32[1,64,1536]{2,1,0:T(8,128)S(1)}, f32[1,64,1536]{2,1,0:T(8,128)S(1)}, u32[]{:S(2)}, u32[]{:S(2)}) collective-permute-start(f32[1,64,1536]{2,1,0:T(8,128)S(1)} %shard_map.73._), channel_id=1, source_target_pairs={{0,16},{8,24},{16,0},{24,8},{1,17},{9,25},{17,1},{25,9},{2,18},{10... | collective-permute-start | bytes 1179656 | tf_op jit(solution)/shard_map/ppermute | solution.py:253
  78.2 0.8 copy-start.6
  78.9 0.8 copy-start.5
  88.5 0.9 copy-start.4
  92.3 19.1 %collective-permute-start.6 = (f32[64,3072]{1,0:T(8,128)S(1)}, f32[64,3072]{1,0:T(8,128)S(1)}, u32[]{:S(2)}, u32[]{:S(2)}) collective-permute-start(f32[64,3072]{1,0:T(8,128)S(1)} %shard_map.76.block_ref._.refs_6_.refs_0_), channel_id=1, source_target_pairs={{0,8},{8,0},{16,24},{24,16},{1,9},{9,1},{17,25},{25,17},{2,10},{10... | collective-permute-start | bytes 2359304 | tf_op jit(solution)/shard_map/ppermute | solution.py:253
  93.8 18.8 %collective-permute-start.7 = (f32[64,3072]{1,0:T(8,128)S(1)}, f32[64,3072]{1,0:T(8,128)S(1)}, u32[]{:S(2)}, u32[]{:S(2)}) collective-permute-start(f32[64,3072]{1,0:T(8,128)S(1)} %shard_map.76.block_ref._.refs_6_.refs_0_), channel_id=1, source_target_pairs={{0,16},{8,24},{16,0},{24,8},{1,17},{9,25},{17,1},{25,9},{2,18},{10... | collective-permute-start | bytes 2359304 | tf_op jit(solution)/shard_map/ppermute | solution.py:253
  104.6 8.7 %collective-permute-start.10 = (f32[64,2560]{1,0:T(8,128)S(1)}, f32[64,2560]{1,0:T(8,128)S(1)}, u32[]{:S(2)}, u32[]{:S(2)}) collective-permute-start(f32[64,2560]{1,0:T(8,128)S(1)} %get-tuple-element.54.refs_0_), channel_id=1, source_target_pairs={{0,1},{1,0},{2,3},{3,2},{4,5},{5,4},{6,7},{7,6},{8,9},{9,8},{10,11... | collective-permute-start | bytes 1966088 | tf_op jit(solution)/shard_map/ppermute | solution.py:253
  104.6 8.7 %collective-permute-start.9 = (f32[64,2560]{1,0:T(8,128)S(1)}, f32[64,2560]{1,0:T(8,128)S(1)}, u32[]{:S(2)}, u32[]{:S(2)}) collective-permute-start(f32[64,2560]{1,0:T(8,128)S(1)} %get-tuple-element.53.refs_2_.refs_0_), channel_id=1, source_target_pairs={{0,1},{1,0},{2,3},{3,2},{4,5},{5,4},{6,7},{7,6},{8,9},{9,8},{10,11... | collective-permute-start | bytes 1966088 | tf_op jit(solution)/shard_map/ppermute | solution.py:253
  112.7 17.9 %collective-permute-start.8 = (f32[64,3072]{1,0:T(8,128)S(1)}, f32[64,3072]{1,0:T(8,128)S(1)}, u32[]{:S(2)}, u32[]{:S(2)}) collective-permute-start(f32[64,3072]{1,0:T(8,128)S(1)} %shard_map.79.refs_2_), channel_id=1, source_target_pairs={{0,8},{8,0},{16,24},{24,16},{1,9},{9,1},{17,25},{25,17},{2,10},{10... | collective-permute-start | bytes 2359304 | tf_op jit(solution)/shard_map/ppermute | solution.py:253
  113.4 9.4 %collective-permute-start.11 = (f32[64,2560]{1,0:T(8,128)S(1)}, f32[64,2560]{1,0:T(8,128)S(1)}, u32[]{:S(2)}, u32[]{:S(2)}) collective-permute-start(f32[64,2560]{1,0:T(8,128)S(1)} %shard_map.81.refs_9_.refs_1_.refs_2_.refs_3_), channel_id=1, source_target_pairs={{0,2},{7,5},{8,10},{15,13},{16,18},{23,21},{24,26},{31,29}} | collective-permute-start | bytes 1966088 | tf_op jit(solution)/shard_map/ppermute | solution.py:503
  114.8 15.9 %collective-permute-start.14 = (f32[64,2560]{1,0:T(8,128)S(1)}, f32[64,2560]{1,0:T(8,128)S(1)}, u32[]{:S(2)}, u32[]{:S(2)}) collective-permute-start(f32[64,2560]{1,0:T(8,128)S(1)} %shard_map.80.refs_2_.refs_1_.refs_0_), channel_id=1, source_target_pairs={{0,2},{7,5},{8,10},{15,13},{16,18},{23,21},{24,26},{31,29}} | collective-permute-start | bytes 1966088 | tf_op jit(solution)/shard_map/ppermute | solution.py:503
  118.7 12.0 %collective-permute-start.15 = (f32[64,2560]{1,0:T(8,128)S(1)}, f32[64,2560]{1,0:T(8,128)S(1)}, u32[]{:S(2)}, u32[]{:S(2)}) collective-permute-start(f32[64,2560]{1,0:T(8,128)S(1)} %get-tuple-element.64.refs_0_), channel_id=1, source_target_pairs={{0,1},{1,0},{2,3},{3,2},{4,5},{5,4},{6,7},{7,6},{8,9},{9,8},{10,11... | collective-permute-start | bytes 1966088 | tf_op jit(solution)/shard_map/ppermute | solution.py:253
  118.8 12.0 %collective-permute-start.16 = (f32[64,2560]{1,0:T(8,128)S(1)}, f32[64,2560]{1,0:T(8,128)S(1)}, u32[]{:S(2)}, u32[]{:S(2)}) collective-permute-start(f32[64,2560]{1,0:T(8,128)S(1)} %get-tuple-element.61.refs_9_.refs_1_), channel_id=1, source_target_pairs={{0,1},{1,0},{2,3},{3,2},{4,5},{5,4},{6,7},{7,6},{8,9},{9,8},{10,11... | collective-permute-start | bytes 1966088 | tf_op jit(solution)/shard_map/ppermute | solution.py:253
  122.8 12.2 %collective-permute-start.12 = (f32[64,2560]{1,0:T(8,128)S(1)}, f32[64,2560]{1,0:T(8,128)S(1)}, u32[]{:S(2)}, u32[]{:S(2)}) collective-permute-start(f32[64,2560]{1,0:T(8,128)S(1)} %get-tuple-element.62.refs_0_), channel_id=1, source_target_pairs={{0,1},{1,0},{2,3},{3,2},{4,5},{5,4},{6,7},{7,6},{8,9},{9,8},{10,11... | collective-permute-start | bytes 1966088 | tf_op jit(solution)/shard_map/ppermute | solution.py:253
  130.6 4.4 %collective-permute-start.13 = (f32[64,2560]{1,0:T(8,128)S(1)}, f32[64,2560]{1,0:T(8,128)S(1)}, u32[]{:S(2)}, u32[]{:S(2)}) collective-permute-start(f32[64,2560]{1,0:T(8,128)S(1)} %get-tuple-element.63.refs_1_), channel_id=1, source_target_pairs={{0,1},{1,0},{2,3},{3,2},{4,5},{5,4},{6,7},{7,6},{8,9},{9,8},{10,11... | collective-permute-start | bytes 1966088 | tf_op jit(solution)/shard_map/ppermute | solution.py:253
  131.5 12.7 %collective-permute-start.18 = (f32[64,2560]{1,0:T(8,128)S(1)}, f32[64,2560]{1,0:T(8,128)S(1)}, u32[]{:S(2)}, u32[]{:S(2)}) collective-permute-start(f32[64,2560]{1,0:T(8,128)S(1)} %shard_map.87.refs_4_), channel_id=1, source_target_pairs={{0,2},{2,4},{7,5},{5,3},{8,10},{10,12},{15,13},{13,11},{16,18},{18... | collective-permute-start | bytes 1966088 | tf_op jit(solution)/shard_map/ppermute | solution.py:522
  135.8 14.3 %collective-permute-start.17 = (f32[64,2560]{1,0:T(8,128)S(1)}, f32[64,2560]{1,0:T(8,128)S(1)}, u32[]{:S(2)}, u32[]{:S(2)}) collective-permute-start(f32[64,2560]{1,0:T(8,128)S(1)} %shard_map.89.refs_10_), channel_id=1, source_target_pairs={{0,2},{2,4},{7,5},{5,3},{8,10},{10,12},{15,13},{13,11},{16,18},{18... | collective-permute-start | bytes 1966088 | tf_op jit(solution)/shard_map/ppermute | solution.py:522
  141.1 14.1 %collective-permute-start.22 = (f32[64,2560]{1,0:T(8,128)S(1)}, f32[64,2560]{1,0:T(8,128)S(1)}, u32[]{:S(2)}, u32[]{:S(2)}) collective-permute-start(f32[64,2560]{1,0:T(8,128)S(1)} %shard_map.90.refs_10_.refs_0_), channel_id=1, source_target_pairs={{0,1},{1,0},{2,3},{3,2},{4,5},{5,4},{6,7},{7,6},{8,9},{9,8},{10,11... | collective-permute-start | bytes 1966088 | tf_op jit(solution)/shard_map/ppermute | solution.py:253
  144.9 12.3 %collective-permute-start.21 = (f32[64,2560]{1,0:T(8,128)S(1)}, f32[64,2560]{1,0:T(8,128)S(1)}, u32[]{:S(2)}, u32[]{:S(2)}) collective-permute-start(f32[64,2560]{1,0:T(8,128)S(1)} %shard_map.92._), channel_id=1, source_target_pairs={{0,2},{2,4},{4,6},{7,5},{5,3},{3,1},{8,10},{10,12},{12,14},{15,13}... | collective-permute-start | bytes 1966088 | tf_op jit(solution)/shard_map/ppermute | solution.py:522
  148.2 14.0 %collective-permute-start.20 = (f32[64,2560]{1,0:T(8,128)S(1)}, f32[64,2560]{1,0:T(8,128)S(1)}, u32[]{:S(2)}, u32[]{:S(2)}) collective-permute-start(f32[64,2560]{1,0:T(8,128)S(1)} %shard_map.91._.refs_0_), channel_id=1, source_target_pairs={{0,1},{1,0},{2,3},{3,2},{4,5},{5,4},{6,7},{7,6},{8,9},{9,8},{10,11... | collective-permute-start | bytes 1966088 | tf_op jit(solution)/shard_map/ppermute | solution.py:253
  150.7 13.4 %collective-permute-start.19 = (f32[64,2560]{1,0:T(8,128)S(1)}, f32[64,2560]{1,0:T(8,128)S(1)}, u32[]{:S(2)}, u32[]{:S(2)}) collective-permute-start(f32[64,2560]{1,0:T(8,128)S(1)} %shard_map.93.refs_2_), channel_id=1, source_target_pairs={{0,2},{2,4},{4,6},{7,5},{5,3},{3,1},{8,10},{10,12},{12,14},{15,13}... | collective-permute-start | bytes 1966088 | tf_op jit(solution)/shard_map/ppermute | solution.py:522
  157.8 17.5 %collective-permute-start.26 = (f32[64,2560]{1,0:T(8,128)S(1)}, f32[64,2560]{1,0:T(8,128)S(1)}, u32[]{:S(2)}, u32[]{:S(2)}) collective-permute-start(f32[64,2560]{1,0:T(8,128)S(1)} %shard_map.95.refs_2_), channel_id=1, source_target_pairs={{0,2},{2,4},{4,6},{7,5},{5,3},{3,1},{8,10},{10,12},{12,14},{15,13}... | collective-permute-start | bytes 1966088 | tf_op jit(solution)/shard_map/ppermute | solution.py:522
  164.8 13.4 %collective-permute-start.25 = (f32[64,2560]{1,0:T(8,128)S(1)}, f32[64,2560]{1,0:T(8,128)S(1)}, u32[]{:S(2)}, u32[]{:S(2)}) collective-permute-start(f32[64,2560]{1,0:T(8,128)S(1)} %shard_map.97.refs_4_), channel_id=1, source_target_pairs={{0,2},{2,4},{4,6},{7,5},{5,3},{3,1},{8,10},{10,12},{12,14},{15,13}... | collective-permute-start | bytes 1966088 | tf_op jit(solution)/shard_map/ppermute | solution.py:522
  174.7 4.8 %collective-permute-start.24 = (f32[64,2560]{1,0:T(8,128)S(1)}, f32[64,2560]{1,0:T(8,128)S(1)}, u32[]{:S(2)}, u32[]{:S(2)}) collective-permute-start(f32[64,2560]{1,0:T(8,128)S(1)} %shard_map.100._.refs_4_), channel_id=1, source_target_pairs={{0,1},{1,0},{2,3},{3,2},{4,5},{5,4},{6,7},{7,6},{8,9},{9,8},{10,11... | collective-permute-start | bytes 1966088 | tf_op jit(solution)/shard_map/ppermute | solution.py:253
  174.7 4.8 %collective-permute-start.23 = (f32[64,2560]{1,0:T(8,128)S(1)}, f32[64,2560]{1,0:T(8,128)S(1)}, u32[]{:S(2)}, u32[]{:S(2)}) collective-permute-start(f32[64,2560]{1,0:T(8,128)S(1)} %shard_map.99._.refs_1_), channel_id=1, source_target_pairs={{0,1},{1,0},{2,3},{3,2},{4,5},{5,4},{6,7},{7,6},{8,9},{9,8},{10,11... | collective-permute-start | bytes 1966088 | tf_op jit(solution)/shard_map/ppermute | solution.py:253
  175.8 5.5 %collective-permute-start.30 = (f32[64,2560]{1,0:T(8,128)S(1)}, f32[64,2560]{1,0:T(8,128)S(1)}, u32[]{:S(2)}, u32[]{:S(2)}) collective-permute-start(f32[64,2560]{1,0:T(8,128)S(1)} %shard_map.101._), channel_id=1, source_target_pairs={{2,4},{4,6},{5,3},{3,1},{10,12},{12,14},{13,11},{11,9},{18,20},{20... | collective-permute-start | bytes 1966088 | tf_op jit(solution)/shard_map/ppermute | solution.py:522
  178.8 3.8 %collective-permute-start.29 = (f32[64,2560]{1,0:T(8,128)S(1)}, f32[64,2560]{1,0:T(8,128)S(1)}, u32[]{:S(2)}, u32[]{:S(2)}) collective-permute-start(f32[64,2560]{1,0:T(8,128)S(1)} %shard_map.102.refs_2_), channel_id=1, source_target_pairs={{2,4},{4,6},{5,3},{3,1},{10,12},{12,14},{13,11},{11,9},{18,20},{20... | collective-permute-start | bytes 1966088 | tf_op jit(solution)/shard_map/ppermute | solution.py:522
  180.8 2.4 %collective-permute-start.28 = (f32[64,2560]{1,0:T(8,128)S(1)}, f32[64,2560]{1,0:T(8,128)S(1)}, u32[]{:S(2)}, u32[]{:S(2)}) collective-permute-start(f32[64,2560]{1,0:T(8,128)S(1)} %shard_map.105._.refs_4_), channel_id=1, source_target_pairs={{0,1},{1,0},{2,3},{3,2},{4,5},{5,4},{6,7},{7,6},{8,9},{9,8},{10,11... | collective-permute-start | bytes 1966088 | tf_op jit(solution)/shard_map/ppermute | solution.py:253
  180.9 3.0 %collective-permute-start.27 = (f32[64,2560]{1,0:T(8,128)S(1)}, f32[64,2560]{1,0:T(8,128)S(1)}, u32[]{:S(2)}, u32[]{:S(2)}) collective-permute-start(f32[64,2560]{1,0:T(8,128)S(1)} %shard_map.104._.refs_4_.refs_1_), channel_id=1, source_target_pairs={{0,1},{1,0},{2,3},{3,2},{4,5},{5,4},{6,7},{7,6},{8,9},{9,8},{10,11... | collective-permute-start | bytes 1966088 | tf_op jit(solution)/shard_map/ppermute | solution.py:253
  181.9 14.2 %collective-permute-start.32 = (f32[64,2560]{1,0:T(8,128)S(1)}, f32[64,2560]{1,0:T(8,128)S(1)}, u32[]{:S(2)}, u32[]{:S(2)}) collective-permute-start(f32[64,2560]{1,0:T(8,128)S(1)} %shard_map.106._), channel_id=1, source_target_pairs={{4,6},{3,1},{12,14},{11,9},{20,22},{19,17},{28,30},{27,25}} | collective-permute-start | bytes 1966088 | tf_op jit(solution)/shard_map/ppermute | solution.py:522
  182.6 21.0 %slice-start = ((s8[4718592]{0:T(1024)(128)(4,1)}), s8[4194304]{0:T(1024)(128)(4,1)S(1)}, s32[]{:S(2)}) async-start(s8[4718592]{0:T(1024)(128)(4,1)} %bitcast.3), calls=%async_computation.2 | async-start | bytes 8388608
  183.9 19.8 %slice-start.1 = ((s8[4718592]{0:T(1024)(128)(4,1)}), s8[524288]{0:T(1024)(128)(4,1)S(1)}, s32[]{:S(2)}) async-start(s8[4718592]{0:T(1024)(128)(4,1)} %bitcast.3), calls=%async_computation.3 | async-start | bytes 1048576
  184.5 18.8 %collective-permute-start.31 = (f32[64,2560]{1,0:T(8,128)S(1)}, f32[64,2560]{1,0:T(8,128)S(1)}, u32[]{:S(2)}, u32[]{:S(2)}) collective-permute-start(f32[64,2560]{1,0:T(8,128)S(1)} %shard_map.109._.refs_7_.refs_1_), channel_id=1, source_target_pairs={{0,1},{1,0},{2,3},{3,2},{4,5},{5,4},{6,7},{7,6},{8,9},{9,8},{10,11... | collective-permute-start | bytes 1966088 | tf_op jit(solution)/shard_map/ppermute | solution.py:253
  196.8 6.9 %collective-permute-start.33 = (f32[64,2560]{1,0:T(8,128)S(1)}, f32[64,2560]{1,0:T(8,128)S(1)}, u32[]{:S(2)}, u32[]{:S(2)}) collective-permute-start(f32[64,2560]{1,0:T(8,128)S(1)} %shard_map.111.refs_10_.refs_12_.refs_1_), channel_id=1, source_target_pairs={{0,1},{1,0},{2,3},{3,2},{4,5},{5,4},{6,7},{7,6},{8,9},{9,8},{10,11... | collective-permute-start | bytes 1966088 | tf_op jit(solution)/shard_map/ppermute | solution.py:253
  201.9 7.5 %collective-permute-start.34 = (f32[64,2560]{1,0:T(8,128)S(1)}, f32[64,2560]{1,0:T(8,128)S(1)}, u32[]{:S(2)}, u32[]{:S(2)}) collective-permute-start(f32[64,2560]{1,0:T(8,128)S(1)} %shard_map.107.refs_2_), channel_id=1, source_target_pairs={{4,6},{3,1},{12,14},{11,9},{20,22},{19,17},{28,30},{27,25}} | collective-permute-start | bytes 1966088 | tf_op jit(solution)/shard_map/ppermute | solution.py:522
  202.6 13.9 %collective-permute-start.35 = (f32[64,2560]{1,0:T(8,128)S(1)}, f32[64,2560]{1,0:T(8,128)S(1)}, u32[]{:S(2)}, u32[]{:S(2)}) collective-permute-start(f32[64,2560]{1,0:T(8,128)S(1)} %shard_map.110._.refs_4_), channel_id=1, source_target_pairs={{0,1},{1,0},{2,3},{3,2},{4,5},{5,4},{6,7},{7,6},{8,9},{9,8},{10,11... | collective-permute-start | bytes 1966088 | tf_op jit(solution)/shard_map/ppermute | solution.py:253
  210.1 8.6 %collective-permute-start.36 = (f32[64,2560]{1,0:T(8,128)S(1)}, f32[64,2560]{1,0:T(8,128)S(1)}, u32[]{:S(2)}, u32[]{:S(2)}) collective-permute-start(f32[64,2560]{1,0:T(8,128)S(1)} %shard_map.113._.refs_1_), channel_id=1, source_target_pairs={{0,1},{1,0},{2,3},{3,2},{4,5},{5,4},{6,7},{7,6},{8,9},{9,8},{10,11... | collective-permute-start | bytes 1966088 | tf_op jit(solution)/shard_map/ppermute | solution.py:253

commit v3 on v2

--- a/solution.py
+++ b/solution.py
@@ -168,37 +168,25 @@
     width_all = loadings.shape[0] if first_call else loadings.shape[1]
     width = width_all // genes_n
     half_rows = rows // 2
-    steps = half_rows // STEP
-    side = genes // 2
+    piece = STEP // 2
+    pieces = half_rows // piece
     keep_ids = [k for k in range(genes_n) if k not in send_ids]
     total_cols = half_rows + first_call * width_all
 
-    def body(me_ref, left_ref, right_ref, *refs):
-        at = pl.program_id(0)
+    def body(me_ref, counts_ref, *refs):
         firsts = [pl.multiple_of((k ^ me_ref[0]) * width, width) for k in range(genes_n)]
         if first_call:
-            load_ref, _, send_ref, keep_ref, load_t, load_bf, load_f, turned, sems = refs
-
-            @pl.when(at == 0)
-            def _():
-                reads = [
-                    pltpu.make_async_copy(
-                        load_ref.at[pl.ds(first, width), :],
-                        load_f.at[pl.ds(k * width, width), :],
-                        sems.at[k],
-                    )
-                    for k, first in enumerate(firsts)
-                ]
-                for copy in reads:
-                    copy.start()
-                for k, copy in enumerate(reads):
-                    copy.wait()
-                    here = slice(k * width, (k + 1) * width)
-                    load_bf[here, :] = load_f[here, :].astype(BF16)
-                load_t[...] = load_bf[...].T
-
+            load_ref, _, send_ref, keep_ref, load_t, held, sems, load_bf, load_f, turned = refs
         else:
-            load_t, _, send_ref, keep_ref = refs
+            load_t, _, send_ref, keep_ref, held, sems = refs
+        copies = [
+            pltpu.make_async_copy(
+                counts_ref.at[pl.ds(half * half_rows + i * piece, piece), :],
+                held.at[pl.ds(i * piece, piece), :],
+                sems.at[i],
+            )
+            for i in range(pieces)
+        ]
 
         def put(part, cols):
             for i, k in enumerate(send_ids):
@@ -206,47 +194,53 @@
             for i, k in enumerate(keep_ids):
                 keep_ref[i, :, cols] = part[k * width : (k + 1) * width]
 
-        part = dot(left_ref[...], load_t[:side, :], PLAIN)
-        part = part + dot(right_ref[...], load_t[side:, :], PLAIN)
-        put(part.T, pl.ds(pl.multiple_of(at * STEP, STEP), STEP))
-
         if first_call:
-
-            @pl.when(at == 0)
-            def _():
-                local = dot(load_bf[...], load_t[...], PLAIN)
-                for k, first in enumerate(firsts):
-                    turned[pl.ds(first, width), :] = local[k * width : (k + 1) * width]
-                put(turned[...].T, slice(half_rows, total_cols))
-
-    out = shape(genes_n // 2, width, total_cols)
-    out_spec = pl.BlockSpec((genes_n // 2, width, total_cols), lambda i, m: (0, 0, 0))
-    outs, out_specs, scratch = (out, out), (out_spec, out_spec), []
+            reads = [
+                pltpu.make_async_copy(
+                    load_ref.at[pl.ds(first, width), :],
+                    load_f.at[pl.ds(k * width, width), :],
+                    sems.at[pieces + k],
+                )
+                for k, first in enumerate(firsts)
+            ]
+            for copy in reads + copies:
+                copy.start()
+            for k, copy in enumerate(reads):
+                copy.wait()
+                here = slice(k * width, (k + 1) * width)
+                load_bf[here, :] = load_f[here, :].astype(BF16)
+            load_t[...] = load_bf[...].T
+            local = dot(load_bf[...], load_t[...], PLAIN)
+            for k, first in enumerate(firsts):
+                turned[pl.ds(first, width), :] = local[k * width : (k + 1) * width]
+            put(turned[...].T, slice(half_rows, total_cols))
+        else:
+            for copy in copies:
+                copy.start()
+        for i in range(0, pieces, 2):
+            copies[i].wait()
+            copies[i + 1].wait()
+            at = slice(i * piece, (i + 2) * piece)
+            put(dot(held[at, :], load_t[...], PLAIN).T, at)
+
+    outs = (shape(genes_n // 2, width, total_cols),) * 2
+    scratch = [pltpu.VMEM((half_rows, genes), BF16), pltpu.SemaphoreType.DMA((pieces + genes_n,))]
     if first_call:
         outs += (shape(genes, width_all, dtype=BF16),)
-        out_specs += (pl.BlockSpec((genes, width_all), lambda i, m: (0, 0)),)
-        scratch = [
+        scratch += [
             pltpu.VMEM((width_all, genes), BF16),
             pltpu.VMEM((width_all, genes), F32),
             pltpu.VMEM((width_all, width_all), F32),
-            pltpu.SemaphoreType.DMA((genes_n,)),
         ]
-        load_spec = ANY_SPEC
-    else:
-        load_spec = pl.BlockSpec((genes, width_all), lambda i, m: (0, 0))
-    grid_spec = pltpu.PrefetchScalarGridSpec(
-        num_scalar_prefetch=1,
-        grid=(steps,),
-        in_specs=[
-            pl.BlockSpec((STEP, side), lambda i, m: (i + half * steps, 0)),
-            pl.BlockSpec((STEP, side), lambda i, m: (i + half * steps, 1)),
-            load_spec,
-            ANY_SPEC,
-        ],
-        out_specs=out_specs,
+    return kernel_call(
+        body,
+        outs,
+        7,
+        limit=36,
+        in_specs=[SMEM_SPEC, ANY_SPEC, ANY_SPEC if first_call else VMEM_SPEC, ANY_SPEC],
+        out_specs=(VMEM_SPEC,) * len(outs),
         scratch_shapes=scratch,
-    )
-    return kernel_call(body, outs, 7, limit=36, grid_spec=grid_spec)(me, counts, counts, loadings, token)
+    )(me, counts, loadings, token)
 
 
 def swap(block, axis, bit):
@@ -339,21 +333,42 @@
     )(payload, back, numer, plain)
 
 
-def sent_on(blocks, token):
-    n = len(blocks)
+def sent_on(sources, token):
+    n = len(sources)
+    width, rows = sources[0][0].shape
+    half_rows = rows // 2
 
     def body(*refs):
-        for src, dst in zip(refs[:n], refs[n + 1 :]):
-            dst[...] = src[...]
-
-    return kernel_call(
-        body,
-        tuple(shape(*b.shape) for b in blocks),
+        for (_, half), src, dst in zip(sources, refs[:n], refs[n + 1 :]):
+            dst[...] = src[:, half * half_rows : (half + 1) * half_rows]
+
+    return kernel_call(
+        body,
+        (shape(width, half_rows),) * n,
         0.02,
         limit=1,
         in_specs=[VMEM_SPEC] * n + [ANY_SPEC],
         out_specs=(VMEM_SPEC,) * n,
-    )(*blocks, token)
+    )(*[block for block, _ in sources], token)
+
+
+def joined(halves, token):
+    n = len(halves)
+    width, half_rows = halves[0][0].shape
+
+    def body(*refs):
+        for i in range(n):
+            for j in range(2):
+                refs[2 * n + 1 + i][:, j * half_rows : (j + 1) * half_rows] = refs[2 * i + j][...]
+
+    return kernel_call(
+        body,
+        (shape(width, 2 * half_rows),) * n,
+        0.02,
+        limit=1,
+        in_specs=[VMEM_SPEC] * (2 * n) + [ANY_SPEC],
+        out_specs=(VMEM_SPEC,) * n,
+    )(*[x for pair in halves for x in pair], token)
 
 
 def turned_back(blocks, ids, width, me, token):
@@ -547,6 +562,11 @@
     return end, swap(end, "bin", 1)
 
 
+def split(x):
+    high = x.astype(BF16)
+    return high, (x - high.astype(F32)).astype(BF16)
+
+
 def shares(loadings, sums, ids, cols, me, token):
     width_all, genes = loadings.shape
     width = width_all // len(ids)
@@ -572,7 +592,8 @@
         for j, first in enumerate(firsts):
             load[j * width : (j + 1) * width, :] = load_ref[pl.ds(first, width), :]
         value = load[...]
-        value = value / dot(gram[...], value, PLAIN, lax.Precision.HIGHEST)
+        (gram_hi, gram_lo), (hi, lo) = split(gram[...]), split(value)
+        value = value / (dot(gram_hi, hi, PLAIN) + (dot(gram_hi, lo, PLAIN) + dot(gram_lo, hi, PLAIN)))
         for j, first in enumerate(firsts):
             out_ref[pl.ds(first, width), :] = value[j * width : (j + 1) * width]
 
@@ -695,10 +716,14 @@
     for k in bits:
         blocks[k] = swap(own_block, "gene", k)
 
+    coming = {}
+
     def come_on(group, token):
-        outs = sent_on([blocks[k & (k - 1)] for k in group], token)
-        for k, out in zip(group, outs):
-            blocks[k] = swap(out, "gene", k & -k)
+        axes = [(k & -k, 1 << (k.bit_length() - 1)) for k in group]
+        sources = [(blocks[k ^ bit], j) for k, pair in zip(group, axes) for j, bit in enumerate(pair)]
+        outs = sent_on(sources, token)
+        for i, (k, pair) in enumerate(zip(group, axes)):
+            coming[k] = [swap(outs[2 * i + j], "gene", bit) for j, bit in enumerate(pair)]
         return outs[-1]
 
     pending = [[None] * len(groups) for _ in range(HALVES)]
@@ -756,7 +781,9 @@
     last_slot = chunks + line - 3
     for t in range(1, last_slot + 1):
         if t in firsts and firsts[t] + 1 < len(groups):
-            token = awaited([blocks[k] for k in groups[firsts[t] + 1]], token)
+            later = groups[firsts[t] + 1]
+            for k, block in zip(later, joined([coming[k] for k in later], token)):
+                blocks[k] = token = block
             token = awaited([come[half][-1] for half in range(HALVES)], token)
         for half in range(HALVES):
             if t in firsts:
@@ -776,12 +803,10 @@
             both(end, c)
     rest = [c for c in range(chunks) if c not in ends[0]]
     for c in rest:
-        token = end(c, 0, token)
+        both(end, c)
     sums = [(own[0][c],) + ends[0][c] for c in range(chunks)]
     loadings_new = None
     share, token = shares(loadings, sums, ids, counts.shape[1] // HALVES, me1, token)
-    for c in rest:
-        token = end(c, 1, token)
     for c in range(chunks - 1):
         loadings_new, token = final(c, loadings_new, token)
     for half in range(HALVES):

time: 220 us -> 219 us (level)
  waiting for transfers between devices: 49.9 us -> 46.3 us
  starting transfers between devices: 73.1 us -> 76.6 us
    ppermute x23 -> x24, waiting for transfers between devices: 38.7 us -> 33.3 us  [swap(): lax.ppermute(block, axis, [(i, i ^ bit) for i in range(lax.axis_size(axis...]
    ppermute x23 -> x24, starting transfers between devices: 31 us -> 33.2 us  [swap(): lax.ppermute(block, axis, [(i, i ^ bit) for i in range(lax.axis_size(axis...]
    pallas_call x3 -> x4, Pallas kernels: 20.8 us -> 21.5 us  [the longest x2 21.4 us: numer_part(): kernel_call(body, outs, 7, limit=36, in_specs=[SMEM_SPEC, ANY_SPEC, ANY_S...]
  transfers between devices with their start and end apart: 39 -> 40, of which waited for: 15 -> 13; matrix products, arithmetic and copies ran while one was open for 0% -> 0% of each run, Pallas kernels for 36% -> 36%
where the time goes in v3:
time: 219 us
  Pallas kernels  89.6 us (41%)
  starting transfers between devices  76.6 us (35%)
  waiting for transfers between devices  46.3 us (21%)
  local copies, waits for them, and re-layouts  4.19 us (2%)
    ppermute x24, waiting for transfers between devices, swap(): lax.ppermute(block, axis, [(i, i ^ bit) for i in range(lax.axis_size(axis...  33.3 us
    ppermute x24, starting transfers between devices, swap(): lax.ppermute(block, axis, [(i, i ^ bit) for i in range(lax.axis_size(axis...  33.2 us
    ppermute x10, starting transfers between devices, line_slot(): return (lax.ppermute(send, 'bin', hops), send)  26.1 us
    pallas_call x2, Pallas kernels, numer_part(): kernel_call(body, outs, 7, limit=36, in_specs=[SMEM_SPEC, ANY_SPEC, ANY_S...  21.4 us
    pallas_call x4, Pallas kernels, cross_part(): kernel_call(body, (shape(width, cols + width_all),) * n, 0.02, limit=8, i...  11.2 us
    pallas_call x1, Pallas kernels, first_cross(): kernel_call(body, (shape(width, cols + width_all),) * HALVES + (pltpu.VME...  10.2 us
    ppermute x10, waiting for transfers between devices, line_slot(): return (lax.ppermute(send, 'bin', hops), send)  7.33 us
    all_to_all x1, starting transfers between devices, on_device(): lax.all_to_all(payload, 'bin', split_axis=0, concat_axis=0, tiled=True)  6.33 us
  transfers between devices with their start and end apart: 40, of which 13 were waited for; matrix products, arithmetic and copies ran while one was open for 0% of the time, Pallas kernels for 36%

profile of v3, /device:TPU:0, one launch (start us, length us, event | category | flops | bytes accessed | tf_op | source)
XLA Modules:
  0.0 218.7 jit_solution(17647015416756144263)
XLA Ops:
  1.3 1.9 copy-done
  3.2 3.4 %shard_map.68.refs_1_.pay_ref = f32[8,72,384]{2,1,0:T(8,128)} custom-call(s32[1]{0:T(128)} %bitcast.me_ref, f32[3072,256]{1,0:T(8,128)S(1)} %copy-done, f32[8,1,384]{2,1,0:T(1,128)S(1)} %bitcast.5), custom_call_target="tpu_custom_call" | custom-call | bytes 11070000 | tf_op jit(solution)/shard_map/pallas_call | solution.py:64
  6.6 6.3 %all-to-all-start = ((f32[8,72,384]{2,1,0:T(8,128)}), f32[8,72,384]{2,1,0:T(8,128)S(1)}, u32[]{:S(2)}, u32[]{:S(2)}) async-start(f32[8,72,384]{2,1,0:T(8,128)} %shard_map.68.refs_1_.pay_ref), calls=%async_computation | async-start | bytes 1769472 | tf_op jit(solution)/shard_map/all_to_all | solution.py:674
  13.0 11.3 %shard_map.69 = (f32[2,64,1792]{2,1,0:T(8,128)S(1)}, f32[2,64,1792]{2,1,0:T(8,128)S(1)}, bf16[4608,256]{1,0:T(8,128)(2,1)S(1)}) custom-call(s32[1]{0:T(128)} %bitcast.me_ref, bf16[3072,4608]{1,0:T(8,128)(2,1)} %counts_ref.5, f32[256,4608]{1,0:T(8,128)} %load_ref.1, f32[8,72,384]{2,1,0:T(8,128)} %shard_map.68.refs_1_.pay_ref), custom_call_target="tpu_custom_call" | custom-call | bytes 25830000 | tf_op jit(solution)/shard_map/pallas_call | solution.py:235
  24.3 1.6 collective-permute-start.3
  25.9 10.1 %shard_map.70 = (f32[2,64,1536]{2,1,0:T(8,128)}, f32[2,64,1536]{2,1,0:T(8,128)S(1)}) custom-call(s32[1]{0:T(128)} %bitcast.me_ref, bf16[3072,4608]{1,0:T(8,128)(2,1)} %counts_ref.5, bf16[4608,256]{1,0:T(8,128)(2,1)S(1)} %get-tuple-element.44.refs_0_, f32[2,64,1792]{2,1,0:T(8,128)S(1)} %get-tuple-element.45.refs_1_.refs_0_.refs_3_), custom_call_target="tpu_custom_call" | custom-call | bytes 25830000 | tf_op jit(solution)/shard_map/pallas_call | solution.py:235
  36.0 1.6 collective-permute-start.2
  37.6 2.7 %shard_map.71 = (f32[12,72,256]{2,1,0:T(8,128)S(1)}, f32[72,256]{1,0:T(8,128)S(1)}, f32[72,256]{1,0:T(8,128)S(1)}, s32[1,3072]{1,0:T(1,128)S(1)}) custom-call(s32[1]{0:T(128)} %bitcast.2.me_ref, f32[8,72,384]{2,1,0:T(8,128)S(1)} %all-to-all-done.got_ref, s32[12,256]{1,0:T(8,128)S(1)} %copy-done.3, f32[2,64,1536]{2,1,0:T(8,128)S(1)} %get-tuple-element.46._.refs_0_), custom_call_target="tpu_custom_call" | custom-call | bytes 11070000 | tf_op jit(solution)/shard_map/pallas_call | solution.py:106
  40.3 1.9 collective-permute-start
  42.1 1.5 collective-permute-start.1
  43.6 3.6 %collective-permute-done.3.refs_1_.refs_4_ = f32[2,64,1792]{2,1,0:T(8,128)} collective-permute-done((f32[2,64,1792]{2,1,0:T(8,128)S(1)}, f32[2,64,1792]{2,1,0:T(8,128)}, u32[]{:S(2)}, u32[]{:S(2)}) %collective-permute-start.3) | collective-permute-done | bytes 917536 | tf_op jit(solution)/shard_map/ppermute | solution.py:247
  48.4 7.6 %collective-permute-done.2.refs_1_ = f32[2,64,1536]{2,1,0:T(8,128)} collective-permute-done((f32[2,64,1536]{2,1,0:T(8,128)}, f32[2,64,1536]{2,1,0:T(8,128)}, u32[]{:S(2)}, u32[]{:S(2)}) %collective-permute-start.2) | collective-permute-done | bytes 786464 | tf_op jit(solution)/shard_map/ppermute | solution.py:247
  57.3 4.2 %shard_map.74.refs_7_ = f32[8,72,384]{2,1,0:T(8,128)} custom-call(f32[12,72,256]{2,1,0:T(8,128)S(1)} %get-tuple-element.47.refs_2_.grid_ref, f32[72,256]{1,0:T(8,128)S(1)} %collective-permute-done.above_ref, f32[72,256]{1,0:T(8,128)S(1)} %collective-permute-done.1.below_ref, s32[1,3072]{1,0:T(1,128)S(1)} %get-tuple-element.50.cell_ref, ...), custom_call_target="tpu_custom_call" | custom-call | bytes 14760000 | tf_op jit(solution)/shard_map/pallas_call | solution.py:155
  61.4 4.7 %all-to-all-start.1 = ((f32[8,72,384]{2,1,0:T(8,128)}), f32[8,72,384]{2,1,0:T(8,128)S(1)}, u32[]{:S(2)}, u32[]{:S(2)}) async-start(f32[8,72,384]{2,1,0:T(8,128)} %shard_map.74.refs_7_), calls=%async_computation.1 | async-start | bytes 1769472 | tf_op jit(solution)/shard_map/all_to_all | solution.py:708
  66.2 1.5 collective-permute-start.5
  68.2 10.7 %collective-permute-done.4.refs_2_ = f32[1,64,1536]{2,1,0:T(8,128)S(1)} collective-permute-done((f32[1,64,1536]{2,1,0:T(8,128)S(1)}, f32[1,64,1536]{2,1,0:T(8,128)S(1)}, u32[]{:S(2)}, u32[]{:S(2)}) %collective-permute-start.4) | collective-permute-done | bytes 393248 | tf_op jit(solution)/shard_map/ppermute | solution.py:247
  80.5 5.9 %shard_map.75 = (f32[64,3072]{1,0:T(8,128)}, f32[64,3072]{1,0:T(8,128)}) custom-call(f32[2,64,1536]{2,1,0:T(8,128)} %copy-done.2, f32[2,64,1536]{2,1,0:T(8,128)} %collective-permute-done.2.refs_1_, f32[1,64,1536]{2,1,0:T(8,128)} %copy-done.6, f32[2,64,1792]{2,1,0:T(8,128)} %copy-done.1, f32[2,64,1792]{2,1,0:T(8,128)} %collective-permute-done.3.refs_1_.refs_4_, ...), custom_call_target="tpu_custom_call" | custom-call | bytes 14760000 | tf_op jit(solution)/shard_map/pallas_call | solution.py:299
  86.4 2.9 %all-to-all-done.1.back_ref = f32[8,72,384]{2,1,0:T(8,128)S(1)} async-done(((f32[8,72,384]{2,1,0:T(8,128)}), f32[8,72,384]{2,1,0:T(8,128)S(1)}, u32[]{:S(2)}, u32[]{:S(2)}) %all-to-all-start.1) | async-done | bytes 884768 | tf_op jit(solution)/shard_map/all_to_all | solution.py:708
  90.2 2.8 %shard_map.76.block_ref._.refs_6_.refs_0_ = f32[64,3072]{1,0:T(8,128)S(1)} custom-call(f32[8,72,384]{2,1,0:T(8,128)} %shard_map.68.refs_1_.pay_ref, f32[8,72,384]{2,1,0:T(8,128)} %copy-done.4, f32[64,3072]{1,0:T(8,128)} %get-tuple-element.53.numer_ref, f32[64,3072]{1,0:T(8,128)} %get-tuple-element.54.plain_ref), custom_call_target="tpu_custom_call" | custom-call | bytes 73800 | tf_op jit(solution)/shard_map/pallas_call | solution.py:326
  93.0 1.6 collective-permute-start.6
  95.1 10.2 %shard_map.77 = (f32[64,2560]{1,0:T(8,128)S(1)}, f32[64,2560]{1,0:T(8,128)S(1)}, bf16[512,4608]{1,0:T(8,128)(2,1)S(1)}, bf16[512,4608]{1,0:T(8,128)(2,1)S(1)}, b...) custom-call(bf16[3072,4608]{1,0:T(8,128)(2,1)} %counts_ref.5, ...), custom_call_target="tpu_custom_call" | custom-call | bytes 73800 | tf_op jit(solution)/shard_map/pallas_call | solution.py:437
  105.9 6.3 %collective-permute-done.6.refs_0_.refs_1_.refs_7_ = f32[64,3072]{1,0:T(8,128)S(1)} collective-permute-done((f32[64,3072]{1,0:T(8,128)S(1)}, f32[64,3072]{1,0:T(8,128)S(1)}, u32[]{:S(2)}, u32[]{:S(2)}) %collective-permute-start.6) | collective-permute-done | bytes 786464 | tf_op jit(solution)/shard_map/ppermute | solution.py:247
  113.6 1.3 collective-permute-start.12
  116.1 1.5 collective-permute-start.15
  117.7 2.6 %shard_map.82 = (f32[64,2560]{1,0:T(8,128)S(1)}, f32[64,2560]{1,0:T(8,128)S(1)}) custom-call(bf16[512,4608]{1,0:T(8,128)(2,1)S(1)} %get-tuple-element.58.refs_0_, bf16[512,4608]{1,0:T(8,128)(2,1)S(1)} %get-tuple-element.59.refs_1_, bf16[512,4608]{1,0:T(8,128)(2,1)S(1)} %get-tuple-element.60.refs_2_, bf16[512,4608]{1,0:T(8,128)(2,1)S(1)} %get-tuple-element.61.refs_3_, ...), custom_call_target="tpu_custom_call" | custom-call | bytes 73800 | tf_op jit(solution)/shard_map/pallas_call | solution.py:475
  120.3 3.6 %collective-permute-done.8.refs_0_ = f32[64,1536]{1,0:T(8,128)S(1)} collective-permute-done((f32[64,1536]{1,0:T(8,128)S(1)}, f32[64,1536]{1,0:T(8,128)S(1)}, u32[]{:S(2)}, u32[]{:S(2)}) %collective-permute-start.8) | collective-permute-done | bytes 393248 | tf_op jit(solution)/shard_map/ppermute | solution.py:247
  123.9 2.5 %shard_map.83 = (f32[64,2560]{1,0:T(8,128)S(1)}, f32[64,2560]{1,0:T(8,128)S(1)}) custom-call(bf16[512,4608]{1,0:T(8,128)(2,1)S(1)} %get-tuple-element.58.refs_0_, bf16[512,4608]{1,0:T(8,128)(2,1)S(1)} %get-tuple-element.59.refs_1_, bf16[512,4608]{1,0:T(8,128)(2,1)S(1)} %get-tuple-element.60.refs_2_, bf16[512,4608]{1,0:T(8,128)(2,1)S(1)} %get-tuple-element.61.refs_3_, ...), custom_call_target="tpu_custom_call" | custom-call | bytes 73800 | tf_op jit(solution)/shard_map/pallas_call | solution.py:475
  127.2 2.8 %collective-permute-done.15.refs_0_.come_ref = f32[64,2560]{1,0:T(8,128)S(1)} collective-permute-done((f32[64,2560]{1,0:T(8,128)S(1)}, f32[64,2560]{1,0:T(8,128)S(1)}, u32[]{:S(2)}, u32[]{:S(2)}) %collective-permute-start.15) | collective-permute-done | bytes 655392 | tf_op jit(solution)/shard_map/ppermute | solution.py:518
  130.8 4.5 %collective-permute-start.19 = (f32[64,2560]{1,0:T(8,128)S(1)}, f32[64,2560]{1,0:T(8,128)S(1)}, u32[]{:S(2)}, u32[]{:S(2)}) collective-permute-start(f32[64,2560]{1,0:T(8,128)S(1)} %shard_map.87.refs_4_), channel_id=1, source_target_pairs={{0,2},{2,4},{7,5},{5,3},{8,10},{10,12},{15,13},{13,11},{16,18},{18... | collective-permute-start | bytes 1966088 | tf_op jit(solution)/shard_map/ppermute | solution.py:537
  136.0 1.9 collective-permute-start.18
  138.0 3.1 %shard_map.90.refs_10_.refs_0_ = f32[64,2560]{1,0:T(8,128)S(1)} custom-call(bf16[512,4608]{1,0:T(8,128)(2,1)S(1)} %get-tuple-element.58.refs_0_, bf16[512,4608]{1,0:T(8,128)(2,1)S(1)} %get-tuple-element.59.refs_1_, bf16[512,4608]{1,0:T(8,128)(2,1)S(1)} %get-tuple-element.60.refs_2_, bf16[512,4608]{1,0:T(8,128)(2,1)S(1)} %get-tuple-element.61.refs_3_, ...), custom_call_target="tpu_custom_call" | custom-call | bytes 73800 | tf_op jit(solution)/shard_map/pallas_call | solution.py:475
  141.1 3.1 %shard_map.91._.refs_0_ = f32[64,2560]{1,0:T(8,128)S(1)} custom-call(bf16[512,4608]{1,0:T(8,128)(2,1)S(1)} %get-tuple-element.58.refs_0_, bf16[512,4608]{1,0:T(8,128)(2,1)S(1)} %get-tuple-element.59.refs_1_, bf16[512,4608]{1,0:T(8,128)(2,1)S(1)} %get-tuple-element.60.refs_2_, bf16[512,4608]{1,0:T(8,128)(2,1)S(1)} %get-tuple-element.61.refs_3_, ...), custom_call_target="tpu_custom_call" | custom-call | bytes 73800 | tf_op jit(solution)/shard_map/pallas_call | solution.py:475
  144.8 3.5 %collective-permute-start.22 = (f32[64,2560]{1,0:T(8,128)S(1)}, f32[64,2560]{1,0:T(8,128)S(1)}, u32[]{:S(2)}, u32[]{:S(2)}) collective-permute-start(f32[64,2560]{1,0:T(8,128)S(1)} %shard_map.92._), channel_id=1, source_target_pairs={{0,2},{2,4},{4,6},{7,5},{5,3},{3,1},{8,10},{10,12},{12,14},{15,13}... | collective-permute-start | bytes 1966088 | tf_op jit(solution)/shard_map/ppermute | solution.py:537
  148.5 1.9 collective-permute-done.18.come_ref.refs_1_.refs_0_
  150.9 4.5 %collective-permute-start.20 = (f32[64,2560]{1,0:T(8,128)S(1)}, f32[64,2560]{1,0:T(8,128)S(1)}, u32[]{:S(2)}, u32[]{:S(2)}) collective-permute-start(f32[64,2560]{1,0:T(8,128)S(1)} %shard_map.93.refs_2_), channel_id=1, source_target_pairs={{0,2},{2,4},{4,6},{7,5},{5,3},{3,1},{8,10},{10,12},{12,14},{15,13}... | collective-permute-start | bytes 1966088 | tf_op jit(solution)/shard_map/ppermute | solution.py:537
  155.5 1.9 collective-permute-done.22.come_ref.refs_2_.refs_1_.refs_0_
  158.0 4.5 %collective-permute-start.27 = (f32[64,2560]{1,0:T(8,128)S(1)}, f32[64,2560]{1,0:T(8,128)S(1)}, u32[]{:S(2)}, u32[]{:S(2)}) collective-permute-start(f32[64,2560]{1,0:T(8,128)S(1)} %shard_map.95.refs_2_), channel_id=1, source_target_pairs={{0,2},{2,4},{4,6},{7,5},{5,3},{3,1},{8,10},{10,12},{12,14},{15,13}... | collective-permute-start | bytes 1966088 | tf_op jit(solution)/shard_map/ppermute | solution.py:537
  162.5 1.9 collective-permute-done.20.come_ref.refs_2_.refs_1_.refs_0_
  165.0 4.5 %collective-permute-start.26 = (f32[64,2560]{1,0:T(8,128)S(1)}, f32[64,2560]{1,0:T(8,128)S(1)}, u32[]{:S(2)}, u32[]{:S(2)}) collective-permute-start(f32[64,2560]{1,0:T(8,128)S(1)} %shard_map.97.refs_4_), channel_id=1, source_target_pairs={{0,2},{2,4},{4,6},{7,5},{5,3},{3,1},{8,10},{10,12},{12,14},{15,13}... | collective-permute-start | bytes 1966088 | tf_op jit(solution)/shard_map/ppermute | solution.py:537
  169.4 4.2 %shard_map.98 = (f32[3072,256]{1,0:T(8,128)}, f32[8,128]{1,0:T(8,128)S(1)}) custom-call(s32[1]{0:T(128)} %bitcast.me_ref, f32[64,3072]{1,0:T(8,128)S(1)} %shard_map.76.block_ref._.refs_6_.refs_0_, f32[64,3072]{1,0:T(8,128)S(1)} %collective-permute-done.6.refs_0_.refs_1_.refs_7_, f32[64,3072]{1,0:T(8,128)S(1)} %collective-permute-done.7.refs_1_.refs_0_.refs_8_.refs_2_, ...), custom_call_target="tpu_custom_call" | custom-call | bytes 73800 | tf_op jit(solution)/shard_map/pallas_call | solution.py:394
  176.7 1.7 collective-permute-done.26.come_ref.refs_2_.refs_1_.refs_0_
  185.0 12.0 %collective-permute-start.32 = (f32[64,2560]{1,0:T(8,128)S(1)}, f32[64,2560]{1,0:T(8,128)S(1)}, u32[]{:S(2)}, u32[]{:S(2)}) collective-permute-start(f32[64,2560]{1,0:T(8,128)S(1)} %shard_map.109._.refs_7_.refs_1_), channel_id=1, source_target_pairs={{0,1},{1,0},{2,3},{3,2},{4,5},{5,4},{6,7},{7,6},{8,9},{9,8},{10,11... | collective-permute-start | bytes 1966088 | tf_op jit(solution)/shard_map/ppermute | solution.py:247
  198.3 3.9 %collective-permute-start.34 = (f32[64,2560]{1,0:T(8,128)S(1)}, f32[64,2560]{1,0:T(8,128)S(1)}, u32[]{:S(2)}, u32[]{:S(2)}) collective-permute-start(f32[64,2560]{1,0:T(8,128)S(1)} %shard_map.111._.refs_10_.refs_1_), channel_id=1, source_target_pairs={{0,1},{1,0},{2,3},{3,2},{4,5},{5,4},{6,7},{7,6},{8,9},{9,8},{10,11... | collective-permute-start | bytes 1966088 | tf_op jit(solution)/shard_map/ppermute | solution.py:247
  202.8 6.3 %collective-permute-start.37 = (f32[64,2560]{1,0:T(8,128)S(1)}, f32[64,2560]{1,0:T(8,128)S(1)}, u32[]{:S(2)}, u32[]{:S(2)}) collective-permute-start(f32[64,2560]{1,0:T(8,128)S(1)} %shard_map.112.refs_12_.refs_1_), channel_id=1, source_target_pairs={{0,1},{1,0},{2,3},{3,2},{4,5},{5,4},{6,7},{7,6},{8,9},{9,8},{10,11... | collective-permute-start | bytes 1966088 | tf_op jit(solution)/shard_map/ppermute | solution.py:247
  209.2 3.9 %shard_map.113 = (f32[256,4608]{1,0:T(8,128)S(1)}, f32[8,128]{1,0:T(8,128)S(1)}) custom-call(s32[1]{0:T(128)} %bitcast.me_ref, f32[256,4608]{1,0:T(8,128)S(1)} %bitcast.4, f32[64,2560]{1,0:T(8,128)S(1)} %shard_map.80.refs_2_.refs_1_.refs_0_, f32[64,2560]{1,0:T(8,128)S(1)} %shard_map.99._.refs_1_, f32[64,2560]{1,0:T(8,128)S(1)} %collective-permute-done.24.refs_0_.refs_2_, ...), custom_call_target="tpu_custom_call" | custom-call | bytes 73800 | tf_op jit(solution)/shard_map/pallas_call | solution.py:601
  213.1 1.2 shard_map.114
  214.4 1.3 shard_map.115
  215.6 1.2 shard_map.116
  (104 shorter events, 28.1 us)
Async XLA Ops:
  1.3 1.9 copy-start
  6.6 31.0 %all-to-all-start = ((f32[8,72,384]{2,1,0:T(8,128)}), f32[8,72,384]{2,1,0:T(8,128)S(1)}, u32[]{:S(2)}, u32[]{:S(2)}) async-start(f32[8,72,384]{2,1,0:T(8,128)} %shard_map.68.refs_1_.pay_ref), calls=%async_computation | async-start | bytes 1769472 | tf_op jit(solution)/shard_map/all_to_all | solution.py:674
  24.3 11.7 %copy-start.1 = (f32[2,64,1792]{2,1,0:T(8,128)}, f32[2,64,1792]{2,1,0:T(8,128)S(1)}, u32[]{:S(2)}) copy-start(f32[2,64,1792]{2,1,0:T(8,128)S(1)} %get-tuple-element.45.refs_1_.refs_0_.refs_3_) | copy-start | bytes 2752516
  24.3 22.9 %collective-permute-start.3 = (f32[2,64,1792]{2,1,0:T(8,128)S(1)}, f32[2,64,1792]{2,1,0:T(8,128)}, u32[]{:S(2)}, u32[]{:S(2)}) collective-permute-start(f32[2,64,1792]{2,1,0:T(8,128)S(1)} %get-tuple-element.52), channel_id=1, source_target_pairs={{0,16},{8,24},{16,0},{24,8},{1,17},{9,25},{17,1},{25,9},{2,18},{10... | collective-permute-start | bytes 2752520 | tf_op jit(solution)/shard_map/ppermute | solution.py:247
  25.9 11.7 %copy-start.3 = (s32[12,256]{1,0:T(8,128)S(1)}, s32[12,256]{1,0:T(8,128)}, u32[]{:S(2)}) copy-start(s32[12,256]{1,0:T(8,128)} %code_ref.3) | copy-start | bytes 36868
  36.0 20.1 %copy-start.2 = (f32[2,64,1536]{2,1,0:T(8,128)}, f32[2,64,1536]{2,1,0:T(8,128)S(1)}, u32[]{:S(2)}) copy-start(f32[2,64,1536]{2,1,0:T(8,128)S(1)} %get-tuple-element.46._.refs_0_) | copy-start | bytes 2359300
  36.0 20.1 %collective-permute-start.2 = (f32[2,64,1536]{2,1,0:T(8,128)}, f32[2,64,1536]{2,1,0:T(8,128)}, u32[]{:S(2)}, u32[]{:S(2)}) collective-permute-start(f32[2,64,1536]{2,1,0:T(8,128)} %get-tuple-element.51), channel_id=1, source_target_pairs={{0,8},{8,0},{16,24},{24,16},{1,9},{9,1},{17,25},{25,17},{2,10},{10... | collective-permute-start | bytes 2359304 | tf_op jit(solution)/shard_map/ppermute | solution.py:247
  40.3 17.0 %collective-permute-start = (f32[72,256]{1,0:T(8,128)S(1)}, f32[72,256]{1,0:T(8,128)S(1)}, u32[]{:S(2)}, u32[]{:S(2)}) collective-permute-start(f32[72,256]{1,0:T(8,128)S(1)} %get-tuple-element.48), channel_id=1, source_target_pairs={{0,1},{1,2},{2,3},{3,4},{4,5},{5,6},{6,7},{8,9},{9,10},{10,11},{11... | collective-permute-start | bytes 221192 | tf_op jit(solution)/shard_map/ppermute | solution.py:701
  42.1 15.1 %collective-permute-start.1 = (f32[72,256]{1,0:T(8,128)S(1)}, f32[72,256]{1,0:T(8,128)S(1)}, u32[]{:S(2)}, u32[]{:S(2)}) collective-permute-start(f32[72,256]{1,0:T(8,128)S(1)} %get-tuple-element.49), channel_id=1, source_target_pairs={{1,0},{2,1},{3,2},{4,3},{5,4},{6,5},{7,6},{9,8},{10,9},{11,10},{12... | collective-permute-start | bytes 221192 | tf_op jit(solution)/shard_map/ppermute | solution.py:702
  61.4 27.8 %all-to-all-start.1 = ((f32[8,72,384]{2,1,0:T(8,128)}), f32[8,72,384]{2,1,0:T(8,128)S(1)}, u32[]{:S(2)}, u32[]{:S(2)}) async-start(f32[8,72,384]{2,1,0:T(8,128)} %shard_map.74.refs_7_), calls=%async_computation.1 | async-start | bytes 1769472 | tf_op jit(solution)/shard_map/all_to_all | solution.py:708
  66.2 12.9 %collective-permute-start.5 = (f32[1,64,1792]{2,1,0:T(8,128)S(1)}, f32[1,64,1792]{2,1,0:T(8,128)S(1)}, u32[]{:S(2)}, u32[]{:S(2)}) collective-permute-start(f32[1,64,1792]{2,1,0:T(8,128)S(1)} %shard_map.72.refs_2_), channel_id=1, source_target_pairs={{0,8},{8,0},{16,24},{24,16},{1,9},{9,1},{17,25},{25,17},{2,10},{10... | collective-permute-start | bytes 1376264 | tf_op jit(solution)/shard_map/ppermute | solution.py:247
  67.7 11.2 %collective-permute-start.4 = (f32[1,64,1536]{2,1,0:T(8,128)S(1)}, f32[1,64,1536]{2,1,0:T(8,128)S(1)}, u32[]{:S(2)}, u32[]{:S(2)}) collective-permute-start(f32[1,64,1536]{2,1,0:T(8,128)S(1)} %shard_map.73._), channel_id=1, source_target_pairs={{0,16},{8,24},{16,0},{24,8},{1,17},{9,25},{17,1},{25,9},{2,18},{10... | collective-permute-start | bytes 1179656 | tf_op jit(solution)/shard_map/ppermute | solution.py:247
  79.7 0.8 copy-start.5
  89.3 0.9 copy-start.4
  93.0 19.1 %collective-permute-start.6 = (f32[64,3072]{1,0:T(8,128)S(1)}, f32[64,3072]{1,0:T(8,128)S(1)}, u32[]{:S(2)}, u32[]{:S(2)}) collective-permute-start(f32[64,3072]{1,0:T(8,128)S(1)} %shard_map.76.block_ref._.refs_6_.refs_0_), channel_id=1, source_target_pairs={{0,8},{8,0},{16,24},{24,16},{1,9},{9,1},{17,25},{25,17},{2,10},{10... | collective-permute-start | bytes 2359304 | tf_op jit(solution)/shard_map/ppermute | solution.py:247
  94.6 18.8 %collective-permute-start.7 = (f32[64,3072]{1,0:T(8,128)S(1)}, f32[64,3072]{1,0:T(8,128)S(1)}, u32[]{:S(2)}, u32[]{:S(2)}) collective-permute-start(f32[64,3072]{1,0:T(8,128)S(1)} %shard_map.76.block_ref._.refs_6_.refs_0_), channel_id=1, source_target_pairs={{0,16},{8,24},{16,0},{24,8},{1,17},{9,25},{17,1},{25,9},{2,18},{10... | collective-permute-start | bytes 2359304 | tf_op jit(solution)/shard_map/ppermute | solution.py:247
  105.3 8.1 %collective-permute-start.11 = (f32[64,2560]{1,0:T(8,128)S(1)}, f32[64,2560]{1,0:T(8,128)S(1)}, u32[]{:S(2)}, u32[]{:S(2)}) collective-permute-start(f32[64,2560]{1,0:T(8,128)S(1)} %get-tuple-element.64.refs_0_), channel_id=1, source_target_pairs={{0,1},{1,0},{2,3},{3,2},{4,5},{5,4},{6,7},{7,6},{8,9},{9,8},{10,11... | collective-permute-start | bytes 1966088 | tf_op jit(solution)/shard_map/ppermute | solution.py:247
  105.4 8.1 %collective-permute-start.10 = (f32[64,2560]{1,0:T(8,128)S(1)}, f32[64,2560]{1,0:T(8,128)S(1)}, u32[]{:S(2)}, u32[]{:S(2)}) collective-permute-start(f32[64,2560]{1,0:T(8,128)S(1)} %get-tuple-element.55.refs_2_.refs_0_), channel_id=1, source_target_pairs={{0,1},{1,0},{2,3},{3,2},{4,5},{5,4},{6,7},{7,6},{8,9},{9,8},{10,11... | collective-permute-start | bytes 1966088 | tf_op jit(solution)/shard_map/ppermute | solution.py:247
  113.6 13.4 %collective-permute-start.12 = (f32[64,2560]{1,0:T(8,128)S(1)}, f32[64,2560]{1,0:T(8,128)S(1)}, u32[]{:S(2)}, u32[]{:S(2)}) collective-permute-start(f32[64,2560]{1,0:T(8,128)S(1)} %shard_map.81.refs_9_.refs_1_.refs_2_.refs_3_), channel_id=1, source_target_pairs={{0,2},{7,5},{8,10},{15,13},{16,18},{23,21},{24,26},{31,29}} | collective-permute-start | bytes 1966088 | tf_op jit(solution)/shard_map/ppermute | solution.py:518
  115.0 8.9 %collective-permute-start.8 = (f32[64,1536]{1,0:T(8,128)S(1)}, f32[64,1536]{1,0:T(8,128)S(1)}, u32[]{:S(2)}, u32[]{:S(2)}) collective-permute-start(f32[64,1536]{1,0:T(8,128)S(1)} %get-tuple-element.56), channel_id=1, source_target_pairs={{0,8},{8,0},{16,24},{24,16},{1,9},{9,1},{17,25},{25,17},{2,10},{10... | collective-permute-start | bytes 1179656 | tf_op jit(solution)/shard_map/ppermute | solution.py:247
  115.6 10.8 %collective-permute-start.9 = (f32[64,1536]{1,0:T(8,128)S(1)}, f32[64,1536]{1,0:T(8,128)S(1)}, u32[]{:S(2)}, u32[]{:S(2)}) collective-permute-start(f32[64,1536]{1,0:T(8,128)S(1)} %get-tuple-element.57.refs_2_), channel_id=1, source_target_pairs={{0,16},{8,24},{16,0},{24,8},{1,17},{9,25},{17,1},{25,9},{2,18},{10... | collective-permute-start | bytes 1179656 | tf_op jit(solution)/shard_map/ppermute | solution.py:247
  116.1 13.9 %collective-permute-start.15 = (f32[64,2560]{1,0:T(8,128)S(1)}, f32[64,2560]{1,0:T(8,128)S(1)}, u32[]{:S(2)}, u32[]{:S(2)}) collective-permute-start(f32[64,2560]{1,0:T(8,128)S(1)} %shard_map.80.refs_2_.refs_1_.refs_0_), channel_id=1, source_target_pairs={{0,2},{7,5},{8,10},{15,13},{16,18},{23,21},{24,26},{31,29}} | collective-permute-start | bytes 1966088 | tf_op jit(solution)/shard_map/ppermute | solution.py:518
  120.2 9.8 %collective-permute-start.16 = (f32[64,2560]{1,0:T(8,128)S(1)}, f32[64,2560]{1,0:T(8,128)S(1)}, u32[]{:S(2)}, u32[]{:S(2)}) collective-permute-start(f32[64,2560]{1,0:T(8,128)S(1)} %get-tuple-element.68.refs_0_), channel_id=1, source_target_pairs={{0,1},{1,0},{2,3},{3,2},{4,5},{5,4},{6,7},{7,6},{8,9},{9,8},{10,11... | collective-permute-start | bytes 1966088 | tf_op jit(solution)/shard_map/ppermute | solution.py:247
  123.9 6.2 %collective-permute-start.17 = (f32[64,2560]{1,0:T(8,128)S(1)}, f32[64,2560]{1,0:T(8,128)S(1)}, u32[]{:S(2)}, u32[]{:S(2)}) collective-permute-start(f32[64,2560]{1,0:T(8,128)S(1)} %get-tuple-element.65.refs_9_.refs_1_), channel_id=1, source_target_pairs={{0,1},{1,0},{2,3},{3,2},{4,5},{5,4},{6,7},{7,6},{8,9},{9,8},{10,11... | collective-permute-start | bytes 1966088 | tf_op jit(solution)/shard_map/ppermute | solution.py:247
  126.4 8.8 %collective-permute-start.13 = (f32[64,2560]{1,0:T(8,128)S(1)}, f32[64,2560]{1,0:T(8,128)S(1)}, u32[]{:S(2)}, u32[]{:S(2)}) collective-permute-start(f32[64,2560]{1,0:T(8,128)S(1)} %get-tuple-element.67.refs_0_), channel_id=1, source_target_pairs={{0,1},{1,0},{2,3},{3,2},{4,5},{5,4},{6,7},{7,6},{8,9},{9,8},{10,11... | collective-permute-start | bytes 1966088 | tf_op jit(solution)/shard_map/ppermute | solution.py:247
  127.0 8.3 %collective-permute-start.14 = (f32[64,2560]{1,0:T(8,128)S(1)}, f32[64,2560]{1,0:T(8,128)S(1)}, u32[]{:S(2)}, u32[]{:S(2)}) collective-permute-start(f32[64,2560]{1,0:T(8,128)S(1)} %get-tuple-element.66.refs_2_.refs_1_), channel_id=1, source_target_pairs={{0,1},{1,0},{2,3},{3,2},{4,5},{5,4},{6,7},{7,6},{8,9},{9,8},{10,11... | collective-permute-start | bytes 1966088 | tf_op jit(solution)/shard_map/ppermute | solution.py:247
  130.8 13.4 %collective-permute-start.19 = (f32[64,2560]{1,0:T(8,128)S(1)}, f32[64,2560]{1,0:T(8,128)S(1)}, u32[]{:S(2)}, u32[]{:S(2)}) collective-permute-start(f32[64,2560]{1,0:T(8,128)S(1)} %shard_map.87.refs_4_), channel_id=1, source_target_pairs={{0,2},{2,4},{7,5},{5,3},{8,10},{10,12},{15,13},{13,11},{16,18},{18... | collective-permute-start | bytes 1966088 | tf_op jit(solution)/shard_map/ppermute | solution.py:537
  136.0 14.3 %collective-permute-start.18 = (f32[64,2560]{1,0:T(8,128)S(1)}, f32[64,2560]{1,0:T(8,128)S(1)}, u32[]{:S(2)}, u32[]{:S(2)}) collective-permute-start(f32[64,2560]{1,0:T(8,128)S(1)} %shard_map.89.refs_10_), channel_id=1, source_target_pairs={{0,2},{2,4},{7,5},{5,3},{8,10},{10,12},{15,13},{13,11},{16,18},{18... | collective-permute-start | bytes 1966088 | tf_op jit(solution)/shard_map/ppermute | solution.py:537
  141.1 14.3 %collective-permute-start.23 = (f32[64,2560]{1,0:T(8,128)S(1)}, f32[64,2560]{1,0:T(8,128)S(1)}, u32[]{:S(2)}, u32[]{:S(2)}) collective-permute-start(f32[64,2560]{1,0:T(8,128)S(1)} %shard_map.90.refs_10_.refs_0_), channel_id=1, source_target_pairs={{0,1},{1,0},{2,3},{3,2},{4,5},{5,4},{6,7},{7,6},{8,9},{9,8},{10,11... | collective-permute-start | bytes 1966088 | tf_op jit(solution)/shard_map/ppermute | solution.py:247
  144.8 12.5 %collective-permute-start.22 = (f32[64,2560]{1,0:T(8,128)S(1)}, f32[64,2560]{1,0:T(8,128)S(1)}, u32[]{:S(2)}, u32[]{:S(2)}) collective-permute-start(f32[64,2560]{1,0:T(8,128)S(1)} %shard_map.92._), channel_id=1, source_target_pairs={{0,2},{2,4},{4,6},{7,5},{5,3},{3,1},{8,10},{10,12},{12,14},{15,13}... | collective-permute-start | bytes 1966088 | tf_op jit(solution)/shard_map/ppermute | solution.py:537
  148.4 14.0 %collective-permute-start.21 = (f32[64,2560]{1,0:T(8,128)S(1)}, f32[64,2560]{1,0:T(8,128)S(1)}, u32[]{:S(2)}, u32[]{:S(2)}) collective-permute-start(f32[64,2560]{1,0:T(8,128)S(1)} %shard_map.91._.refs_0_), channel_id=1, source_target_pairs={{0,1},{1,0},{2,3},{3,2},{4,5},{5,4},{6,7},{7,6},{8,9},{9,8},{10,11... | collective-permute-start | bytes 1966088 | tf_op jit(solution)/shard_map/ppermute | solution.py:247
  150.9 13.4 %collective-permute-start.20 = (f32[64,2560]{1,0:T(8,128)S(1)}, f32[64,2560]{1,0:T(8,128)S(1)}, u32[]{:S(2)}, u32[]{:S(2)}) collective-permute-start(f32[64,2560]{1,0:T(8,128)S(1)} %shard_map.93.refs_2_), channel_id=1, source_target_pairs={{0,2},{2,4},{4,6},{7,5},{5,3},{3,1},{8,10},{10,12},{12,14},{15,13}... | collective-permute-start | bytes 1966088 | tf_op jit(solution)/shard_map/ppermute | solution.py:537
  158.0 17.5 %collective-permute-start.27 = (f32[64,2560]{1,0:T(8,128)S(1)}, f32[64,2560]{1,0:T(8,128)S(1)}, u32[]{:S(2)}, u32[]{:S(2)}) collective-permute-start(f32[64,2560]{1,0:T(8,128)S(1)} %shard_map.95.refs_2_), channel_id=1, source_target_pairs={{0,2},{2,4},{4,6},{7,5},{5,3},{3,1},{8,10},{10,12},{12,14},{15,13}... | collective-permute-start | bytes 1966088 | tf_op jit(solution)/shard_map/ppermute | solution.py:537
  165.0 13.4 %collective-permute-start.26 = (f32[64,2560]{1,0:T(8,128)S(1)}, f32[64,2560]{1,0:T(8,128)S(1)}, u32[]{:S(2)}, u32[]{:S(2)}) collective-permute-start(f32[64,2560]{1,0:T(8,128)S(1)} %shard_map.97.refs_4_), channel_id=1, source_target_pairs={{0,2},{2,4},{4,6},{7,5},{5,3},{3,1},{8,10},{10,12},{12,14},{15,13}... | collective-permute-start | bytes 1966088 | tf_op jit(solution)/shard_map/ppermute | solution.py:537
  174.9 4.8 %collective-permute-start.25 = (f32[64,2560]{1,0:T(8,128)S(1)}, f32[64,2560]{1,0:T(8,128)S(1)}, u32[]{:S(2)}, u32[]{:S(2)}) collective-permute-start(f32[64,2560]{1,0:T(8,128)S(1)} %shard_map.100._.refs_4_), channel_id=1, source_target_pairs={{0,1},{1,0},{2,3},{3,2},{4,5},{5,4},{6,7},{7,6},{8,9},{9,8},{10,11... | collective-permute-start | bytes 1966088 | tf_op jit(solution)/shard_map/ppermute | solution.py:247
  174.9 4.8 %collective-permute-start.24 = (f32[64,2560]{1,0:T(8,128)S(1)}, f32[64,2560]{1,0:T(8,128)S(1)}, u32[]{:S(2)}, u32[]{:S(2)}) collective-permute-start(f32[64,2560]{1,0:T(8,128)S(1)} %shard_map.99._.refs_1_), channel_id=1, source_target_pairs={{0,1},{1,0},{2,3},{3,2},{4,5},{5,4},{6,7},{7,6},{8,9},{9,8},{10,11... | collective-permute-start | bytes 1966088 | tf_op jit(solution)/shard_map/ppermute | solution.py:247
  176.0 5.8 %collective-permute-start.31 = (f32[64,2560]{1,0:T(8,128)S(1)}, f32[64,2560]{1,0:T(8,128)S(1)}, u32[]{:S(2)}, u32[]{:S(2)}) collective-permute-start(f32[64,2560]{1,0:T(8,128)S(1)} %shard_map.101._), channel_id=1, source_target_pairs={{2,4},{4,6},{5,3},{3,1},{10,12},{12,14},{13,11},{11,9},{18,20},{20... | collective-permute-start | bytes 1966088 | tf_op jit(solution)/shard_map/ppermute | solution.py:537
  179.0 4.1 %collective-permute-start.30 = (f32[64,2560]{1,0:T(8,128)S(1)}, f32[64,2560]{1,0:T(8,128)S(1)}, u32[]{:S(2)}, u32[]{:S(2)}) collective-permute-start(f32[64,2560]{1,0:T(8,128)S(1)} %shard_map.102.refs_2_), channel_id=1, source_target_pairs={{2,4},{4,6},{5,3},{3,1},{10,12},{12,14},{13,11},{11,9},{18,20},{20... | collective-permute-start | bytes 1966088 | tf_op jit(solution)/shard_map/ppermute | solution.py:537
  181.2 3.1 %collective-permute-start.29 = (f32[64,2560]{1,0:T(8,128)S(1)}, f32[64,2560]{1,0:T(8,128)S(1)}, u32[]{:S(2)}, u32[]{:S(2)}) collective-permute-start(f32[64,2560]{1,0:T(8,128)S(1)} %shard_map.105._.refs_4_), channel_id=1, source_target_pairs={{0,1},{1,0},{2,3},{3,2},{4,5},{5,4},{6,7},{7,6},{8,9},{9,8},{10,11... | collective-permute-start | bytes 1966088 | tf_op jit(solution)/shard_map/ppermute | solution.py:247
  181.3 3.1 %collective-permute-start.28 = (f32[64,2560]{1,0:T(8,128)S(1)}, f32[64,2560]{1,0:T(8,128)S(1)}, u32[]{:S(2)}, u32[]{:S(2)}) collective-permute-start(f32[64,2560]{1,0:T(8,128)S(1)} %shard_map.104._.refs_4_.refs_1_), channel_id=1, source_target_pairs={{0,1},{1,0},{2,3},{3,2},{4,5},{5,4},{6,7},{7,6},{8,9},{9,8},{10,11... | collective-permute-start | bytes 1966088 | tf_op jit(solution)/shard_map/ppermute | solution.py:247
  182.4 15.3 %collective-permute-start.33 = (f32[64,2560]{1,0:T(8,128)S(1)}, f32[64,2560]{1,0:T(8,128)S(1)}, u32[]{:S(2)}, u32[]{:S(2)}) collective-permute-start(f32[64,2560]{1,0:T(8,128)S(1)} %shard_map.106._), channel_id=1, source_target_pairs={{4,6},{3,1},{12,14},{11,9},{20,22},{19,17},{28,30},{27,25}} | collective-permute-start | bytes 1966088 | tf_op jit(solution)/shard_map/ppermute | solution.py:537
  183.6 18.6 %collective-permute-start.35 = (f32[64,2560]{1,0:T(8,128)S(1)}, f32[64,2560]{1,0:T(8,128)S(1)}, u32[]{:S(2)}, u32[]{:S(2)}) collective-permute-start(f32[64,2560]{1,0:T(8,128)S(1)} %shard_map.107.refs_2_), channel_id=1, source_target_pairs={{4,6},{3,1},{12,14},{11,9},{20,22},{19,17},{28,30},{27,25}} | collective-permute-start | bytes 1966088 | tf_op jit(solution)/shard_map/ppermute | solution.py:537
  184.4 24.8 %slice-start = ((s8[4718592]{0:T(1024)(128)(4,1)}), s8[4194304]{0:T(1024)(128)(4,1)S(1)}, s32[]{:S(2)}) async-start(s8[4718592]{0:T(1024)(128)(4,1)} %bitcast.3), calls=%async_computation.2 | async-start | bytes 8388608
  185.0 24.2 %slice-start.1 = ((s8[4718592]{0:T(1024)(128)(4,1)}), s8[524288]{0:T(1024)(128)(4,1)S(1)}, s32[]{:S(2)}) async-start(s8[4718592]{0:T(1024)(128)(4,1)} %bitcast.3), calls=%async_computation.3 | async-start | bytes 1048576
  185.0 24.1 %collective-permute-start.32 = (f32[64,2560]{1,0:T(8,128)S(1)}, f32[64,2560]{1,0:T(8,128)S(1)}, u32[]{:S(2)}, u32[]{:S(2)}) collective-permute-start(f32[64,2560]{1,0:T(8,128)S(1)} %shard_map.109._.refs_7_.refs_1_), channel_id=1, source_target_pairs={{0,1},{1,0},{2,3},{3,2},{4,5},{5,4},{6,7},{7,6},{8,9},{9,8},{10,11... | collective-permute-start | bytes 1966088 | tf_op jit(solution)/shard_map/ppermute | solution.py:247
  198.3 10.9 %collective-permute-start.34 = (f32[64,2560]{1,0:T(8,128)S(1)}, f32[64,2560]{1,0:T(8,128)S(1)}, u32[]{:S(2)}, u32[]{:S(2)}) collective-permute-start(f32[64,2560]{1,0:T(8,128)S(1)} %shard_map.111._.refs_10_.refs_1_), channel_id=1, source_target_pairs={{0,1},{1,0},{2,3},{3,2},{4,5},{5,4},{6,7},{7,6},{8,9},{9,8},{10,11... | collective-permute-start | bytes 1966088 | tf_op jit(solution)/shard_map/ppermute | solution.py:247
  202.1 13.5 %collective-permute-start.36 = (f32[64,2560]{1,0:T(8,128)S(1)}, f32[64,2560]{1,0:T(8,128)S(1)}, u32[]{:S(2)}, u32[]{:S(2)}) collective-permute-start(f32[64,2560]{1,0:T(8,128)S(1)} %shard_map.110._.refs_4_), channel_id=1, source_target_pairs={{0,1},{1,0},{2,3},{3,2},{4,5},{5,4},{6,7},{7,6},{8,9},{9,8},{10,11... | collective-permute-start | bytes 1966088 | tf_op jit(solution)/shard_map/ppermute | solution.py:247
  202.8 15.0 %collective-permute-start.37 = (f32[64,2560]{1,0:T(8,128)S(1)}, f32[64,2560]{1,0:T(8,128)S(1)}, u32[]{:S(2)}, u32[]{:S(2)}) collective-permute-start(f32[64,2560]{1,0:T(8,128)S(1)} %shard_map.112.refs_12_.refs_1_), channel_id=1, source_target_pairs={{0,1},{1,0},{2,3},{3,2},{4,5},{5,4},{6,7},{7,6},{8,9},{9,8},{10,11... | collective-permute-start | bytes 1966088 | tf_op jit(solution)/shard_map/ppermute | solution.py:247
  (1 other events, 0.8 us)

commit v4 on v3

--- a/solution.py
+++ b/solution.py
@@ -162,26 +162,26 @@
     )(grid, above, below, cell, edge_codes, token)
 
 
-def numer_part(counts, loadings, me, genes_n, half, send_ids, token):
+def numer_part(counts, loadings, gram, me, genes_n, part, send_ids, token):
     rows, genes = counts.shape
     first_call = loadings.dtype == F32
     width_all = loadings.shape[0] if first_call else loadings.shape[1]
     width = width_all // genes_n
-    half_rows = rows // 2
+    start, some_rows = part
     piece = STEP // 2
-    pieces = half_rows // piece
+    pieces = some_rows // piece
     keep_ids = [k for k in range(genes_n) if k not in send_ids]
-    total_cols = half_rows + first_call * width_all
+    total_cols = some_rows + (not first_call) * width_all
 
     def body(me_ref, counts_ref, *refs):
         firsts = [pl.multiple_of((k ^ me_ref[0]) * width, width) for k in range(genes_n)]
         if first_call:
-            load_ref, _, send_ref, keep_ref, load_t, held, sems, load_bf, load_f, turned = refs
+            load_ref, _, send_ref, keep_ref, load_t, gram_ref, held, sems, load_bf, load_f = refs
         else:
-            load_t, _, send_ref, keep_ref, held, sems = refs
+            load_t, gram_ref, _, send_ref, keep_ref, held, sems = refs
         copies = [
             pltpu.make_async_copy(
-                counts_ref.at[pl.ds(half * half_rows + i * piece, piece), :],
+                counts_ref.at[pl.ds(start + i * piece, piece), :],
                 held.at[pl.ds(i * piece, piece), :],
                 sems.at[i],
             )
@@ -212,11 +212,11 @@
             load_t[...] = load_bf[...].T
             local = dot(load_bf[...], load_t[...], PLAIN)
             for k, first in enumerate(firsts):
-                turned[pl.ds(first, width), :] = local[k * width : (k + 1) * width]
-            put(turned[...].T, slice(half_rows, total_cols))
+                gram_ref[pl.ds(first, width), :] = local[k * width : (k + 1) * width]
         else:
             for copy in copies:
                 copy.start()
+            put(gram_ref[...].T, slice(some_rows, total_cols))
         for i in range(0, pieces, 2):
             copies[i].wait()
             copies[i + 1].wait()
@@ -224,23 +224,25 @@
             put(dot(held[at, :], load_t[...], PLAIN).T, at)
 
     outs = (shape(genes_n // 2, width, total_cols),) * 2
-    scratch = [pltpu.VMEM((half_rows, genes), BF16), pltpu.SemaphoreType.DMA((pieces + genes_n,))]
+    scratch = [pltpu.VMEM((some_rows, genes), BF16), pltpu.SemaphoreType.DMA((pieces + genes_n,))]
     if first_call:
-        outs += (shape(genes, width_all, dtype=BF16),)
+        outs += (shape(genes, width_all, dtype=BF16), shape(width_all, width_all))
         scratch += [
             pltpu.VMEM((width_all, genes), BF16),
             pltpu.VMEM((width_all, genes), F32),
-            pltpu.VMEM((width_all, width_all), F32),
         ]
+    loads = [loadings] if first_call else [loadings, gram]
     return kernel_call(
         body,
         outs,
         7,
-        limit=36,
-        in_specs=[SMEM_SPEC, ANY_SPEC, ANY_SPEC if first_call else VMEM_SPEC, ANY_SPEC],
+        limit=40,
+        in_specs=[SMEM_SPEC, ANY_SPEC]
+        + [ANY_SPEC if first_call else VMEM_SPEC] * len(loads)
+        + [ANY_SPEC],
         out_specs=(VMEM_SPEC,) * len(outs),
         scratch_shapes=scratch,
-    )(me, counts, loadings, token)
+    )(me, counts, *loads, token)
 
 
 def swap(block, axis, bit):
@@ -271,7 +273,7 @@
 def plain_terms(first, second, factors, token):
     rows, width_all = factors.shape
     width = first[0].shape[1]
-    half_rows = rows // 2
+    third = rows // 3
     n = len(first)
 
     def body(*refs):
@@ -285,25 +287,27 @@
 
         @pl.when(pl.program_id(0) == 0)
         def _():
-            gram[...] = total(refs[n : 2 * n], slice(half_rows, half_rows + width_all))
-            numer_ref[...] = total(refs[:n], slice(0, half_rows))
-
-        @pl.when(pl.program_id(0) == 1)
-        def _():
-            numer_ref[...] = total(refs[n : 2 * n], slice(0, half_rows))
+            gram[...] = total(refs[:n], slice(third, third + width_all))
+            numer_ref[...] = total(refs[:n], slice(0, third))
+
+        for i in (1, 2):
+
+            @pl.when(pl.program_id(0) == i)
+            def _():
+                numer_ref[...] = total(refs[n : 2 * n], slice((i - 1) * third, i * third))
 
         plain_ref[...] = dot(fac_ref[...], gram[...], MINOR, lax.Precision.HIGHEST).T
 
-    out_spec = pl.BlockSpec((width, half_rows), lambda i: (0, i))
+    out_spec = pl.BlockSpec((width, third), lambda i: (0, i))
     arrays = list(first) + list(second)
     return kernel_call(
         body,
         (pltpu.HBM((width, rows), F32),) * 2,
         4,
         limit=24,
-        grid=(2,),
+        grid=(3,),
         in_specs=[pl.BlockSpec((1,) + x.shape[1:], lambda i: (0, 0, 0)) for x in arrays]
-        + [pl.BlockSpec((half_rows, width_all), lambda i: (i, 0)), ANY_SPEC],
+        + [pl.BlockSpec((third, width_all), lambda i: (i, 0)), ANY_SPEC],
         out_specs=(out_spec, out_spec),
         scratch_shapes=[pltpu.VMEM((width, width_all), F32)],
     )(*arrays, factors, token)
@@ -409,7 +413,7 @@
 def first_cross(block, counts, width_all, token):
     width, rows = block.shape
     genes = counts.shape[1]
-    cols = genes // HALVES
+    cols, extra = genes // HALVES, width_all // HALVES
     step = STEP
     steps = rows // step
 
@@ -425,8 +429,8 @@
             copy.start()
         put_rounded(fac, [block_ref], width)
         near = near_products(fac[...], fac[...], width_all)
-        for out in outs:
-            out[:, cols:] = near
+        for h, out in enumerate(outs):
+            out[:, cols:] = near[:, h * extra : (h + 1) * extra]
         for i, copy in enumerate(copies):
             copy.wait()
             at = slice(i * step, (i + 1) * step)
@@ -436,7 +440,7 @@
 
     return kernel_call(
         body,
-        (shape(width, cols + width_all),) * HALVES + (pltpu.VMEM((step, genes), BF16),) * steps,
+        (shape(width, cols + extra),) * HALVES + (pltpu.VMEM((step, genes), BF16),) * steps,
         0.02,
         limit=8,
         in_specs=[ANY_SPEC, VMEM_SPEC, ANY_SPEC],
@@ -447,7 +451,7 @@
 
 def cross_part(blocks, n_old, held, half, width_all, tokens):
     width, rows = blocks[0].shape
-    cols = held[0].shape[1] // HALVES
+    cols, extra = held[0].shape[1] // HALVES, width_all // HALVES
     steps = 3
     step = cols // steps
     n = len(blocks) - n_old
@@ -470,11 +474,12 @@
                 more = dot(new[:, here], piece[:, at], PLAIN)
                 part = more if part is None else part + more
             put(part, slice(i * step, (i + 1) * step))
-        put(near_products(new, fac[...], width_all), slice(cols, cols + width_all))
-
-    return kernel_call(
-        body,
-        (shape(width, cols + width_all),) * n,
+        near = near_products(new, fac[...], width_all)
+        put(near[:, half * extra : (half + 1) * extra], slice(cols, cols + extra))
+
+    return kernel_call(
+        body,
+        (shape(width, cols + extra),) * n,
         0.02,
         limit=8,
         in_specs=[VMEM_SPEC] * (len(held) + len(blocks)) + [ANY_SPEC] * len(tokens),
@@ -572,7 +577,8 @@
     width = width_all // len(ids)
     steps = 6
     step = genes // steps
-    arrays = [x for terms in sums for x in terms]
+    extra = width_all // HALVES
+    arrays = [x for pair in sums for terms in pair for x in terms]
 
     def body(me_ref, load_ref, *refs):
         out_ref, tiny, load, gram = refs[-4:]
@@ -580,10 +586,13 @@
 
         @pl.when(pl.program_id(0) == 0)
         def _():
-            behind = slice(cols, cols + width_all)
-            for j in range(len(sums)):
-                own, end, other = refs[3 * j : 3 * j + 3]
-                gram[j * width : (j + 1) * width, :] = own[:, behind] + (end[:, behind] + other[:, behind])
+            behind = slice(cols, cols + extra)
+            for i in range(len(sums) * HALVES):
+                own, end, other = refs[3 * i : 3 * i + 3]
+                j, h = i // HALVES, i % HALVES
+                gram[j * width : (j + 1) * width, h * extra : (h + 1) * extra] = own[:, behind] + (
+                    end[:, behind] + other[:, behind]
+                )
             low = gram[...]
             row = lax.broadcasted_iota(jnp.int32, low.shape, 0) // width
             col = lax.broadcasted_iota(jnp.int32, low.shape, 1) // width
@@ -676,13 +685,17 @@
 
     orders = (bits, bits[::-1])
     token, load = payload, pltpu.with_memory_space_constraint(loadings, pltpu.HBM)
-    parts, keeps = [None, None], [None, None]
+    parts, keeps, gram = [None, None], [None, None], None
+    third = rows // 3
+    numer_parts = ((0, third), (third, rows - third))
     for half in (1, 0):
         bit = orders[half][0]
         send_ids = [k for k in range(genes_n) if k & bit]
         keeps[half] = [k for k in range(genes_n) if not k & bit]
-        send, keep, *made = numer_part(counts, load, me1, genes_n, half, send_ids, token)
-        load = made[0] if made else load
+        send, keep, *made = numer_part(
+            counts, load, gram, me1, genes_n, numer_parts[half], send_ids, token
+        )
+        load, gram = made or (load, gram)
         token = keep
         parts[half] = [keep, swap(send, "gene", bit)]
 
@@ -804,7 +817,7 @@
     rest = [c for c in range(chunks) if c not in ends[0]]
     for c in rest:
         both(end, c)
-    sums = [(own[0][c],) + ends[0][c] for c in range(chunks)]
+    sums = [[(own[h][c],) + ends[h][c] for h in range(HALVES)] for c in range(chunks)]
     loadings_new = None
     share, token = shares(loadings, sums, ids, counts.shape[1] // HALVES, me1, token)
     for c in range(chunks - 1):

time: 219 us -> 218 us (level)
  waiting for transfers between devices: 46.3 us -> 41.4 us
  starting transfers between devices: 76.6 us -> 79.1 us
    ppermute x24, starting transfers between devices: 33.2 us -> 35.6 us  [swap(): lax.ppermute(block, axis, [(i, i ^ bit) for i in range(lax.axis_size(axis...]
  transfers between devices with their start and end apart: 40 -> 40, of which waited for: 13 -> 14; matrix products, arithmetic and copies ran while one was open for 0% -> 0% of each run, Pallas kernels for 36% -> 33%
where the time goes in v4:
time: 218 us; the launch traced here: 217 us
  Pallas kernels  90.9 us (42%)
  starting transfers between devices  79.1 us (36%)
  waiting for transfers between devices  41.4 us (19%)
  local copies, waits for them, and re-layouts  3.62 us (2%)
    ppermute x24, starting transfers between devices, swap(): lax.ppermute(block, axis, [(i, i ^ bit) for i in range(lax.axis_size(axis...  35.6 us
    ppermute x24, waiting for transfers between devices, swap(): lax.ppermute(block, axis, [(i, i ^ bit) for i in range(lax.axis_size(axis...  31.8 us
    ppermute x10, starting transfers between devices, line_slot(): return (lax.ppermute(send, 'bin', hops), send)  26 us
    pallas_call x2, Pallas kernels, numer_part(): kernel_call(body, outs, 7, limit=40, in_specs=[SMEM_SPEC, ANY_SPEC] + [AN...  22.6 us
    pallas_call x4, Pallas kernels, cross_part(): kernel_call(body, (shape(width, cols + extra),) * n, 0.02, limit=8, in_sp...  11.2 us
    pallas_call x1, Pallas kernels, first_cross(): kernel_call(body, (shape(width, cols + extra),) * HALVES + (pltpu.VMEM((s...  10.1 us
    all_to_all x1, starting transfers between devices, on_device(): lax.all_to_all(payload, 'bin', split_axis=0, concat_axis=0, tiled=True)  6.33 us
    pallas_call x1, Pallas kernels, plain_terms(): kernel_call(body, (pltpu.HBM((width, rows), F32),) * 2, 4, limit=24, grid...  6.22 us
  transfers between devices with their start and end apart: 40, of which 14 were waited for; matrix products, arithmetic and copies ran while one was open for 0% of the time, Pallas kernels for 33%

profile of v4, /device:TPU:0, one launch (start us, length us, event | category | flops | bytes accessed | tf_op | source)
XLA Modules:
  0.0 217.1 jit_solution(6607172141409829294)
XLA Ops:
  1.3 1.9 copy-done
  3.2 3.4 %shard_map.68.refs_1_.pay_ref = f32[8,72,384]{2,1,0:T(8,128)} custom-call(s32[1]{0:T(128)} %bitcast.me_ref, f32[3072,256]{1,0:T(8,128)S(1)} %copy-done, f32[8,1,384]{2,1,0:T(1,128)S(1)} %bitcast.5), custom_call_target="tpu_custom_call" | custom-call | bytes 11070000 | tf_op jit(solution)/shard_map/pallas_call | solution.py:64
  6.7 6.3 %all-to-all-start = ((f32[8,72,384]{2,1,0:T(8,128)}), f32[8,72,384]{2,1,0:T(8,128)S(1)}, u32[]{:S(2)}, u32[]{:S(2)}) async-start(f32[8,72,384]{2,1,0:T(8,128)} %shard_map.68.refs_1_.pay_ref), calls=%async_computation | async-start | bytes 1769472 | tf_op jit(solution)/shard_map/all_to_all | solution.py:683
  13.0 14.9 %shard_map.69 = (f32[2,64,2048]{2,1,0:T(8,128)}, f32[2,64,2048]{2,1,0:T(8,128)S(1)}, bf16[4608,256]{1,0:T(8,128)(2,1)S(1)}, f32[256,256]{1,0:T(8,128)S(1)}) custom-call(s32[1]{0:T(128)} %bitcast.me_ref, bf16[3072,4608]{1,0:T(8,128)(2,1)} %counts_ref.5, f32[256,4608]{1,0:T(8,128)} %load_ref.1, f32[8,72,384]{2,1,0:T(8,128)} %shard_map.68.refs_1_.pay_ref), custom_call_target="tpu_custom_call" | custom-call | bytes 25830000 | tf_op jit(solution)/shard_map/pallas_call | solution.py:235
  27.9 1.6 collective-permute-start.3
  29.5 7.7 %shard_map.70 = (f32[2,64,1280]{2,1,0:T(8,128)S(1)}, f32[2,64,1280]{2,1,0:T(8,128)S(1)}) custom-call(s32[1]{0:T(128)} %bitcast.me_ref, bf16[3072,4608]{1,0:T(8,128)(2,1)} %counts_ref.5, bf16[4608,256]{1,0:T(8,128)(2,1)S(1)} %get-tuple-element.45.refs_0_, f32[256,256]{1,0:T(8,128)S(1)} %get-tuple-element.46.refs_1_, ...), custom_call_target="tpu_custom_call" | custom-call | bytes 25830000 | tf_op jit(solution)/shard_map/pallas_call | solution.py:235
  37.3 1.6 collective-permute-start.2
  38.8 2.7 %shard_map.71 = (f32[12,72,256]{2,1,0:T(8,128)S(1)}, f32[72,256]{1,0:T(8,128)S(1)}, f32[72,256]{1,0:T(8,128)S(1)}, s32[1,3072]{1,0:T(1,128)S(1)}) custom-call(s32[1]{0:T(128)} %bitcast.2.me_ref, f32[8,72,384]{2,1,0:T(8,128)S(1)} %all-to-all-done.got_ref, s32[12,256]{1,0:T(8,128)S(1)} %copy-done.3, f32[2,64,1280]{2,1,0:T(8,128)S(1)} %get-tuple-element.48._.refs_0_), custom_call_target="tpu_custom_call" | custom-call | bytes 11070000 | tf_op jit(solution)/shard_map/pallas_call | solution.py:106
  41.5 1.9 collective-permute-start
  43.4 1.5 collective-permute-start.1
  44.9 9.0 %collective-permute-done.3.refs_1_.refs_4_ = f32[2,64,2048]{2,1,0:T(8,128)} collective-permute-done((f32[2,64,2048]{2,1,0:T(8,128)}, f32[2,64,2048]{2,1,0:T(8,128)}, u32[]{:S(2)}, u32[]{:S(2)}) %collective-permute-start.3) | collective-permute-done | bytes 1048608 | tf_op jit(solution)/shard_map/ppermute | solution.py:249
  56.3 4.2 %shard_map.74.refs_7_ = f32[8,72,384]{2,1,0:T(8,128)} custom-call(f32[12,72,256]{2,1,0:T(8,128)S(1)} %get-tuple-element.49.refs_2_.grid_ref, f32[72,256]{1,0:T(8,128)S(1)} %collective-permute-done.above_ref, f32[72,256]{1,0:T(8,128)S(1)} %collective-permute-done.1.below_ref, s32[1,3072]{1,0:T(1,128)S(1)} %get-tuple-element.52.cell_ref, ...), custom_call_target="tpu_custom_call" | custom-call | bytes 14760000 | tf_op jit(solution)/shard_map/pallas_call | solution.py:155
  60.4 4.7 %all-to-all-start.1 = ((f32[8,72,384]{2,1,0:T(8,128)}), f32[8,72,384]{2,1,0:T(8,128)S(1)}, u32[]{:S(2)}, u32[]{:S(2)}) async-start(f32[8,72,384]{2,1,0:T(8,128)} %shard_map.74.refs_7_), calls=%async_computation.1 | async-start | bytes 1769472 | tf_op jit(solution)/shard_map/all_to_all | solution.py:721
  65.2 1.5 collective-permute-start.5
  66.7 1.5 collective-permute-start.4
  68.2 8.3 %collective-permute-done.4.refs_2_ = f32[1,64,1280]{2,1,0:T(8,128)S(1)} collective-permute-done((f32[1,64,1280]{2,1,0:T(8,128)S(1)}, f32[1,64,1280]{2,1,0:T(8,128)S(1)}, u32[]{:S(2)}, u32[]{:S(2)}) %collective-permute-start.4) | collective-permute-done | bytes 327712 | tf_op jit(solution)/shard_map/ppermute | solution.py:249
  76.5 3.0 %collective-permute-done.5.refs_5_ = f32[1,64,2048]{2,1,0:T(8,128)S(1)} collective-permute-done((f32[1,64,2048]{2,1,0:T(8,128)S(1)}, f32[1,64,2048]{2,1,0:T(8,128)S(1)}, u32[]{:S(2)}, u32[]{:S(2)}) %collective-permute-start.5) | collective-permute-done | bytes 524320 | tf_op jit(solution)/shard_map/ppermute | solution.py:249
  80.3 6.2 %shard_map.75 = (f32[64,3072]{1,0:T(8,128)}, f32[64,3072]{1,0:T(8,128)}) custom-call(f32[2,64,1280]{2,1,0:T(8,128)} %copy-done.2, f32[2,64,1280]{2,1,0:T(8,128)} %collective-permute-done.2.refs_1_, f32[1,64,1280]{2,1,0:T(8,128)} %copy-done.6, f32[2,64,2048]{2,1,0:T(8,128)} %copy-done.1, f32[2,64,2048]{2,1,0:T(8,128)} %collective-permute-done.3.refs_1_.refs_4_, ...), custom_call_target="tpu_custom_call" | custom-call | bytes 14760000 | tf_op jit(solution)/shard_map/pallas_call | solution.py:303
  86.5 1.7 all-to-all-done.1.back_ref
  89.2 2.8 %shard_map.76.block_ref._.refs_6_.refs_0_ = f32[64,3072]{1,0:T(8,128)S(1)} custom-call(f32[8,72,384]{2,1,0:T(8,128)} %shard_map.68.refs_1_.pay_ref, f32[8,72,384]{2,1,0:T(8,128)} %copy-done.4, f32[64,3072]{1,0:T(8,128)} %get-tuple-element.55.numer_ref, f32[64,3072]{1,0:T(8,128)} %get-tuple-element.56.plain_ref), custom_call_target="tpu_custom_call" | custom-call | bytes 73800 | tf_op jit(solution)/shard_map/pallas_call | solution.py:330
  92.0 1.6 collective-permute-start.6
  93.6 1.5 collective-permute-start.7
  95.1 10.1 %shard_map.77 = (f32[64,2432]{1,0:T(8,128)S(1)}, f32[64,2432]{1,0:T(8,128)S(1)}, bf16[512,4608]{1,0:T(8,128)(2,1)S(1)}, bf16[512,4608]{1,0:T(8,128)(2,1)S(1)}, b...) custom-call(bf16[3072,4608]{1,0:T(8,128)(2,1)} %counts_ref.5, ...), custom_call_target="tpu_custom_call" | custom-call | bytes 73800 | tf_op jit(solution)/shard_map/pallas_call | solution.py:441
  105.8 5.3 %collective-permute-done.6.refs_0_.refs_1_.refs_7_ = f32[64,3072]{1,0:T(8,128)S(1)} collective-permute-done((f32[64,3072]{1,0:T(8,128)S(1)}, f32[64,3072]{1,0:T(8,128)S(1)}, u32[]{:S(2)}, u32[]{:S(2)}) %collective-permute-start.6) | collective-permute-done | bytes 786464 | tf_op jit(solution)/shard_map/ppermute | solution.py:249
  112.6 1.6 collective-permute-start.12
  114.7 1.5 collective-permute-start.9
  116.3 1.5 collective-permute-start.15
  117.8 2.5 %shard_map.82 = (f32[64,2432]{1,0:T(8,128)S(1)}, f32[64,2432]{1,0:T(8,128)S(1)}) custom-call(bf16[512,4608]{1,0:T(8,128)(2,1)S(1)} %get-tuple-element.60.refs_0_, bf16[512,4608]{1,0:T(8,128)(2,1)S(1)} %get-tuple-element.61.refs_1_, bf16[512,4608]{1,0:T(8,128)(2,1)S(1)} %get-tuple-element.62.refs_2_, bf16[512,4608]{1,0:T(8,128)(2,1)S(1)} %get-tuple-element.63.refs_3_, ...), custom_call_target="tpu_custom_call" | custom-call | bytes 73800 | tf_op jit(solution)/shard_map/pallas_call | solution.py:480
  120.4 2.4 %collective-permute-done.8.refs_0_ = f32[64,1536]{1,0:T(8,128)S(1)} collective-permute-done((f32[64,1536]{1,0:T(8,128)S(1)}, f32[64,1536]{1,0:T(8,128)S(1)}, u32[]{:S(2)}, u32[]{:S(2)}) %collective-permute-start.8) | collective-permute-done | bytes 393248 | tf_op jit(solution)/shard_map/ppermute | solution.py:249
  122.8 2.5 %shard_map.83 = (f32[64,2432]{1,0:T(8,128)S(1)}, f32[64,2432]{1,0:T(8,128)S(1)}) custom-call(bf16[512,4608]{1,0:T(8,128)(2,1)S(1)} %get-tuple-element.60.refs_0_, bf16[512,4608]{1,0:T(8,128)(2,1)S(1)} %get-tuple-element.61.refs_1_, bf16[512,4608]{1,0:T(8,128)(2,1)S(1)} %get-tuple-element.62.refs_2_, bf16[512,4608]{1,0:T(8,128)(2,1)S(1)} %get-tuple-element.63.refs_3_, ...), custom_call_target="tpu_custom_call" | custom-call | bytes 73800 | tf_op jit(solution)/shard_map/pallas_call | solution.py:480
  126.2 2.3 %collective-permute-done.15.refs_0_.come_ref = f32[64,2432]{1,0:T(8,128)S(1)} collective-permute-done((f32[64,2432]{1,0:T(8,128)S(1)}, f32[64,2432]{1,0:T(8,128)S(1)}, u32[]{:S(2)}, u32[]{:S(2)}) %collective-permute-start.15) | collective-permute-done | bytes 622624 | tf_op jit(solution)/shard_map/ppermute | solution.py:523
  129.3 4.5 %collective-permute-start.19 = (f32[64,2432]{1,0:T(8,128)S(1)}, f32[64,2432]{1,0:T(8,128)S(1)}, u32[]{:S(2)}, u32[]{:S(2)}) collective-permute-start(f32[64,2432]{1,0:T(8,128)S(1)} %shard_map.87.refs_4_), channel_id=1, source_target_pairs={{0,2},{2,4},{7,5},{5,3},{8,10},{10,12},{15,13},{13,11},{16,18},{18... | collective-permute-start | bytes 1867784 | tf_op jit(solution)/shard_map/ppermute | solution.py:542
  134.5 1.9 collective-permute-start.18
  136.5 3.1 %shard_map.90.refs_10_.refs_0_ = f32[64,2432]{1,0:T(8,128)S(1)} custom-call(bf16[512,4608]{1,0:T(8,128)(2,1)S(1)} %get-tuple-element.60.refs_0_, bf16[512,4608]{1,0:T(8,128)(2,1)S(1)} %get-tuple-element.61.refs_1_, bf16[512,4608]{1,0:T(8,128)(2,1)S(1)} %get-tuple-element.62.refs_2_, bf16[512,4608]{1,0:T(8,128)(2,1)S(1)} %get-tuple-element.63.refs_3_, ...), custom_call_target="tpu_custom_call" | custom-call | bytes 73800 | tf_op jit(solution)/shard_map/pallas_call | solution.py:480
  139.6 3.1 %shard_map.91._.refs_0_ = f32[64,2432]{1,0:T(8,128)S(1)} custom-call(bf16[512,4608]{1,0:T(8,128)(2,1)S(1)} %get-tuple-element.60.refs_0_, bf16[512,4608]{1,0:T(8,128)(2,1)S(1)} %get-tuple-element.61.refs_1_, bf16[512,4608]{1,0:T(8,128)(2,1)S(1)} %get-tuple-element.62.refs_2_, bf16[512,4608]{1,0:T(8,128)(2,1)S(1)} %get-tuple-element.63.refs_3_, ...), custom_call_target="tpu_custom_call" | custom-call | bytes 73800 | tf_op jit(solution)/shard_map/pallas_call | solution.py:480
  143.3 3.2 %collective-permute-start.22 = (f32[64,2432]{1,0:T(8,128)S(1)}, f32[64,2432]{1,0:T(8,128)S(1)}, u32[]{:S(2)}, u32[]{:S(2)}) collective-permute-start(f32[64,2432]{1,0:T(8,128)S(1)} %shard_map.92._), channel_id=1, source_target_pairs={{0,2},{2,4},{4,6},{7,5},{5,3},{3,1},{8,10},{10,12},{12,14},{15,13}... | collective-permute-start | bytes 1867784 | tf_op jit(solution)/shard_map/ppermute | solution.py:542
  146.6 1.5 collective-permute-done.18.come_ref.refs_1_.refs_0_
  148.7 4.5 %collective-permute-start.20 = (f32[64,2432]{1,0:T(8,128)S(1)}, f32[64,2432]{1,0:T(8,128)S(1)}, u32[]{:S(2)}, u32[]{:S(2)}) collective-permute-start(f32[64,2432]{1,0:T(8,128)S(1)} %shard_map.93.refs_2_), channel_id=1, source_target_pairs={{0,2},{2,4},{4,6},{7,5},{5,3},{3,1},{8,10},{10,12},{12,14},{15,13}... | collective-permute-start | bytes 1867784 | tf_op jit(solution)/shard_map/ppermute | solution.py:542
  153.3 1.5 collective-permute-done.22.come_ref.refs_2_.refs_1_.refs_0_
  155.4 4.4 %collective-permute-start.27 = (f32[64,2432]{1,0:T(8,128)S(1)}, f32[64,2432]{1,0:T(8,128)S(1)}, u32[]{:S(2)}, u32[]{:S(2)}) collective-permute-start(f32[64,2432]{1,0:T(8,128)S(1)} %shard_map.95.refs_2_), channel_id=1, source_target_pairs={{0,2},{2,4},{4,6},{7,5},{5,3},{3,1},{8,10},{10,12},{12,14},{15,13}... | collective-permute-start | bytes 1867784 | tf_op jit(solution)/shard_map/ppermute | solution.py:542
  160.0 1.5 collective-permute-done.20.come_ref.refs_2_.refs_1_.refs_0_
  162.1 4.5 %collective-permute-start.26 = (f32[64,2432]{1,0:T(8,128)S(1)}, f32[64,2432]{1,0:T(8,128)S(1)}, u32[]{:S(2)}, u32[]{:S(2)}) collective-permute-start(f32[64,2432]{1,0:T(8,128)S(1)} %shard_map.97.refs_4_), channel_id=1, source_target_pairs={{0,2},{2,4},{4,6},{7,5},{5,3},{3,1},{8,10},{10,12},{12,14},{15,13}... | collective-permute-start | bytes 1867784 | tf_op jit(solution)/shard_map/ppermute | solution.py:542
  166.5 4.2 %shard_map.98 = (f32[3072,256]{1,0:T(8,128)}, f32[8,128]{1,0:T(8,128)S(1)}) custom-call(s32[1]{0:T(128)} %bitcast.me_ref, f32[64,3072]{1,0:T(8,128)S(1)} %shard_map.76.block_ref._.refs_6_.refs_0_, f32[64,3072]{1,0:T(8,128)S(1)} %collective-permute-done.6.refs_0_.refs_1_.refs_7_, f32[64,3072]{1,0:T(8,128)S(1)} %collective-permute-done.7.refs_1_.refs_0_.refs_8_.refs_2_, ...), custom_call_target="tpu_custom_call" | custom-call | bytes 73800 | tf_op jit(solution)/shard_map/pallas_call | solution.py:398
  181.5 11.9 %collective-permute-start.32 = (f32[64,2432]{1,0:T(8,128)S(1)}, f32[64,2432]{1,0:T(8,128)S(1)}, u32[]{:S(2)}, u32[]{:S(2)}) collective-permute-start(f32[64,2432]{1,0:T(8,128)S(1)} %shard_map.109._.refs_13_.refs_1_), channel_id=1, source_target_pairs={{0,1},{1,0},{2,3},{3,2},{4,5},{5,4},{6,7},{7,6},{8,9},{9,8},{10,11... | collective-permute-start | bytes 1867784 | tf_op jit(solution)/shard_map/ppermute | solution.py:249
  195.4 9.5 %collective-permute-start.37 = (f32[64,2432]{1,0:T(8,128)S(1)}, f32[64,2432]{1,0:T(8,128)S(1)}, u32[]{:S(2)}, u32[]{:S(2)}) collective-permute-start(f32[64,2432]{1,0:T(8,128)S(1)} %shard_map.112.refs_22_.refs_24_.refs_1_), channel_id=1, source_target_pairs={{0,1},{1,0},{2,3},{3,2},{4,5},{5,4},{6,7},{7,6},{8,9},{9,8},{10,11... | collective-permute-start | bytes 1867784 | tf_op jit(solution)/shard_map/ppermute | solution.py:249
  204.9 1.6 collective-permute-done.37.refs_23_.refs_2_
  207.4 3.9 %shard_map.113 = (f32[256,4608]{1,0:T(8,128)S(1)}, f32[8,128]{1,0:T(8,128)S(1)}) custom-call(s32[1]{0:T(128)} %bitcast.me_ref, f32[256,4608]{1,0:T(8,128)S(1)} %bitcast.4, f32[64,2432]{1,0:T(8,128)S(1)} %shard_map.80.refs_2_.refs_1_.refs_0_, f32[64,2432]{1,0:T(8,128)S(1)} %shard_map.99._.refs_1_, f32[64,2432]{1,0:T(8,128)S(1)} %collective-permute-done.24.refs_0_.refs_2_, ...), custom_call_target="tpu_custom_call" | custom-call | bytes 73800 | tf_op jit(solution)/shard_map/pallas_call | solution.py:610
  211.4 1.3 shard_map.114
  (104 shorter events, 30.4 us)
Async XLA Ops:
  1.3 1.9 copy-start
  6.7 32.2 %all-to-all-start = ((f32[8,72,384]{2,1,0:T(8,128)}), f32[8,72,384]{2,1,0:T(8,128)S(1)}, u32[]{:S(2)}, u32[]{:S(2)}) async-start(f32[8,72,384]{2,1,0:T(8,128)} %shard_map.68.refs_1_.pay_ref), calls=%async_computation | async-start | bytes 1769472 | tf_op jit(solution)/shard_map/all_to_all | solution.py:683
  27.9 9.4 %copy-start.1 = (f32[2,64,2048]{2,1,0:T(8,128)}, f32[2,64,2048]{2,1,0:T(8,128)S(1)}, u32[]{:S(2)}) copy-start(f32[2,64,2048]{2,1,0:T(8,128)S(1)} %get-tuple-element.47.refs_2_.refs_0_.refs_3_) | copy-start | bytes 3145732
  27.9 25.9 %collective-permute-start.3 = (f32[2,64,2048]{2,1,0:T(8,128)}, f32[2,64,2048]{2,1,0:T(8,128)}, u32[]{:S(2)}, u32[]{:S(2)}) collective-permute-start(f32[2,64,2048]{2,1,0:T(8,128)} %get-tuple-element.54), channel_id=1, source_target_pairs={{0,16},{8,24},{16,0},{24,8},{1,17},{9,25},{17,1},{25,9},{2,18},{10... | collective-permute-start | bytes 3145736 | tf_op jit(solution)/shard_map/ppermute | solution.py:249
  29.5 9.3 %copy-start.3 = (s32[12,256]{1,0:T(8,128)S(1)}, s32[12,256]{1,0:T(8,128)}, u32[]{:S(2)}) copy-start(s32[12,256]{1,0:T(8,128)} %code_ref.3) | copy-start | bytes 36868
  37.2 17.9 %copy-start.2 = (f32[2,64,1280]{2,1,0:T(8,128)}, f32[2,64,1280]{2,1,0:T(8,128)S(1)}, u32[]{:S(2)}) copy-start(f32[2,64,1280]{2,1,0:T(8,128)S(1)} %get-tuple-element.48._.refs_0_) | copy-start | bytes 1966084
  37.3 17.8 %collective-permute-start.2 = (f32[2,64,1280]{2,1,0:T(8,128)S(1)}, f32[2,64,1280]{2,1,0:T(8,128)}, u32[]{:S(2)}, u32[]{:S(2)}) collective-permute-start(f32[2,64,1280]{2,1,0:T(8,128)S(1)} %get-tuple-element.53), channel_id=1, source_target_pairs={{0,8},{8,0},{16,24},{24,16},{1,9},{9,1},{17,25},{25,17},{2,10},{10... | collective-permute-start | bytes 1966088 | tf_op jit(solution)/shard_map/ppermute | solution.py:249
  41.5 14.7 %collective-permute-start = (f32[72,256]{1,0:T(8,128)S(1)}, f32[72,256]{1,0:T(8,128)S(1)}, u32[]{:S(2)}, u32[]{:S(2)}) collective-permute-start(f32[72,256]{1,0:T(8,128)S(1)} %get-tuple-element.50), channel_id=1, source_target_pairs={{0,1},{1,2},{2,3},{3,4},{4,5},{5,6},{6,7},{8,9},{9,10},{10,11},{11... | collective-permute-start | bytes 221192 | tf_op jit(solution)/shard_map/ppermute | solution.py:714
  43.4 12.9 %collective-permute-start.1 = (f32[72,256]{1,0:T(8,128)S(1)}, f32[72,256]{1,0:T(8,128)S(1)}, u32[]{:S(2)}, u32[]{:S(2)}) collective-permute-start(f32[72,256]{1,0:T(8,128)S(1)} %get-tuple-element.51), channel_id=1, source_target_pairs={{1,0},{2,1},{3,2},{4,3},{5,4},{6,5},{7,6},{9,8},{10,9},{11,10},{12... | collective-permute-start | bytes 221192 | tf_op jit(solution)/shard_map/ppermute | solution.py:715
  60.4 27.8 %all-to-all-start.1 = ((f32[8,72,384]{2,1,0:T(8,128)}), f32[8,72,384]{2,1,0:T(8,128)S(1)}, u32[]{:S(2)}, u32[]{:S(2)}) async-start(f32[8,72,384]{2,1,0:T(8,128)} %shard_map.74.refs_7_), calls=%async_computation.1 | async-start | bytes 1769472 | tf_op jit(solution)/shard_map/all_to_all | solution.py:721
  65.2 14.3 %collective-permute-start.5 = (f32[1,64,2048]{2,1,0:T(8,128)S(1)}, f32[1,64,2048]{2,1,0:T(8,128)S(1)}, u32[]{:S(2)}, u32[]{:S(2)}) collective-permute-start(f32[1,64,2048]{2,1,0:T(8,128)S(1)} %shard_map.72.refs_2_), channel_id=1, source_target_pairs={{0,8},{8,0},{16,24},{24,16},{1,9},{9,1},{17,25},{25,17},{2,10},{10... | collective-permute-start | bytes 1572872 | tf_op jit(solution)/shard_map/ppermute | solution.py:249
  66.7 9.8 %collective-permute-start.4 = (f32[1,64,1280]{2,1,0:T(8,128)S(1)}, f32[1,64,1280]{2,1,0:T(8,128)S(1)}, u32[]{:S(2)}, u32[]{:S(2)}) collective-permute-start(f32[1,64,1280]{2,1,0:T(8,128)S(1)} %shard_map.73._), channel_id=1, source_target_pairs={{0,16},{8,24},{16,0},{24,8},{1,17},{9,25},{17,1},{25,9},{2,18},{10... | collective-permute-start | bytes 983048 | tf_op jit(solution)/shard_map/ppermute | solution.py:249
  76.5 3.0 %copy-start.6 = (f32[1,64,1280]{2,1,0:T(8,128)}, f32[1,64,1280]{2,1,0:T(8,128)S(1)}, u32[]{:S(2)}) copy-start(f32[1,64,1280]{2,1,0:T(8,128)S(1)} %collective-permute-done.4.refs_2_) | copy-start | bytes 983044
  88.2 0.9 copy-start.4
  92.0 19.1 %collective-permute-start.6 = (f32[64,3072]{1,0:T(8,128)S(1)}, f32[64,3072]{1,0:T(8,128)S(1)}, u32[]{:S(2)}, u32[]{:S(2)}) collective-permute-start(f32[64,3072]{1,0:T(8,128)S(1)} %shard_map.76.block_ref._.refs_6_.refs_0_), channel_id=1, source_target_pairs={{0,8},{8,0},{16,24},{24,16},{1,9},{9,1},{17,25},{25,17},{2,10},{10... | collective-permute-start | bytes 2359304 | tf_op jit(solution)/shard_map/ppermute | solution.py:249
  93.6 18.8 %collective-permute-start.7 = (f32[64,3072]{1,0:T(8,128)S(1)}, f32[64,3072]{1,0:T(8,128)S(1)}, u32[]{:S(2)}, u32[]{:S(2)}) collective-permute-start(f32[64,3072]{1,0:T(8,128)S(1)} %shard_map.76.block_ref._.refs_6_.refs_0_), channel_id=1, source_target_pairs={{0,16},{8,24},{16,0},{24,8},{1,17},{9,25},{17,1},{25,9},{2,18},{10... | collective-permute-start | bytes 2359304 | tf_op jit(solution)/shard_map/ppermute | solution.py:249
  105.2 7.2 %collective-permute-start.11 = (f32[64,2432]{1,0:T(8,128)S(1)}, f32[64,2432]{1,0:T(8,128)S(1)}, u32[]{:S(2)}, u32[]{:S(2)}) collective-permute-start(f32[64,2432]{1,0:T(8,128)S(1)} %get-tuple-element.66.refs_0_), channel_id=1, source_target_pairs={{0,1},{1,0},{2,3},{3,2},{4,5},{5,4},{6,7},{7,6},{8,9},{9,8},{10,11... | collective-permute-start | bytes 1867784 | tf_op jit(solution)/shard_map/ppermute | solution.py:249
  105.3 7.2 %collective-permute-start.10 = (f32[64,2432]{1,0:T(8,128)S(1)}, f32[64,2432]{1,0:T(8,128)S(1)}, u32[]{:S(2)}, u32[]{:S(2)}) collective-permute-start(f32[64,2432]{1,0:T(8,128)S(1)} %get-tuple-element.57.refs_2_.refs_0_), channel_id=1, source_target_pairs={{0,1},{1,0},{2,3},{3,2},{4,5},{5,4},{6,7},{7,6},{8,9},{9,8},{10,11... | collective-permute-start | bytes 1867784 | tf_op jit(solution)/shard_map/ppermute | solution.py:249
  112.6 13.4 %collective-permute-start.12 = (f32[64,2432]{1,0:T(8,128)S(1)}, f32[64,2432]{1,0:T(8,128)S(1)}, u32[]{:S(2)}, u32[]{:S(2)}) collective-permute-start(f32[64,2432]{1,0:T(8,128)S(1)} %shard_map.81.refs_9_.refs_1_.refs_2_.refs_3_), channel_id=1, source_target_pairs={{0,2},{7,5},{8,10},{15,13},{16,18},{23,21},{24,26},{31,29}} | collective-permute-start | bytes 1867784 | tf_op jit(solution)/shard_map/ppermute | solution.py:523
  114.1 8.7 %collective-permute-start.8 = (f32[64,1536]{1,0:T(8,128)S(1)}, f32[64,1536]{1,0:T(8,128)S(1)}, u32[]{:S(2)}, u32[]{:S(2)}) collective-permute-start(f32[64,1536]{1,0:T(8,128)S(1)} %get-tuple-element.58), channel_id=1, source_target_pairs={{0,8},{8,0},{16,24},{24,16},{1,9},{9,1},{17,25},{25,17},{2,10},{10... | collective-permute-start | bytes 1179656 | tf_op jit(solution)/shard_map/ppermute | solution.py:249
  114.7 10.6 %collective-permute-start.9 = (f32[64,1536]{1,0:T(8,128)S(1)}, f32[64,1536]{1,0:T(8,128)S(1)}, u32[]{:S(2)}, u32[]{:S(2)}) collective-permute-start(f32[64,1536]{1,0:T(8,128)S(1)} %get-tuple-element.59.refs_2_), channel_id=1, source_target_pairs={{0,16},{8,24},{16,0},{24,8},{1,17},{9,25},{17,1},{25,9},{2,18},{10... | collective-permute-start | bytes 1179656 | tf_op jit(solution)/shard_map/ppermute | solution.py:249
  116.3 12.2 %collective-permute-start.15 = (f32[64,2432]{1,0:T(8,128)S(1)}, f32[64,2432]{1,0:T(8,128)S(1)}, u32[]{:S(2)}, u32[]{:S(2)}) collective-permute-start(f32[64,2432]{1,0:T(8,128)S(1)} %shard_map.80.refs_2_.refs_1_.refs_0_), channel_id=1, source_target_pairs={{0,2},{7,5},{8,10},{15,13},{16,18},{23,21},{24,26},{31,29}} | collective-permute-start | bytes 1867784 | tf_op jit(solution)/shard_map/ppermute | solution.py:523
  120.3 8.2 %collective-permute-start.16 = (f32[64,2432]{1,0:T(8,128)S(1)}, f32[64,2432]{1,0:T(8,128)S(1)}, u32[]{:S(2)}, u32[]{:S(2)}) collective-permute-start(f32[64,2432]{1,0:T(8,128)S(1)} %get-tuple-element.70.refs_0_), channel_id=1, source_target_pairs={{0,1},{1,0},{2,3},{3,2},{4,5},{5,4},{6,7},{7,6},{8,9},{9,8},{10,11... | collective-permute-start | bytes 1867784 | tf_op jit(solution)/shard_map/ppermute | solution.py:249
  122.8 5.7 %collective-permute-start.17 = (f32[64,2432]{1,0:T(8,128)S(1)}, f32[64,2432]{1,0:T(8,128)S(1)}, u32[]{:S(2)}, u32[]{:S(2)}) collective-permute-start(f32[64,2432]{1,0:T(8,128)S(1)} %get-tuple-element.67.refs_9_.refs_1_), channel_id=1, source_target_pairs={{0,1},{1,0},{2,3},{3,2},{4,5},{5,4},{6,7},{7,6},{8,9},{9,8},{10,11... | collective-permute-start | bytes 1867784 | tf_op jit(solution)/shard_map/ppermute | solution.py:249
  125.4 8.4 %collective-permute-start.13 = (f32[64,2432]{1,0:T(8,128)S(1)}, f32[64,2432]{1,0:T(8,128)S(1)}, u32[]{:S(2)}, u32[]{:S(2)}) collective-permute-start(f32[64,2432]{1,0:T(8,128)S(1)} %get-tuple-element.69.refs_0_), channel_id=1, source_target_pairs={{0,1},{1,0},{2,3},{3,2},{4,5},{5,4},{6,7},{7,6},{8,9},{9,8},{10,11... | collective-permute-start | bytes 1867784 | tf_op jit(solution)/shard_map/ppermute | solution.py:249
  125.9 7.8 %collective-permute-start.14 = (f32[64,2432]{1,0:T(8,128)S(1)}, f32[64,2432]{1,0:T(8,128)S(1)}, u32[]{:S(2)}, u32[]{:S(2)}) collective-permute-start(f32[64,2432]{1,0:T(8,128)S(1)} %get-tuple-element.68.refs_2_.refs_1_), channel_id=1, source_target_pairs={{0,1},{1,0},{2,3},{3,2},{4,5},{5,4},{6,7},{7,6},{8,9},{9,8},{10,11... | collective-permute-start | bytes 1867784 | tf_op jit(solution)/shard_map/ppermute | solution.py:249
  129.3 13.4 %collective-permute-start.19 = (f32[64,2432]{1,0:T(8,128)S(1)}, f32[64,2432]{1,0:T(8,128)S(1)}, u32[]{:S(2)}, u32[]{:S(2)}) collective-permute-start(f32[64,2432]{1,0:T(8,128)S(1)} %shard_map.87.refs_4_), channel_id=1, source_target_pairs={{0,2},{2,4},{7,5},{5,3},{8,10},{10,12},{15,13},{13,11},{16,18},{18... | collective-permute-start | bytes 1867784 | tf_op jit(solution)/shard_map/ppermute | solution.py:542
  134.5 13.6 %collective-permute-start.18 = (f32[64,2432]{1,0:T(8,128)S(1)}, f32[64,2432]{1,0:T(8,128)S(1)}, u32[]{:S(2)}, u32[]{:S(2)}) collective-permute-start(f32[64,2432]{1,0:T(8,128)S(1)} %shard_map.89.refs_10_), channel_id=1, source_target_pairs={{0,2},{2,4},{7,5},{5,3},{8,10},{10,12},{15,13},{13,11},{16,18},{18... | collective-permute-start | bytes 1867784 | tf_op jit(solution)/shard_map/ppermute | solution.py:542
  139.6 13.7 %collective-permute-start.23 = (f32[64,2432]{1,0:T(8,128)S(1)}, f32[64,2432]{1,0:T(8,128)S(1)}, u32[]{:S(2)}, u32[]{:S(2)}) collective-permute-start(f32[64,2432]{1,0:T(8,128)S(1)} %shard_map.90.refs_10_.refs_0_), channel_id=1, source_target_pairs={{0,1},{1,0},{2,3},{3,2},{4,5},{5,4},{6,7},{7,6},{8,9},{9,8},{10,11... | collective-permute-start | bytes 1867784 | tf_op jit(solution)/shard_map/ppermute | solution.py:249
  143.3 11.5 %collective-permute-start.22 = (f32[64,2432]{1,0:T(8,128)S(1)}, f32[64,2432]{1,0:T(8,128)S(1)}, u32[]{:S(2)}, u32[]{:S(2)}) collective-permute-start(f32[64,2432]{1,0:T(8,128)S(1)} %shard_map.92._), channel_id=1, source_target_pairs={{0,2},{2,4},{4,6},{7,5},{5,3},{3,1},{8,10},{10,12},{12,14},{15,13}... | collective-permute-start | bytes 1867784 | tf_op jit(solution)/shard_map/ppermute | solution.py:542
  146.5 13.3 %collective-permute-start.21 = (f32[64,2432]{1,0:T(8,128)S(1)}, f32[64,2432]{1,0:T(8,128)S(1)}, u32[]{:S(2)}, u32[]{:S(2)}) collective-permute-start(f32[64,2432]{1,0:T(8,128)S(1)} %shard_map.91._.refs_0_), channel_id=1, source_target_pairs={{0,1},{1,0},{2,3},{3,2},{4,5},{5,4},{6,7},{7,6},{8,9},{9,8},{10,11... | collective-permute-start | bytes 1867784 | tf_op jit(solution)/shard_map/ppermute | solution.py:249
  148.7 12.7 %collective-permute-start.20 = (f32[64,2432]{1,0:T(8,128)S(1)}, f32[64,2432]{1,0:T(8,128)S(1)}, u32[]{:S(2)}, u32[]{:S(2)}) collective-permute-start(f32[64,2432]{1,0:T(8,128)S(1)} %shard_map.93.refs_2_), channel_id=1, source_target_pairs={{0,2},{2,4},{4,6},{7,5},{5,3},{3,1},{8,10},{10,12},{12,14},{15,13}... | collective-permute-start | bytes 1867784 | tf_op jit(solution)/shard_map/ppermute | solution.py:542
  155.4 17.1 %collective-permute-start.27 = (f32[64,2432]{1,0:T(8,128)S(1)}, f32[64,2432]{1,0:T(8,128)S(1)}, u32[]{:S(2)}, u32[]{:S(2)}) collective-permute-start(f32[64,2432]{1,0:T(8,128)S(1)} %shard_map.95.refs_2_), channel_id=1, source_target_pairs={{0,2},{2,4},{4,6},{7,5},{5,3},{3,1},{8,10},{10,12},{12,14},{15,13}... | collective-permute-start | bytes 1867784 | tf_op jit(solution)/shard_map/ppermute | solution.py:542
  162.1 12.7 %collective-permute-start.26 = (f32[64,2432]{1,0:T(8,128)S(1)}, f32[64,2432]{1,0:T(8,128)S(1)}, u32[]{:S(2)}, u32[]{:S(2)}) collective-permute-start(f32[64,2432]{1,0:T(8,128)S(1)} %shard_map.97.refs_4_), channel_id=1, source_target_pairs={{0,2},{2,4},{4,6},{7,5},{5,3},{3,1},{8,10},{10,12},{12,14},{15,13}... | collective-permute-start | bytes 1867784 | tf_op jit(solution)/shard_map/ppermute | solution.py:542
  171.9 4.1 %collective-permute-start.25 = (f32[64,2432]{1,0:T(8,128)S(1)}, f32[64,2432]{1,0:T(8,128)S(1)}, u32[]{:S(2)}, u32[]{:S(2)}) collective-permute-start(f32[64,2432]{1,0:T(8,128)S(1)} %shard_map.100._.refs_4_), channel_id=1, source_target_pairs={{0,1},{1,0},{2,3},{3,2},{4,5},{5,4},{6,7},{7,6},{8,9},{9,8},{10,11... | collective-permute-start | bytes 1867784 | tf_op jit(solution)/shard_map/ppermute | solution.py:249
  172.0 4.1 %collective-permute-start.24 = (f32[64,2432]{1,0:T(8,128)S(1)}, f32[64,2432]{1,0:T(8,128)S(1)}, u32[]{:S(2)}, u32[]{:S(2)}) collective-permute-start(f32[64,2432]{1,0:T(8,128)S(1)} %shard_map.99._.refs_1_), channel_id=1, source_target_pairs={{0,1},{1,0},{2,3},{3,2},{4,5},{5,4},{6,7},{7,6},{8,9},{9,8},{10,11... | collective-permute-start | bytes 1867784 | tf_op jit(solution)/shard_map/ppermute | solution.py:249
  173.1 5.0 %collective-permute-start.31 = (f32[64,2432]{1,0:T(8,128)S(1)}, f32[64,2432]{1,0:T(8,128)S(1)}, u32[]{:S(2)}, u32[]{:S(2)}) collective-permute-start(f32[64,2432]{1,0:T(8,128)S(1)} %shard_map.101._), channel_id=1, source_target_pairs={{2,4},{4,6},{5,3},{3,1},{10,12},{12,14},{13,11},{11,9},{18,20},{20... | collective-permute-start | bytes 1867784 | tf_op jit(solution)/shard_map/ppermute | solution.py:542
  175.4 4.2 %collective-permute-start.30 = (f32[64,2432]{1,0:T(8,128)S(1)}, f32[64,2432]{1,0:T(8,128)S(1)}, u32[]{:S(2)}, u32[]{:S(2)}) collective-permute-start(f32[64,2432]{1,0:T(8,128)S(1)} %shard_map.102.refs_2_), channel_id=1, source_target_pairs={{2,4},{4,6},{5,3},{3,1},{10,12},{12,14},{13,11},{11,9},{18,20},{20... | collective-permute-start | bytes 1867784 | tf_op jit(solution)/shard_map/ppermute | solution.py:542
  177.3 3.5 %collective-permute-start.29 = (f32[64,2432]{1,0:T(8,128)S(1)}, f32[64,2432]{1,0:T(8,128)S(1)}, u32[]{:S(2)}, u32[]{:S(2)}) collective-permute-start(f32[64,2432]{1,0:T(8,128)S(1)} %shard_map.105._.refs_10_.refs_4_), channel_id=1, source_target_pairs={{0,1},{1,0},{2,3},{3,2},{4,5},{5,4},{6,7},{7,6},{8,9},{9,8},{10,11... | collective-permute-start | bytes 1867784 | tf_op jit(solution)/shard_map/ppermute | solution.py:249
  178.0 2.9 %collective-permute-start.28 = (f32[64,2432]{1,0:T(8,128)S(1)}, f32[64,2432]{1,0:T(8,128)S(1)}, u32[]{:S(2)}, u32[]{:S(2)}) collective-permute-start(f32[64,2432]{1,0:T(8,128)S(1)} %shard_map.104._.refs_7_.refs_1_), channel_id=1, source_target_pairs={{0,1},{1,0},{2,3},{3,2},{4,5},{5,4},{6,7},{7,6},{8,9},{9,8},{10,11... | collective-permute-start | bytes 1867784 | tf_op jit(solution)/shard_map/ppermute | solution.py:249
  178.6 15.5 %collective-permute-start.34 = (f32[64,2432]{1,0:T(8,128)S(1)}, f32[64,2432]{1,0:T(8,128)S(1)}, u32[]{:S(2)}, u32[]{:S(2)}) collective-permute-start(f32[64,2432]{1,0:T(8,128)S(1)} %shard_map.106._), channel_id=1, source_target_pairs={{4,6},{3,1},{12,14},{11,9},{20,22},{19,17},{28,30},{27,25}} | collective-permute-start | bytes 1867784 | tf_op jit(solution)/shard_map/ppermute | solution.py:542
  180.1 14.6 %collective-permute-start.36 = (f32[64,2432]{1,0:T(8,128)S(1)}, f32[64,2432]{1,0:T(8,128)S(1)}, u32[]{:S(2)}, u32[]{:S(2)}) collective-permute-start(f32[64,2432]{1,0:T(8,128)S(1)} %shard_map.107.refs_2_), channel_id=1, source_target_pairs={{4,6},{3,1},{12,14},{11,9},{20,22},{19,17},{28,30},{27,25}} | collective-permute-start | bytes 1867784 | tf_op jit(solution)/shard_map/ppermute | solution.py:542
  180.9 26.5 %slice-start = ((s8[4718592]{0:T(1024)(128)(4,1)}), s8[4194304]{0:T(1024)(128)(4,1)S(1)}, s32[]{:S(2)}) async-start(s8[4718592]{0:T(1024)(128)(4,1)} %bitcast.3), calls=%async_computation.2 | async-start | bytes 8388608
  181.5 25.9 %slice-start.1 = ((s8[4718592]{0:T(1024)(128)(4,1)}), s8[524288]{0:T(1024)(128)(4,1)S(1)}, s32[]{:S(2)}) async-start(s8[4718592]{0:T(1024)(128)(4,1)} %bitcast.3), calls=%async_computation.3 | async-start | bytes 1048576
  181.5 23.4 %collective-permute-start.32 = (f32[64,2432]{1,0:T(8,128)S(1)}, f32[64,2432]{1,0:T(8,128)S(1)}, u32[]{:S(2)}, u32[]{:S(2)}) collective-permute-start(f32[64,2432]{1,0:T(8,128)S(1)} %shard_map.109._.refs_13_.refs_1_), channel_id=1, source_target_pairs={{0,1},{1,0},{2,3},{3,2},{4,5},{5,4},{6,7},{7,6},{8,9},{9,8},{10,11... | collective-permute-start | bytes 1867784 | tf_op jit(solution)/shard_map/ppermute | solution.py:249
  194.0 10.9 %collective-permute-start.33 = (f32[64,2432]{1,0:T(8,128)S(1)}, f32[64,2432]{1,0:T(8,128)S(1)}, u32[]{:S(2)}, u32[]{:S(2)}) collective-permute-start(f32[64,2432]{1,0:T(8,128)S(1)} %shard_map.110._.refs_16_.refs_4_), channel_id=1, source_target_pairs={{0,1},{1,0},{2,3},{3,2},{4,5},{5,4},{6,7},{7,6},{8,9},{9,8},{10,11... | collective-permute-start | bytes 1867784 | tf_op jit(solution)/shard_map/ppermute | solution.py:249
  195.4 11.2 %collective-permute-start.37 = (f32[64,2432]{1,0:T(8,128)S(1)}, f32[64,2432]{1,0:T(8,128)S(1)}, u32[]{:S(2)}, u32[]{:S(2)}) collective-permute-start(f32[64,2432]{1,0:T(8,128)S(1)} %shard_map.112.refs_22_.refs_24_.refs_1_), channel_id=1, source_target_pairs={{0,1},{1,0},{2,3},{3,2},{4,5},{5,4},{6,7},{7,6},{8,9},{9,8},{10,11... | collective-permute-start | bytes 1867784 | tf_op jit(solution)/shard_map/ppermute | solution.py:249
  204.8 2.6 %collective-permute-start.35 = (f32[64,2432]{1,0:T(8,128)S(1)}, f32[64,2432]{1,0:T(8,128)S(1)}, u32[]{:S(2)}, u32[]{:S(2)}) collective-permute-start(f32[64,2432]{1,0:T(8,128)S(1)} %shard_map.111._.refs_19_.refs_1_), channel_id=1, source_target_pairs={{0,1},{1,0},{2,3},{3,2},{4,5},{5,4},{6,7},{7,6},{8,9},{9,8},{10,11... | collective-permute-start | bytes 1867784 | tf_op jit(solution)/shard_map/ppermute | solution.py:249
  (1 other events, 0.8 us)

commit v5 on v4

--- a/solution.py
+++ b/solution.py
@@ -572,98 +572,70 @@
     return high, (x - high.astype(F32)).astype(BF16)
 
 
-def shares(loadings, sums, ids, cols, me, token):
+def new_loadings(loadings, sums, ids, me, token):
     width_all, genes = loadings.shape
     width = width_all // len(ids)
-    steps = 6
-    step = genes // steps
-    extra = width_all // HALVES
+    cols, extra = genes // HALVES, width_all // HALVES
+    per = 3
+    step = cols // per
     arrays = [x for pair in sums for terms in pair for x in terms]
 
     def body(me_ref, load_ref, *refs):
-        out_ref, tiny, load, gram = refs[-4:]
+        out_ref, load, gram, cross = refs[-4:]
+        at = pl.program_id(0)
         firsts = [pl.multiple_of((k ^ me_ref[0]) * width, width) for k in ids]
-
-        @pl.when(pl.program_id(0) == 0)
+        terms = lambda j, h: refs[3 * (j * HALVES + h) : 3 * (j * HALVES + h) + 3]
+
+        @pl.when(at == 0)
         def _():
             behind = slice(cols, cols + extra)
-            for i in range(len(sums) * HALVES):
-                own, end, other = refs[3 * i : 3 * i + 3]
-                j, h = i // HALVES, i % HALVES
-                gram[j * width : (j + 1) * width, h * extra : (h + 1) * extra] = own[:, behind] + (
-                    end[:, behind] + other[:, behind]
-                )
+            for j in range(len(ids)):
+                for h in range(HALVES):
+                    own, end, other = terms(j, h)
+                    gram[j * width : (j + 1) * width, h * extra : (h + 1) * extra] = own[:, behind] + (
+                        end[:, behind] + other[:, behind]
+                    )
             low = gram[...]
             row = lax.broadcasted_iota(jnp.int32, low.shape, 0) // width
             col = lax.broadcasted_iota(jnp.int32, low.shape, 1) // width
             gram[...] = jnp.where(col <= row, low, low.T)
 
+        for h in range(HALVES):
+
+            @pl.when(at // per == h)
+            def _():
+                here = pl.ds(pl.multiple_of((at - h * per) * step, step), step)
+                for j in range(len(ids)):
+                    own, end, other = terms(j, h)
+                    cross[j * width : (j + 1) * width, :] = own[:, here] + (end[:, here] + other[:, here])
+
         for j, first in enumerate(firsts):
             load[j * width : (j + 1) * width, :] = load_ref[pl.ds(first, width), :]
         value = load[...]
         (gram_hi, gram_lo), (hi, lo) = split(gram[...]), split(value)
-        value = value / (dot(gram_hi, hi, PLAIN) + (dot(gram_hi, lo, PLAIN) + dot(gram_lo, hi, PLAIN)))
+        below = dot(gram_hi, hi, PLAIN) + (dot(gram_hi, lo, PLAIN) + dot(gram_lo, hi, PLAIN))
+        value = value * cross[...] / below
         for j, first in enumerate(firsts):
             out_ref[pl.ds(first, width), :] = value[j * width : (j + 1) * width]
 
     block = pl.BlockSpec((width_all, step), lambda i, f: (0, i))
     return kernel_call(
         body,
-        (shape(width_all, genes), shape(8, 128)),
-        0.02,
-        limit=12,
+        pltpu.HBM((width_all, genes), F32),
+        0.02,
+        limit=16,
         grid_spec=pltpu.PrefetchScalarGridSpec(
             num_scalar_prefetch=1,
-            grid=(steps,),
+            grid=(HALVES * per,),
             in_specs=[block] + [VMEM_SPEC] * len(arrays) + [ANY_SPEC],
-            out_specs=(block, VMEM_SPEC),
+            out_specs=block,
             scratch_shapes=[
                 pltpu.VMEM((width_all, step), F32),
                 pltpu.VMEM((width_all, width_all), F32),
+                pltpu.VMEM((width_all, step), F32),
             ],
         ),
     )(me, loadings, *arrays, token)
-
-
-def new_loadings(share, parts, k, width, me, before, token):
-    width_all, genes = share.shape
-    halves = sorted(parts)
-    cols = genes // HALVES
-    arrays = [x for h in halves for x in parts[h]]
-
-    def body(me_ref, share_ref, _, *refs):
-        out_ref = refs[-2]
-        at = pl.ds(pl.multiple_of((k ^ me_ref[0]) * width, width), width)
-        for i, h in enumerate(halves):
-            own, end, other = refs[3 * i : 3 * i + 3]
-            here = slice(h * cols, (h + 1) * cols)
-            total = own[:, :cols] + (end[:, :cols] + other[:, :cols])
-            out_ref[:, i * cols : (i + 1) * cols] = share_ref[at, here] * total
-
-    operands = [me, share, token] + arrays
-    specs = [VMEM_SPEC, ANY_SPEC] + [VMEM_SPEC] * len(arrays)
-    aliases = {}
-    if before is not None:
-        operands.append(before)
-        specs.append(ANY_SPEC)
-        aliases = {len(operands) - 1: 0}
-    column = 0 if len(halves) == HALVES else halves[0]
-    return kernel_call(
-        body,
-        (pltpu.HBM((width_all, genes), F32), shape(8, 128)),
-        0.02,
-        limit=6,
-        grid_spec=pltpu.PrefetchScalarGridSpec(
-            num_scalar_prefetch=1,
-            grid=(1,),
-            in_specs=specs,
-            out_specs=(
-                pl.BlockSpec((width, len(halves) * cols), lambda i, m: (k ^ m[0], column)),
-                VMEM_SPEC,
-            ),
-        ),
-        input_output_aliases=aliases,
-    )(*operands)
 
 
 def on_device(counts, factors, loadings, position, edge_codes):
@@ -766,10 +738,6 @@
     def end(c, half, token):
         ends[half][c] = line_end(flags, come[half][c : c + line - 1], token)
         return ends[half][c][0]
-
-    def final(c, before, token, halves=range(HALVES)):
-        sums = {h: (own[h][c],) + ends[h][c] for h in halves}
-        return new_loadings(share, sums, ids[c], width, me1, before, token)
 
     def both(step, *args):
         nonlocal token
@@ -797,7 +765,8 @@
             later = groups[firsts[t] + 1]
             for k, block in zip(later, joined([coming[k] for k in later], token)):
                 blocks[k] = token = block
-            token = awaited([come[half][-1] for half in range(HALVES)], token)
+            for half in range(HALVES):
+                token = awaited([come[half][-1]], token)
         for half in range(HALVES):
             if t in firsts:
                 token = own_chunks(firsts[t], half, token)
@@ -818,12 +787,7 @@
     for c in rest:
         both(end, c)
     sums = [[(own[h][c],) + ends[h][c] for h in range(HALVES)] for c in range(chunks)]
-    loadings_new = None
-    share, token = shares(loadings, sums, ids, counts.shape[1] // HALVES, me1, token)
-    for c in range(chunks - 1):
-        loadings_new, token = final(c, loadings_new, token)
-    for half in range(HALVES):
-        loadings_new, token = final(chunks - 1, loadings_new, token, [half])
+    loadings_new = new_loadings(loadings, sums, ids, me1, token)
     return factors_new, loadings_new
 
 

time: 218 us -> 214 us (0.982)
  Pallas kernels: 90.9 us -> 86.8 us
    pallas_call x6 -> x1, Pallas kernels: 9.65 us -> 5.67 us  [new_loadings(): kernel_call(body, pltpu.HBM((width_all, genes), F32), 0.02, limit=16, gri...]
where the time goes in v5:
time: 214 us; the launch traced here: 213 us
  Pallas kernels  86.8 us (41%)
  starting transfers between devices  79.1 us (37%)
  waiting for transfers between devices  41.3 us (19%)
  local copies, waits for them, and re-layouts  3.62 us (2%)
    ppermute x24, starting transfers between devices, swap(): lax.ppermute(block, axis, [(i, i ^ bit) for i in range(lax.axis_size(axis...  35.8 us
    ppermute x24, waiting for transfers between devices, swap(): lax.ppermute(block, axis, [(i, i ^ bit) for i in range(lax.axis_size(axis...  31.6 us
    ppermute x10, starting transfers between devices, line_slot(): return (lax.ppermute(send, 'bin', hops), send)  25.8 us
    pallas_call x2, Pallas kernels, numer_part(): kernel_call(body, outs, 7, limit=40, in_specs=[SMEM_SPEC, ANY_SPEC] + [AN...  22.6 us
    pallas_call x4, Pallas kernels, cross_part(): kernel_call(body, (shape(width, cols + extra),) * n, 0.02, limit=8, in_sp...  11.2 us
    pallas_call x1, Pallas kernels, first_cross(): kernel_call(body, (shape(width, cols + extra),) * HALVES + (pltpu.VMEM((s...  10.2 us
    all_to_all x1, starting transfers between devices, on_device(): lax.all_to_all(payload, 'bin', split_axis=0, concat_axis=0, tiled=True)  6.33 us
    pallas_call x1, Pallas kernels, plain_terms(): kernel_call(body, (pltpu.HBM((width, rows), F32),) * 2, 4, limit=24, grid...  6.24 us
  transfers between devices with their start and end apart: 40, of which 14 were waited for; matrix products, arithmetic and copies ran while one was open for 0% of the time, Pallas kernels for 33%

profile of v5, /device:TPU:0, one launch (start us, length us, event | category | flops | bytes accessed | tf_op | source)
XLA Modules:
  0.0 212.9 jit_solution(13940995472702961763)
XLA Ops:
  1.3 1.9 copy-done
  3.2 3.4 %shard_map.68.refs_1_.pay_ref = f32[8,72,384]{2,1,0:T(8,128)} custom-call(s32[1]{0:T(128)} %bitcast.me_ref, f32[3072,256]{1,0:T(8,128)S(1)} %copy-done, f32[8,1,384]{2,1,0:T(1,128)S(1)} %bitcast.5), custom_call_target="tpu_custom_call" | custom-call | bytes 11070000 | tf_op jit(solution)/shard_map/pallas_call | solution.py:64
  6.6 6.3 %all-to-all-start = ((f32[8,72,384]{2,1,0:T(8,128)}), f32[8,72,384]{2,1,0:T(8,128)S(1)}, u32[]{:S(2)}, u32[]{:S(2)}) async-start(f32[8,72,384]{2,1,0:T(8,128)} %shard_map.68.refs_1_.pay_ref), calls=%async_computation | async-start | bytes 1769472 | tf_op jit(solution)/shard_map/all_to_all | solution.py:655
  12.9 14.9 %shard_map.69 = (f32[2,64,2048]{2,1,0:T(8,128)}, f32[2,64,2048]{2,1,0:T(8,128)S(1)}, bf16[4608,256]{1,0:T(8,128)(2,1)S(1)}, f32[256,256]{1,0:T(8,128)S(1)}) custom-call(s32[1]{0:T(128)} %bitcast.me_ref, bf16[3072,4608]{1,0:T(8,128)(2,1)} %counts_ref.5, f32[256,4608]{1,0:T(8,128)} %load_ref.1, f32[8,72,384]{2,1,0:T(8,128)} %shard_map.68.refs_1_.pay_ref), custom_call_target="tpu_custom_call" | custom-call | bytes 25830000 | tf_op jit(solution)/shard_map/pallas_call | solution.py:235
  27.9 1.6 collective-permute-start.3
  29.4 7.7 %shard_map.70 = (f32[2,64,1280]{2,1,0:T(8,128)S(1)}, f32[2,64,1280]{2,1,0:T(8,128)S(1)}) custom-call(s32[1]{0:T(128)} %bitcast.me_ref, bf16[3072,4608]{1,0:T(8,128)(2,1)} %counts_ref.5, bf16[4608,256]{1,0:T(8,128)(2,1)S(1)} %get-tuple-element.34.refs_0_, f32[256,256]{1,0:T(8,128)S(1)} %get-tuple-element.35.refs_1_, ...), custom_call_target="tpu_custom_call" | custom-call | bytes 25830000 | tf_op jit(solution)/shard_map/pallas_call | solution.py:235
  37.2 1.6 collective-permute-start.2
  38.8 2.7 %shard_map.71 = (f32[12,72,256]{2,1,0:T(8,128)S(1)}, f32[72,256]{1,0:T(8,128)S(1)}, f32[72,256]{1,0:T(8,128)S(1)}, s32[1,3072]{1,0:T(1,128)S(1)}) custom-call(s32[1]{0:T(128)} %bitcast.2.me_ref, f32[8,72,384]{2,1,0:T(8,128)S(1)} %all-to-all-done.got_ref, s32[12,256]{1,0:T(8,128)S(1)} %copy-done.3, f32[2,64,1280]{2,1,0:T(8,128)S(1)} %get-tuple-element.37._.refs_0_), custom_call_target="tpu_custom_call" | custom-call | bytes 11070000 | tf_op jit(solution)/shard_map/pallas_call | solution.py:106
  41.5 1.9 collective-permute-start
  43.3 1.5 collective-permute-start.1
  44.8 9.0 %collective-permute-done.3.refs_1_.refs_4_ = f32[2,64,2048]{2,1,0:T(8,128)} collective-permute-done((f32[2,64,2048]{2,1,0:T(8,128)}, f32[2,64,2048]{2,1,0:T(8,128)}, u32[]{:S(2)}, u32[]{:S(2)}) %collective-permute-start.3) | collective-permute-done | bytes 1048608 | tf_op jit(solution)/shard_map/ppermute | solution.py:249
  53.8 1.3 shard_map.72.refs_2_
  56.2 4.2 %shard_map.74.refs_7_ = f32[8,72,384]{2,1,0:T(8,128)} custom-call(f32[12,72,256]{2,1,0:T(8,128)S(1)} %get-tuple-element.38.refs_2_.grid_ref, f32[72,256]{1,0:T(8,128)S(1)} %collective-permute-done.above_ref, f32[72,256]{1,0:T(8,128)S(1)} %collective-permute-done.1.below_ref, s32[1,3072]{1,0:T(1,128)S(1)} %get-tuple-element.41.cell_ref, ...), custom_call_target="tpu_custom_call" | custom-call | bytes 14760000 | tf_op jit(solution)/shard_map/pallas_call | solution.py:155
  60.4 4.7 %all-to-all-start.1 = ((f32[8,72,384]{2,1,0:T(8,128)}), f32[8,72,384]{2,1,0:T(8,128)S(1)}, u32[]{:S(2)}, u32[]{:S(2)}) async-start(f32[8,72,384]{2,1,0:T(8,128)} %shard_map.74.refs_7_), calls=%async_computation.1 | async-start | bytes 1769472 | tf_op jit(solution)/shard_map/all_to_all | solution.py:693
  65.1 1.5 collective-permute-start.5
  66.6 1.5 collective-permute-start.4
  68.1 8.3 %collective-permute-done.4.refs_2_ = f32[1,64,1280]{2,1,0:T(8,128)S(1)} collective-permute-done((f32[1,64,1280]{2,1,0:T(8,128)S(1)}, f32[1,64,1280]{2,1,0:T(8,128)S(1)}, u32[]{:S(2)}, u32[]{:S(2)}) %collective-permute-start.4) | collective-permute-done | bytes 327712 | tf_op jit(solution)/shard_map/ppermute | solution.py:249
  76.5 3.0 %collective-permute-done.5.refs_5_ = f32[1,64,2048]{2,1,0:T(8,128)S(1)} collective-permute-done((f32[1,64,2048]{2,1,0:T(8,128)S(1)}, f32[1,64,2048]{2,1,0:T(8,128)S(1)}, u32[]{:S(2)}, u32[]{:S(2)}) %collective-permute-start.5) | collective-permute-done | bytes 524320 | tf_op jit(solution)/shard_map/ppermute | solution.py:249
  80.2 6.2 %shard_map.75 = (f32[64,3072]{1,0:T(8,128)}, f32[64,3072]{1,0:T(8,128)}) custom-call(f32[2,64,1280]{2,1,0:T(8,128)} %copy-done.2, f32[2,64,1280]{2,1,0:T(8,128)} %collective-permute-done.2.refs_1_, f32[1,64,1280]{2,1,0:T(8,128)} %copy-done.6, f32[2,64,2048]{2,1,0:T(8,128)} %copy-done.1, f32[2,64,2048]{2,1,0:T(8,128)} %collective-permute-done.3.refs_1_.refs_4_, ...), custom_call_target="tpu_custom_call" | custom-call | bytes 14760000 | tf_op jit(solution)/shard_map/pallas_call | solution.py:303
  86.5 1.7 all-to-all-done.1.back_ref
  89.1 2.8 %shard_map.76.block_ref._.refs_6_.refs_0_ = f32[64,3072]{1,0:T(8,128)S(1)} custom-call(f32[8,72,384]{2,1,0:T(8,128)} %shard_map.68.refs_1_.pay_ref, f32[8,72,384]{2,1,0:T(8,128)} %copy-done.4, f32[64,3072]{1,0:T(8,128)} %get-tuple-element.44.numer_ref, f32[64,3072]{1,0:T(8,128)} %get-tuple-element.45.plain_ref), custom_call_target="tpu_custom_call" | custom-call | bytes 73800 | tf_op jit(solution)/shard_map/pallas_call | solution.py:330
  92.0 1.6 collective-permute-start.6
  93.5 1.5 collective-permute-start.7
  95.0 10.2 %shard_map.77 = (f32[64,2432]{1,0:T(8,128)S(1)}, f32[64,2432]{1,0:T(8,128)S(1)}, bf16[512,4608]{1,0:T(8,128)(2,1)S(1)}, bf16[512,4608]{1,0:T(8,128)(2,1)S(1)}, b...) custom-call(bf16[3072,4608]{1,0:T(8,128)(2,1)} %counts_ref.5, ...), custom_call_target="tpu_custom_call" | custom-call | bytes 73800 | tf_op jit(solution)/shard_map/pallas_call | solution.py:441
  105.8 5.3 %collective-permute-done.6.refs_0_.refs_1_.refs_7_ = f32[64,3072]{1,0:T(8,128)S(1)} collective-permute-done((f32[64,3072]{1,0:T(8,128)S(1)}, f32[64,3072]{1,0:T(8,128)S(1)}, u32[]{:S(2)}, u32[]{:S(2)}) %collective-permute-start.6) | collective-permute-done | bytes 786464 | tf_op jit(solution)/shard_map/ppermute | solution.py:249
  112.5 1.6 collective-permute-start.15
  114.6 1.5 collective-permute-start.9
  116.2 1.5 collective-permute-start.12
  117.8 2.5 %shard_map.82 = (f32[64,2432]{1,0:T(8,128)S(1)}, f32[64,2432]{1,0:T(8,128)S(1)}) custom-call(bf16[512,4608]{1,0:T(8,128)(2,1)S(1)} %get-tuple-element.49.refs_0_, bf16[512,4608]{1,0:T(8,128)(2,1)S(1)} %get-tuple-element.50.refs_1_, bf16[512,4608]{1,0:T(8,128)(2,1)S(1)} %get-tuple-element.51.refs_2_, bf16[512,4608]{1,0:T(8,128)(2,1)S(1)} %get-tuple-element.52.refs_3_, ...), custom_call_target="tpu_custom_call" | custom-call | bytes 73800 | tf_op jit(solution)/shard_map/pallas_call | solution.py:480
  120.4 2.3 %collective-permute-done.8.refs_0_ = f32[64,1536]{1,0:T(8,128)S(1)} collective-permute-done((f32[64,1536]{1,0:T(8,128)S(1)}, f32[64,1536]{1,0:T(8,128)S(1)}, u32[]{:S(2)}, u32[]{:S(2)}) %collective-permute-start.8) | collective-permute-done | bytes 393248 | tf_op jit(solution)/shard_map/ppermute | solution.py:249
  122.7 2.5 %shard_map.83 = (f32[64,2432]{1,0:T(8,128)S(1)}, f32[64,2432]{1,0:T(8,128)S(1)}) custom-call(bf16[512,4608]{1,0:T(8,128)(2,1)S(1)} %get-tuple-element.49.refs_0_, bf16[512,4608]{1,0:T(8,128)(2,1)S(1)} %get-tuple-element.50.refs_1_, bf16[512,4608]{1,0:T(8,128)(2,1)S(1)} %get-tuple-element.51.refs_2_, bf16[512,4608]{1,0:T(8,128)(2,1)S(1)} %get-tuple-element.52.refs_3_, ...), custom_call_target="tpu_custom_call" | custom-call | bytes 73800 | tf_op jit(solution)/shard_map/pallas_call | solution.py:480
  126.0 2.4 %collective-permute-done.12.refs_0_.come_ref = f32[64,2432]{1,0:T(8,128)S(1)} collective-permute-done((f32[64,2432]{1,0:T(8,128)S(1)}, f32[64,2432]{1,0:T(8,128)S(1)}, u32[]{:S(2)}, u32[]{:S(2)}) %collective-permute-start.12) | collective-permute-done | bytes 622624 | tf_op jit(solution)/shard_map/ppermute | solution.py:523
  129.1 4.5 %collective-permute-start.19 = (f32[64,2432]{1,0:T(8,128)S(1)}, f32[64,2432]{1,0:T(8,128)S(1)}, u32[]{:S(2)}, u32[]{:S(2)}) collective-permute-start(f32[64,2432]{1,0:T(8,128)S(1)} %shard_map.88.refs_4_), channel_id=1, source_target_pairs={{0,2},{2,4},{7,5},{5,3},{8,10},{10,12},{15,13},{13,11},{16,18},{18... | collective-permute-start | bytes 1867784 | tf_op jit(solution)/shard_map/ppermute | solution.py:542
  134.4 1.9 collective-permute-start.18
  136.3 3.1 %shard_map.91.refs_10_.refs_0_ = f32[64,2432]{1,0:T(8,128)S(1)} custom-call(bf16[512,4608]{1,0:T(8,128)(2,1)S(1)} %get-tuple-element.49.refs_0_, bf16[512,4608]{1,0:T(8,128)(2,1)S(1)} %get-tuple-element.50.refs_1_, bf16[512,4608]{1,0:T(8,128)(2,1)S(1)} %get-tuple-element.51.refs_2_, bf16[512,4608]{1,0:T(8,128)(2,1)S(1)} %get-tuple-element.52.refs_3_, ...), custom_call_target="tpu_custom_call" | custom-call | bytes 73800 | tf_op jit(solution)/shard_map/pallas_call | solution.py:480
  139.5 3.1 %shard_map.92._.refs_0_ = f32[64,2432]{1,0:T(8,128)S(1)} custom-call(bf16[512,4608]{1,0:T(8,128)(2,1)S(1)} %get-tuple-element.49.refs_0_, bf16[512,4608]{1,0:T(8,128)(2,1)S(1)} %get-tuple-element.50.refs_1_, bf16[512,4608]{1,0:T(8,128)(2,1)S(1)} %get-tuple-element.51.refs_2_, bf16[512,4608]{1,0:T(8,128)(2,1)S(1)} %get-tuple-element.52.refs_3_, ...), custom_call_target="tpu_custom_call" | custom-call | bytes 73800 | tf_op jit(solution)/shard_map/pallas_call | solution.py:480
  143.2 3.2 %collective-permute-start.22 = (f32[64,2432]{1,0:T(8,128)S(1)}, f32[64,2432]{1,0:T(8,128)S(1)}, u32[]{:S(2)}, u32[]{:S(2)}) collective-permute-start(f32[64,2432]{1,0:T(8,128)S(1)} %shard_map.93._), channel_id=1, source_target_pairs={{0,2},{2,4},{4,6},{7,5},{5,3},{3,1},{8,10},{10,12},{12,14},{15,13}... | collective-permute-start | bytes 1867784 | tf_op jit(solution)/shard_map/ppermute | solution.py:542
  146.5 1.5 collective-permute-done.18.come_ref.refs_1_.refs_0_
  148.6 4.5 %collective-permute-start.20 = (f32[64,2432]{1,0:T(8,128)S(1)}, f32[64,2432]{1,0:T(8,128)S(1)}, u32[]{:S(2)}, u32[]{:S(2)}) collective-permute-start(f32[64,2432]{1,0:T(8,128)S(1)} %shard_map.94.refs_2_), channel_id=1, source_target_pairs={{0,2},{2,4},{4,6},{7,5},{5,3},{3,1},{8,10},{10,12},{12,14},{15,13}... | collective-permute-start | bytes 1867784 | tf_op jit(solution)/shard_map/ppermute | solution.py:542
  153.2 1.5 collective-permute-done.22.come_ref.refs_2_.refs_1_.refs_0_
  155.3 4.4 %collective-permute-start.27 = (f32[64,2432]{1,0:T(8,128)S(1)}, f32[64,2432]{1,0:T(8,128)S(1)}, u32[]{:S(2)}, u32[]{:S(2)}) collective-permute-start(f32[64,2432]{1,0:T(8,128)S(1)} %shard_map.96.refs_2_), channel_id=1, source_target_pairs={{0,2},{2,4},{4,6},{7,5},{5,3},{3,1},{8,10},{10,12},{12,14},{15,13}... | collective-permute-start | bytes 1867784 | tf_op jit(solution)/shard_map/ppermute | solution.py:542
  159.8 1.5 collective-permute-done.20.come_ref.refs_2_.refs_1_.refs_0_
  161.9 4.4 %collective-permute-start.26 = (f32[64,2432]{1,0:T(8,128)S(1)}, f32[64,2432]{1,0:T(8,128)S(1)}, u32[]{:S(2)}, u32[]{:S(2)}) collective-permute-start(f32[64,2432]{1,0:T(8,128)S(1)} %shard_map.98.refs_4_), channel_id=1, source_target_pairs={{0,2},{2,4},{4,6},{7,5},{5,3},{3,1},{8,10},{10,12},{12,14},{15,13}... | collective-permute-start | bytes 1867784 | tf_op jit(solution)/shard_map/ppermute | solution.py:542
  166.4 4.2 %shard_map.99 = (f32[3072,256]{1,0:T(8,128)}, f32[8,128]{1,0:T(8,128)S(1)}) custom-call(s32[1]{0:T(128)} %bitcast.me_ref, f32[64,3072]{1,0:T(8,128)S(1)} %shard_map.76.block_ref._.refs_6_.refs_0_, f32[64,3072]{1,0:T(8,128)S(1)} %collective-permute-done.6.refs_0_.refs_1_.refs_7_, f32[64,3072]{1,0:T(8,128)S(1)} %collective-permute-done.7.refs_1_.refs_0_.refs_8_.refs_2_, ...), custom_call_target="tpu_custom_call" | custom-call | bytes 73800 | tf_op jit(solution)/shard_map/pallas_call | solution.py:398
  181.1 12.1 %collective-permute-start.32 = (f32[64,2432]{1,0:T(8,128)S(1)}, f32[64,2432]{1,0:T(8,128)S(1)}, u32[]{:S(2)}, u32[]{:S(2)}) collective-permute-start(f32[64,2432]{1,0:T(8,128)S(1)} %shard_map.110._.refs_13_), channel_id=1, source_target_pairs={{0,1},{1,0},{2,3},{3,2},{4,5},{5,4},{6,7},{7,6},{8,9},{9,8},{10,11... | collective-permute-start | bytes 1867784 | tf_op jit(solution)/shard_map/ppermute | solution.py:249
  195.2 9.5 %collective-permute-start.37 = (f32[64,2432]{1,0:T(8,128)S(1)}, f32[64,2432]{1,0:T(8,128)S(1)}, u32[]{:S(2)}, u32[]{:S(2)}) collective-permute-start(f32[64,2432]{1,0:T(8,128)S(1)} %shard_map.113.refs_22_.refs_24_), channel_id=1, source_target_pairs={{0,1},{1,0},{2,3},{3,2},{4,5},{5,4},{6,7},{7,6},{8,9},{9,8},{10,11... | collective-permute-start | bytes 1867784 | tf_op jit(solution)/shard_map/ppermute | solution.py:249
  204.8 1.6 collective-permute-done.37.refs_23_
  207.3 5.7 %shard_map.114 = f32[256,4608]{1,0:T(8,128)} custom-call(s32[1]{0:T(128)} %bitcast.me_ref, f32[256,4608]{1,0:T(8,128)S(1)} %bitcast.4, f32[64,2432]{1,0:T(8,128)S(1)} %shard_map.80.refs_2_.refs_1_.refs_0_, f32[64,2432]{1,0:T(8,128)S(1)} %shard_map.100._.refs_1_, f32[64,2432]{1,0:T(8,128)S(1)} %collective-permute-done.24.refs_0_.refs_2_, ...), custom_call_target="tpu_custom_call" | custom-call | bytes 73800 | tf_op jit(solution)/shard_map/pallas_call | solution.py:622
  (100 shorter events, 24.4 us)
Async XLA Ops:
  1.3 1.9 copy-start
  6.6 32.2 %all-to-all-start = ((f32[8,72,384]{2,1,0:T(8,128)}), f32[8,72,384]{2,1,0:T(8,128)S(1)}, u32[]{:S(2)}, u32[]{:S(2)}) async-start(f32[8,72,384]{2,1,0:T(8,128)} %shard_map.68.refs_1_.pay_ref), calls=%async_computation | async-start | bytes 1769472 | tf_op jit(solution)/shard_map/all_to_all | solution.py:655
  27.8 9.4 %copy-start.1 = (f32[2,64,2048]{2,1,0:T(8,128)}, f32[2,64,2048]{2,1,0:T(8,128)S(1)}, u32[]{:S(2)}) copy-start(f32[2,64,2048]{2,1,0:T(8,128)S(1)} %get-tuple-element.36.refs_2_.refs_0_.refs_3_) | copy-start | bytes 3145732
  27.9 25.9 %collective-permute-start.3 = (f32[2,64,2048]{2,1,0:T(8,128)}, f32[2,64,2048]{2,1,0:T(8,128)}, u32[]{:S(2)}, u32[]{:S(2)}) collective-permute-start(f32[2,64,2048]{2,1,0:T(8,128)} %get-tuple-element.43), channel_id=1, source_target_pairs={{0,16},{8,24},{16,0},{24,8},{1,17},{9,25},{17,1},{25,9},{2,18},{10... | collective-permute-start | bytes 3145736 | tf_op jit(solution)/shard_map/ppermute | solution.py:249
  29.4 9.3 %copy-start.3 = (s32[12,256]{1,0:T(8,128)S(1)}, s32[12,256]{1,0:T(8,128)}, u32[]{:S(2)}) copy-start(s32[12,256]{1,0:T(8,128)} %code_ref.3) | copy-start | bytes 36868
  37.2 17.9 %copy-start.2 = (f32[2,64,1280]{2,1,0:T(8,128)}, f32[2,64,1280]{2,1,0:T(8,128)S(1)}, u32[]{:S(2)}) copy-start(f32[2,64,1280]{2,1,0:T(8,128)S(1)} %get-tuple-element.37._.refs_0_) | copy-start | bytes 1966084
  37.2 17.8 %collective-permute-start.2 = (f32[2,64,1280]{2,1,0:T(8,128)S(1)}, f32[2,64,1280]{2,1,0:T(8,128)}, u32[]{:S(2)}, u32[]{:S(2)}) collective-permute-start(f32[2,64,1280]{2,1,0:T(8,128)S(1)} %get-tuple-element.42), channel_id=1, source_target_pairs={{0,8},{8,0},{16,24},{24,16},{1,9},{9,1},{17,25},{25,17},{2,10},{10... | collective-permute-start | bytes 1966088 | tf_op jit(solution)/shard_map/ppermute | solution.py:249
  41.5 14.7 %collective-permute-start = (f32[72,256]{1,0:T(8,128)S(1)}, f32[72,256]{1,0:T(8,128)S(1)}, u32[]{:S(2)}, u32[]{:S(2)}) collective-permute-start(f32[72,256]{1,0:T(8,128)S(1)} %get-tuple-element.39), channel_id=1, source_target_pairs={{0,1},{1,2},{2,3},{3,4},{4,5},{5,6},{6,7},{8,9},{9,10},{10,11},{11... | collective-permute-start | bytes 221192 | tf_op jit(solution)/shard_map/ppermute | solution.py:686
  43.3 12.9 %collective-permute-start.1 = (f32[72,256]{1,0:T(8,128)S(1)}, f32[72,256]{1,0:T(8,128)S(1)}, u32[]{:S(2)}, u32[]{:S(2)}) collective-permute-start(f32[72,256]{1,0:T(8,128)S(1)} %get-tuple-element.40), channel_id=1, source_target_pairs={{1,0},{2,1},{3,2},{4,3},{5,4},{6,5},{7,6},{9,8},{10,9},{11,10},{12... | collective-permute-start | bytes 221192 | tf_op jit(solution)/shard_map/ppermute | solution.py:687
  60.4 27.8 %all-to-all-start.1 = ((f32[8,72,384]{2,1,0:T(8,128)}), f32[8,72,384]{2,1,0:T(8,128)S(1)}, u32[]{:S(2)}, u32[]{:S(2)}) async-start(f32[8,72,384]{2,1,0:T(8,128)} %shard_map.74.refs_7_), calls=%async_computation.1 | async-start | bytes 1769472 | tf_op jit(solution)/shard_map/all_to_all | solution.py:693
  65.1 14.3 %collective-permute-start.5 = (f32[1,64,2048]{2,1,0:T(8,128)S(1)}, f32[1,64,2048]{2,1,0:T(8,128)S(1)}, u32[]{:S(2)}, u32[]{:S(2)}) collective-permute-start(f32[1,64,2048]{2,1,0:T(8,128)S(1)} %shard_map.72.refs_2_), channel_id=1, source_target_pairs={{0,8},{8,0},{16,24},{24,16},{1,9},{9,1},{17,25},{25,17},{2,10},{10... | collective-permute-start | bytes 1572872 | tf_op jit(solution)/shard_map/ppermute | solution.py:249
  66.6 9.8 %collective-permute-start.4 = (f32[1,64,1280]{2,1,0:T(8,128)S(1)}, f32[1,64,1280]{2,1,0:T(8,128)S(1)}, u32[]{:S(2)}, u32[]{:S(2)}) collective-permute-start(f32[1,64,1280]{2,1,0:T(8,128)S(1)} %shard_map.73._), channel_id=1, source_target_pairs={{0,16},{8,24},{16,0},{24,8},{1,17},{9,25},{17,1},{25,9},{2,18},{10... | collective-permute-start | bytes 983048 | tf_op jit(solution)/shard_map/ppermute | solution.py:249
  76.5 3.0 %copy-start.6 = (f32[1,64,1280]{2,1,0:T(8,128)}, f32[1,64,1280]{2,1,0:T(8,128)S(1)}, u32[]{:S(2)}) copy-start(f32[1,64,1280]{2,1,0:T(8,128)S(1)} %collective-permute-done.4.refs_2_) | copy-start | bytes 983044
  88.2 0.9 copy-start.4
  92.0 19.1 %collective-permute-start.6 = (f32[64,3072]{1,0:T(8,128)S(1)}, f32[64,3072]{1,0:T(8,128)S(1)}, u32[]{:S(2)}, u32[]{:S(2)}) collective-permute-start(f32[64,3072]{1,0:T(8,128)S(1)} %shard_map.76.block_ref._.refs_6_.refs_0_), channel_id=1, source_target_pairs={{0,8},{8,0},{16,24},{24,16},{1,9},{9,1},{17,25},{25,17},{2,10},{10... | collective-permute-start | bytes 2359304 | tf_op jit(solution)/shard_map/ppermute | solution.py:249
  93.5 18.8 %collective-permute-start.7 = (f32[64,3072]{1,0:T(8,128)S(1)}, f32[64,3072]{1,0:T(8,128)S(1)}, u32[]{:S(2)}, u32[]{:S(2)}) collective-permute-start(f32[64,3072]{1,0:T(8,128)S(1)} %shard_map.76.block_ref._.refs_6_.refs_0_), channel_id=1, source_target_pairs={{0,16},{8,24},{16,0},{24,8},{1,17},{9,25},{17,1},{25,9},{2,18},{10... | collective-permute-start | bytes 2359304 | tf_op jit(solution)/shard_map/ppermute | solution.py:249
  105.2 7.2 %collective-permute-start.11 = (f32[64,2432]{1,0:T(8,128)S(1)}, f32[64,2432]{1,0:T(8,128)S(1)}, u32[]{:S(2)}, u32[]{:S(2)}) collective-permute-start(f32[64,2432]{1,0:T(8,128)S(1)} %get-tuple-element.55.refs_0_), channel_id=1, source_target_pairs={{0,1},{1,0},{2,3},{3,2},{4,5},{5,4},{6,7},{7,6},{8,9},{9,8},{10,11... | collective-permute-start | bytes 1867784 | tf_op jit(solution)/shard_map/ppermute | solution.py:249
  105.3 10.9 %collective-permute-start.10 = (f32[64,2432]{1,0:T(8,128)S(1)}, f32[64,2432]{1,0:T(8,128)S(1)}, u32[]{:S(2)}, u32[]{:S(2)}) collective-permute-start(f32[64,2432]{1,0:T(8,128)S(1)} %get-tuple-element.46.refs_2_.refs_0_), channel_id=1, source_target_pairs={{0,1},{1,0},{2,3},{3,2},{4,5},{5,4},{6,7},{7,6},{8,9},{9,8},{10,11... | collective-permute-start | bytes 1867784 | tf_op jit(solution)/shard_map/ppermute | solution.py:249
  112.5 13.4 %collective-permute-start.15 = (f32[64,2432]{1,0:T(8,128)S(1)}, f32[64,2432]{1,0:T(8,128)S(1)}, u32[]{:S(2)}, u32[]{:S(2)}) collective-permute-start(f32[64,2432]{1,0:T(8,128)S(1)} %shard_map.80.refs_2_.refs_1_.refs_0_), channel_id=1, source_target_pairs={{0,2},{7,5},{8,10},{15,13},{16,18},{23,21},{24,26},{31,29}} | collective-permute-start | bytes 1867784 | tf_op jit(solution)/shard_map/ppermute | solution.py:523
  114.0 8.7 %collective-permute-start.8 = (f32[64,1536]{1,0:T(8,128)S(1)}, f32[64,1536]{1,0:T(8,128)S(1)}, u32[]{:S(2)}, u32[]{:S(2)}) collective-permute-start(f32[64,1536]{1,0:T(8,128)S(1)} %get-tuple-element.47), channel_id=1, source_target_pairs={{0,8},{8,0},{16,24},{24,16},{1,9},{9,1},{17,25},{25,17},{2,10},{10... | collective-permute-start | bytes 1179656 | tf_op jit(solution)/shard_map/ppermute | solution.py:249
  114.6 10.6 %collective-permute-start.9 = (f32[64,1536]{1,0:T(8,128)S(1)}, f32[64,1536]{1,0:T(8,128)S(1)}, u32[]{:S(2)}, u32[]{:S(2)}) collective-permute-start(f32[64,1536]{1,0:T(8,128)S(1)} %get-tuple-element.48.refs_2_), channel_id=1, source_target_pairs={{0,16},{8,24},{16,0},{24,8},{1,17},{9,25},{17,1},{25,9},{2,18},{10... | collective-permute-start | bytes 1179656 | tf_op jit(solution)/shard_map/ppermute | solution.py:249
  116.2 12.2 %collective-permute-start.12 = (f32[64,2432]{1,0:T(8,128)S(1)}, f32[64,2432]{1,0:T(8,128)S(1)}, u32[]{:S(2)}, u32[]{:S(2)}) collective-permute-start(f32[64,2432]{1,0:T(8,128)S(1)} %shard_map.81.refs_9_.refs_1_.refs_2_.refs_3_), channel_id=1, source_target_pairs={{0,2},{7,5},{8,10},{15,13},{16,18},{23,21},{24,26},{31,29}} | collective-permute-start | bytes 1867784 | tf_op jit(solution)/shard_map/ppermute | solution.py:523
  120.4 8.1 %collective-permute-start.16 = (f32[64,2432]{1,0:T(8,128)S(1)}, f32[64,2432]{1,0:T(8,128)S(1)}, u32[]{:S(2)}, u32[]{:S(2)}) collective-permute-start(f32[64,2432]{1,0:T(8,128)S(1)} %get-tuple-element.59.refs_0_), channel_id=1, source_target_pairs={{0,1},{1,0},{2,3},{3,2},{4,5},{5,4},{6,7},{7,6},{8,9},{9,8},{10,11... | collective-permute-start | bytes 1867784 | tf_op jit(solution)/shard_map/ppermute | solution.py:249
  122.7 5.7 %collective-permute-start.17 = (f32[64,2432]{1,0:T(8,128)S(1)}, f32[64,2432]{1,0:T(8,128)S(1)}, u32[]{:S(2)}, u32[]{:S(2)}) collective-permute-start(f32[64,2432]{1,0:T(8,128)S(1)} %get-tuple-element.56.refs_9_.refs_1_), channel_id=1, source_target_pairs={{0,1},{1,0},{2,3},{3,2},{4,5},{5,4},{6,7},{7,6},{8,9},{9,8},{10,11... | collective-permute-start | bytes 1867784 | tf_op jit(solution)/shard_map/ppermute | solution.py:249
  125.2 8.4 %collective-permute-start.13 = (f32[64,2432]{1,0:T(8,128)S(1)}, f32[64,2432]{1,0:T(8,128)S(1)}, u32[]{:S(2)}, u32[]{:S(2)}) collective-permute-start(f32[64,2432]{1,0:T(8,128)S(1)} %get-tuple-element.58.refs_0_), channel_id=1, source_target_pairs={{0,1},{1,0},{2,3},{3,2},{4,5},{5,4},{6,7},{7,6},{8,9},{9,8},{10,11... | collective-permute-start | bytes 1867784 | tf_op jit(solution)/shard_map/ppermute | solution.py:249
  125.8 7.8 %collective-permute-start.14 = (f32[64,2432]{1,0:T(8,128)S(1)}, f32[64,2432]{1,0:T(8,128)S(1)}, u32[]{:S(2)}, u32[]{:S(2)}) collective-permute-start(f32[64,2432]{1,0:T(8,128)S(1)} %get-tuple-element.57.refs_2_.refs_1_), channel_id=1, source_target_pairs={{0,1},{1,0},{2,3},{3,2},{4,5},{5,4},{6,7},{7,6},{8,9},{9,8},{10,11... | collective-permute-start | bytes 1867784 | tf_op jit(solution)/shard_map/ppermute | solution.py:249
  129.1 13.4 %collective-permute-start.19 = (f32[64,2432]{1,0:T(8,128)S(1)}, f32[64,2432]{1,0:T(8,128)S(1)}, u32[]{:S(2)}, u32[]{:S(2)}) collective-permute-start(f32[64,2432]{1,0:T(8,128)S(1)} %shard_map.88.refs_4_), channel_id=1, source_target_pairs={{0,2},{2,4},{7,5},{5,3},{8,10},{10,12},{15,13},{13,11},{16,18},{18... | collective-permute-start | bytes 1867784 | tf_op jit(solution)/shard_map/ppermute | solution.py:542
  134.4 13.6 %collective-permute-start.18 = (f32[64,2432]{1,0:T(8,128)S(1)}, f32[64,2432]{1,0:T(8,128)S(1)}, u32[]{:S(2)}, u32[]{:S(2)}) collective-permute-start(f32[64,2432]{1,0:T(8,128)S(1)} %shard_map.90.refs_10_), channel_id=1, source_target_pairs={{0,2},{2,4},{7,5},{5,3},{8,10},{10,12},{15,13},{13,11},{16,18},{18... | collective-permute-start | bytes 1867784 | tf_op jit(solution)/shard_map/ppermute | solution.py:542
  139.4 13.7 %collective-permute-start.23 = (f32[64,2432]{1,0:T(8,128)S(1)}, f32[64,2432]{1,0:T(8,128)S(1)}, u32[]{:S(2)}, u32[]{:S(2)}) collective-permute-start(f32[64,2432]{1,0:T(8,128)S(1)} %shard_map.91.refs_10_.refs_0_), channel_id=1, source_target_pairs={{0,1},{1,0},{2,3},{3,2},{4,5},{5,4},{6,7},{7,6},{8,9},{9,8},{10,11... | collective-permute-start | bytes 1867784 | tf_op jit(solution)/shard_map/ppermute | solution.py:249
  143.2 11.5 %collective-permute-start.22 = (f32[64,2432]{1,0:T(8,128)S(1)}, f32[64,2432]{1,0:T(8,128)S(1)}, u32[]{:S(2)}, u32[]{:S(2)}) collective-permute-start(f32[64,2432]{1,0:T(8,128)S(1)} %shard_map.93._), channel_id=1, source_target_pairs={{0,2},{2,4},{4,6},{7,5},{5,3},{3,1},{8,10},{10,12},{12,14},{15,13}... | collective-permute-start | bytes 1867784 | tf_op jit(solution)/shard_map/ppermute | solution.py:542
  146.4 13.3 %collective-permute-start.21 = (f32[64,2432]{1,0:T(8,128)S(1)}, f32[64,2432]{1,0:T(8,128)S(1)}, u32[]{:S(2)}, u32[]{:S(2)}) collective-permute-start(f32[64,2432]{1,0:T(8,128)S(1)} %shard_map.92._.refs_0_), channel_id=1, source_target_pairs={{0,1},{1,0},{2,3},{3,2},{4,5},{5,4},{6,7},{7,6},{8,9},{9,8},{10,11... | collective-permute-start | bytes 1867784 | tf_op jit(solution)/shard_map/ppermute | solution.py:249
  148.6 12.7 %collective-permute-start.20 = (f32[64,2432]{1,0:T(8,128)S(1)}, f32[64,2432]{1,0:T(8,128)S(1)}, u32[]{:S(2)}, u32[]{:S(2)}) collective-permute-start(f32[64,2432]{1,0:T(8,128)S(1)} %shard_map.94.refs_2_), channel_id=1, source_target_pairs={{0,2},{2,4},{4,6},{7,5},{5,3},{3,1},{8,10},{10,12},{12,14},{15,13}... | collective-permute-start | bytes 1867784 | tf_op jit(solution)/shard_map/ppermute | solution.py:542
  155.3 17.1 %collective-permute-start.27 = (f32[64,2432]{1,0:T(8,128)S(1)}, f32[64,2432]{1,0:T(8,128)S(1)}, u32[]{:S(2)}, u32[]{:S(2)}) collective-permute-start(f32[64,2432]{1,0:T(8,128)S(1)} %shard_map.96.refs_2_), channel_id=1, source_target_pairs={{0,2},{2,4},{4,6},{7,5},{5,3},{3,1},{8,10},{10,12},{12,14},{15,13}... | collective-permute-start | bytes 1867784 | tf_op jit(solution)/shard_map/ppermute | solution.py:542
  161.9 12.7 %collective-permute-start.26 = (f32[64,2432]{1,0:T(8,128)S(1)}, f32[64,2432]{1,0:T(8,128)S(1)}, u32[]{:S(2)}, u32[]{:S(2)}) collective-permute-start(f32[64,2432]{1,0:T(8,128)S(1)} %shard_map.98.refs_4_), channel_id=1, source_target_pairs={{0,2},{2,4},{4,6},{7,5},{5,3},{3,1},{8,10},{10,12},{12,14},{15,13}... | collective-permute-start | bytes 1867784 | tf_op jit(solution)/shard_map/ppermute | solution.py:542
  171.8 4.1 %collective-permute-start.25 = (f32[64,2432]{1,0:T(8,128)S(1)}, f32[64,2432]{1,0:T(8,128)S(1)}, u32[]{:S(2)}, u32[]{:S(2)}) collective-permute-start(f32[64,2432]{1,0:T(8,128)S(1)} %shard_map.101._.refs_4_), channel_id=1, source_target_pairs={{0,1},{1,0},{2,3},{3,2},{4,5},{5,4},{6,7},{7,6},{8,9},{9,8},{10,11... | collective-permute-start | bytes 1867784 | tf_op jit(solution)/shard_map/ppermute | solution.py:249
  171.9 4.1 %collective-permute-start.24 = (f32[64,2432]{1,0:T(8,128)S(1)}, f32[64,2432]{1,0:T(8,128)S(1)}, u32[]{:S(2)}, u32[]{:S(2)}) collective-permute-start(f32[64,2432]{1,0:T(8,128)S(1)} %shard_map.100._.refs_1_), channel_id=1, source_target_pairs={{0,1},{1,0},{2,3},{3,2},{4,5},{5,4},{6,7},{7,6},{8,9},{9,8},{10,11... | collective-permute-start | bytes 1867784 | tf_op jit(solution)/shard_map/ppermute | solution.py:249
  172.9 5.0 %collective-permute-start.31 = (f32[64,2432]{1,0:T(8,128)S(1)}, f32[64,2432]{1,0:T(8,128)S(1)}, u32[]{:S(2)}, u32[]{:S(2)}) collective-permute-start(f32[64,2432]{1,0:T(8,128)S(1)} %shard_map.102._), channel_id=1, source_target_pairs={{2,4},{4,6},{5,3},{3,1},{10,12},{12,14},{13,11},{11,9},{18,20},{20... | collective-permute-start | bytes 1867784 | tf_op jit(solution)/shard_map/ppermute | solution.py:542
  175.2 3.9 %collective-permute-start.30 = (f32[64,2432]{1,0:T(8,128)S(1)}, f32[64,2432]{1,0:T(8,128)S(1)}, u32[]{:S(2)}, u32[]{:S(2)}) collective-permute-start(f32[64,2432]{1,0:T(8,128)S(1)} %shard_map.103.refs_2_), channel_id=1, source_target_pairs={{2,4},{4,6},{5,3},{3,1},{10,12},{12,14},{13,11},{11,9},{18,20},{20... | collective-permute-start | bytes 1867784 | tf_op jit(solution)/shard_map/ppermute | solution.py:542
  177.2 3.2 %collective-permute-start.29 = (f32[64,2432]{1,0:T(8,128)S(1)}, f32[64,2432]{1,0:T(8,128)S(1)}, u32[]{:S(2)}, u32[]{:S(2)}) collective-permute-start(f32[64,2432]{1,0:T(8,128)S(1)} %shard_map.106._.refs_10_), channel_id=1, source_target_pairs={{0,1},{1,0},{2,3},{3,2},{4,5},{5,4},{6,7},{7,6},{8,9},{9,8},{10,11... | collective-permute-start | bytes 1867784 | tf_op jit(solution)/shard_map/ppermute | solution.py:249
  177.8 2.6 %collective-permute-start.28 = (f32[64,2432]{1,0:T(8,128)S(1)}, f32[64,2432]{1,0:T(8,128)S(1)}, u32[]{:S(2)}, u32[]{:S(2)}) collective-permute-start(f32[64,2432]{1,0:T(8,128)S(1)} %shard_map.105._.refs_7_), channel_id=1, source_target_pairs={{0,1},{1,0},{2,3},{3,2},{4,5},{5,4},{6,7},{7,6},{8,9},{9,8},{10,11... | collective-permute-start | bytes 1867784 | tf_op jit(solution)/shard_map/ppermute | solution.py:249
  178.5 15.5 %collective-permute-start.34 = (f32[64,2432]{1,0:T(8,128)S(1)}, f32[64,2432]{1,0:T(8,128)S(1)}, u32[]{:S(2)}, u32[]{:S(2)}) collective-permute-start(f32[64,2432]{1,0:T(8,128)S(1)} %shard_map.107._), channel_id=1, source_target_pairs={{4,6},{3,1},{12,14},{11,9},{20,22},{19,17},{28,30},{27,25}} | collective-permute-start | bytes 1867784 | tf_op jit(solution)/shard_map/ppermute | solution.py:542
  179.7 14.9 %collective-permute-start.36 = (f32[64,2432]{1,0:T(8,128)S(1)}, f32[64,2432]{1,0:T(8,128)S(1)}, u32[]{:S(2)}, u32[]{:S(2)}) collective-permute-start(f32[64,2432]{1,0:T(8,128)S(1)} %shard_map.108.refs_2_), channel_id=1, source_target_pairs={{4,6},{3,1},{12,14},{11,9},{20,22},{19,17},{28,30},{27,25}} | collective-permute-start | bytes 1867784 | tf_op jit(solution)/shard_map/ppermute | solution.py:542
  180.5 26.8 %slice-start = ((s8[4718592]{0:T(1024)(128)(4,1)}), s8[4194304]{0:T(1024)(128)(4,1)S(1)}, s32[]{:S(2)}) async-start(s8[4718592]{0:T(1024)(128)(4,1)} %bitcast.3), calls=%async_computation.2 | async-start | bytes 8388608
  181.1 26.2 %slice-start.1 = ((s8[4718592]{0:T(1024)(128)(4,1)}), s8[524288]{0:T(1024)(128)(4,1)S(1)}, s32[]{:S(2)}) async-start(s8[4718592]{0:T(1024)(128)(4,1)} %bitcast.3), calls=%async_computation.3 | async-start | bytes 1048576
  181.1 23.7 %collective-permute-start.32 = (f32[64,2432]{1,0:T(8,128)S(1)}, f32[64,2432]{1,0:T(8,128)S(1)}, u32[]{:S(2)}, u32[]{:S(2)}) collective-permute-start(f32[64,2432]{1,0:T(8,128)S(1)} %shard_map.110._.refs_13_), channel_id=1, source_target_pairs={{0,1},{1,0},{2,3},{3,2},{4,5},{5,4},{6,7},{7,6},{8,9},{9,8},{10,11... | collective-permute-start | bytes 1867784 | tf_op jit(solution)/shard_map/ppermute | solution.py:249
  193.9 10.9 %collective-permute-start.33 = (f32[64,2432]{1,0:T(8,128)S(1)}, f32[64,2432]{1,0:T(8,128)S(1)}, u32[]{:S(2)}, u32[]{:S(2)}) collective-permute-start(f32[64,2432]{1,0:T(8,128)S(1)} %shard_map.111._.refs_16_), channel_id=1, source_target_pairs={{0,1},{1,0},{2,3},{3,2},{4,5},{5,4},{6,7},{7,6},{8,9},{9,8},{10,11... | collective-permute-start | bytes 1867784 | tf_op jit(solution)/shard_map/ppermute | solution.py:249
  195.2 11.2 %collective-permute-start.37 = (f32[64,2432]{1,0:T(8,128)S(1)}, f32[64,2432]{1,0:T(8,128)S(1)}, u32[]{:S(2)}, u32[]{:S(2)}) collective-permute-start(f32[64,2432]{1,0:T(8,128)S(1)} %shard_map.113.refs_22_.refs_24_), channel_id=1, source_target_pairs={{0,1},{1,0},{2,3},{3,2},{4,5},{5,4},{6,7},{7,6},{8,9},{9,8},{10,11... | collective-permute-start | bytes 1867784 | tf_op jit(solution)/shard_map/ppermute | solution.py:249
  204.7 2.6 %collective-permute-start.35 = (f32[64,2432]{1,0:T(8,128)S(1)}, f32[64,2432]{1,0:T(8,128)S(1)}, u32[]{:S(2)}, u32[]{:S(2)}) collective-permute-start(f32[64,2432]{1,0:T(8,128)S(1)} %shard_map.112._.refs_19_), channel_id=1, source_target_pairs={{0,1},{1,0},{2,3},{3,2},{4,5},{5,4},{6,7},{7,6},{8,9},{9,8},{10,11... | collective-permute-start | bytes 1867784 | tf_op jit(solution)/shard_map/ppermute | solution.py:249
  (1 other events, 0.8 us)

commit v6 on v5

--- a/solution.py
+++ b/solution.py
@@ -776,12 +776,12 @@
             both(product, g)
             if g + 1 < len(groups):
                 token = come_on(groups[g + 1], token)
-        if t == chunks - 1:
+        if t == last_slot - 1:
             factors_new, token = turned_back([blocks[k] for k in ids], ids, width, me1, token)
-        c = t - (line - 1)
-        if c - 1 in ends[0]:
-            token = awaited([ends[half][c - 1][1] for half in range(HALVES)], token)
-        if 0 <= c < chunks:
+        due = range(1) if t == last_slot - 1 else range(1, t - line + 2) if t == last_slot else []
+        for c in due:
+            if c - 1 in ends[0]:
+                token = awaited([ends[half][c - 1][1] for half in range(HALVES)], token)
             both(end, c)
     rest = [c for c in range(chunks) if c not in ends[0]]
     for c in rest:

time: 214 us -> 220 us (1.028)
  waiting for transfers between devices: 41.3 us -> 51 us
  starting transfers between devices: 79.1 us -> 75.3 us
    ppermute x10, waiting for transfers between devices: 5.58 us -> 11.6 us  [line_slot(): return (lax.ppermute(send, 'bin', hops), send)]
    ppermute x24, starting transfers between devices: 35.8 us -> 32 us  [swap(): lax.ppermute(block, axis, [(i, i ^ bit) for i in range(lax.axis_size(axis...]
    ppermute x24, waiting for transfers between devices: 31.6 us -> 35.3 us  [swap(): lax.ppermute(block, axis, [(i, i ^ bit) for i in range(lax.axis_size(axis...]
  transfers between devices with their start and end apart: 40 -> 40, of which waited for: 14 -> 21; matrix products, arithmetic and copies ran while one was open for 0% -> 0% of each run, Pallas kernels for 33% -> 31%
where the time goes in v6:
time: 220 us; the launch traced here: 219 us
  Pallas kernels  87.1 us (40%)
  starting transfers between devices  75.3 us (34%)
  waiting for transfers between devices  51 us (23%)
  local copies, waits for them, and re-layouts  3.61 us (2%)
    ppermute x24, waiting for transfers between devices, swap(): lax.ppermute(block, axis, [(i, i ^ bit) for i in range(lax.axis_size(axis...  35.3 us
    ppermute x24, starting transfers between devices, swap(): lax.ppermute(block, axis, [(i, i ^ bit) for i in range(lax.axis_size(axis...  32 us
    ppermute x10, starting transfers between devices, line_slot(): return (lax.ppermute(send, 'bin', hops), send)  25.8 us
    pallas_call x2, Pallas kernels, numer_part(): kernel_call(body, outs, 7, limit=40, in_specs=[SMEM_SPEC, ANY_SPEC] + [AN...  22.6 us
    ppermute x10, waiting for transfers between devices, line_slot(): return (lax.ppermute(send, 'bin', hops), send)  11.6 us
    pallas_call x4, Pallas kernels, cross_part(): kernel_call(body, (shape(width, cols + extra),) * n, 0.02, limit=8, in_sp...  11.2 us
    pallas_call x1, Pallas kernels, first_cross(): kernel_call(body, (shape(width, cols + extra),) * HALVES + (pltpu.VMEM((s...  10.2 us
    all_to_all x1, starting transfers between devices, on_device(): lax.all_to_all(payload, 'bin', split_axis=0, concat_axis=0, tiled=True)  6.33 us
  transfers between devices with their start and end apart: 40, of which 21 were waited for; matrix products, arithmetic and copies ran while one was open for 0% of the time, Pallas kernels for 31%

profile of v6, /device:TPU:0, one launch (start us, length us, event | category | flops | bytes accessed | tf_op | source)
XLA Modules:
  0.0 219.0 jit_solution(1334246675821366815)
XLA Ops:
  1.3 1.9 copy-done
  3.2 3.4 %shard_map.68.refs_1_.pay_ref = f32[8,72,384]{2,1,0:T(8,128)} custom-call(s32[1]{0:T(128)} %bitcast.me_ref, f32[3072,256]{1,0:T(8,128)S(1)} %copy-done, f32[8,1,384]{2,1,0:T(1,128)S(1)} %bitcast.5), custom_call_target="tpu_custom_call" | custom-call | bytes 11070000 | tf_op jit(solution)/shard_map/pallas_call | solution.py:64
  6.6 6.3 %all-to-all-start = ((f32[8,72,384]{2,1,0:T(8,128)}), f32[8,72,384]{2,1,0:T(8,128)S(1)}, u32[]{:S(2)}, u32[]{:S(2)}) async-start(f32[8,72,384]{2,1,0:T(8,128)} %shard_map.68.refs_1_.pay_ref), calls=%async_computation | async-start | bytes 1769472 | tf_op jit(solution)/shard_map/all_to_all | solution.py:655
  12.9 14.9 %shard_map.69 = (f32[2,64,2048]{2,1,0:T(8,128)}, f32[2,64,2048]{2,1,0:T(8,128)S(1)}, bf16[4608,256]{1,0:T(8,128)(2,1)S(1)}, f32[256,256]{1,0:T(8,128)S(1)}) custom-call(s32[1]{0:T(128)} %bitcast.me_ref, bf16[3072,4608]{1,0:T(8,128)(2,1)} %counts_ref.5, f32[256,4608]{1,0:T(8,128)} %load_ref.1, f32[8,72,384]{2,1,0:T(8,128)} %shard_map.68.refs_1_.pay_ref), custom_call_target="tpu_custom_call" | custom-call | bytes 25830000 | tf_op jit(solution)/shard_map/pallas_call | solution.py:235
  27.9 1.6 collective-permute-start.3
  29.4 7.7 %shard_map.70 = (f32[2,64,1280]{2,1,0:T(8,128)S(1)}, f32[2,64,1280]{2,1,0:T(8,128)S(1)}) custom-call(s32[1]{0:T(128)} %bitcast.me_ref, bf16[3072,4608]{1,0:T(8,128)(2,1)} %counts_ref.5, bf16[4608,256]{1,0:T(8,128)(2,1)S(1)} %get-tuple-element.34.refs_0_, f32[256,256]{1,0:T(8,128)S(1)} %get-tuple-element.35.refs_1_, ...), custom_call_target="tpu_custom_call" | custom-call | bytes 25830000 | tf_op jit(solution)/shard_map/pallas_call | solution.py:235
  37.2 1.6 collective-permute-start.2
  38.8 2.7 %shard_map.71 = (f32[12,72,256]{2,1,0:T(8,128)S(1)}, f32[72,256]{1,0:T(8,128)S(1)}, f32[72,256]{1,0:T(8,128)S(1)}, s32[1,3072]{1,0:T(1,128)S(1)}) custom-call(s32[1]{0:T(128)} %bitcast.2.me_ref, f32[8,72,384]{2,1,0:T(8,128)S(1)} %all-to-all-done.got_ref, s32[12,256]{1,0:T(8,128)S(1)} %copy-done.3, f32[2,64,1280]{2,1,0:T(8,128)S(1)} %get-tuple-element.37._.refs_0_), custom_call_target="tpu_custom_call" | custom-call | bytes 11070000 | tf_op jit(solution)/shard_map/pallas_call | solution.py:106
  41.5 1.9 collective-permute-start
  43.3 1.5 collective-permute-start.1
  44.8 9.0 %collective-permute-done.3.refs_1_.refs_4_ = f32[2,64,2048]{2,1,0:T(8,128)} collective-permute-done((f32[2,64,2048]{2,1,0:T(8,128)}, f32[2,64,2048]{2,1,0:T(8,128)}, u32[]{:S(2)}, u32[]{:S(2)}) %collective-permute-start.3) | collective-permute-done | bytes 1048608 | tf_op jit(solution)/shard_map/ppermute | solution.py:249
  56.2 4.2 %shard_map.74.refs_7_ = f32[8,72,384]{2,1,0:T(8,128)} custom-call(f32[12,72,256]{2,1,0:T(8,128)S(1)} %get-tuple-element.38.refs_2_.grid_ref, f32[72,256]{1,0:T(8,128)S(1)} %collective-permute-done.above_ref, f32[72,256]{1,0:T(8,128)S(1)} %collective-permute-done.1.below_ref, s32[1,3072]{1,0:T(1,128)S(1)} %get-tuple-element.41.cell_ref, ...), custom_call_target="tpu_custom_call" | custom-call | bytes 14760000 | tf_op jit(solution)/shard_map/pallas_call | solution.py:155
  60.4 4.7 %all-to-all-start.1 = ((f32[8,72,384]{2,1,0:T(8,128)}), f32[8,72,384]{2,1,0:T(8,128)S(1)}, u32[]{:S(2)}, u32[]{:S(2)}) async-start(f32[8,72,384]{2,1,0:T(8,128)} %shard_map.74.refs_7_), calls=%async_computation.1 | async-start | bytes 1769472 | tf_op jit(solution)/shard_map/all_to_all | solution.py:693
  65.1 1.5 collective-permute-start.5
  66.6 1.5 collective-permute-start.4
  68.1 8.3 %collective-permute-done.4.refs_2_ = f32[1,64,1280]{2,1,0:T(8,128)S(1)} collective-permute-done((f32[1,64,1280]{2,1,0:T(8,128)S(1)}, f32[1,64,1280]{2,1,0:T(8,128)S(1)}, u32[]{:S(2)}, u32[]{:S(2)}) %collective-permute-start.4) | collective-permute-done | bytes 327712 | tf_op jit(solution)/shard_map/ppermute | solution.py:249
  76.5 3.0 %collective-permute-done.5.refs_5_ = f32[1,64,2048]{2,1,0:T(8,128)S(1)} collective-permute-done((f32[1,64,2048]{2,1,0:T(8,128)S(1)}, f32[1,64,2048]{2,1,0:T(8,128)S(1)}, u32[]{:S(2)}, u32[]{:S(2)}) %collective-permute-start.5) | collective-permute-done | bytes 524320 | tf_op jit(solution)/shard_map/ppermute | solution.py:249
  80.2 6.2 %shard_map.75 = (f32[64,3072]{1,0:T(8,128)}, f32[64,3072]{1,0:T(8,128)}) custom-call(f32[2,64,1280]{2,1,0:T(8,128)} %copy-done.2, f32[2,64,1280]{2,1,0:T(8,128)} %collective-permute-done.2.refs_1_, f32[1,64,1280]{2,1,0:T(8,128)} %copy-done.6, f32[2,64,2048]{2,1,0:T(8,128)} %copy-done.1, f32[2,64,2048]{2,1,0:T(8,128)} %collective-permute-done.3.refs_1_.refs_4_, ...), custom_call_target="tpu_custom_call" | custom-call | bytes 14760000 | tf_op jit(solution)/shard_map/pallas_call | solution.py:303
  86.5 1.7 all-to-all-done.1.back_ref
  89.1 2.8 %shard_map.76.block_ref._.refs_6_.refs_0_ = f32[64,3072]{1,0:T(8,128)S(1)} custom-call(f32[8,72,384]{2,1,0:T(8,128)} %shard_map.68.refs_1_.pay_ref, f32[8,72,384]{2,1,0:T(8,128)} %copy-done.4, f32[64,3072]{1,0:T(8,128)} %get-tuple-element.44.numer_ref, f32[64,3072]{1,0:T(8,128)} %get-tuple-element.45.plain_ref), custom_call_target="tpu_custom_call" | custom-call | bytes 73800 | tf_op jit(solution)/shard_map/pallas_call | solution.py:330
  92.0 1.6 collective-permute-start.6
  93.5 1.5 collective-permute-start.7
  95.0 10.2 %shard_map.77 = (f32[64,2432]{1,0:T(8,128)S(1)}, f32[64,2432]{1,0:T(8,128)S(1)}, bf16[512,4608]{1,0:T(8,128)(2,1)S(1)}, bf16[512,4608]{1,0:T(8,128)(2,1)S(1)}, b...) custom-call(bf16[3072,4608]{1,0:T(8,128)(2,1)} %counts_ref.5, ...), custom_call_target="tpu_custom_call" | custom-call | bytes 73800 | tf_op jit(solution)/shard_map/pallas_call | solution.py:441
  105.8 5.3 %collective-permute-done.6.refs_0_.refs_1_.refs_7_ = f32[64,3072]{1,0:T(8,128)S(1)} collective-permute-done((f32[64,3072]{1,0:T(8,128)S(1)}, f32[64,3072]{1,0:T(8,128)S(1)}, u32[]{:S(2)}, u32[]{:S(2)}) %collective-permute-start.6) | collective-permute-done | bytes 786464 | tf_op jit(solution)/shard_map/ppermute | solution.py:249
  112.5 1.6 collective-permute-start.15
  114.6 1.5 collective-permute-start.9
  116.2 1.5 collective-permute-start.12
  117.8 2.5 %shard_map.82 = (f32[64,2432]{1,0:T(8,128)S(1)}, f32[64,2432]{1,0:T(8,128)S(1)}) custom-call(bf16[512,4608]{1,0:T(8,128)(2,1)S(1)} %get-tuple-element.49.refs_0_, bf16[512,4608]{1,0:T(8,128)(2,1)S(1)} %get-tuple-element.50.refs_1_, bf16[512,4608]{1,0:T(8,128)(2,1)S(1)} %get-tuple-element.51.refs_2_, bf16[512,4608]{1,0:T(8,128)(2,1)S(1)} %get-tuple-element.52.refs_3_, ...), custom_call_target="tpu_custom_call" | custom-call | bytes 73800 | tf_op jit(solution)/shard_map/pallas_call | solution.py:480
  120.4 2.3 %collective-permute-done.8.refs_0_ = f32[64,1536]{1,0:T(8,128)S(1)} collective-permute-done((f32[64,1536]{1,0:T(8,128)S(1)}, f32[64,1536]{1,0:T(8,128)S(1)}, u32[]{:S(2)}, u32[]{:S(2)}) %collective-permute-start.8) | collective-permute-done | bytes 393248 | tf_op jit(solution)/shard_map/ppermute | solution.py:249
  122.7 2.5 %shard_map.83 = (f32[64,2432]{1,0:T(8,128)S(1)}, f32[64,2432]{1,0:T(8,128)S(1)}) custom-call(bf16[512,4608]{1,0:T(8,128)(2,1)S(1)} %get-tuple-element.49.refs_0_, bf16[512,4608]{1,0:T(8,128)(2,1)S(1)} %get-tuple-element.50.refs_1_, bf16[512,4608]{1,0:T(8,128)(2,1)S(1)} %get-tuple-element.51.refs_2_, bf16[512,4608]{1,0:T(8,128)(2,1)S(1)} %get-tuple-element.52.refs_3_, ...), custom_call_target="tpu_custom_call" | custom-call | bytes 73800 | tf_op jit(solution)/shard_map/pallas_call | solution.py:480
  126.0 2.4 %collective-permute-done.12.refs_0_.come_ref = f32[64,2432]{1,0:T(8,128)S(1)} collective-permute-done((f32[64,2432]{1,0:T(8,128)S(1)}, f32[64,2432]{1,0:T(8,128)S(1)}, u32[]{:S(2)}, u32[]{:S(2)}) %collective-permute-start.12) | collective-permute-done | bytes 622624 | tf_op jit(solution)/shard_map/ppermute | solution.py:523
  129.1 4.5 %collective-permute-start.19 = (f32[64,2432]{1,0:T(8,128)S(1)}, f32[64,2432]{1,0:T(8,128)S(1)}, u32[]{:S(2)}, u32[]{:S(2)}) collective-permute-start(f32[64,2432]{1,0:T(8,128)S(1)} %shard_map.88.refs_4_), channel_id=1, source_target_pairs={{0,2},{2,4},{7,5},{5,3},{8,10},{10,12},{15,13},{13,11},{16,18},{18... | collective-permute-start | bytes 1867784 | tf_op jit(solution)/shard_map/ppermute | solution.py:542
  134.4 1.9 collective-permute-start.18
  136.3 3.1 %shard_map.91.refs_10_.refs_0_ = f32[64,2432]{1,0:T(8,128)S(1)} custom-call(bf16[512,4608]{1,0:T(8,128)(2,1)S(1)} %get-tuple-element.49.refs_0_, bf16[512,4608]{1,0:T(8,128)(2,1)S(1)} %get-tuple-element.50.refs_1_, bf16[512,4608]{1,0:T(8,128)(2,1)S(1)} %get-tuple-element.51.refs_2_, bf16[512,4608]{1,0:T(8,128)(2,1)S(1)} %get-tuple-element.52.refs_3_, ...), custom_call_target="tpu_custom_call" | custom-call | bytes 73800 | tf_op jit(solution)/shard_map/pallas_call | solution.py:480
  139.5 3.1 %shard_map.92._.refs_0_ = f32[64,2432]{1,0:T(8,128)S(1)} custom-call(bf16[512,4608]{1,0:T(8,128)(2,1)S(1)} %get-tuple-element.49.refs_0_, bf16[512,4608]{1,0:T(8,128)(2,1)S(1)} %get-tuple-element.50.refs_1_, bf16[512,4608]{1,0:T(8,128)(2,1)S(1)} %get-tuple-element.51.refs_2_, bf16[512,4608]{1,0:T(8,128)(2,1)S(1)} %get-tuple-element.52.refs_3_, ...), custom_call_target="tpu_custom_call" | custom-call | bytes 73800 | tf_op jit(solution)/shard_map/pallas_call | solution.py:480
  143.2 3.2 %collective-permute-start.22 = (f32[64,2432]{1,0:T(8,128)S(1)}, f32[64,2432]{1,0:T(8,128)S(1)}, u32[]{:S(2)}, u32[]{:S(2)}) collective-permute-start(f32[64,2432]{1,0:T(8,128)S(1)} %shard_map.93._), channel_id=1, source_target_pairs={{0,2},{2,4},{4,6},{7,5},{5,3},{3,1},{8,10},{10,12},{12,14},{15,13}... | collective-permute-start | bytes 1867784 | tf_op jit(solution)/shard_map/ppermute | solution.py:542
  146.5 1.5 collective-permute-done.18.come_ref.refs_1_.refs_0_
  148.6 4.5 %collective-permute-start.20 = (f32[64,2432]{1,0:T(8,128)S(1)}, f32[64,2432]{1,0:T(8,128)S(1)}, u32[]{:S(2)}, u32[]{:S(2)}) collective-permute-start(f32[64,2432]{1,0:T(8,128)S(1)} %shard_map.94.refs_2_), channel_id=1, source_target_pairs={{0,2},{2,4},{4,6},{7,5},{5,3},{3,1},{8,10},{10,12},{12,14},{15,13}... | collective-permute-start | bytes 1867784 | tf_op jit(solution)/shard_map/ppermute | solution.py:542
  153.2 1.5 collective-permute-done.22.come_ref.refs_2_.refs_1_.refs_0_
  155.3 4.4 %collective-permute-start.25 = (f32[64,2432]{1,0:T(8,128)S(1)}, f32[64,2432]{1,0:T(8,128)S(1)}, u32[]{:S(2)}, u32[]{:S(2)}) collective-permute-start(f32[64,2432]{1,0:T(8,128)S(1)} %shard_map.96.refs_2_), channel_id=1, source_target_pairs={{0,2},{2,4},{4,6},{7,5},{5,3},{3,1},{8,10},{10,12},{12,14},{15,13}... | collective-permute-start | bytes 1867784 | tf_op jit(solution)/shard_map/ppermute | solution.py:542
  159.8 1.5 collective-permute-done.20.come_ref.refs_2_.refs_1_.refs_0_
  161.9 4.4 %collective-permute-start.24 = (f32[64,2432]{1,0:T(8,128)S(1)}, f32[64,2432]{1,0:T(8,128)S(1)}, u32[]{:S(2)}, u32[]{:S(2)}) collective-permute-start(f32[64,2432]{1,0:T(8,128)S(1)} %shard_map.98._), channel_id=1, source_target_pairs={{0,2},{2,4},{4,6},{7,5},{5,3},{3,1},{8,10},{10,12},{12,14},{15,13}... | collective-permute-start | bytes 1867784 | tf_op jit(solution)/shard_map/ppermute | solution.py:542
  166.4 1.6 collective-permute-done.25.come_ref.refs_2_.refs_1_.refs_0_
  169.3 5.4 %collective-permute-done.24.come_ref.refs_2_.refs_1_.refs_0_ = f32[64,2432]{1,0:T(8,128)S(1)} collective-permute-done((f32[64,2432]{1,0:T(8,128)S(1)}, f32[64,2432]{1,0:T(8,128)S(1)}, u32[]{:S(2)}, u32[]{:S(2)}) %collective-permute-start.24) | collective-permute-done | bytes 622624 | tf_op jit(solution)/shard_map/ppermute | solution.py:542
  175.9 4.2 %shard_map.101 = (f32[3072,256]{1,0:T(8,128)}, f32[8,128]{1,0:T(8,128)S(1)}) custom-call(s32[1]{0:T(128)} %bitcast.me_ref, f32[64,3072]{1,0:T(8,128)S(1)} %shard_map.76.block_ref._.refs_6_.refs_0_, f32[64,3072]{1,0:T(8,128)S(1)} %collective-permute-done.6.refs_0_.refs_1_.refs_7_, f32[64,3072]{1,0:T(8,128)S(1)} %collective-permute-done.7.refs_1_.refs_0_.refs_8_.refs_2_, ...), custom_call_target="tpu_custom_call" | custom-call | bytes 73800 | tf_op jit(solution)/shard_map/pallas_call | solution.py:398
  186.0 4.1 %collective-permute-start.31 = (f32[64,2432]{1,0:T(8,128)S(1)}, f32[64,2432]{1,0:T(8,128)S(1)}, u32[]{:S(2)}, u32[]{:S(2)}) collective-permute-start(f32[64,2432]{1,0:T(8,128)S(1)} %shard_map.108.refs_2_.refs_10_), channel_id=1, source_target_pairs={{0,1},{1,0},{2,3},{3,2},{4,5},{5,4},{6,7},{7,6},{8,9},{9,8},{10,11... | collective-permute-start | bytes 1867784 | tf_op jit(solution)/shard_map/ppermute | solution.py:249
  195.2 13.8 %collective-permute-start.37 = (f32[64,2432]{1,0:T(8,128)S(1)}, f32[64,2432]{1,0:T(8,128)S(1)}, u32[]{:S(2)}, u32[]{:S(2)}) collective-permute-start(f32[64,2432]{1,0:T(8,128)S(1)} %shard_map.113.refs_22_.refs_24_), channel_id=1, source_target_pairs={{0,1},{1,0},{2,3},{3,2},{4,5},{5,4},{6,7},{7,6},{8,9},{9,8},{10,11... | collective-permute-start | bytes 1867784 | tf_op jit(solution)/shard_map/ppermute | solution.py:249
  213.3 5.7 %shard_map.114 = f32[256,4608]{1,0:T(8,128)} custom-call(s32[1]{0:T(128)} %bitcast.me_ref, f32[256,4608]{1,0:T(8,128)S(1)} %bitcast.4, f32[64,2432]{1,0:T(8,128)S(1)} %shard_map.80.refs_2_.refs_1_.refs_0_, f32[64,2432]{1,0:T(8,128)S(1)} %shard_map.102._.refs_1_, f32[64,2432]{1,0:T(8,128)S(1)} %collective-permute-done.26.refs_0_.refs_2_, ...), custom_call_target="tpu_custom_call" | custom-call | bytes 73800 | tf_op jit(solution)/shard_map/pallas_call | solution.py:622
  (100 shorter events, 30.1 us)
Async XLA Ops:
  1.3 1.9 copy-start
  6.6 32.2 %all-to-all-start = ((f32[8,72,384]{2,1,0:T(8,128)}), f32[8,72,384]{2,1,0:T(8,128)S(1)}, u32[]{:S(2)}, u32[]{:S(2)}) async-start(f32[8,72,384]{2,1,0:T(8,128)} %shard_map.68.refs_1_.pay_ref), calls=%async_computation | async-start | bytes 1769472 | tf_op jit(solution)/shard_map/all_to_all | solution.py:655
  27.8 9.4 %copy-start.1 = (f32[2,64,2048]{2,1,0:T(8,128)}, f32[2,64,2048]{2,1,0:T(8,128)S(1)}, u32[]{:S(2)}) copy-start(f32[2,64,2048]{2,1,0:T(8,128)S(1)} %get-tuple-element.36.refs_2_.refs_0_.refs_3_) | copy-start | bytes 3145732
  27.9 25.9 %collective-permute-start.3 = (f32[2,64,2048]{2,1,0:T(8,128)}, f32[2,64,2048]{2,1,0:T(8,128)}, u32[]{:S(2)}, u32[]{:S(2)}) collective-permute-start(f32[2,64,2048]{2,1,0:T(8,128)} %get-tuple-element.43), channel_id=1, source_target_pairs={{0,16},{8,24},{16,0},{24,8},{1,17},{9,25},{17,1},{25,9},{2,18},{10... | collective-permute-start | bytes 3145736 | tf_op jit(solution)/shard_map/ppermute | solution.py:249
  29.4 9.3 %copy-start.3 = (s32[12,256]{1,0:T(8,128)S(1)}, s32[12,256]{1,0:T(8,128)}, u32[]{:S(2)}) copy-start(s32[12,256]{1,0:T(8,128)} %code_ref.3) | copy-start | bytes 36868
  37.2 17.9 %copy-start.2 = (f32[2,64,1280]{2,1,0:T(8,128)}, f32[2,64,1280]{2,1,0:T(8,128)S(1)}, u32[]{:S(2)}) copy-start(f32[2,64,1280]{2,1,0:T(8,128)S(1)} %get-tuple-element.37._.refs_0_) | copy-start | bytes 1966084
  37.2 17.8 %collective-permute-start.2 = (f32[2,64,1280]{2,1,0:T(8,128)S(1)}, f32[2,64,1280]{2,1,0:T(8,128)}, u32[]{:S(2)}, u32[]{:S(2)}) collective-permute-start(f32[2,64,1280]{2,1,0:T(8,128)S(1)} %get-tuple-element.42), channel_id=1, source_target_pairs={{0,8},{8,0},{16,24},{24,16},{1,9},{9,1},{17,25},{25,17},{2,10},{10... | collective-permute-start | bytes 1966088 | tf_op jit(solution)/shard_map/ppermute | solution.py:249
  41.5 14.7 %collective-permute-start = (f32[72,256]{1,0:T(8,128)S(1)}, f32[72,256]{1,0:T(8,128)S(1)}, u32[]{:S(2)}, u32[]{:S(2)}) collective-permute-start(f32[72,256]{1,0:T(8,128)S(1)} %get-tuple-element.39), channel_id=1, source_target_pairs={{0,1},{1,2},{2,3},{3,4},{4,5},{5,6},{6,7},{8,9},{9,10},{10,11},{11... | collective-permute-start | bytes 221192 | tf_op jit(solution)/shard_map/ppermute | solution.py:686
  43.3 12.9 %collective-permute-start.1 = (f32[72,256]{1,0:T(8,128)S(1)}, f32[72,256]{1,0:T(8,128)S(1)}, u32[]{:S(2)}, u32[]{:S(2)}) collective-permute-start(f32[72,256]{1,0:T(8,128)S(1)} %get-tuple-element.40), channel_id=1, source_target_pairs={{1,0},{2,1},{3,2},{4,3},{5,4},{6,5},{7,6},{9,8},{10,9},{11,10},{12... | collective-permute-start | bytes 221192 | tf_op jit(solution)/shard_map/ppermute | solution.py:687
  60.4 27.8 %all-to-all-start.1 = ((f32[8,72,384]{2,1,0:T(8,128)}), f32[8,72,384]{2,1,0:T(8,128)S(1)}, u32[]{:S(2)}, u32[]{:S(2)}) async-start(f32[8,72,384]{2,1,0:T(8,128)} %shard_map.74.refs_7_), calls=%async_computation.1 | async-start | bytes 1769472 | tf_op jit(solution)/shard_map/all_to_all | solution.py:693
  65.1 14.3 %collective-permute-start.5 = (f32[1,64,2048]{2,1,0:T(8,128)S(1)}, f32[1,64,2048]{2,1,0:T(8,128)S(1)}, u32[]{:S(2)}, u32[]{:S(2)}) collective-permute-start(f32[1,64,2048]{2,1,0:T(8,128)S(1)} %shard_map.72.refs_2_), channel_id=1, source_target_pairs={{0,8},{8,0},{16,24},{24,16},{1,9},{9,1},{17,25},{25,17},{2,10},{10... | collective-permute-start | bytes 1572872 | tf_op jit(solution)/shard_map/ppermute | solution.py:249
  66.6 9.8 %collective-permute-start.4 = (f32[1,64,1280]{2,1,0:T(8,128)S(1)}, f32[1,64,1280]{2,1,0:T(8,128)S(1)}, u32[]{:S(2)}, u32[]{:S(2)}) collective-permute-start(f32[1,64,1280]{2,1,0:T(8,128)S(1)} %shard_map.73._), channel_id=1, source_target_pairs={{0,16},{8,24},{16,0},{24,8},{1,17},{9,25},{17,1},{25,9},{2,18},{10... | collective-permute-start | bytes 983048 | tf_op jit(solution)/shard_map/ppermute | solution.py:249
  76.5 3.0 %copy-start.6 = (f32[1,64,1280]{2,1,0:T(8,128)}, f32[1,64,1280]{2,1,0:T(8,128)S(1)}, u32[]{:S(2)}) copy-start(f32[1,64,1280]{2,1,0:T(8,128)S(1)} %collective-permute-done.4.refs_2_) | copy-start | bytes 983044
  88.2 0.9 copy-start.4
  92.0 19.1 %collective-permute-start.6 = (f32[64,3072]{1,0:T(8,128)S(1)}, f32[64,3072]{1,0:T(8,128)S(1)}, u32[]{:S(2)}, u32[]{:S(2)}) collective-permute-start(f32[64,3072]{1,0:T(8,128)S(1)} %shard_map.76.block_ref._.refs_6_.refs_0_), channel_id=1, source_target_pairs={{0,8},{8,0},{16,24},{24,16},{1,9},{9,1},{17,25},{25,17},{2,10},{10... | collective-permute-start | bytes 2359304 | tf_op jit(solution)/shard_map/ppermute | solution.py:249
  93.5 18.8 %collective-permute-start.7 = (f32[64,3072]{1,0:T(8,128)S(1)}, f32[64,3072]{1,0:T(8,128)S(1)}, u32[]{:S(2)}, u32[]{:S(2)}) collective-permute-start(f32[64,3072]{1,0:T(8,128)S(1)} %shard_map.76.block_ref._.refs_6_.refs_0_), channel_id=1, source_target_pairs={{0,16},{8,24},{16,0},{24,8},{1,17},{9,25},{17,1},{25,9},{2,18},{10... | collective-permute-start | bytes 2359304 | tf_op jit(solution)/shard_map/ppermute | solution.py:249
  105.2 7.2 %collective-permute-start.11 = (f32[64,2432]{1,0:T(8,128)S(1)}, f32[64,2432]{1,0:T(8,128)S(1)}, u32[]{:S(2)}, u32[]{:S(2)}) collective-permute-start(f32[64,2432]{1,0:T(8,128)S(1)} %get-tuple-element.55.refs_0_), channel_id=1, source_target_pairs={{0,1},{1,0},{2,3},{3,2},{4,5},{5,4},{6,7},{7,6},{8,9},{9,8},{10,11... | collective-permute-start | bytes 1867784 | tf_op jit(solution)/shard_map/ppermute | solution.py:249
  105.3 10.9 %collective-permute-start.10 = (f32[64,2432]{1,0:T(8,128)S(1)}, f32[64,2432]{1,0:T(8,128)S(1)}, u32[]{:S(2)}, u32[]{:S(2)}) collective-permute-start(f32[64,2432]{1,0:T(8,128)S(1)} %get-tuple-element.46.refs_2_.refs_0_), channel_id=1, source_target_pairs={{0,1},{1,0},{2,3},{3,2},{4,5},{5,4},{6,7},{7,6},{8,9},{9,8},{10,11... | collective-permute-start | bytes 1867784 | tf_op jit(solution)/shard_map/ppermute | solution.py:249
  112.5 13.4 %collective-permute-start.15 = (f32[64,2432]{1,0:T(8,128)S(1)}, f32[64,2432]{1,0:T(8,128)S(1)}, u32[]{:S(2)}, u32[]{:S(2)}) collective-permute-start(f32[64,2432]{1,0:T(8,128)S(1)} %shard_map.80.refs_2_.refs_1_.refs_0_), channel_id=1, source_target_pairs={{0,2},{7,5},{8,10},{15,13},{16,18},{23,21},{24,26},{31,29}} | collective-permute-start | bytes 1867784 | tf_op jit(solution)/shard_map/ppermute | solution.py:523
  114.0 8.7 %collective-permute-start.8 = (f32[64,1536]{1,0:T(8,128)S(1)}, f32[64,1536]{1,0:T(8,128)S(1)}, u32[]{:S(2)}, u32[]{:S(2)}) collective-permute-start(f32[64,1536]{1,0:T(8,128)S(1)} %get-tuple-element.47), channel_id=1, source_target_pairs={{0,8},{8,0},{16,24},{24,16},{1,9},{9,1},{17,25},{25,17},{2,10},{10... | collective-permute-start | bytes 1179656 | tf_op jit(solution)/shard_map/ppermute | solution.py:249
  114.6 10.6 %collective-permute-start.9 = (f32[64,1536]{1,0:T(8,128)S(1)}, f32[64,1536]{1,0:T(8,128)S(1)}, u32[]{:S(2)}, u32[]{:S(2)}) collective-permute-start(f32[64,1536]{1,0:T(8,128)S(1)} %get-tuple-element.48.refs_2_), channel_id=1, source_target_pairs={{0,16},{8,24},{16,0},{24,8},{1,17},{9,25},{17,1},{25,9},{2,18},{10... | collective-permute-start | bytes 1179656 | tf_op jit(solution)/shard_map/ppermute | solution.py:249
  116.2 12.2 %collective-permute-start.12 = (f32[64,2432]{1,0:T(8,128)S(1)}, f32[64,2432]{1,0:T(8,128)S(1)}, u32[]{:S(2)}, u32[]{:S(2)}) collective-permute-start(f32[64,2432]{1,0:T(8,128)S(1)} %shard_map.81.refs_9_.refs_1_.refs_2_.refs_3_), channel_id=1, source_target_pairs={{0,2},{7,5},{8,10},{15,13},{16,18},{23,21},{24,26},{31,29}} | collective-permute-start | bytes 1867784 | tf_op jit(solution)/shard_map/ppermute | solution.py:523
  120.4 8.1 %collective-permute-start.16 = (f32[64,2432]{1,0:T(8,128)S(1)}, f32[64,2432]{1,0:T(8,128)S(1)}, u32[]{:S(2)}, u32[]{:S(2)}) collective-permute-start(f32[64,2432]{1,0:T(8,128)S(1)} %get-tuple-element.59.refs_0_), channel_id=1, source_target_pairs={{0,1},{1,0},{2,3},{3,2},{4,5},{5,4},{6,7},{7,6},{8,9},{9,8},{10,11... | collective-permute-start | bytes 1867784 | tf_op jit(solution)/shard_map/ppermute | solution.py:249
  122.7 5.7 %collective-permute-start.17 = (f32[64,2432]{1,0:T(8,128)S(1)}, f32[64,2432]{1,0:T(8,128)S(1)}, u32[]{:S(2)}, u32[]{:S(2)}) collective-permute-start(f32[64,2432]{1,0:T(8,128)S(1)} %get-tuple-element.56.refs_9_.refs_1_), channel_id=1, source_target_pairs={{0,1},{1,0},{2,3},{3,2},{4,5},{5,4},{6,7},{7,6},{8,9},{9,8},{10,11... | collective-permute-start | bytes 1867784 | tf_op jit(solution)/shard_map/ppermute | solution.py:249
  125.2 8.4 %collective-permute-start.13 = (f32[64,2432]{1,0:T(8,128)S(1)}, f32[64,2432]{1,0:T(8,128)S(1)}, u32[]{:S(2)}, u32[]{:S(2)}) collective-permute-start(f32[64,2432]{1,0:T(8,128)S(1)} %get-tuple-element.58.refs_0_), channel_id=1, source_target_pairs={{0,1},{1,0},{2,3},{3,2},{4,5},{5,4},{6,7},{7,6},{8,9},{9,8},{10,11... | collective-permute-start | bytes 1867784 | tf_op jit(solution)/shard_map/ppermute | solution.py:249
  125.8 7.8 %collective-permute-start.14 = (f32[64,2432]{1,0:T(8,128)S(1)}, f32[64,2432]{1,0:T(8,128)S(1)}, u32[]{:S(2)}, u32[]{:S(2)}) collective-permute-start(f32[64,2432]{1,0:T(8,128)S(1)} %get-tuple-element.57.refs_2_.refs_1_), channel_id=1, source_target_pairs={{0,1},{1,0},{2,3},{3,2},{4,5},{5,4},{6,7},{7,6},{8,9},{9,8},{10,11... | collective-permute-start | bytes 1867784 | tf_op jit(solution)/shard_map/ppermute | solution.py:249
  129.1 13.4 %collective-permute-start.19 = (f32[64,2432]{1,0:T(8,128)S(1)}, f32[64,2432]{1,0:T(8,128)S(1)}, u32[]{:S(2)}, u32[]{:S(2)}) collective-permute-start(f32[64,2432]{1,0:T(8,128)S(1)} %shard_map.88.refs_4_), channel_id=1, source_target_pairs={{0,2},{2,4},{7,5},{5,3},{8,10},{10,12},{15,13},{13,11},{16,18},{18... | collective-permute-start | bytes 1867784 | tf_op jit(solution)/shard_map/ppermute | solution.py:542
  134.4 13.6 %collective-permute-start.18 = (f32[64,2432]{1,0:T(8,128)S(1)}, f32[64,2432]{1,0:T(8,128)S(1)}, u32[]{:S(2)}, u32[]{:S(2)}) collective-permute-start(f32[64,2432]{1,0:T(8,128)S(1)} %shard_map.90.refs_10_), channel_id=1, source_target_pairs={{0,2},{2,4},{7,5},{5,3},{8,10},{10,12},{15,13},{13,11},{16,18},{18... | collective-permute-start | bytes 1867784 | tf_op jit(solution)/shard_map/ppermute | solution.py:542
  139.4 13.7 %collective-permute-start.23 = (f32[64,2432]{1,0:T(8,128)S(1)}, f32[64,2432]{1,0:T(8,128)S(1)}, u32[]{:S(2)}, u32[]{:S(2)}) collective-permute-start(f32[64,2432]{1,0:T(8,128)S(1)} %shard_map.91.refs_10_.refs_0_), channel_id=1, source_target_pairs={{0,1},{1,0},{2,3},{3,2},{4,5},{5,4},{6,7},{7,6},{8,9},{9,8},{10,11... | collective-permute-start | bytes 1867784 | tf_op jit(solution)/shard_map/ppermute | solution.py:249
  143.2 11.5 %collective-permute-start.22 = (f32[64,2432]{1,0:T(8,128)S(1)}, f32[64,2432]{1,0:T(8,128)S(1)}, u32[]{:S(2)}, u32[]{:S(2)}) collective-permute-start(f32[64,2432]{1,0:T(8,128)S(1)} %shard_map.93._), channel_id=1, source_target_pairs={{0,2},{2,4},{4,6},{7,5},{5,3},{3,1},{8,10},{10,12},{12,14},{15,13}... | collective-permute-start | bytes 1867784 | tf_op jit(solution)/shard_map/ppermute | solution.py:542
  146.4 13.3 %collective-permute-start.21 = (f32[64,2432]{1,0:T(8,128)S(1)}, f32[64,2432]{1,0:T(8,128)S(1)}, u32[]{:S(2)}, u32[]{:S(2)}) collective-permute-start(f32[64,2432]{1,0:T(8,128)S(1)} %shard_map.92._.refs_0_), channel_id=1, source_target_pairs={{0,1},{1,0},{2,3},{3,2},{4,5},{5,4},{6,7},{7,6},{8,9},{9,8},{10,11... | collective-permute-start | bytes 1867784 | tf_op jit(solution)/shard_map/ppermute | solution.py:249
  148.6 12.7 %collective-permute-start.20 = (f32[64,2432]{1,0:T(8,128)S(1)}, f32[64,2432]{1,0:T(8,128)S(1)}, u32[]{:S(2)}, u32[]{:S(2)}) collective-permute-start(f32[64,2432]{1,0:T(8,128)S(1)} %shard_map.94.refs_2_), channel_id=1, source_target_pairs={{0,2},{2,4},{4,6},{7,5},{5,3},{3,1},{8,10},{10,12},{12,14},{15,13}... | collective-permute-start | bytes 1867784 | tf_op jit(solution)/shard_map/ppermute | solution.py:542
  155.3 12.7 %collective-permute-start.25 = (f32[64,2432]{1,0:T(8,128)S(1)}, f32[64,2432]{1,0:T(8,128)S(1)}, u32[]{:S(2)}, u32[]{:S(2)}) collective-permute-start(f32[64,2432]{1,0:T(8,128)S(1)} %shard_map.96.refs_2_), channel_id=1, source_target_pairs={{0,2},{2,4},{4,6},{7,5},{5,3},{3,1},{8,10},{10,12},{12,14},{15,13}... | collective-permute-start | bytes 1867784 | tf_op jit(solution)/shard_map/ppermute | solution.py:542
  161.9 12.7 %collective-permute-start.24 = (f32[64,2432]{1,0:T(8,128)S(1)}, f32[64,2432]{1,0:T(8,128)S(1)}, u32[]{:S(2)}, u32[]{:S(2)}) collective-permute-start(f32[64,2432]{1,0:T(8,128)S(1)} %shard_map.98._), channel_id=1, source_target_pairs={{0,2},{2,4},{4,6},{7,5},{5,3},{3,1},{8,10},{10,12},{12,14},{15,13}... | collective-permute-start | bytes 1867784 | tf_op jit(solution)/shard_map/ppermute | solution.py:542
  168.6 13.5 %collective-permute-start.29 = (f32[64,2432]{1,0:T(8,128)S(1)}, f32[64,2432]{1,0:T(8,128)S(1)}, u32[]{:S(2)}, u32[]{:S(2)}) collective-permute-start(f32[64,2432]{1,0:T(8,128)S(1)} %shard_map.99._), channel_id=1, source_target_pairs={{2,4},{4,6},{5,3},{3,1},{10,12},{12,14},{13,11},{11,9},{18,20},{20... | collective-permute-start | bytes 1867784 | tf_op jit(solution)/shard_map/ppermute | solution.py:542
  175.2 7.4 %collective-permute-start.28 = (f32[64,2432]{1,0:T(8,128)S(1)}, f32[64,2432]{1,0:T(8,128)S(1)}, u32[]{:S(2)}, u32[]{:S(2)}) collective-permute-start(f32[64,2432]{1,0:T(8,128)S(1)} %shard_map.100.refs_4_), channel_id=1, source_target_pairs={{2,4},{4,6},{5,3},{3,1},{10,12},{12,14},{13,11},{11,9},{18,20},{20... | collective-permute-start | bytes 1867784 | tf_op jit(solution)/shard_map/ppermute | solution.py:542
  181.4 2.3 %collective-permute-start.27 = (f32[64,2432]{1,0:T(8,128)S(1)}, f32[64,2432]{1,0:T(8,128)S(1)}, u32[]{:S(2)}, u32[]{:S(2)}) collective-permute-start(f32[64,2432]{1,0:T(8,128)S(1)} %shard_map.103._.refs_4_), channel_id=1, source_target_pairs={{0,1},{1,0},{2,3},{3,2},{4,5},{5,4},{6,7},{7,6},{8,9},{9,8},{10,11... | collective-permute-start | bytes 1867784 | tf_op jit(solution)/shard_map/ppermute | solution.py:249
  182.0 2.6 %collective-permute-start.26 = (f32[64,2432]{1,0:T(8,128)S(1)}, f32[64,2432]{1,0:T(8,128)S(1)}, u32[]{:S(2)}, u32[]{:S(2)}) collective-permute-start(f32[64,2432]{1,0:T(8,128)S(1)} %shard_map.102._.refs_1_), channel_id=1, source_target_pairs={{0,1},{1,0},{2,3},{3,2},{4,5},{5,4},{6,7},{7,6},{8,9},{9,8},{10,11... | collective-permute-start | bytes 1867784 | tf_op jit(solution)/shard_map/ppermute | solution.py:249
  186.0 5.8 %collective-permute-start.31 = (f32[64,2432]{1,0:T(8,128)S(1)}, f32[64,2432]{1,0:T(8,128)S(1)}, u32[]{:S(2)}, u32[]{:S(2)}) collective-permute-start(f32[64,2432]{1,0:T(8,128)S(1)} %shard_map.108.refs_2_.refs_10_), channel_id=1, source_target_pairs={{0,1},{1,0},{2,3},{3,2},{4,5},{5,4},{6,7},{7,6},{8,9},{9,8},{10,11... | collective-permute-start | bytes 1867784 | tf_op jit(solution)/shard_map/ppermute | solution.py:249
  190.1 2.6 %collective-permute-start.30 = (f32[64,2432]{1,0:T(8,128)S(1)}, f32[64,2432]{1,0:T(8,128)S(1)}, u32[]{:S(2)}, u32[]{:S(2)}) collective-permute-start(f32[64,2432]{1,0:T(8,128)S(1)} %shard_map.107._.refs_7_), channel_id=1, source_target_pairs={{0,1},{1,0},{2,3},{3,2},{4,5},{5,4},{6,7},{7,6},{8,9},{9,8},{10,11... | collective-permute-start | bytes 1867784 | tf_op jit(solution)/shard_map/ppermute | solution.py:249
  190.2 3.7 %collective-permute-start.34 = (f32[64,2432]{1,0:T(8,128)S(1)}, f32[64,2432]{1,0:T(8,128)S(1)}, u32[]{:S(2)}, u32[]{:S(2)}) collective-permute-start(f32[64,2432]{1,0:T(8,128)S(1)} %shard_map.104._), channel_id=1, source_target_pairs={{4,6},{3,1},{12,14},{11,9},{20,22},{19,17},{28,30},{27,25}} | collective-permute-start | bytes 1867784 | tf_op jit(solution)/shard_map/ppermute | solution.py:542
  190.9 3.7 %collective-permute-start.36 = (f32[64,2432]{1,0:T(8,128)S(1)}, f32[64,2432]{1,0:T(8,128)S(1)}, u32[]{:S(2)}, u32[]{:S(2)}) collective-permute-start(f32[64,2432]{1,0:T(8,128)S(1)} %shard_map.105.refs_2_), channel_id=1, source_target_pairs={{4,6},{3,1},{12,14},{11,9},{20,22},{19,17},{28,30},{27,25}} | collective-permute-start | bytes 1867784 | tf_op jit(solution)/shard_map/ppermute | solution.py:542
  192.7 20.6 %slice-start = ((s8[4718592]{0:T(1024)(128)(4,1)}), s8[4194304]{0:T(1024)(128)(4,1)S(1)}, s32[]{:S(2)}) async-start(s8[4718592]{0:T(1024)(128)(4,1)} %bitcast.3), calls=%async_computation.2 | async-start | bytes 8388608
  193.3 20.0 %slice-start.1 = ((s8[4718592]{0:T(1024)(128)(4,1)}), s8[524288]{0:T(1024)(128)(4,1)S(1)}, s32[]{:S(2)}) async-start(s8[4718592]{0:T(1024)(128)(4,1)} %bitcast.3), calls=%async_computation.3 | async-start | bytes 1048576
  195.2 15.4 %collective-permute-start.37 = (f32[64,2432]{1,0:T(8,128)S(1)}, f32[64,2432]{1,0:T(8,128)S(1)}, u32[]{:S(2)}, u32[]{:S(2)}) collective-permute-start(f32[64,2432]{1,0:T(8,128)S(1)} %shard_map.113.refs_22_.refs_24_), channel_id=1, source_target_pairs={{0,1},{1,0},{2,3},{3,2},{4,5},{5,4},{6,7},{7,6},{8,9},{9,8},{10,11... | collective-permute-start | bytes 1867784 | tf_op jit(solution)/shard_map/ppermute | solution.py:249
  209.0 2.6 %collective-permute-start.35 = (f32[64,2432]{1,0:T(8,128)S(1)}, f32[64,2432]{1,0:T(8,128)S(1)}, u32[]{:S(2)}, u32[]{:S(2)}) collective-permute-start(f32[64,2432]{1,0:T(8,128)S(1)} %shard_map.112._.refs_19_), channel_id=1, source_target_pairs={{0,1},{1,0},{2,3},{3,2},{4,5},{5,4},{6,7},{7,6},{8,9},{9,8},{10,11... | collective-permute-start | bytes 1867784 | tf_op jit(solution)/shard_map/ppermute | solution.py:249
  209.0 3.4 %collective-permute-start.33 = (f32[64,2432]{1,0:T(8,128)S(1)}, f32[64,2432]{1,0:T(8,128)S(1)}, u32[]{:S(2)}, u32[]{:S(2)}) collective-permute-start(f32[64,2432]{1,0:T(8,128)S(1)} %shard_map.111._.refs_16_), channel_id=1, source_target_pairs={{0,1},{1,0},{2,3},{3,2},{4,5},{5,4},{6,7},{7,6},{8,9},{9,8},{10,11... | collective-permute-start | bytes 1867784 | tf_op jit(solution)/shard_map/ppermute | solution.py:249
  209.5 3.8 %collective-permute-start.32 = (f32[64,2432]{1,0:T(8,128)S(1)}, f32[64,2432]{1,0:T(8,128)S(1)}, u32[]{:S(2)}, u32[]{:S(2)}) collective-permute-start(f32[64,2432]{1,0:T(8,128)S(1)} %shard_map.110._.refs_13_), channel_id=1, source_target_pairs={{0,1},{1,0},{2,3},{3,2},{4,5},{5,4},{6,7},{7,6},{8,9},{9,8},{10,11... | collective-permute-start | bytes 1867784 | tf_op jit(solution)/shard_map/ppermute | solution.py:249
  (1 other events, 0.8 us)
